TPU v7x, 32 devices: a whole 2x2x4 slice. The times are simulated.
32 devices in a mesh: dp: 8 (over z, y), seq: 4 (over x, core).
Axes of the slice: x: 2, y: 2, z: 4, core: 2. Of those that a mesh axis runs over, the one named last changes fastest.
Arguments:
- layer_in: bfloat16 [8192, 2048], P(('dp', 'seq')), may hold values from -6 to 6
- doc_lengths: int32 [8, 8], P('dp'), may hold values from 1 to 896, 1024 in all within a row
- norm_attn: bfloat16 [2048], P(('dp', 'seq')), may hold values from 0.5 to 1.5
- w_qkv: bfloat16 [2048, 2560], P(('dp', 'seq')), may hold values from -0.125 to 0.125
- w_out: bfloat16 [2048, 2048], P(('dp', 'seq')), may hold values from -0.5 to 0.5
- norm_mlp: bfloat16 [2048], P(('dp', 'seq')), may hold values from 0.5 to 1.5
- w_gateup: bfloat16 [2048, 11264], P(('dp', 'seq')), may hold values from -0.125 to 0.125
- w_down: bfloat16 [5632, 2048], P(('dp', 'seq')), may hold values from -0.078125 to 0.078125
- grad_out: bfloat16 [8192, 2048], P(('dp', 'seq')), may hold values from -6 to 6
Outputs:
- layer_out: float32 [8192, 2048], P(('dp', 'seq'))
- grad_in: float32 [8192, 2048], P(('dp', 'seq'))
- grad_norm_attn: float32 [2048], P(('dp', 'seq'))
- grad_w_qkv: float32 [2048, 2560], P(('dp', 'seq'))
- grad_w_out: float32 [2048, 2048], P(('dp', 'seq'))
- grad_norm_mlp: float32 [2048], P(('dp', 'seq'))
- grad_w_gateup: float32 [2048, 11264], P(('dp', 'seq'))
- grad_w_down: float32 [5632, 2048], P(('dp', 'seq'))
Inputs may be any that keep to these rules, and one draw needn't show every extreme that they name: `doc_lengths`: each row holds the lengths of the 8 documents of one group in order; a row sums to 1024, and its longest document has exactly 896 tokens.
All inputs are finite; a program needn't handle non-finite values.
Results may differ from a plain program's by a relative error of at most 0.013.
Values may be sent and summed in bfloat16 or wider, within the bound.
No kernel may reach another device: no remote copies, remote signals or barrier semaphores. Data moves between devices by JAX's collectives and lax.ppermute only.
A program may use at most 384 MiB of HBM per device.

v0:
```python
import math

import jax
import jax.numpy as jnp
from jax import lax
from jax.sharding import PartitionSpec as P

HEADS = 32
HEAD = 64
KVH = 4
FF = 5632


epsilon = 1e-05
rope_base = 10000.0
neg_large = -1e30
narrow_type = jnp.bfloat16
wide_type = jnp.float32


def doc_layout(length_row, row_count):
    doc_ends = jnp.cumsum(length_row)
    doc_starts = doc_ends - length_row
    where_at = jnp.arange(row_count, dtype=jnp.int32)
    segment = jnp.sum((where_at[:, None] >= doc_ends[None, :]).astype(jnp.int32), axis=1)
    member = segment[:, None] == jnp.arange(length_row.shape[0], dtype=jnp.int32)[None, :]
    doc_begin = jnp.sum(jnp.where(member, doc_starts[None, :], 0), axis=1)
    return (segment, where_at - doc_begin)


def angle_tables(position, head_size):
    half_size = head_size // 2
    freq_row = rope_base ** (-2.0 * jnp.arange(half_size, dtype=wide_type) / head_size)
    angles = position.astype(wide_type)[:, None] * freq_row[None, :]
    return (jnp.cos(angles), jnp.sin(angles))


def rotate(vector, cos_table, sin_table):
    half_size = vector.shape[-1] // 2
    front_half = vector[..., :half_size]
    back_half = vector[..., half_size:]
    return jnp.concatenate(
        [
            front_half * cos_table - back_half * sin_table,
            back_half * cos_table + front_half * sin_table,
        ],
        axis=-1,
    )


def unrotate(vector, cos_table, sin_table):
    half_size = vector.shape[-1] // 2
    front_half = vector[..., :half_size]
    back_half = vector[..., half_size:]
    return jnp.concatenate(
        [
            front_half * cos_table + back_half * sin_table,
            back_half * cos_table - front_half * sin_table,
        ],
        axis=-1,
    )


def contract_rows(left, right):
    return lax.dot_general(left, right, (((0,), (0,)), ((), ())), preferred_element_type=wide_type)


def contract_cols(left, right):
    return lax.dot_general(left, right, (((1,), (1,)), ((), ())), preferred_element_type=wide_type)


def norm_back(grad_normed, resid, inverse, gain):
    gain_grad = jnp.sum(grad_normed * resid * inverse, axis=0)
    scaled = grad_normed * gain
    grad_resid = inverse * scaled - resid * (inverse * inverse * inverse) * jnp.mean(
        scaled * resid, axis=-1, keepdims=True
    )
    return (gain_grad, grad_resid)


def attend_forward(queries, keys_rot, values, segment, position, block_rows):
    group_rows = keys_rot.shape[0]
    block_count = group_rows // block_rows
    factor = 1.0 / math.sqrt(keys_rot.shape[1])
    query_blocks = queries.reshape(block_count, block_rows, queries.shape[1], queries.shape[2])
    seg_blocks = segment.reshape(block_count, block_rows)
    pos_blocks = position.reshape(block_count, block_rows)

    def one_block(pieces):
        query_block, seg_block, pos_block = pieces
        scores = (
            jnp.einsum("qhd,kd->hqk", query_block, keys_rot, preferred_element_type=wide_type)
            * factor
        )
        allowed = (seg_block[:, None] == segment[None, :]) & (
            pos_block[:, None] >= position[None, :]
        )
        scores = jnp.where(allowed[None], scores, neg_large)
        row_top = jnp.max(scores, axis=-1, keepdims=True)
        raised = jnp.exp(scores - row_top)
        row_total = jnp.sum(raised, axis=-1, keepdims=True)
        shares = (raised / row_total).astype(narrow_type)
        mixed_heads = jnp.einsum("hqk,kd->qhd", shares, values, preferred_element_type=wide_type)
        return (mixed_heads, (row_top + jnp.log(row_total))[..., 0])

    mixed_heads, log_total = lax.map(one_block, (query_blocks, seg_blocks, pos_blocks))
    return (mixed_heads.reshape(group_rows, queries.shape[1] * queries.shape[2]), log_total)


def attend_backward(
    queries, keys_rot, values, grad_mixed, log_total, segment, position, block_rows
):
    group_rows = keys_rot.shape[0]
    block_count = group_rows // block_rows
    factor = 1.0 / math.sqrt(keys_rot.shape[1])
    query_blocks = queries.reshape(block_count, block_rows, queries.shape[1], queries.shape[2])
    grad_blocks = grad_mixed.reshape(block_count, block_rows, queries.shape[1], queries.shape[2])
    seg_blocks = segment.reshape(block_count, block_rows)
    pos_blocks = position.reshape(block_count, block_rows)

    def one_block(running, pieces):
        grad_keys, grad_values = running
        query_block, grad_block, total_block, seg_block, pos_block = pieces
        scores = (
            jnp.einsum("qhd,kd->hqk", query_block, keys_rot, preferred_element_type=wide_type)
            * factor
        )
        allowed = (seg_block[:, None] == segment[None, :]) & (
            pos_block[:, None] >= position[None, :]
        )
        shares = jnp.where(allowed[None], jnp.exp(scores - total_block[:, :, None]), 0.0)
        grad_shares = jnp.einsum(
            "qhd,kd->hqk", grad_block, values, preferred_element_type=wide_type
        )
        inner_row = jnp.sum(shares * grad_shares, axis=-1, keepdims=True)
        grad_scores = (shares * (grad_shares - inner_row)).astype(narrow_type)
        grad_query = (
            jnp.einsum("hqk,kd->qhd", grad_scores, keys_rot, preferred_element_type=wide_type)
            * factor
        )
        grad_keys = (
            grad_keys
            + jnp.einsum("hqk,qhd->kd", grad_scores, query_block, preferred_element_type=wide_type)
            * factor
        )
        grad_values = grad_values + jnp.einsum(
            "hqk,qhd->kd", shares.astype(narrow_type), grad_block, preferred_element_type=wide_type
        )
        return ((grad_keys, grad_values), grad_query)

    empty = jnp.zeros(keys_rot.shape, wide_type)
    (grad_keys, grad_values), grad_queries = lax.scan(
        one_block, (empty, empty), (query_blocks, grad_blocks, log_total, seg_blocks, pos_blocks)
    )
    return (grad_queries.reshape(queries.shape), grad_keys, grad_values)


def body(layer_in, doc_lengths, norm_attn, w_qkv, w_out, norm_mlp, w_gateup, w_down, grad_out):
    gain_attn, full_qkv, full_out = (
        lax.all_gather(norm_attn, ("dp", "seq"), axis=0, tiled=True),
        lax.all_gather(w_qkv, ("dp", "seq"), axis=0, tiled=True),
        lax.all_gather(w_out, ("dp", "seq"), axis=0, tiled=True),
    )
    seq_count = lax.axis_size("seq")
    tok_rows = layer_in.shape[0]
    group_rows = tok_rows * seq_count
    block_rows = min(512, group_rows)
    per_group = HEADS // KVH
    q_width = per_group * HEAD
    segment, position = doc_layout(doc_lengths[0], group_rows)
    cos_table, sin_table = angle_tables(position, HEAD)
    resid_in = layer_in.astype(wide_type)
    inv_one = lax.rsqrt(jnp.mean(resid_in * resid_in, axis=-1, keepdims=True) + epsilon)
    gain_one = gain_attn.astype(wide_type)
    normed_one = (resid_in * inv_one * gain_one).astype(narrow_type)
    projected = jnp.dot(normed_one, full_qkv, preferred_element_type=wide_type).astype(narrow_type)
    head_cols = lax.all_to_all(projected, "seq", split_axis=1, concat_axis=0, tiled=True)
    queries = rotate(
        head_cols[:, :q_width].astype(wide_type).reshape(group_rows, per_group, HEAD),
        cos_table[:, None, :],
        sin_table[:, None, :],
    ).astype(narrow_type)
    keys_rot = rotate(
        head_cols[:, q_width : q_width + HEAD].astype(wide_type), cos_table, sin_table
    ).astype(narrow_type)
    values = head_cols[:, q_width + HEAD :]
    mixed_heads, log_total = attend_forward(
        queries, keys_rot, values, segment, position, block_rows
    )
    mixed_tok = lax.all_to_all(
        mixed_heads.astype(narrow_type), "seq", split_axis=0, concat_axis=1, tiled=True
    )
    resid_mid = resid_in + jnp.dot(mixed_tok, full_out, preferred_element_type=wide_type)
    gain_mlp, full_gateup, full_down = (
        lax.all_gather(norm_mlp, ("dp", "seq"), axis=0, tiled=True),
        lax.all_gather(w_gateup, ("dp", "seq"), axis=0, tiled=True),
        lax.all_gather(w_down, ("dp", "seq"), axis=0, tiled=True),
    )
    inv_two = lax.rsqrt(jnp.mean(resid_mid * resid_mid, axis=-1, keepdims=True) + epsilon)
    gain_two = gain_mlp.astype(wide_type)
    normed_two = (resid_mid * inv_two * gain_two).astype(narrow_type)
    gate_up = jnp.dot(normed_two, full_gateup, preferred_element_type=wide_type)
    gate_part = gate_up[:, :FF]
    up_part = gate_up[:, FF:]
    gate_sig = jax.nn.sigmoid(gate_part)
    swished = gate_part * gate_sig
    activated = (swished * up_part).astype(narrow_type)
    layer_out = resid_mid + jnp.dot(activated, full_down, preferred_element_type=wide_type)
    grad_act = contract_cols(grad_out, full_down)
    grad_gate = grad_act * up_part * gate_sig * (1.0 + gate_part * (1.0 - gate_sig))
    grad_up = grad_act * swished
    grad_gate_up = jnp.concatenate([grad_gate, grad_up], axis=1).astype(narrow_type)
    grad_normed_two = contract_cols(grad_gate_up, full_gateup)
    gain_grad_two, grad_from_two = norm_back(grad_normed_two, resid_mid, inv_two, gain_two)
    grad_mid = grad_out.astype(wide_type) + grad_from_two
    grad_down = contract_rows(activated, grad_out)
    grad_gateup = contract_rows(normed_two, grad_gate_up)
    grad_mid_low = grad_mid.astype(narrow_type)
    grad_mixed = contract_cols(grad_mid_low, full_out).astype(narrow_type)
    grad_heads = lax.all_to_all(grad_mixed, "seq", split_axis=1, concat_axis=0, tiled=True)
    grad_queries, grad_keys, grad_values = attend_backward(
        queries,
        keys_rot,
        values,
        grad_heads.reshape(group_rows, per_group, HEAD),
        log_total,
        segment,
        position,
        block_rows,
    )
    grad_q_plain = unrotate(grad_queries, cos_table[:, None, :], sin_table[:, None, :]).reshape(
        group_rows, q_width
    )
    grad_k_plain = unrotate(grad_keys, cos_table, sin_table)
    grad_cols = jnp.concatenate([grad_q_plain, grad_k_plain, grad_values], axis=1).astype(
        narrow_type
    )
    grad_projected = lax.all_to_all(grad_cols, "seq", split_axis=0, concat_axis=1, tiled=True)
    grad_normed_one = contract_cols(grad_projected, full_qkv)
    gain_grad_one, grad_from_one = norm_back(grad_normed_one, resid_in, inv_one, gain_one)
    grad_in = grad_mid + grad_from_one
    grad_wout = contract_rows(mixed_tok, grad_mid_low)
    grad_qkv = contract_rows(normed_one, grad_projected)
    grad_norm_mlp, grad_w_gateup, grad_w_down, grad_norm_attn, grad_w_qkv, grad_w_out = (
        lax.psum_scatter(gain_grad_two, ("dp", "seq"), scatter_dimension=0, tiled=True),
        lax.psum_scatter(grad_gateup, ("dp", "seq"), scatter_dimension=0, tiled=True),
        lax.psum_scatter(grad_down, ("dp", "seq"), scatter_dimension=0, tiled=True),
        lax.psum_scatter(gain_grad_one, ("dp", "seq"), scatter_dimension=0, tiled=True),
        lax.psum_scatter(grad_qkv, ("dp", "seq"), scatter_dimension=0, tiled=True),
        lax.psum_scatter(grad_wout, ("dp", "seq"), scatter_dimension=0, tiled=True),
    )
    return (
        layer_out,
        grad_in,
        grad_norm_attn,
        grad_w_qkv,
        grad_w_out,
        grad_norm_mlp,
        grad_w_gateup,
        grad_w_down,
    )


def solution(mesh):
    placed = (
        P(("dp", "seq"), None),
        P("dp", None),
        P(("dp", "seq")),
        P(("dp", "seq"), None),
        P(("dp", "seq"), None),
        P(("dp", "seq")),
        P(("dp", "seq"), None),
        P(("dp", "seq"), None),
        P(("dp", "seq"), None),
    )
    return jax.shard_map(
        body,
        mesh=mesh,
        in_specs=placed,
        out_specs=(
            P(("dp", "seq"), None),
            P(("dp", "seq"), None),
            P(("dp", "seq")),
            P(("dp", "seq"), None),
            P(("dp", "seq"), None),
            P(("dp", "seq")),
            P(("dp", "seq"), None),
            P(("dp", "seq"), None),
        ),
        check_vma=False,
    )
```

profile of v0, /device:TPU:11, one launch (start us, length us, event | category | flops | bytes accessed | tf_op | source)
XLA Modules:
  0.0 2554.0 jit_solution(3850318189736347153)
XLA Ops:
  12.5 40.1 %all-reduce.5 = (bf16[2048]{0:T(1024)(128)(2,1)S(1)}, bf16[2048]{0:T(1024)(128)(2,1)}) all-reduce(bf16[2048]{0:T(1024)(128)(2,1)S(1)} %dynamic-update-slice, bf16[2048]{0:T(1024)(128)(2,1)S(1)} %dynamic-update-slice.1), channel_id=1, replica_groups=mesh['dp'=8,'seq'=4] {'dp','seq'}, use_global_device_ids=true, to_apply=%add | all-reduce | flops 4096 | bytes 16384
  53.5 45.9 %all-gather.5.cloned.1.call-done = bf16[2048,2560]{1,0:T(8,128)(2,1)} async-done(((bf16[64,2560]{1,0:T(8,128)(2,1)}), bf16[2048,2560]{1,0:T(8,128)(2,1)}) %all-gather.5.cloned.1.call-update) | async-done | bytes 10485776 | tf_op jit(solution)/shard_map/all_gather | solution.py:161
  99.5 6.9 convolution_convert_fusion
  106.4 1.2 copy.91
  107.5 4.4 all-to-all-start
  112.8 14.5 all-to-all-done
  127.3 1.3 copy.74
  128.6 1.7 convert.52
  132.3 1.2 fusion.72
  135.1 1.4 pad_maximum_fusion.4
  137.7 1.5 pad_maximum_fusion.6
  139.2 29.4 %while.27 = (s32[]{:T(128)}, bf16[2,512,8,64]{1,3,2,0:T(8,128)(2,1)S(1)}, f32[2,8,512]{2,1,0:T(8,128)}, s32[2,512]{1,0:T(2,128)S(1)}, s32[1024]{0:T(1024)S(1)}, ...) while((s32[]{:T(128)}, ...), condition=%wide.region_7.8_spmd, body=%wide.region_4.7_spmd.sunk | while | flops 1125642240 | bytes 54415492 | solution.py:106
  139.7 3.7 bitcast_reduce_fusion.2
  143.5 4.4 fusion.122
  147.8 5.5 fusion.123
  154.5 3.7 bitcast_reduce_fusion.2
  158.2 4.4 fusion.122
  162.5 5.5 fusion.123
  169.6 2.4 copy.60
  173.6 5.2 all-to-all-start.1
  180.1 11.2 all-to-all-done.1
  192.3 6.7 multiply_reduce_fusion.2
  199.1 236.2 %all-gather.9.cloned.1.call-done = bf16[2048,11264]{1,0:T(8,128)(2,1)} async-done(((bf16[64,11264]{1,0:T(8,128)(2,1)}), bf16[2048,11264]{1,0:T(8,128)(2,1)}) %all-gather.9.cloned.1.call-update) | async-done | bytes 46137360 | tf_op jit(solution)/shard_map/all_gather | solution.py:196
  435.3 23.5 fusion.83
  458.8 121.9 %all-gather.11.cloned.1.call-done = bf16[5632,2048]{1,0:T(8,128)(2,1)} async-done(((bf16[176,2048]{1,0:T(8,128)(2,1)}), bf16[5632,2048]{1,0:T(8,128)(2,1)}) %all-gather.11.cloned.1.call-update) | async-done | bytes 23068688 | tf_op jit(solution)/shard_map/all_gather | solution.py:197
  580.7 18.5 multiply_convert_fusion.1
  599.3 22.0 multiply_reduce_fusion
  621.3 3.2 subtract_add_fusion
  624.6 8.2 fusion.57
  632.8 6.7 convolution_convert_fusion.1
  639.5 2.3 copy.71
  641.8 4.2 all-to-all-start.2
  646.0 26.8 %all-to-all-done.2 = bf16[256,4,512]{0,2,1:T(8,128)(2,1)S(1)} async-done(((bf16[256,4,512]{0,2,1:T(8,128)(2,1)}), bf16[256,4,512]{0,2,1:T(8,128)(2,1)S(1)}, u32[]{:S(2)}, u32[]{:S(2)}) %all-to-all-start.2) | async-done | bytes 1048608 | tf_op jit(solution)/shard_map/all_to_all | solution.py:220
  674.5 1.2 copy.65
  675.7 127.0 %while.28 = (s32[]{:T(128)}, f32[1024,64]{0,1:T(8,128)}, f32[1024,64]{0,1:T(8,128)}, f32[2,512,8,64]{1,0,3,2:T(2,128)}, s32[2,512]{1,0:T(2,128)S(1)}, /*index=5*...) while((s32[]{:T(128)}, f32[1024,64]{0,1:T(8,128)}, ...), condition=%wide.region_12.13_spmd.clone, body=%wide.region_10.12_spmd.clone.sunk | while | flops 2724261888 | bytes 167367056 | solution.py:152
  675.7 3.5 fusion.132
  679.8 1.3 compare_and_fusion.5
  681.1 10.5 fusion.133
  691.6 9.5 fusion.134
  701.1 6.0 fusion.135
  707.1 7.7 fusion.136
  714.8 3.6 fusion.137
  719.6 19.6 dynamic_update_slice.19
  739.2 3.5 fusion.132
  743.3 1.3 compare_and_fusion.5
  744.6 10.5 fusion.133
  755.1 9.5 fusion.134
  764.6 6.0 fusion.135
  770.5 7.7 fusion.136
  778.3 3.6 fusion.137
  783.1 19.6 dynamic_update_slice.19
  803.7 3.3 reshape.326
  809.2 30.3 %all_to_all.67 = bf16[4,256,640]{1,2,0:T(8,128)(2,1)S(1)} all-to-all(bf16[4,256,640]{1,2,0:T(8,128)(2,1)S(1)} %pad_maximum_fusion.3), channel_id=1, replica_groups=mesh['dp'=8,'seq'=4] {'seq'}, dimensions={0} | all-to-all | bytes 2621440 | tf_op jit(solution)/shard_map/all_to_all | solution.py:238
  840.5 8.9 fusion.60
  850.6 20.4 fusion.85
  871.2 1.5 copy-done.4
  872.7 35.4 %fusion.46 = f32[2048,11264]{1,0:T(8,128)} fusion(bf16[256,5632]{1,0:T(8,128)(2,1)} %get-tuple-element.332, bf16[256,5632]{1,0:T(8,128)(2,1)} %get-tuple-element.331, f32[256,2048]{1,0:T(8,128)S(1)} %copy-done.4, f32[2048]{0:T(1024)S(1)} %copy-done.23, f32[256]{0:T(256)S(1)} %copy-done.25), kind=kOutput, calls=%fused_computation.71 | convolution fusion | flops 11824267264 | bytes 100148224 | tf_op jit(solution)/shard_map/dot_general | solution.py:65
  908.1 12.8 convolution_add_fusion
  921.0 8.7 fusion.56
  929.6 42.7 %all-reduce.4 = (f32[2048]{0:T(1024)S(1)}, f32[2048]{0:T(1024)S(1)}) all-reduce(f32[2048]{0:T(1024)S(1)} %get-tuple-element.271, f32[2048]{0:T(1024)S(1)} %copy-done.35), channel_id=2, replica_groups=mesh['dp'=8,'seq'=4] {'dp','seq'}, use_global_device_ids=true, to_apply=%region_15.16.clone | all-reduce | flops 4096 | bytes 32768
  973.5 3.5 fusion.53
  977.0 102.3 %reduce-scatter.5.cloned.1.call-done = f32[64,2560]{1,0:T(8,128)} async-done(((f32[2048,2560]{1,0:T(8,128)}), f32[64,2560]{1,0:T(8,128)}) %reduce-scatter.5.cloned.1.call-update) | async-done | bytes 655376 | tf_op jit(solution)/shard_map/reduce_scatter | solution.py:249
  1079.3 492.8 %reduce-scatter.11.cloned.1.call-done = f32[176,2048]{1,0:T(8,128)} async-done(((f32[5632,2048]{1,0:T(8,128)}), f32[176,2048]{1,0:T(8,128)}) %reduce-scatter.11.cloned.1.call-update) | async-done | bytes 1441808 | tf_op jit(solution)/shard_map/reduce_scatter | solution.py:247
  1572.1 974.9 %reduce-scatter.9.cloned.1.call-done = f32[64,11264]{1,0:T(8,128)} async-done(((f32[2048,11264]{1,0:T(8,128)}), f32[64,11264]{1,0:T(8,128)}) %reduce-scatter.9.cloned.1.call-update) | async-done | bytes 2883600 | tf_op jit(solution)/shard_map/reduce_scatter | solution.py:246
  (180 shorter events, 30.6 us)
Async XLA Ops:
  7.2 45.5 %copy-start.5 = (bf16[256,2048]{1,0:T(8,128)(2,1)S(1)}, bf16[256,2048]{1,0:T(8,128)(2,1)}, u32[]{:S(2)}) copy-start(bf16[256,2048]{1,0:T(8,128)(2,1)} %param.13) | copy-start | bytes 3145732
  7.2 92.3 %all-gather.5.cloned.1.call-start = ((), (), s32[]{:S(2)}) async-start(), calls=%async_computation.8 | async-start | bytes 10813440 | tf_op jit(solution)/shard_map/all_gather | solution.py:161
  7.9 172.2 %all-gather.7.cloned.1.call-start = ((), (), s32[]{:S(2)}) async-start(), calls=%async_computation.9 | async-start | bytes 8650752 | tf_op jit(solution)/shard_map/all_gather | solution.py:162
  8.7 426.6 %all-gather.9.cloned.1.call-start = ((), (), s32[]{:S(2)}) async-start(), calls=%async_computation.10 | async-start | bytes 47579136 | tf_op jit(solution)/shard_map/all_gather | solution.py:196
  9.4 571.4 %all-gather.11.cloned.1.call-start = ((), (), s32[]{:S(2)}) async-start(), calls=%async_computation.11 | async-start | bytes 23789568 | tf_op jit(solution)/shard_map/all_gather | solution.py:197
  52.7 53.7 %copy-start.29 = (f32[2048]{0:T(1024)}, f32[2048]{0:T(1024)S(1)}, u32[]{:S(2)}) copy-start(f32[2048]{0:T(1024)S(1)} %convert_element_type.68) | copy-start | bytes 24580
  53.5 52.8 %copy-start.33 = (f32[256]{0:T(256)}, f32[256]{0:T(256)S(1)}, u32[]{:S(2)}) copy-start(f32[256]{0:T(256)S(1)} %get-tuple-element.349) | copy-start | bytes 3076
  106.4 5.7 copy-start.40
  107.5 19.7 all-to-all-start
  112.1 20.2 copy-start.38
  112.8 19.6 copy-start.31
  133.6 0.7 copy-start.16
  133.6 0.7 copy-start.18
  134.7 4.6 copy-start.20
  135.0 4.2 copy-start.27
  168.7 1.0 copy-start.21
  169.6 3.9 copy-start.14
  172.0 7.2 copy-start.37
  173.6 17.8 all-to-all-start.1
  178.8 798.2 %reduce-scatter.7.cloned.1.call-start = ((), (), s32[]{:S(2)}) async-start(), calls=%async_computation.13 | async-start | bytes 17301504 | tf_op jit(solution)/shard_map/reduce_scatter | solution.py:250
  179.2 442.1 %copy-start.22 = (f32[2048]{0:T(1024)}, f32[2048]{0:T(1024)S(1)}, u32[]{:S(2)}) copy-start(f32[2048]{0:T(1024)S(1)} %convert_element_type.75) | copy-start | bytes 24580
  191.3 1.0 copy-start.7
  199.1 400.2 %copy-start.3 = (f32[256,2048]{1,0:T(8,128)}, f32[256,2048]{1,0:T(8,128)S(1)}, u32[]{:S(2)}) copy-start(f32[256,2048]{1,0:T(8,128)S(1)} %get-tuple-element.353) | copy-start | bytes 6291460
  199.1 422.2 %copy-start.24 = (f32[256]{0:T(256)}, f32[256]{0:T(256)S(1)}, u32[]{:S(2)}) copy-start(f32[256]{0:T(256)S(1)} %get-tuple-element.351) | copy-start | bytes 3076
  621.3 3.3 copy-start.8
  624.6 8.2 copy-start.1
  641.8 31.0 %all-to-all-start.2 = ((bf16[256,4,512]{0,2,1:T(8,128)(2,1)}), bf16[256,4,512]{0,2,1:T(8,128)(2,1)S(1)}, u32[]{:S(2)}, u32[]{:S(2)}) async-start(bf16[256,4,512]{0,2,1:T(8,128)(2,1)} %bitcast.20), calls=%async_computation.2 | async-start | bytes 2097152 | tf_op jit(solution)/shard_map/all_to_all | solution.py:220
  646.0 433.3 %reduce-scatter.5.cloned.1.call-start = ((), (), s32[]{:S(2)}) async-start(), calls=%async_computation.12 | async-start | bytes 21626880 | tf_op jit(solution)/shard_map/reduce_scatter | solution.py:249
  675.7 3.5 copy-start.26
  675.7 4.1 copy-start.28
  701.1 6.0 copy-start
  701.1 6.0 copy-start.9
  701.1 13.7 slice-start
  707.0 7.8 slice-start.1
  714.8 3.7 copy-start.10
  739.2 3.5 copy-start.26
  739.2 4.1 copy-start.28
  764.5 6.0 copy-start
  764.6 6.0 copy-start.9
  764.6 13.7 slice-start
  770.5 7.8 slice-start.1
  778.3 3.7 copy-start.10
  802.7 4.3 copy-start.17
  802.7 4.3 copy-start.19
  807.4 1.1 copy-start.11
  807.4 1.1 copy-start.32
  807.4 1.1 copy-start.39
  808.4 32.1 %copy-start.6 = (bf16[256,2048]{1,0:T(8,128)(2,1)S(1)}, bf16[256,2048]{1,0:T(8,128)(2,1)}, u32[]{:S(2)}) copy-start(bf16[256,2048]{1,0:T(8,128)(2,1)} %param.13) | copy-start | bytes 3145732
  808.5 32.1 %copy-start.30 = (f32[2048]{0:T(1024)S(1)}, f32[2048]{0:T(1024)}, u32[]{:S(2)}) copy-start(f32[2048]{0:T(1024)} %copy-done.29) | copy-start | bytes 24580
  808.5 32.1 %copy-start.34 = (f32[256]{0:T(256)S(1)}, f32[256]{0:T(256)}, u32[]{:S(2)}) copy-start(f32[256]{0:T(256)} %copy-done.33) | copy-start | bytes 3076
  839.4 1.1 copy-start.12
  849.4 1.2 copy-start.15
  849.4 722.7 %reduce-scatter.11.cloned.1.call-start = ((), (), s32[]{:S(2)}) async-start(), calls=%async_computation.15 | async-start | bytes 47579136 | tf_op jit(solution)/shard_map/reduce_scatter | solution.py:247
  871.1 1.6 copy-start.4
  871.1 1.6 copy-start.23
  871.1 1.6 copy-start.25
  871.1 1675.9 %reduce-scatter.9.cloned.1.call-start = ((), (), s32[]{:S(2)}) async-start(), calls=%async_computation.14 | async-start | bytes 95158272 | tf_op jit(solution)/shard_map/reduce_scatter | solution.py:246
  908.1 12.8 copy-start.13
  920.9 8.7 copy-start.35
  921.0 52.6 %copy-start.2 = (f32[256,2048]{1,0:T(8,128)S(1)}, f32[256,2048]{1,0:T(8,128)}, u32[]{:S(2)}) copy-start(f32[256,2048]{1,0:T(8,128)} %copy-done.1) | copy-start | bytes 6291460
  921.0 52.6 %copy-start.36 = (f32[256]{0:T(256)S(1)}, f32[256]{0:T(256)}, u32[]{:S(2)}) copy-start(f32[256]{0:T(256)} %get-tuple-element.348) | copy-start | bytes 3076
Sparse Core Ops, SparseCore 0:
  10.8 88.5 all-gather.4
  102.3 77.7 all-gather.6
  183.0 252.2 all-gather.8
  438.0 142.7 all-gather.10
  632.9 206.0 reduce-scatter.6
  849.6 229.7 reduce-scatter.4
  1082.2 489.8 reduce-scatter.10
  1575.0 971.9 reduce-scatter.8
where the time goes:
time: 2570 us; the launch traced here: 2550 us
  waiting for transfers between devices  2030 us (79%)
  matrix products  260 us (10%)
  blocking collectives  113 us (4%)
  local copies, waits for them, and re-layouts  71.6 us (3%)
  other arithmetic  49.9 us (2%)
    reduce_scatter x1, waiting for transfers between devices, body(): lax.psum_scatter(grad_gateup, ('dp', 'seq'), scatter_dimension=0, tiled=T...  975 us
    reduce_scatter x1, waiting for transfers between devices, body(): lax.psum_scatter(grad_down, ('dp', 'seq'), scatter_dimension=0, tiled=True)  493 us
    all_gather x1, waiting for transfers between devices, body(): lax.all_gather(w_gateup, ('dp', 'seq'), axis=0, tiled=True)  236 us
    all_gather x1, waiting for transfers between devices, body(): lax.all_gather(w_down, ('dp', 'seq'), axis=0, tiled=True)  122 us
    reduce_scatter x1, waiting for transfers between devices, body(): lax.psum_scatter(grad_qkv, ('dp', 'seq'), scatter_dimension=0, tiled=True)  102 us
    unnamed x2, blocking collectives  82.8 us
    dot_general x4, matrix products, contract_rows(): lax.dot_general(left, right, (((0,), (0,)), ((), ())), preferred_element_...  72.9 us
    dot_general x4, matrix products, contract_cols(): lax.dot_general(left, right, (((1,), (1,)), ((), ())), preferred_element_...  56 us
  transfers between devices with their start and end apart: 11, of which 10 were waited for; matrix products, arithmetic and copies ran while one was open for 13% of the time, Pallas kernels for 0%

commit v1 on v0

v1 whole, which is shorter than its diff:
```python
import math

import jax
import jax.numpy as jnp
from jax import lax
from jax.sharding import PartitionSpec as P

HEADS = 32
HEAD = 64
KVH = 4
FF = 5632

epsilon = 1e-05
rope_base = 10000.0
neg_large = -1e30
bf = jnp.bfloat16
f32 = jnp.float32
BOTH = ("dp", "seq")
STRIDE = {"c": 1, "x": 2, "y": 4}


class Net:
    def __init__(self):
        self.count = lax.axis_size(BOTH)
        self.me = lax.axis_index(BOTH)
        self.depth = self.count // 8
        self.z = self.me // 8
        self.bit = {axis: (self.me // s) % 2 for axis, s in STRIDE.items()}

    def swap(self, value, axis):
        s = STRIDE[axis]
        return lax.ppermute(value, BOTH, [(i, i ^ s) for i in range(self.count)])

    def climb(self, value, step, low, high):
        pairs = [(i, i + 8 * step) for i in range(self.count) if low <= i // 8 < high]
        return lax.ppermute(value, BOTH, pairs)

    def pick(self, value, axis, dim, other=False):
        index = self.bit[axis]
        if other:
            index = 1 - index
        return lax.dynamic_index_in_dim(value, index, dim, keepdims=False)

    def pair(self, mine, theirs, axis, dim):
        zero = self.bit[axis] == 0
        first = jnp.where(zero, mine, theirs)
        second = jnp.where(zero, theirs, mine)
        return jnp.stack([first, second], axis=dim)

    def gather(self, value, axis, dim):
        return self.pair(value, self.swap(value, axis), axis, dim)

    def exchange(self, value, axis, dim):
        theirs = self.swap(self.pick(value, axis, dim, other=True), axis)
        return self.pair(self.pick(value, axis, dim), theirs, axis, dim)

    def reduce(self, value, axis, dim):
        theirs = self.swap(self.pick(value, axis, dim, other=True), axis)
        return self.pick(value, axis, dim).astype(f32) + theirs.astype(f32)

    def gather_z(self, value):
        n = self.depth
        up, down = [value], [value]
        for k in range(1, n):
            up.append(self.climb(up[-1], 1, k - 1, n - 1))
            down.append(self.climb(down[-1], -1, 1, n - k + 1))
        whole = jnp.zeros((n,) + value.shape, value.dtype)
        for r in range(n):
            if r == 0:
                piece = value
            else:
                piece = jnp.where(self.z + r < n, down[r], up[n - r])
            whole = lax.dynamic_update_index_in_dim(whole, piece, (self.z + r) % n, 0)
        return whole

    def reduce_z(self, value):
        n = self.depth

        def part(offset):
            return lax.dynamic_index_in_dim(value, (self.z + offset) % n, 0, keepdims=False).astype(f32)

        from_above = from_below = None
        for k in range(n - 1, 0, -1):
            send = part(-k)
            if from_above is not None:
                send = send + from_above.astype(f32)
            from_above = self.climb(send.astype(bf), -1, k, n)
            send = part(k)
            if from_below is not None:
                send = send + from_below.astype(f32)
            from_below = self.climb(send.astype(bf), 1, 0, n - k)
        total = part(0)
        if n > 1:
            total = total + from_above.astype(f32) + from_below.astype(f32)
        return total


def doc_layout(length_row, row_count):
    docs = jnp.arange(length_row.shape[0], dtype=jnp.int32)
    doc_ends = jnp.sum(jnp.where(docs[None, :] <= docs[:, None], length_row[None, :], 0), axis=1)
    doc_starts = doc_ends - length_row
    where_at = jnp.arange(row_count, dtype=jnp.int32)
    segment = jnp.sum((where_at[:, None] >= doc_ends[None, :]).astype(jnp.int32), axis=1)
    member = segment[:, None] == docs[None, :]
    doc_begin = jnp.sum(jnp.where(member, doc_starts[None, :], 0), axis=1)
    return (segment, where_at - doc_begin)


def angle_tables(position, head_size):
    half_size = head_size // 2
    freq_row = rope_base ** (-2.0 * jnp.arange(half_size, dtype=f32) / head_size)
    angles = position.astype(f32)[:, None] * freq_row[None, :]
    return (jnp.cos(angles), jnp.sin(angles))


def rotate(vector, cos_table, sin_table):
    half_size = vector.shape[-1] // 2
    front_half = vector[..., :half_size]
    back_half = vector[..., half_size:]
    return jnp.concatenate(
        [
            front_half * cos_table - back_half * sin_table,
            back_half * cos_table + front_half * sin_table,
        ],
        axis=-1,
    )


def unrotate(vector, cos_table, sin_table):
    return rotate(vector, cos_table, -sin_table)


def contract_rows(left, right):
    return lax.dot_general(left, right, (((0,), (0,)), ((), ())), preferred_element_type=f32)


def contract_cols(left, right):
    return lax.dot_general(left, right, (((1,), (1,)), ((), ())), preferred_element_type=f32)


def norm_back(scaled, resid, inverse):
    return inverse * scaled - resid * (inverse * inverse * inverse) * jnp.mean(
        scaled * resid, axis=-1, keepdims=True
    )


def attend_forward(queries, keys_rot, values, segment, position, block_rows):
    group_rows = keys_rot.shape[0]
    block_count = group_rows // block_rows
    factor = 1.0 / math.sqrt(keys_rot.shape[1])
    query_blocks = queries.reshape(block_count, block_rows, queries.shape[1], queries.shape[2])
    seg_blocks = segment.reshape(block_count, block_rows)
    pos_blocks = position.reshape(block_count, block_rows)

    def one_block(pieces):
        query_block, seg_block, pos_block = pieces
        scores = (
            jnp.einsum("qhd,kd->hqk", query_block, keys_rot, preferred_element_type=f32) * factor
        )
        allowed = (seg_block[:, None] == segment[None, :]) & (
            pos_block[:, None] >= position[None, :]
        )
        scores = jnp.where(allowed[None], scores, neg_large)
        row_top = jnp.max(scores, axis=-1, keepdims=True)
        raised = jnp.exp(scores - row_top)
        row_total = jnp.sum(raised, axis=-1, keepdims=True)
        shares = (raised / row_total).astype(bf)
        mixed_heads = jnp.einsum("hqk,kd->qhd", shares, values, preferred_element_type=f32)
        return (mixed_heads, (row_top + jnp.log(row_total))[..., 0])

    mixed_heads, log_total = lax.map(one_block, (query_blocks, seg_blocks, pos_blocks))
    return (mixed_heads.reshape(group_rows, queries.shape[1] * queries.shape[2]), log_total)


def attend_backward(queries, keys_rot, values, grad_mixed, log_total, segment, position, block_rows):
    group_rows = keys_rot.shape[0]
    block_count = group_rows // block_rows
    factor = 1.0 / math.sqrt(keys_rot.shape[1])
    query_blocks = queries.reshape(block_count, block_rows, queries.shape[1], queries.shape[2])
    grad_blocks = grad_mixed.reshape(block_count, block_rows, queries.shape[1], queries.shape[2])
    seg_blocks = segment.reshape(block_count, block_rows)
    pos_blocks = position.reshape(block_count, block_rows)

    def one_block(running, pieces):
        grad_keys, grad_values = running
        query_block, grad_block, total_block, seg_block, pos_block = pieces
        scores = (
            jnp.einsum("qhd,kd->hqk", query_block, keys_rot, preferred_element_type=f32) * factor
        )
        allowed = (seg_block[:, None] == segment[None, :]) & (
            pos_block[:, None] >= position[None, :]
        )
        shares = jnp.where(allowed[None], jnp.exp(scores - total_block[:, :, None]), 0.0)
        grad_shares = jnp.einsum("qhd,kd->hqk", grad_block, values, preferred_element_type=f32)
        inner_row = jnp.sum(shares * grad_shares, axis=-1, keepdims=True)
        grad_scores = (shares * (grad_shares - inner_row)).astype(bf)
        grad_query = (
            jnp.einsum("hqk,kd->qhd", grad_scores, keys_rot, preferred_element_type=f32) * factor
        )
        grad_keys = (
            grad_keys
            + jnp.einsum("hqk,qhd->kd", grad_scores, query_block, preferred_element_type=f32)
            * factor
        )
        grad_values = grad_values + jnp.einsum(
            "hqk,qhd->kd", shares.astype(bf), grad_block, preferred_element_type=f32
        )
        return ((grad_keys, grad_values), grad_query)

    empty = jnp.zeros(keys_rot.shape, f32)
    (grad_keys, grad_values), grad_queries = lax.scan(
        one_block, (empty, empty), (query_blocks, grad_blocks, log_total, seg_blocks, pos_blocks)
    )
    return (grad_queries.reshape(queries.shape), grad_keys, grad_values)


def gather_tokens(net, value):
    half = value.shape[1] // 2
    left = net.gather(net.gather(value[:, :half], "x", 0), "y", 0)
    right = net.gather(net.gather(value[:, half:], "y", 0), "x", 1)
    mine = jnp.concatenate([left, right], axis=-1)
    whole = net.gather(mine, "c", 2)
    return whole.reshape(-1, value.shape[1])


def reduce_tokens(net, value):
    parts = value.reshape(2, 2, 2, value.shape[0] // 8, value.shape[1])
    parts = net.reduce(parts, "c", 2).astype(bf)
    half = value.shape[1] // 2
    left = net.reduce(net.reduce(parts[..., :half], "x", 1).astype(bf), "y", 0)
    right = net.reduce(net.reduce(parts[..., half:], "y", 0).astype(bf), "x", 0)
    return jnp.concatenate([left, right], axis=-1)


def body(layer_in, doc_lengths, norm_attn, w_qkv, w_out, norm_mlp, w_gateup, w_down, grad_out):
    net = Net()
    depth = net.depth
    rows, width = layer_in.shape
    group_rows = rows * 4
    block_rows = min(512, group_rows)
    per_group = HEADS // KVH
    q_width = per_group * HEAD
    cols = q_width + 2 * HEAD
    w_rows = w_qkv.shape[0]
    ff_rows = w_down.shape[0]
    ff_mine = ff_rows * depth
    ff_wide = -(-ff_mine // 256) * 256
    gain_one = norm_attn.astype(f32)[:, None]
    gain_two = norm_mlp.astype(f32)[:, None]

    group_in = net.gather(net.gather(layer_in, "x", 0), "c", 1).reshape(group_rows, width)
    qkv = (w_qkv.astype(f32) * gain_one).astype(bf).reshape(w_rows, 2, 2, cols)
    qkv = net.exchange(qkv, "x", 1)
    qkv = net.exchange(qkv, "c", 2)
    qkv = qkv.transpose(1, 2, 0, 3).reshape(4 * w_rows, cols)
    qkv = net.gather(net.gather_z(qkv), "y", 1).reshape(depth * 8 * w_rows, cols)

    out_z = net.gather_z(w_out)
    out_half = width // 2
    out_left = net.gather(net.gather(out_z[..., :out_half], "x", 1), "y", 1)
    out_right = net.gather(net.gather(out_z[..., out_half:], "y", 1), "x", 2)
    full_out = net.gather(jnp.concatenate([out_left, out_right], axis=-1), "c", 3)
    full_out = full_out.reshape(-1, width)

    gateup = (w_gateup.astype(f32) * gain_two).astype(bf)
    gateup = gateup.reshape(w_rows, 2, depth, 2, 2, 2, ff_rows).transpose(3, 4, 5, 0, 1, 2, 6)
    gateup = gateup.reshape(2, 2, 2, w_rows, 2, ff_mine)
    gateup = net.exchange(gateup, "y", 0)
    gateup = net.exchange(gateup, "x", 1)
    gateup = net.exchange(gateup, "c", 2)
    gateup = gateup.reshape(8 * w_rows, 2, ff_mine)
    wide_gap = ((0, 0), (0, ff_wide - ff_mine))
    gate_w = net.gather_z(gateup[:, 0]).reshape(-1, ff_mine)
    up_w = net.gather_z(gateup[:, 1]).reshape(-1, ff_mine)
    full_gateup = jnp.concatenate([jnp.pad(gate_w, wide_gap), jnp.pad(up_w, wide_gap)], axis=1)
    full_down = jnp.pad(
        net.gather_z(w_down).reshape(ff_mine, width), ((0, ff_wide - ff_mine), (0, 0))
    )

    segment, position = doc_layout(doc_lengths[0], group_rows)
    cos_table, sin_table = angle_tables(position, HEAD)
    wide_in = group_in.astype(f32)
    normed_one = (
        wide_in * lax.rsqrt(jnp.mean(wide_in * wide_in, axis=-1, keepdims=True) + epsilon)
    ).astype(bf)
    head_cols = jnp.dot(normed_one, qkv, preferred_element_type=f32).astype(bf)
    queries = rotate(
        head_cols[:, :q_width].astype(f32).reshape(group_rows, per_group, HEAD),
        cos_table[:, None, :],
        sin_table[:, None, :],
    ).astype(bf)
    keys_rot = rotate(
        head_cols[:, q_width : q_width + HEAD].astype(f32), cos_table, sin_table
    ).astype(bf)
    values = head_cols[:, q_width + HEAD :]
    mixed_heads, log_total = attend_forward(queries, keys_rot, values, segment, position, block_rows)
    mixed_tok = lax.all_to_all(mixed_heads.astype(bf), "seq", split_axis=0, concat_axis=1, tiled=True)
    resid_in = layer_in.astype(f32)
    resid_mid = resid_in + jnp.dot(mixed_tok, full_out, preferred_element_type=f32)

    inv_two = lax.rsqrt(jnp.mean(resid_mid * resid_mid, axis=-1, keepdims=True) + epsilon)
    normed_two = gather_tokens(net, (resid_mid * inv_two).astype(bf))
    many_out = gather_tokens(net, grad_out)
    grad_act = contract_cols(many_out, full_down)
    gate_up = jnp.dot(normed_two, full_gateup, preferred_element_type=f32)
    gate_part = gate_up[:, :ff_wide]
    up_part = gate_up[:, ff_wide:]
    gate_sig = jax.nn.sigmoid(gate_part)
    swished = gate_part * gate_sig
    activated = (swished * up_part).astype(bf)
    grad_gate = grad_act * up_part * gate_sig * (1.0 + gate_part * (1.0 - gate_sig))
    grad_up = grad_act * swished
    grad_gate_up = jnp.concatenate([grad_gate, grad_up], axis=1).astype(bf)
    scaled_two = reduce_tokens(net, contract_cols(grad_gate_up, full_gateup).astype(bf))
    grad_gateup = contract_rows(normed_two, grad_gate_up).astype(bf)
    grad_down = contract_rows(activated, many_out).astype(bf)
    layer_out = resid_mid + reduce_tokens(
        net, jnp.dot(activated, full_down, preferred_element_type=f32).astype(bf)
    )

    grad_mid = grad_out.astype(f32) + norm_back(scaled_two, resid_mid, inv_two)
    grad_mid_low = grad_mid.astype(bf)
    grad_mixed = contract_cols(grad_mid_low, full_out).astype(bf)
    grad_heads = lax.all_to_all(grad_mixed, "seq", split_axis=1, concat_axis=0, tiled=True)
    grad_queries, grad_keys, grad_values = attend_backward(
        queries,
        keys_rot,
        values,
        grad_heads.reshape(group_rows, per_group, HEAD),
        log_total,
        segment,
        position,
        block_rows,
    )
    grad_q_plain = unrotate(grad_queries, cos_table[:, None, :], sin_table[:, None, :]).reshape(
        group_rows, q_width
    )
    grad_k_plain = unrotate(grad_keys, cos_table, sin_table)
    grad_cols = jnp.concatenate([grad_q_plain, grad_k_plain, grad_values], axis=1).astype(bf)
    part_one = contract_cols(grad_cols, qkv).astype(bf).reshape(2, 2, rows, width)
    part_one = net.reduce(part_one, "c", 1).astype(bf)
    scaled_one = net.reduce(part_one, "x", 0)
    inv_one = lax.rsqrt(jnp.mean(resid_in * resid_in, axis=-1, keepdims=True) + epsilon)
    grad_in = grad_mid + norm_back(scaled_one, resid_in, inv_one)

    sum_gate = net.reduce_z(grad_gateup[:, :ff_mine].reshape(depth, 8 * w_rows, ff_mine))
    sum_up = net.reduce_z(
        grad_gateup[:, ff_wide : ff_wide + ff_mine].reshape(depth, 8 * w_rows, ff_mine)
    )
    sum_gateup = jnp.stack([sum_gate.astype(bf), sum_up.astype(bf)], axis=1)
    sum_gateup = sum_gateup.reshape(2, 2, 2, w_rows, 2, ff_mine)
    sum_gateup = net.exchange(sum_gateup, "c", 2)
    sum_gateup = net.exchange(sum_gateup, "x", 1)
    sum_gateup = net.exchange(sum_gateup, "y", 0)
    sum_gateup = sum_gateup.reshape(2, 2, 2, w_rows, 2, depth, ff_rows).transpose(3, 4, 5, 0, 1, 2, 6)
    sum_gateup = sum_gateup.reshape(w_rows, 2 * FF).astype(f32)
    grad_w_gateup = sum_gateup * gain_two
    grad_norm_mlp = jnp.sum(sum_gateup * w_gateup.astype(f32), axis=1)

    grad_w_down = net.reduce_z(grad_down[:ff_mine].reshape(depth, ff_rows, width))

    grad_out_w = contract_rows(mixed_tok, grad_mid_low).astype(bf)
    grad_out_w = net.reduce(grad_out_w.reshape(depth, 2, 2, 2, w_rows, width), "c", 3).astype(bf)
    sum_left = net.reduce(
        net.reduce(grad_out_w[..., :out_half], "x", 2).astype(bf), "y", 1
    ).astype(bf)
    sum_right = net.reduce(
        net.reduce(grad_out_w[..., out_half:], "y", 1).astype(bf), "x", 1
    ).astype(bf)
    grad_w_out = net.reduce_z(jnp.concatenate([sum_left, sum_right], axis=-1))

    grad_qkv = contract_rows(normed_one, grad_cols).astype(bf)
    grad_qkv = net.reduce(grad_qkv.reshape(depth, 2, 4 * w_rows, cols), "y", 1).astype(bf)
    sum_qkv = net.reduce_z(grad_qkv).astype(bf).reshape(2, 2, w_rows, cols)
    sum_qkv = net.exchange(sum_qkv, "c", 1)
    sum_qkv = net.exchange(sum_qkv, "x", 0)
    sum_qkv = sum_qkv.transpose(2, 0, 1, 3).reshape(w_rows, 4 * cols).astype(f32)
    grad_w_qkv = sum_qkv * gain_one
    grad_norm_attn = jnp.sum(sum_qkv * w_qkv.astype(f32), axis=1)

    return (
        layer_out,
        grad_in,
        grad_norm_attn,
        grad_w_qkv,
        grad_w_out,
        grad_norm_mlp,
        grad_w_gateup,
        grad_w_down,
    )


def solution(mesh):
    rows = P(("dp", "seq"), None)
    flat = P(("dp", "seq"))
    return jax.shard_map(
        body,
        mesh=mesh,
        in_specs=(rows, P("dp", None), flat, rows, rows, flat, rows, rows, rows),
        out_specs=(rows, rows, flat, rows, rows, flat, rows, rows),
        check_vma=False,
    )
```

time: 2570 us -> 1160 us (0.45)
  waiting for transfers between devices: 2030 us -> 281 us
  starting transfers between devices: 14.4 us -> 233 us
  local copies, waits for them, and re-layouts: 71.6 us -> 253 us
  other arithmetic: 49.9 us -> 184 us
  blocking collectives: 113 us -> 0 us
  matrix products: 260 us -> 189 us
    reduce_scatter x4 -> x0, waiting for transfers between devices: 1570 us -> none  [the longest x1 975 us: body(): lax.psum_scatter(grad_gateup, ('dp', 'seq'), scatter_dimension=0, tiled=T...]
    all_gather x4 -> x0, waiting for transfers between devices: 405 us -> none  [the longest x1 236 us: body(): lax.all_gather(w_gateup, ('dp', 'seq'), axis=0, tiled=True)]
    ppermute x0 -> x106, waiting for transfers between devices: none -> 276 us  [the longest x46 160 us: swap(): return lax.ppermute(value, BOTH, [(i, i ^ s) for i in range(self.count)])]
    ppermute x0 -> x106, starting transfers between devices: none -> 220 us  [the longest x60 157 us: climb(): return lax.ppermute(value, BOTH, pairs)]
    unnamed x2 -> x0, blocking collectives: 82.8 us -> none
    another operation x8 -> x45, other arithmetic: 4.26 us -> 60.6 us  [the longest x38 58.2 us: pair(): return jnp.stack([first, second], axis=dim)]
    dot_general x4, matrix products: 72.9 us -> 30.1 us  [contract_rows(): lax.dot_general(left, right, (((0,), (0,)), ((), ())), preferred_element_...]
    dynamic_slice x0 -> x7, local copies, waits for them, and re-layouts: none -> 42.1 us  [the longest x1 30.4 us: part(): lax.dynamic_index_in_dim(value, (self.z + offset) % n, 0, keepdims=False)]
  transfers between devices with their start and end apart: 11 -> 108, of which waited for: 10 -> 38; matrix products, arithmetic and copies ran while one was open for 13% -> 40% of each run, Pallas kernels for 0% -> 0%
where the time goes in v1:
time: 1160 us; the launch traced here: 1140 us
  waiting for transfers between devices  281 us (24%)
  local copies, waits for them, and re-layouts  253 us (22%)
  starting transfers between devices  233 us (20%)
  matrix products  189 us (16%)
  other arithmetic  184 us (16%)
    ppermute x46, waiting for transfers between devices, swap(): return lax.ppermute(value, BOTH, [(i, i ^ s) for i in range(self.count)])  160 us
    ppermute x60, starting transfers between devices, climb(): return lax.ppermute(value, BOTH, pairs)  157 us
    ppermute x60, waiting for transfers between devices, climb(): return lax.ppermute(value, BOTH, pairs)  117 us
    ppermute x46, starting transfers between devices, swap(): return lax.ppermute(value, BOTH, [(i, i ^ s) for i in range(self.count)])  63 us
    another operation x38, other arithmetic, pair(): return jnp.stack([first, second], axis=dim)  58.2 us
    dot_general x4, matrix products, contract_cols(): lax.dot_general(left, right, (((1,), (1,)), ((), ())), preferred_element_...  43.5 us
    dynamic_update_slice x4, local copies, waits for them, and re-layouts, attend_forward(): lax.map(one_block, (query_blocks, seg_blocks, pos_blocks))  41.4 us
    dynamic_slice x1, local copies, waits for them, and re-layouts, part(): lax.dynamic_index_in_dim(value, (self.z + offset) % n, 0, keepdims=False)  30.4 us
  transfers between devices with their start and end apart: 108, of which 38 were waited for; matrix products, arithmetic and copies ran while one was open for 40% of the time, Pallas kernels for 0%

profile of v1, /device:TPU:11, one launch (start us, length us, event | category | flops | bytes accessed | tf_op | source)
XLA Modules:
  0.0 1145.0 jit_solution(15695526372025354426)
XLA Ops:
  52.3 10.1 collective-permute-done.13
  81.1 6.7 collective-permute-done
  116.3 8.3 collective-permute-start.1
  127.6 10.0 collective-permute-done.56
  157.9 11.5 %collective-permute-done.20 = bf16[4,2,64,1024]{3,2,1,0:T(8,128)(2,1)} collective-permute-done((bf16[4,2,64,1024]{3,2,1,0:T(8,128)(2,1)}, bf16[4,2,64,1024]{3,2,1,0:T(8,128)(2,1)}, u32[]{:S(2)}, u32[]{:S(2)}) %collective-permute-start.20) | collective-permute-done | bytes 1048608 | tf_op jit(solution)/shard_map/ppermute | solution.py:32
  169.4 5.3 collective-permute-start.31
  196.4 26.6 %while.27 = (s32[]{:T(128)}, bf16[2,512,8,64]{1,3,2,0:T(8,128)(2,1)S(1)}, f32[2,8,512]{2,1,0:T(8,128)S(1)}, s32[2,512]{1,0:T(2,128)S(1)}, s32[1024]{0:T(1024)S(1...) while((s32[]{:T(128)}, ...), condition=%wide.region_7.8_spmd, body=%wide.region_4.7_spmd.sunk | while | flops 1125642240 | bytes 54415484 | solution.py:171
  204.3 5.5 fusion.231
  217.5 5.5 fusion.231
  235.4 6.6 select_bitcast_fusion.5
  242.0 7.5 pad_maximum_fusion
  249.6 6.2 multiply_reduce_fusion.2
  265.5 5.6 collective-permute-done.22
  285.3 10.7 collective-permute-done.23
  298.2 5.7 collective-permute-start.32
  328.3 6.1 collective-permute-done.38
  368.1 5.3 select_bitcast_fusion.1
  373.4 6.2 pad_maximum_fusion.2
  379.6 8.3 copy.291
  387.9 5.3 select_bitcast_fusion.3
  393.2 6.2 pad_maximum_fusion.1
  399.4 8.4 copy.274
  407.8 20.6 %fusion.89 = f32[2048,1536]{0,1:T(8,128)} fusion(bf16[2048,2048]{1,0:T(8,128)(2,1)} %bitcast.747, bf16[2048,704]{1,0:T(8,128)(2,1)} %bitcast.754, bf16[2048,704]{1,0:T(8,128)(2,1)} %bitcast.88), kind=kOutput, calls=%fused_computation.225 | convolution fusion | flops 12910067712 | bytes 26738688 | tf_op jit(solution)/shard_map/dot_general | solution.py:305
  428.4 15.0 %multiply_convert_fusion.2 = (bf16[2048,768]{0,1:T(8,128)(2,1)}, bf16[2048,768]{0,1:T(8,128)(2,1)}, bf16[2048,768]{0,1:T(8,128)(2,1)S(1)}) fusion(f32[2048,1536]{0,1:T(8,128)} %fusion.89, bf16[2048,2048]{1,0:T(8,128)(2,1)S(1)} %bitcast.745, bf16[704,2048]{1,0:T(8,128)(2,1)} %bitcast.99), kind=kOutput, calls=%fused_computation.82 | convolution fusion | flops 6466043904 | bytes 33292288 | tf_op jit(solution)/shard_map/dot_general | solution.py:138
  443.4 8.1 fusion.191
  451.5 10.9 convolution_convert_fusion.3
  462.4 15.9 %convolution_convert_fusion = bf16[2048,1536]{0,1:T(8,128)(2,1)S(1)} fusion(bf16[2048,2048]{1,0:T(8,128)(2,1)} %bitcast.748, bf16[2048,768]{0,1:T(8,128)(2,1)S(1)} %copy-done.115, bf16[2048,768]{0,1:T(8,128)(2,1)S(1)} %copy-done.114), kind=kOutput, calls=%fused_computation.75 | convolution fusion | flops 12900630528 | bytes 20971520 | tf_op jit(solution)/shard_map/dot_general | solution.py:134
  478.4 19.4 %convolution_convert_fusion.2 = bf16[2048,2048]{1,0:T(8,128)(2,1)} fusion(bf16[2048,768]{0,1:T(8,128)(2,1)} %get-tuple-element.349, bf16[2048,768]{0,1:T(8,128)(2,1)} %get-tuple-element.348, bf16[2048,704]{1,0:T(8,128)(2,1)} %bitcast.755, bf16[2048,704]{1,0:T(8,128)(2,1)} %bitcast.88), kind=kOutput, calls=%fused_computation.77 | convolution fusion | flops 12926844928 | bytes 20447232 | tf_op jit(solution)/shard_map/dot_general | solution.py:138
  504.5 6.0 reshape.566
  510.5 7.6 reshape.567
  518.1 30.4 %constant_dynamic-slice_fusion.10 = (bf16[1,512,704]{1,0,2:T(2,128)(2,1)S(1)}, bf16[1,512,704]{1,0,2:T(2,128)(2,1)S(1)}, bf16[1,512,704]{1,0,2:T(2,128)(2,1)S(1)...) fusion(bf16[4,512,704]{1,0,2:T(4,128)(2,1)} %reshape.567, ...), kind=kLoop, calls=%fused_computation.460 | loop fusion | bytes 20185116 | tf_op jit(solution)/shard_map/jit(dynamic_index_in_dim)/dynamic_slice | solution.py:80
  573.2 11.0 collective-permute-done.88
  585.8 29.0 %collective-permute-start.95 = (bf16[512,704]{0,1:T(8,128)(2,1)S(1)}, bf16[512,704]{0,1:T(8,128)(2,1)S(1)}, u32[]{:S(2)}, u32[]{:S(2)}) collective-permute-start(bf16[512,704]{0,1:T(8,128)(2,1)S(1)} %fusion.76), channel_id=1, source_target_pairs={{0,8},{1,9},{2,10},{3,11},{4,12},{5,13},{6,14},{7,15},{8,16},{9,17... | collective-permute-start | bytes 2162696 | tf_op jit(solution)/shard_map/ppermute | solution.py:36
  616.4 12.7 %collective-permute-done.92 = bf16[512,704]{0,1:T(8,128)(2,1)S(1)} collective-permute-done((bf16[512,704]{0,1:T(8,128)(2,1)S(1)}, bf16[512,704]{0,1:T(8,128)(2,1)S(1)}, u32[]{:S(2)}, u32[]{:S(2)}) %collective-permute-start.92) | collective-permute-done | bytes 720928 | tf_op jit(solution)/shard_map/ppermute | solution.py:36
  633.9 10.7 collective-permute-done.86
  652.4 7.6 collective-permute-done.101
  661.9 13.5 %collective-permute-done.93 = bf16[512,704]{0,1:T(8,128)(2,1)S(1)} collective-permute-done((bf16[512,704]{0,1:T(8,128)(2,1)S(1)}, bf16[512,704]{0,1:T(8,128)(2,1)S(1)}, u32[]{:S(2)}, u32[]{:S(2)}) %collective-permute-start.93) | collective-permute-done | bytes 720928 | tf_op jit(solution)/shard_map/ppermute | solution.py:36
  685.7 5.3 collective-permute-done.87
  699.9 5.5 fusion.48
  717.6 11.5 %collective-permute-done.59 = bf16[2,256,1024]{2,1,0:T(8,128)(2,1)} collective-permute-done((bf16[2,256,1024]{2,1,0:T(8,128)(2,1)}, bf16[2,256,1024]{2,1,0:T(8,128)(2,1)}, u32[]{:S(2)}, u32[]{:S(2)}) %collective-permute-start.59) | collective-permute-done | bytes 1048608 | tf_op jit(solution)/shard_map/ppermute | solution.py:32
  731.6 7.6 collective-permute-start.97
  740.9 10.7 collective-permute-done.49
  754.5 11.1 collective-permute-done.60
  768.0 7.9 collective-permute-done.50
  785.8 9.5 all-to-all-start.1
  812.0 121.5 %while.28 = (s32[]{:T(128)}, f32[1024,64]{0,1:T(8,128)}, f32[1024,64]{0,1:T(8,128)}, f32[2,512,8,64]{1,0,3,2:T(2,128)}, s32[2,512]{1,0:T(2,128)}, /*index=5*/s32...) while((s32[]{:T(128)}, f32[1024,64]{0,1:T(8,128)}, ...), condition=%wide.region_13.14_spmd.clone, body=%wide.region_11.13_spmd.clone.sunk | while | flops 2724261888 | bytes 178361232 | solution.py:211
  818.0 10.5 fusion.241
  828.5 6.9 fusion.242
  839.8 19.6 %dynamic_update_slice.123 = f32[2,512,8,64]{1,0,3,2:T(2,128)} dynamic-update-slice(f32[2,512,8,64]{1,0,3,2:T(2,128)} %get-tuple-element.712, f32[1,512,8,64]{1,0,3,2:T(1,128)S(1)} %copy.431, s32[]{:T(128)} %get-tuple-element.709, s32[]{:T(128)} %constant.535.clone.1..sunk, s32[]{:T(128)} %constant.535.clone.1..sunk, s32[]{:T(128)} %constant.535.clone.1..sunk) | dynamic-update-slice | bytes 2097156 | tf_op jit(solution)/shard_map/while/body/jit(dynamic_update_index_in_dim)/dynamic_update_slice | solution.py:171
  859.4 5.1 fusion.243
  864.5 7.5 fusion.244
  878.8 10.5 fusion.241
  889.3 6.9 fusion.242
  900.5 19.6 %dynamic_update_slice.123 = f32[2,512,8,64]{1,0,3,2:T(2,128)} dynamic-update-slice(f32[2,512,8,64]{1,0,3,2:T(2,128)} %get-tuple-element.712, f32[1,512,8,64]{1,0,3,2:T(1,128)S(1)} %copy.431, s32[]{:T(128)} %get-tuple-element.709, s32[]{:T(128)} %constant.535.clone.1..sunk, s32[]{:T(128)} %constant.535.clone.1..sunk, s32[]{:T(128)} %constant.535.clone.1..sunk) | dynamic-update-slice | bytes 2097156 | tf_op jit(solution)/shard_map/while/body/jit(dynamic_update_index_in_dim)/dynamic_update_slice | solution.py:171
  920.1 5.1 fusion.243
  925.3 7.5 fusion.244
  960.7 14.3 %collective-permute-done.65 = bf16[4,256,640]{2,1,0:T(8,128)(2,1)S(1)} collective-permute-done((bf16[4,256,640]{2,1,0:T(8,128)(2,1)S(1)}, bf16[4,256,640]{2,1,0:T(8,128)(2,1)S(1)}, u32[]{:S(2)}, u32[]{:S(2)}) %collective-permute-start.65) | collective-permute-done | bytes 1310752 | tf_op jit(solution)/shard_map/ppermute | solution.py:32
  983.2 8.6 collective-permute-done.99
  1003.7 5.2 copy.324
  1008.9 7.3 reshape.611
  1020.2 5.6 convolution_convert_fusion.4
  1055.2 24.2 %collective-permute-done.73 = bf16[2,64,640]{2,1,0:T(8,128)(2,1)S(1)} collective-permute-done((bf16[2,64,640]{2,1,0:T(8,128)(2,1)S(1)}, bf16[2,64,640]{2,1,0:T(8,128)(2,1)S(1)}, u32[]{:S(2)}, u32[]{:S(2)}) %collective-permute-start.73) | collective-permute-done | bytes 163872 | tf_op jit(solution)/shard_map/ppermute | solution.py:32
  1091.7 21.6 %collective-permute-done.78 = bf16[4,64,1024]{2,1,0:T(8,128)(2,1)} collective-permute-done((bf16[4,64,1024]{2,1,0:T(8,128)(2,1)}, bf16[4,64,1024]{2,1,0:T(8,128)(2,1)}, u32[]{:S(2)}, u32[]{:S(2)}) %collective-permute-start.78) | collective-permute-done | bytes 524320 | tf_op jit(solution)/shard_map/ppermute | solution.py:32
  1118.8 6.6 collective-permute-done.82
  (708 shorter events, 509.8 us)
Async XLA Ops:
  0.7 38.3 %collective-permute-start.12 = (bf16[64,2048]{1,0:T(8,128)(2,1)}, bf16[64,2048]{1,0:T(8,128)(2,1)}, u32[]{:S(2)}, u32[]{:S(2)}) collective-permute-start(bf16[64,2048]{1,0:T(8,128)(2,1)} %param.17), channel_id=1, source_target_pairs={{0,8},{1,9},{2,10},{3,11},{4,12},{5,13},{6,14},{7,15},{8,16},{9,17... | collective-permute-start | bytes 786440 | tf_op jit(solution)/shard_map/ppermute | solution.py:36
  4.0 37.4 %collective-permute-start.11 = (bf16[64,2048]{1,0:T(8,128)(2,1)}, bf16[64,2048]{1,0:T(8,128)(2,1)}, u32[]{:S(2)}, u32[]{:S(2)}) collective-permute-start(bf16[64,2048]{1,0:T(8,128)(2,1)} %param.17), channel_id=1, source_target_pairs={{8,0},{9,1},{10,2},{11,3},{12,4},{13,5},{14,6},{15,7},{16,8},{17,9... | collective-permute-start | bytes 786440 | tf_op jit(solution)/shard_map/ppermute | solution.py:36
  9.0 36.3 %collective-permute-start.53 = (bf16[256,1024]{1,0:T(8,128)(2,1)}, bf16[256,1024]{1,0:T(8,128)(2,1)}, u32[]{:S(2)}, u32[]{:S(2)}) collective-permute-start(bf16[256,1024]{1,0:T(8,128)(2,1)} %get-tuple-element.457), channel_id=1, source_target_pairs={{0,2},{1,3},{2,0},{3,1},{4,6},{5,7},{6,4},{7,5},{8,10},{9,11},{10,... | collective-permute-start | bytes 1572872 | tf_op jit(solution)/shard_map/ppermute | solution.py:32
  9.3 38.0 %collective-permute-start.55 = (bf16[256,1024]{1,0:T(8,128)(2,1)}, bf16[256,1024]{1,0:T(8,128)(2,1)}, u32[]{:S(2)}, u32[]{:S(2)}) collective-permute-start(bf16[256,1024]{1,0:T(8,128)(2,1)} %get-tuple-element.458), channel_id=1, source_target_pairs={{0,4},{1,5},{2,6},{3,7},{4,0},{5,1},{6,2},{7,3},{8,12},{9,13},{10,... | collective-permute-start | bytes 1572872 | tf_op jit(solution)/shard_map/ppermute | solution.py:32
  36.6 27.8 %collective-permute-start.27 = (bf16[2,2,64,2,704]{4,2,3,1,0:T(8,128)(2,1)}, bf16[2,2,64,2,704]{4,2,3,1,0:T(8,128)(2,1)S(1)}, u32[]{:S(2)}, u32[]{:S(2)}) collective-permute-start(bf16[2,2,64,2,704]{4,2,3,1,0:T(8,128)(2,1)} %dynamic-slice_bitcast_fusion.12), channel_id=1, source_target_pairs={{0,4},{1,5},{2,6},{3,7},{4,0},{5,1},{6,2},{7,3},{8,12},{9,13},{10,... | collective-permute-start | bytes 2162696 | tf_op jit(solution)/shard_map/ppermute | solution.py:32
  38.9 64.0 %collective-permute-start.43 = (bf16[176,2048]{1,0:T(8,128)(2,1)}, bf16[176,2048]{1,0:T(8,128)(2,1)S(1)}, u32[]{:S(2)}, u32[]{:S(2)}) collective-permute-start(bf16[176,2048]{1,0:T(8,128)(2,1)} %param.20), channel_id=1, source_target_pairs={{0,8},{1,9},{2,10},{3,11},{4,12},{5,13},{6,14},{7,15},{8,16},{9,17... | collective-permute-start | bytes 2162696 | tf_op jit(solution)/shard_map/ppermute | solution.py:36
  41.5 21.0 %collective-permute-start.13 = (bf16[64,2048]{1,0:T(8,128)(2,1)}, bf16[64,2048]{1,0:T(8,128)(2,1)S(1)}, u32[]{:S(2)}, u32[]{:S(2)}) collective-permute-start(bf16[64,2048]{1,0:T(8,128)(2,1)} %collective-permute-done.12), channel_id=1, source_target_pairs={{8,16},{9,17},{10,18},{11,19},{12,20},{13,21},{14,22},{15,23},{16,... | collective-permute-start | bytes 786440 | tf_op jit(solution)/shard_map/ppermute | solution.py:36
  47.3 22.0 %collective-permute-start.5 = (bf16[256,640]{1,0:T(8,128)(2,1)S(1)}, bf16[256,640]{1,0:T(8,128)(2,1)S(1)}, u32[]{:S(2)}, u32[]{:S(2)}) collective-permute-start(bf16[256,640]{1,0:T(8,128)(2,1)S(1)} %bitcast.763), channel_id=1, source_target_pairs={{0,8},{1,9},{2,10},{3,11},{4,12},{5,13},{6,14},{7,15},{8,16},{9,17... | collective-permute-start | bytes 983048 | tf_op jit(solution)/shard_map/ppermute | solution.py:36
  65.3 22.6 %collective-permute-start = (bf16[256,2048]{1,0:T(8,128)(2,1)S(1)}, bf16[256,2048]{1,0:T(8,128)(2,1)S(1)}, u32[]{:S(2)}, u32[]{:S(2)}) collective-permute-start(bf16[256,2048]{1,0:T(8,128)(2,1)S(1)} %copy-done.15), channel_id=1, source_target_pairs={{0,2},{1,3},{2,0},{3,1},{4,6},{5,7},{6,4},{7,5},{8,10},{9,11},{10,... | collective-permute-start | bytes 3145736 | tf_op jit(solution)/shard_map/ppermute | solution.py:32
  93.0 33.3 %collective-permute-start.54 = (bf16[2,256,1024]{2,1,0:T(8,128)(2,1)S(1)}, bf16[2,256,1024]{2,1,0:T(8,128)(2,1)S(1)}, u32[]{:S(2)}, u32[]{:S(2)}) collective-permute-start(bf16[2,256,1024]{2,1,0:T(8,128)(2,1)S(1)} %pad_maximum_fusion.18), channel_id=1, source_target_pairs={{0,4},{1,5},{2,6},{3,7},{4,0},{5,1},{6,2},{7,3},{8,12},{9,13},{10,... | collective-permute-start | bytes 3145736 | tf_op jit(solution)/shard_map/ppermute | solution.py:32
  102.9 34.7 %collective-permute-start.56 = (bf16[2,256,1024]{2,1,0:T(8,128)(2,1)S(1)}, bf16[2,256,1024]{2,1,0:T(8,128)(2,1)S(1)}, u32[]{:S(2)}, u32[]{:S(2)}) collective-permute-start(bf16[2,256,1024]{2,1,0:T(8,128)(2,1)S(1)} %pad_maximum_fusion.19), channel_id=1, source_target_pairs={{0,2},{1,3},{2,0},{3,1},{4,6},{5,7},{6,4},{7,5},{8,10},{9,11},{10,... | collective-permute-start | bytes 3145736 | tf_op jit(solution)/shard_map/ppermute | solution.py:32
  113.5 32.2 %collective-permute-start.46 = (bf16[176,2048]{1,0:T(8,128)(2,1)S(1)}, bf16[176,2048]{1,0:T(8,128)(2,1)}, u32[]{:S(2)}, u32[]{:S(2)}) collective-permute-start(bf16[176,2048]{1,0:T(8,128)(2,1)S(1)} %collective-permute-done.42), channel_id=1, source_target_pairs={{8,0},{9,1},{10,2},{11,3},{12,4},{13,5},{14,6},{15,7},{16,8},{17,9... | collective-permute-start | bytes 2162696 | tf_op jit(solution)/shard_map/ppermute | solution.py:36
  116.3 67.1 %collective-permute-start.1 = (bf16[2,256,2048]{2,1,0:T(8,128)(2,1)}, bf16[2,256,2048]{2,1,0:T(8,128)(2,1)}, u32[]{:S(2)}, u32[]{:S(2)}) collective-permute-start(bf16[2,256,2048]{2,1,0:T(8,128)(2,1)} %pad_maximum_fusion.7), channel_id=1, source_target_pairs={{0,1},{1,0},{2,3},{3,2},{4,5},{5,4},{6,7},{7,6},{8,9},{9,8},{10,11... | collective-permute-start | bytes 6291464 | tf_op jit(solution)/shard_map/ppermute | solution.py:32
  125.0 29.3 %collective-permute-start.18 = (bf16[4,2,64,1024]{3,2,0,1:T(8,128)(2,1)}, bf16[4,2,64,1024]{3,2,0,1:T(8,128)(2,1)}, u32[]{:S(2)}, u32[]{:S(2)}) collective-permute-start(bf16[4,2,64,1024]{3,2,0,1:T(8,128)(2,1)} %pad_maximum_fusion.14), channel_id=1, source_target_pairs={{0,4},{1,5},{2,6},{3,7},{4,0},{5,1},{6,2},{7,3},{8,12},{9,13},{10,... | collective-permute-start | bytes 3145736 | tf_op jit(solution)/shard_map/ppermute | solution.py:32
  144.3 25.1 %collective-permute-start.20 = (bf16[4,2,64,1024]{3,2,1,0:T(8,128)(2,1)}, bf16[4,2,64,1024]{3,2,1,0:T(8,128)(2,1)}, u32[]{:S(2)}, u32[]{:S(2)}) collective-permute-start(bf16[4,2,64,1024]{3,2,1,0:T(8,128)(2,1)} %pad_maximum_fusion.15), channel_id=1, source_target_pairs={{0,2},{1,3},{2,0},{3,1},{4,6},{5,7},{6,4},{7,5},{8,10},{9,11},{10,... | collective-permute-start | bytes 3145736 | tf_op jit(solution)/shard_map/ppermute | solution.py:32
  145.7 33.0 %collective-permute-start.10 = (bf16[4,256,640]{2,1,0:T(8,128)(2,1)}, bf16[4,256,640]{2,1,0:T(8,128)(2,1)}, u32[]{:S(2)}, u32[]{:S(2)}) collective-permute-start(bf16[4,256,640]{2,1,0:T(8,128)(2,1)} %bitcast_dynamic-update-slice_fusion.7), channel_id=1, source_target_pairs={{0,4},{1,5},{2,6},{3,7},{4,0},{5,1},{6,2},{7,3},{8,12},{9,13},{10,... | collective-permute-start | bytes 3932168 | tf_op jit(solution)/shard_map/ppermute | solution.py:32
  146.9 115.6 %collective-permute-start.47 = (bf16[176,2048]{1,0:T(8,128)(2,1)}, bf16[176,2048]{1,0:T(8,128)(2,1)}, u32[]{:S(2)}, u32[]{:S(2)}) collective-permute-start(bf16[176,2048]{1,0:T(8,128)(2,1)} %collective-permute-done.46), channel_id=1, source_target_pairs={{8,0},{9,1},{10,2},{11,3},{12,4},{13,5},{14,6},{15,7}} | collective-permute-start | bytes 2162696 | tf_op jit(solution)/shard_map/ppermute | solution.py:36
  154.3 124.0 %collective-permute-start.30 = (bf16[512,704]{0,1:T(8,128)(2,1)}, bf16[512,704]{0,1:T(8,128)(2,1)}, u32[]{:S(2)}, u32[]{:S(2)}) collective-permute-start(bf16[512,704]{0,1:T(8,128)(2,1)} %copy.279), channel_id=1, source_target_pairs={{8,0},{9,1},{10,2},{11,3},{12,4},{13,5},{14,6},{15,7},{16,8},{17,9... | collective-permute-start | bytes 2162696 | tf_op jit(solution)/shard_map/ppermute | solution.py:36
  169.4 113.4 %collective-permute-start.31 = (bf16[512,704]{0,1:T(8,128)(2,1)}, bf16[512,704]{0,1:T(8,128)(2,1)}, u32[]{:S(2)}, u32[]{:S(2)}) collective-permute-start(bf16[512,704]{0,1:T(8,128)(2,1)} %copy.279), channel_id=1, source_target_pairs={{0,8},{1,9},{2,10},{3,11},{4,12},{5,13},{6,14},{7,15},{8,16},{9,17... | collective-permute-start | bytes 2162696 | tf_op jit(solution)/shard_map/ppermute | solution.py:36
  178.7 56.7 %collective-permute-start.21 = (bf16[4,2,2,64,2048]{4,3,2,1,0:T(8,128)(2,1)}, bf16[4,2,2,64,2048]{4,3,2,1,0:T(8,128)(2,1)}, u32[]{:S(2)}, u32[]{:S(2)}) collective-permute-start(bf16[4,2,2,64,2048]{4,3,2,1,0:T(8,128)(2,1)} %maximum_maximum_fusion), channel_id=1, source_target_pairs={{0,1},{1,0},{2,3},{3,2},{4,5},{5,4},{6,7},{7,6},{8,9},{9,8},{10,11... | collective-permute-start | bytes 12582920 | tf_op jit(solution)/shard_map/ppermute | solution.py:32
  262.5 35.7 %collective-permute-start.36 = (bf16[512,704]{0,1:T(8,128)(2,1)}, bf16[512,704]{0,1:T(8,128)(2,1)S(1)}, u32[]{:S(2)}, u32[]{:S(2)}) collective-permute-start(bf16[512,704]{0,1:T(8,128)(2,1)} %copy.284), channel_id=1, source_target_pairs={{8,0},{9,1},{10,2},{11,3},{12,4},{13,5},{14,6},{15,7},{16,8},{17,9... | collective-permute-start | bytes 2162696 | tf_op jit(solution)/shard_map/ppermute | solution.py:36
  272.4 23.5 %collective-permute-start.23 = (bf16[2,256,1024]{2,1,0:T(8,128)(2,1)S(1)}, bf16[2,256,1024]{2,1,0:T(8,128)(2,1)S(1)}, u32[]{:S(2)}, u32[]{:S(2)}) collective-permute-start(bf16[2,256,1024]{2,1,0:T(8,128)(2,1)S(1)} %pad_maximum_fusion.16), channel_id=1, source_target_pairs={{0,4},{1,5},{2,6},{3,7},{4,0},{5,1},{6,2},{7,3},{8,12},{9,13},{10,... | collective-permute-start | bytes 3145736 | tf_op jit(solution)/shard_map/ppermute | solution.py:32
  274.0 36.2 %collective-permute-start.25 = (bf16[2,256,1024]{2,1,0:T(8,128)(2,1)S(1)}, bf16[2,256,1024]{2,1,0:T(8,128)(2,1)S(1)}, u32[]{:S(2)}, u32[]{:S(2)}) collective-permute-start(bf16[2,256,1024]{2,1,0:T(8,128)(2,1)S(1)} %pad_maximum_fusion.17), channel_id=1, source_target_pairs={{0,2},{1,3},{2,0},{3,1},{4,6},{5,7},{6,4},{7,5},{8,10},{9,11},{10,... | collective-permute-start | bytes 3145736 | tf_op jit(solution)/shard_map/ppermute | solution.py:32
  278.3 25.6 %collective-permute-start.37 = (bf16[512,704]{0,1:T(8,128)(2,1)}, bf16[512,704]{0,1:T(8,128)(2,1)}, u32[]{:S(2)}, u32[]{:S(2)}) collective-permute-start(bf16[512,704]{0,1:T(8,128)(2,1)} %copy.284), channel_id=1, source_target_pairs={{0,8},{1,9},{2,10},{3,11},{4,12},{5,13},{6,14},{7,15},{8,16},{9,17... | collective-permute-start | bytes 2162696 | tf_op jit(solution)/shard_map/ppermute | solution.py:36
  282.8 23.1 %collective-permute-start.34 = (bf16[512,704]{0,1:T(8,128)(2,1)}, bf16[512,704]{0,1:T(8,128)(2,1)}, u32[]{:S(2)}, u32[]{:S(2)}) collective-permute-start(bf16[512,704]{0,1:T(8,128)(2,1)} %collective-permute-done.30), channel_id=1, source_target_pairs={{8,0},{9,1},{10,2},{11,3},{12,4},{13,5},{14,6},{15,7},{16,8},{17,9... | collective-permute-start | bytes 2162696 | tf_op jit(solution)/shard_map/ppermute | solution.py:36
  296.0 72.1 %collective-permute-start.57 = (bf16[2,2,256,2048]{3,2,0,1:T(8,128)(2,1)}, bf16[2,2,256,2048]{3,2,0,1:T(8,128)(2,1)}, u32[]{:S(2)}, u32[]{:S(2)}) collective-permute-start(bf16[2,2,256,2048]{3,2,0,1:T(8,128)(2,1)} %maximum_maximum_fusion.2), channel_id=1, source_target_pairs={{0,1},{1,0},{2,3},{3,2},{4,5},{5,4},{6,7},{7,6},{8,9},{9,8},{10,11... | collective-permute-start | bytes 12582920 | tf_op jit(solution)/shard_map/ppermute | solution.py:32
  305.9 28.5 %collective-permute-start.38 = (bf16[512,704]{0,1:T(8,128)(2,1)}, bf16[512,704]{0,1:T(8,128)(2,1)}, u32[]{:S(2)}, u32[]{:S(2)}) collective-permute-start(bf16[512,704]{0,1:T(8,128)(2,1)} %collective-permute-done.37), channel_id=1, source_target_pairs={{8,16},{9,17},{10,18},{11,19},{12,20},{13,21},{14,22},{15,23},{16,... | collective-permute-start | bytes 2162696 | tf_op jit(solution)/shard_map/ppermute | solution.py:36
  310.1 30.8 %collective-permute-start.35 = (bf16[512,704]{0,1:T(8,128)(2,1)}, bf16[512,704]{0,1:T(8,128)(2,1)}, u32[]{:S(2)}, u32[]{:S(2)}) collective-permute-start(bf16[512,704]{0,1:T(8,128)(2,1)} %collective-permute-done.34), channel_id=1, source_target_pairs={{8,0},{9,1},{10,2},{11,3},{12,4},{13,5},{14,6},{15,7}} | collective-permute-start | bytes 2162696 | tf_op jit(solution)/shard_map/ppermute | solution.py:36
  318.9 69.0 %collective-permute-start.26 = (bf16[2,2,256,2048]{3,2,0,1:T(8,128)(2,1)}, bf16[2,2,256,2048]{3,2,0,1:T(8,128)(2,1)}, u32[]{:S(2)}, u32[]{:S(2)}) collective-permute-start(bf16[2,2,256,2048]{3,2,0,1:T(8,128)(2,1)} %maximum_maximum_fusion.1), channel_id=1, source_target_pairs={{0,1},{1,0},{2,3},{3,2},{4,5},{5,4},{6,7},{7,6},{8,9},{9,8},{10,11... | collective-permute-start | bytes 12582920 | tf_op jit(solution)/shard_map/ppermute | solution.py:32
  323.3 23.5 %collective-permute-start.33 = (bf16[512,704]{0,1:T(8,128)(2,1)}, bf16[512,704]{0,1:T(8,128)(2,1)}, u32[]{:S(2)}, u32[]{:S(2)}) collective-permute-start(bf16[512,704]{0,1:T(8,128)(2,1)} %collective-permute-done.32), channel_id=1, source_target_pairs={{16,24},{17,25},{18,26},{19,27},{20,28},{21,29},{22,30},{23,31}} | collective-permute-start | bytes 2162696 | tf_op jit(solution)/shard_map/ppermute | solution.py:36
  555.8 144.1 %collective-permute-start.58 = (bf16[2,2,256,2048]{3,2,1,0:T(8,128)(2,1)}, bf16[2,2,256,2048]{3,2,1,0:T(8,128)(2,1)}, u32[]{:S(2)}, u32[]{:S(2)}) collective-permute-start(bf16[2,2,256,2048]{3,2,1,0:T(8,128)(2,1)} %dynamic-slice_bitcast_fusion.1), channel_id=1, source_target_pairs={{0,1},{1,0},{2,3},{3,2},{4,5},{5,4},{6,7},{7,6},{8,9},{9,8},{10,11... | collective-permute-start | bytes 12582920 | tf_op jit(solution)/shard_map/ppermute | solution.py:32
  556.6 29.2 %collective-permute-start.100 = (bf16[176,2048]{1,0:T(8,128)(2,1)S(1)}, bf16[176,2048]{1,0:T(8,128)(2,1)S(1)}, u32[]{:S(2)}, u32[]{:S(2)}) collective-permute-start(bf16[176,2048]{1,0:T(8,128)(2,1)S(1)} %get-tuple-element.371), channel_id=1, source_target_pairs={{24,16},{25,17},{26,18},{27,19},{28,20},{29,21},{30,22},{31,23}} | collective-permute-start | bytes 2162696 | tf_op jit(solution)/shard_map/ppermute | solution.py:36
  563.3 20.9 %collective-permute-start.88 = (bf16[512,704]{0,1:T(8,128)(2,1)S(1)}, bf16[512,704]{0,1:T(8,128)(2,1)S(1)}, u32[]{:S(2)}, u32[]{:S(2)}) collective-permute-start(bf16[512,704]{0,1:T(8,128)(2,1)S(1)} %bitcast.771), channel_id=1, source_target_pairs={{0,8},{1,9},{2,10},{3,11},{4,12},{5,13},{6,14},{7,15}} | collective-permute-start | bytes 2162696 | tf_op jit(solution)/shard_map/ppermute | solution.py:36
  568.8 46.1 %collective-permute-start.103 = (bf16[176,2048]{1,0:T(8,128)(2,1)S(1)}, bf16[176,2048]{1,0:T(8,128)(2,1)S(1)}, u32[]{:S(2)}, u32[]{:S(2)}) collective-permute-start(bf16[176,2048]{1,0:T(8,128)(2,1)S(1)} %get-tuple-element.372), channel_id=1, source_target_pairs={{0,8},{1,9},{2,10},{3,11},{4,12},{5,13},{6,14},{7,15}} | collective-permute-start | bytes 2162696 | tf_op jit(solution)/shard_map/ppermute | solution.py:36
  570.4 139.7 %collective-permute-start.48 = (bf16[2,2,256,2048]{3,2,1,0:T(8,128)(2,1)}, bf16[2,2,256,2048]{3,2,1,0:T(8,128)(2,1)}, u32[]{:S(2)}, u32[]{:S(2)}) collective-permute-start(bf16[2,2,256,2048]{3,2,1,0:T(8,128)(2,1)} %dynamic-slice_bitcast_fusion.2), channel_id=1, source_target_pairs={{0,1},{1,0},{2,3},{3,2},{4,5},{5,4},{6,7},{7,6},{8,9},{9,8},{10,11... | collective-permute-start | bytes 12582920 | tf_op jit(solution)/shard_map/ppermute | solution.py:32
  584.2 44.9 %collective-permute-start.92 = (bf16[512,704]{0,1:T(8,128)(2,1)S(1)}, bf16[512,704]{0,1:T(8,128)(2,1)S(1)}, u32[]{:S(2)}, u32[]{:S(2)}) collective-permute-start(bf16[512,704]{0,1:T(8,128)(2,1)S(1)} %fusion.78), channel_id=1, source_target_pairs={{16,8},{17,9},{18,10},{19,11},{20,12},{21,13},{22,14},{23,15},{24,... | collective-permute-start | bytes 2162696 | tf_op jit(solution)/shard_map/ppermute | solution.py:36
  585.8 46.7 %collective-permute-start.95 = (bf16[512,704]{0,1:T(8,128)(2,1)S(1)}, bf16[512,704]{0,1:T(8,128)(2,1)S(1)}, u32[]{:S(2)}, u32[]{:S(2)}) collective-permute-start(bf16[512,704]{0,1:T(8,128)(2,1)S(1)} %fusion.76), channel_id=1, source_target_pairs={{0,8},{1,9},{2,10},{3,11},{4,12},{5,13},{6,14},{7,15},{8,16},{9,17... | collective-permute-start | bytes 2162696 | tf_op jit(solution)/shard_map/ppermute | solution.py:36
  614.9 29.7 %collective-permute-start.86 = (bf16[512,704]{0,1:T(8,128)(2,1)S(1)}, bf16[512,704]{0,1:T(8,128)(2,1)S(1)}, u32[]{:S(2)}, u32[]{:S(2)}) collective-permute-start(bf16[512,704]{0,1:T(8,128)(2,1)S(1)} %fusion.84), channel_id=1, source_target_pairs={{16,8},{17,9},{18,10},{19,11},{20,12},{21,13},{22,14},{23,15},{24,... | collective-permute-start | bytes 2162696 | tf_op jit(solution)/shard_map/ppermute | solution.py:36
  632.6 27.4 %collective-permute-start.101 = (bf16[176,2048]{1,0:T(8,128)(2,1)S(1)}, bf16[176,2048]{1,0:T(8,128)(2,1)S(1)}, u32[]{:S(2)}, u32[]{:S(2)}) collective-permute-start(bf16[176,2048]{1,0:T(8,128)(2,1)S(1)} %fusion.73), channel_id=1, source_target_pairs={{16,8},{17,9},{18,10},{19,11},{20,12},{21,13},{22,14},{23,15},{24,... | collective-permute-start | bytes 2162696 | tf_op jit(solution)/shard_map/ppermute | solution.py:36
  644.5 30.9 %collective-permute-start.93 = (bf16[512,704]{0,1:T(8,128)(2,1)S(1)}, bf16[512,704]{0,1:T(8,128)(2,1)S(1)}, u32[]{:S(2)}, u32[]{:S(2)}) collective-permute-start(bf16[512,704]{0,1:T(8,128)(2,1)S(1)} %fusion.79), channel_id=1, source_target_pairs={{8,0},{9,1},{10,2},{11,3},{12,4},{13,5},{14,6},{15,7},{16,8},{17,9... | collective-permute-start | bytes 2162696 | tf_op jit(solution)/shard_map/ppermute | solution.py:36
  647.9 32.3 %collective-permute-start.96 = (bf16[512,704]{0,1:T(8,128)(2,1)S(1)}, bf16[512,704]{0,1:T(8,128)(2,1)S(1)}, u32[]{:S(2)}, u32[]{:S(2)}) collective-permute-start(bf16[512,704]{0,1:T(8,128)(2,1)S(1)} %fusion.77), channel_id=1, source_target_pairs={{0,8},{1,9},{2,10},{3,11},{4,12},{5,13},{6,14},{7,15},{8,16},{9,17... | collective-permute-start | bytes 2162696 | tf_op jit(solution)/shard_map/ppermute | solution.py:36
  660.0 31.0 %collective-permute-start.87 = (bf16[512,704]{0,1:T(8,128)(2,1)}, bf16[512,704]{0,1:T(8,128)(2,1)}, u32[]{:S(2)}, u32[]{:S(2)}) collective-permute-start(bf16[512,704]{0,1:T(8,128)(2,1)} %fusion.85), channel_id=1, source_target_pairs={{8,0},{9,1},{10,2},{11,3},{12,4},{13,5},{14,6},{15,7},{16,8},{17,9... | collective-permute-start | bytes 2162696 | tf_op jit(solution)/shard_map/ppermute | solution.py:36
  680.2 115.1 %collective-permute-start.104 = (bf16[176,2048]{1,0:T(8,128)(2,1)}, bf16[176,2048]{1,0:T(8,128)(2,1)}, u32[]{:S(2)}, u32[]{:S(2)}) collective-permute-start(bf16[176,2048]{1,0:T(8,128)(2,1)} %get-tuple-element.370), channel_id=1, source_target_pairs={{0,8},{1,9},{2,10},{3,11},{4,12},{5,13},{6,14},{7,15},{8,16},{9,17... | collective-permute-start | bytes 2162696 | tf_op jit(solution)/shard_map/ppermute | solution.py:36
  691.0 285.8 %collective-permute-start.102 = (bf16[176,2048]{1,0:T(8,128)(2,1)}, bf16[176,2048]{1,0:T(8,128)(2,1)}, u32[]{:S(2)}, u32[]{:S(2)}) collective-permute-start(bf16[176,2048]{1,0:T(8,128)(2,1)} %get-tuple-element.369), channel_id=1, source_target_pairs={{8,0},{9,1},{10,2},{11,3},{12,4},{13,5},{14,6},{15,7},{16,8},{17,9... | collective-permute-start | bytes 2162696 | tf_op jit(solution)/shard_map/ppermute | solution.py:36
  707.1 22.1 %collective-permute-start.59 = (bf16[2,256,1024]{2,1,0:T(8,128)(2,1)}, bf16[2,256,1024]{2,1,0:T(8,128)(2,1)}, u32[]{:S(2)}, u32[]{:S(2)}) collective-permute-start(bf16[2,256,1024]{2,1,0:T(8,128)(2,1)} %dynamic-slice_bitcast_fusion.9), channel_id=1, source_target_pairs={{0,2},{1,3},{2,0},{3,1},{4,6},{5,7},{6,4},{7,5},{8,10},{9,11},{10,... | collective-permute-start | bytes 3145736 | tf_op jit(solution)/shard_map/ppermute | solution.py:32
  709.3 22.3 %collective-permute-start.61 = (bf16[2,256,1024]{2,1,0:T(8,128)(2,1)}, bf16[2,256,1024]{2,1,0:T(8,128)(2,1)}, u32[]{:S(2)}, u32[]{:S(2)}) collective-permute-start(bf16[2,256,1024]{2,1,0:T(8,128)(2,1)} %dynamic-slice_bitcast_fusion.8), channel_id=1, source_target_pairs={{0,4},{1,5},{2,6},{3,7},{4,0},{5,1},{6,2},{7,3},{8,12},{9,13},{10,... | collective-permute-start | bytes 3145736 | tf_op jit(solution)/shard_map/ppermute | solution.py:32
  714.8 36.8 %collective-permute-start.49 = (bf16[2,256,1024]{2,1,0:T(8,128)(2,1)S(1)}, bf16[2,256,1024]{2,1,0:T(8,128)(2,1)S(1)}, u32[]{:S(2)}, u32[]{:S(2)}) collective-permute-start(bf16[2,256,1024]{2,1,0:T(8,128)(2,1)S(1)} %dynamic-slice_bitcast_fusion.11), channel_id=1, source_target_pairs={{0,2},{1,3},{2,0},{3,1},{4,6},{5,7},{6,4},{7,5},{8,10},{9,11},{10,... | collective-permute-start | bytes 3145736 | tf_op jit(solution)/shard_map/ppermute | solution.py:32
  729.2 23.5 %collective-permute-start.51 = (bf16[2,256,1024]{2,1,0:T(8,128)(2,1)S(1)}, bf16[2,256,1024]{2,1,0:T(8,128)(2,1)S(1)}, u32[]{:S(2)}, u32[]{:S(2)}) collective-permute-start(bf16[2,256,1024]{2,1,0:T(8,128)(2,1)S(1)} %dynamic-slice_bitcast_fusion.10), channel_id=1, source_target_pairs={{0,4},{1,5},{2,6},{3,7},{4,0},{5,1},{6,2},{7,3},{8,12},{9,13},{10,... | collective-permute-start | bytes 3145736 | tf_op jit(solution)/shard_map/ppermute | solution.py:32
  731.6 68.2 %collective-permute-start.97 = (bf16[2,2,64,2,704]{4,2,3,1,0:T(8,128)(2,1)}, bf16[2,2,64,2,704]{4,2,3,1,0:T(8,128)(2,1)}, u32[]{:S(2)}, u32[]{:S(2)}) collective-permute-start(bf16[2,2,64,2,704]{4,2,3,1,0:T(8,128)(2,1)} %bitcast.660), channel_id=1, source_target_pairs={{0,1},{1,0},{2,3},{3,2},{4,5},{5,4},{6,7},{7,6},{8,9},{9,8},{10,11... | collective-permute-start | bytes 2162696 | tf_op jit(solution)/shard_map/ppermute | solution.py:32
  785.8 22.1 %all-to-all-start.1 = ((bf16[256,4,512]{0,2,1:T(8,128)(2,1)}), bf16[256,4,512]{0,2,1:T(8,128)(2,1)}, u32[]{:S(2)}, u32[]{:S(2)}) async-start(bf16[256,4,512]{0,2,1:T(8,128)(2,1)} %bitcast.752), calls=%async_computation.1 | async-start | bytes 2097152 | tf_op jit(solution)/shard_map/all_to_all | solution.py:324
  797.5 179.3 %collective-permute-start.105 = (bf16[176,2048]{1,0:T(8,128)(2,1)}, bf16[176,2048]{1,0:T(8,128)(2,1)}, u32[]{:S(2)}, u32[]{:S(2)}) collective-permute-start(bf16[176,2048]{1,0:T(8,128)(2,1)} %fusion.72), channel_id=1, source_target_pairs={{0,8},{1,9},{2,10},{3,11},{4,12},{5,13},{6,14},{7,15},{8,16},{9,17... | collective-permute-start | bytes 2162696 | tf_op jit(solution)/shard_map/ppermute | solution.py:36
  803.3 155.3 %collective-permute-start.98 = (bf16[2,2,64,2,704]{4,2,3,1,0:T(8,128)(2,1)}, bf16[2,2,64,2,704]{4,2,3,1,0:T(8,128)(2,1)}, u32[]{:S(2)}, u32[]{:S(2)}) collective-permute-start(bf16[2,2,64,2,704]{4,2,3,1,0:T(8,128)(2,1)} %bitcast.659), channel_id=1, source_target_pairs={{0,2},{1,3},{2,0},{3,1},{4,6},{5,7},{6,4},{7,5},{8,10},{9,11},{10,... | collective-permute-start | bytes 2162696 | tf_op jit(solution)/shard_map/ppermute | solution.py:32
  945.5 29.5 %collective-permute-start.65 = (bf16[4,256,640]{2,1,0:T(8,128)(2,1)S(1)}, bf16[4,256,640]{2,1,0:T(8,128)(2,1)S(1)}, u32[]{:S(2)}, u32[]{:S(2)}) collective-permute-start(bf16[4,256,640]{2,1,0:T(8,128)(2,1)S(1)} %dynamic-slice_bitcast_fusion.4), channel_id=1, source_target_pairs={{0,4},{1,5},{2,6},{3,7},{4,0},{5,1},{6,2},{7,3},{8,12},{9,13},{10,... | collective-permute-start | bytes 3932168 | tf_op jit(solution)/shard_map/ppermute | solution.py:32
  957.7 86.9 %collective-permute-start.74 = (bf16[4,2,2,64,2048]{4,3,0,2,1:T(8,128)(2,1)}, bf16[4,2,2,64,2048]{4,3,0,2,1:T(8,128)(2,1)}, u32[]{:S(2)}, u32[]{:S(2)}) collective-permute-start(bf16[4,2,2,64,2048]{4,3,0,2,1:T(8,128)(2,1)} %bitcast.657), channel_id=1, source_target_pairs={{0,1},{1,0},{2,3},{3,2},{4,5},{5,4},{6,7},{7,6},{8,9},{9,8},{10,11... | collective-permute-start | bytes 12582920 | tf_op jit(solution)/shard_map/ppermute | solution.py:32
  959.9 31.9 %collective-permute-start.99 = (bf16[2,2,64,2,704]{4,2,3,1,0:T(8,128)(2,1)S(1)}, bf16[2,2,64,2,704]{4,2,3,1,0:T(8,128)(2,1)S(1)}, u32[]{:S(2)}, u32[]{:S(2)}) collective-permute-start(bf16[2,2,64,2,704]{4,2,3,1,0:T(8,128)(2,1)S(1)} %fusion.94), channel_id=1, source_target_pairs={{0,4},{1,5},{2,6},{3,7},{4,0},{5,1},{6,2},{7,3},{8,12},{9,13},{10,... | collective-permute-start | bytes 2162696 | tf_op jit(solution)/shard_map/ppermute | solution.py:32
  979.8 36.4 %collective-permute-start.69 = (bf16[256,640]{1,0:T(8,128)(2,1)}, bf16[256,640]{1,0:T(8,128)(2,1)}, u32[]{:S(2)}, u32[]{:S(2)}) collective-permute-start(bf16[256,640]{1,0:T(8,128)(2,1)} %get-tuple-element.446), channel_id=1, source_target_pairs={{0,8},{1,9},{2,10},{3,11},{4,12},{5,13},{6,14},{7,15}} | collective-permute-start | bytes 983048 | tf_op jit(solution)/shard_map/ppermute | solution.py:36
  981.9 34.3 %collective-permute-start.67 = (bf16[256,640]{1,0:T(8,128)(2,1)}, bf16[256,640]{1,0:T(8,128)(2,1)}, u32[]{:S(2)}, u32[]{:S(2)}) collective-permute-start(bf16[256,640]{1,0:T(8,128)(2,1)} %fusion.119), channel_id=1, source_target_pairs={{16,8},{17,9},{18,10},{19,11},{20,12},{21,13},{22,14},{23,15},{24,... | collective-permute-start | bytes 983048 | tf_op jit(solution)/shard_map/ppermute | solution.py:36
  1027.3 23.0 %collective-permute-start.63 = (bf16[2,256,2048]{2,1,0:T(8,128)(2,1)}, bf16[2,256,2048]{2,1,0:T(8,128)(2,1)S(1)}, u32[]{:S(2)}, u32[]{:S(2)}) collective-permute-start(bf16[2,256,2048]{2,1,0:T(8,128)(2,1)} %dynamic-slice_bitcast_fusion.3), channel_id=1, source_target_pairs={{0,1},{1,0},{2,3},{3,2},{4,5},{5,4},{6,7},{7,6},{8,9},{9,8},{10,11... | collective-permute-start | bytes 6291464 | tf_op jit(solution)/shard_map/ppermute | solution.py:32
  1049.5 29.9 %collective-permute-start.77 = (bf16[4,2,64,1024]{3,2,0,1:T(8,128)(2,1)S(1)}, bf16[4,2,64,1024]{3,2,0,1:T(8,128)(2,1)S(1)}, u32[]{:S(2)}, u32[]{:S(2)}) collective-permute-start(bf16[4,2,64,1024]{3,2,0,1:T(8,128)(2,1)S(1)} %dynamic-slice_bitcast_fusion.5), channel_id=1, source_target_pairs={{0,4},{1,5},{2,6},{3,7},{4,0},{5,1},{6,2},{7,3},{8,12},{9,13},{10,... | collective-permute-start | bytes 3145736 | tf_op jit(solution)/shard_map/ppermute | solution.py:32
  1051.4 30.6 %collective-permute-start.75 = (bf16[4,2,64,1024]{3,2,0,1:T(8,128)(2,1)S(1)}, bf16[4,2,64,1024]{3,2,0,1:T(8,128)(2,1)S(1)}, u32[]{:S(2)}, u32[]{:S(2)}) collective-permute-start(bf16[4,2,64,1024]{3,2,0,1:T(8,128)(2,1)S(1)} %dynamic-slice_bitcast_fusion.6), channel_id=1, source_target_pairs={{0,2},{1,3},{2,0},{3,1},{4,6},{5,7},{6,4},{7,5},{8,10},{9,11},{10,... | collective-permute-start | bytes 3145736 | tf_op jit(solution)/shard_map/ppermute | solution.py:32
  1052.6 26.7 %collective-permute-start.73 = (bf16[2,64,640]{2,1,0:T(8,128)(2,1)S(1)}, bf16[2,64,640]{2,1,0:T(8,128)(2,1)S(1)}, u32[]{:S(2)}, u32[]{:S(2)}) collective-permute-start(bf16[2,64,640]{2,1,0:T(8,128)(2,1)S(1)} %fusion.149), channel_id=1, source_target_pairs={{0,2},{1,3},{2,0},{3,1},{4,6},{5,7},{6,4},{7,5},{8,10},{9,11},{10,... | collective-permute-start | bytes 491528 | tf_op jit(solution)/shard_map/ppermute | solution.py:32
  1054.1 64.0 %collective-permute-start.64 = (bf16[256,2048]{1,0:T(8,128)(2,1)}, bf16[256,2048]{1,0:T(8,128)(2,1)S(1)}, u32[]{:S(2)}, u32[]{:S(2)}) collective-permute-start(bf16[256,2048]{1,0:T(8,128)(2,1)} %dynamic-slice_bitcast_fusion.7), channel_id=1, source_target_pairs={{0,2},{1,3},{2,0},{3,1},{4,6},{5,7},{6,4},{7,5},{8,10},{9,11},{10,... | collective-permute-start | bytes 3145736 | tf_op jit(solution)/shard_map/ppermute | solution.py:32
  1080.8 32.4 %collective-permute-start.78 = (bf16[4,64,1024]{2,1,0:T(8,128)(2,1)}, bf16[4,64,1024]{2,1,0:T(8,128)(2,1)}, u32[]{:S(2)}, u32[]{:S(2)}) collective-permute-start(bf16[4,64,1024]{2,1,0:T(8,128)(2,1)} %dynamic-slice_bitcast_fusion.15), channel_id=1, source_target_pairs={{0,2},{1,3},{2,0},{3,1},{4,6},{5,7},{6,4},{7,5},{8,10},{9,11},{10,... | collective-permute-start | bytes 1572872 | tf_op jit(solution)/shard_map/ppermute | solution.py:32
  1084.2 30.4 %collective-permute-start.76 = (bf16[4,64,1024]{2,1,0:T(8,128)(2,1)}, bf16[4,64,1024]{2,1,0:T(8,128)(2,1)}, u32[]{:S(2)}, u32[]{:S(2)}) collective-permute-start(bf16[4,64,1024]{2,1,0:T(8,128)(2,1)} %dynamic-slice_bitcast_fusion.16), channel_id=1, source_target_pairs={{0,4},{1,5},{2,6},{3,7},{4,0},{5,1},{6,2},{7,3},{8,12},{9,13},{10,... | collective-permute-start | bytes 1572872 | tf_op jit(solution)/shard_map/ppermute | solution.py:32
  (174 other events, 1940.6 us)

commit v2 on v0

v2 whole, which is shorter than its diff:
```python
import math

import jax
import jax.numpy as jnp
from jax import lax
from jax.experimental import pallas as pl
from jax.experimental.pallas import tpu as pltpu
from jax.sharding import Mesh
from jax.sharding import PartitionSpec as P

HEADS = 32
HEAD = 64
KVH = 4
FF = 5632

epsilon = 1e-05
rope_base = 10000.0
neg_large = -1e30
bf = jnp.bfloat16
f32 = jnp.float32
QUAD = ("y", "x", "c")
TAIL = 64


def doc_layout(length_row, row_count):
    docs = jnp.arange(length_row.shape[0], dtype=jnp.int32)
    doc_ends = jnp.sum(jnp.where(docs[None, :] <= docs[:, None], length_row[None, :], 0), axis=1)
    doc_starts = doc_ends - length_row
    where_at = jnp.arange(row_count, dtype=jnp.int32)
    segment = jnp.sum((where_at[:, None] >= doc_ends[None, :]).astype(jnp.int32), axis=1)
    member = segment[:, None] == docs[None, :]
    doc_begin = jnp.sum(jnp.where(member, doc_starts[None, :], 0), axis=1)
    return where_at - doc_begin


def angle_tables(position):
    half_size = HEAD // 2
    freq_row = rope_base ** (-2.0 * jnp.arange(half_size, dtype=f32) / HEAD)
    angles = position.astype(f32)[:, None] * freq_row[None, :]
    cos_part, sin_part = jnp.cos(angles), jnp.sin(angles)
    return (
        jnp.concatenate([cos_part] * 4, axis=1),
        jnp.concatenate([-sin_part, sin_part] * 2, axis=1),
    )


def contract_rows(left, right):
    return lax.dot_general(left, right, (((0,), (0,)), ((), ())), preferred_element_type=f32)


def contract_cols(left, right):
    return lax.dot_general(left, right, (((1,), (1,)), ((), ())), preferred_element_type=f32)


def norm_back(scaled, resid, inverse):
    return inverse * scaled - resid * (inverse * inverse * inverse) * jnp.mean(
        scaled * resid, axis=-1, keepdims=True
    )


def turn(vector, cos_table, sin_table):
    half = HEAD // 2
    lane = lax.broadcasted_iota(jnp.int32, vector.shape, 1)
    partner = jnp.where(
        lane % HEAD < half,
        pltpu.roll(vector, vector.shape[1] - half, 1),
        pltpu.roll(vector, half, 1),
    )
    return vector * cos_table + partner * sin_table


def set_keys(both_ref, cos_table, sin_table, key_ref, value_ref):
    both = both_ref[...].astype(f32)
    first = lax.broadcasted_iota(jnp.int32, both.shape, 1) < HEAD
    keys = jnp.where(first, turn(both, cos_table, sin_table), 0.0)
    values = jnp.where(first, 0.0, both)
    key_ref[0] = keys.astype(bf)
    key_ref[1] = pltpu.roll(keys, HEAD, 1).astype(bf)
    value_ref[0] = pltpu.roll(values, HEAD, 1).astype(bf)
    value_ref[1] = values.astype(bf)


def turned_queries(query_ref, cos_table, sin_table):
    turned = turn(query_ref[...].astype(f32), cos_table, sin_table).astype(bf)
    return turned * jnp.asarray(1.0 / math.sqrt(HEAD), bf)


def forward_kernel(query_ref, both_ref, cos_ref, sin_ref, start_ref, mixed_ref, key_ref, value_ref):
    count = query_ref.shape[0]
    block = min(256, count)

    @pl.when(pl.program_id(0) == 0)
    def _():
        set_keys(both_ref, cos_ref[...], sin_ref[...], key_ref, value_ref)

    queries = turned_queries(query_ref, cos_ref[...], sin_ref[...])
    for i in range(count // block):
        here, reach = slice(i * block, (i + 1) * block), (i + 1) * block
        key_at = lax.broadcasted_iota(jnp.int32, (block, reach), 1)
        query_at = lax.broadcasted_iota(jnp.int32, (block, reach), 0) + i * block
        allowed = (key_at <= query_at) & (key_at >= start_ref[here, :])
        mixed = None
        for h in range(2):
            scores = contract_cols(queries[here], key_ref[h, :reach])
            scores = jnp.where(allowed, scores, neg_large)
            raised = jnp.exp(scores - jnp.max(scores, axis=1, keepdims=True))
            shares = (raised * (1.0 / jnp.sum(raised, axis=1, keepdims=True))).astype(bf)
            part = jnp.dot(shares, value_ref[h, :reach], preferred_element_type=f32)
            mixed = part if mixed is None else mixed + part
        mixed_ref[here, :] = mixed.astype(bf)


def backward_kernel(
    query_ref, both_ref, grad_ref, cos_ref, sin_ref, start_ref, out_ref, key_ref, value_ref, dk_ref, dv_ref
):
    count = query_ref.shape[0]
    block = min(256, count)
    step = pl.program_id(0)
    last = pl.num_programs(0) - 1

    @pl.when(step == 0)
    def _():
        set_keys(both_ref, cos_ref[...], sin_ref[...], key_ref, value_ref)
        dk_ref[...] = jnp.zeros_like(dk_ref)
        dv_ref[...] = jnp.zeros_like(dv_ref)

    @pl.when(step < last)
    def _():
        queries = turned_queries(query_ref, cos_ref[...], sin_ref[...])
        for i in range(count // block):
            here, reach = slice(i * block, (i + 1) * block), (i + 1) * block
            key_at = lax.broadcasted_iota(jnp.int32, (reach, block), 0)
            query_at = lax.broadcasted_iota(jnp.int32, (reach, block), 1) + i * block
            allowed = (key_at <= query_at) & (key_at >= start_ref[:, here])
            grads = grad_ref[here, :]
            first = lax.broadcasted_iota(jnp.int32, (reach, 2 * HEAD), 1) < HEAD
            grad_query, to_keys, to_values = None, [], []
            for h in range(2):
                scores = contract_cols(key_ref[h, :reach], queries[here])
                scores = jnp.where(allowed, scores, neg_large)
                raised = jnp.exp(scores - jnp.max(scores, axis=0, keepdims=True))
                shares = raised * (1.0 / jnp.sum(raised, axis=0, keepdims=True))
                grad_shares = contract_cols(value_ref[h, :reach], grads)
                inner = jnp.sum(shares * grad_shares, axis=0, keepdims=True)
                grad_scores = (shares * (grad_shares - inner)).astype(bf)
                to_values.append(jnp.dot(shares.astype(bf), grads, preferred_element_type=f32))
                to_keys.append(jnp.dot(grad_scores, queries[here], preferred_element_type=f32))
                part = contract_rows(grad_scores, key_ref[h, :reach])
                grad_query = part if grad_query is None else grad_query + part
            dv_ref[:reach] += jnp.where(first, to_values[0], to_values[1])
            dk_ref[:reach] += jnp.where(first, to_keys[0], to_keys[1])
            grad_query = grad_query * (1.0 / math.sqrt(HEAD))
            out_ref[here, :] = turn(grad_query, cos_ref[here, :], -sin_ref[here, :]).astype(bf)

    @pl.when(step == last)
    def _():
        grad_keys, grad_values = dk_ref[...], dv_ref[...]
        first = lax.broadcasted_iota(jnp.int32, grad_keys.shape, 1) < HEAD
        grad_keys = turn(grad_keys + pltpu.roll(grad_keys, HEAD, 1), cos_ref[...], -sin_ref[...])
        grad_values = grad_values + pltpu.roll(grad_values, HEAD, 1)
        out_ref[...] = jnp.where(first, grad_keys, grad_values).astype(bf)


def attend_forward(head_cols, cos_table, sin_table, start):
    count, cols = head_cols.shape
    wide = 2 * HEAD
    pairs = cols // wide - 1
    fixed = lambda j: (0, 0)
    return pl.pallas_call(
        forward_kernel,
        grid=(pairs,),
        in_specs=[
            pl.BlockSpec((count, wide), lambda j: (0, j)),
            pl.BlockSpec((count, wide), lambda j: (0, pairs)),
            pl.BlockSpec((count, wide), fixed),
            pl.BlockSpec((count, wide), fixed),
            pl.BlockSpec((count, 1), fixed),
        ],
        out_specs=pl.BlockSpec((count, wide), lambda j: (0, j)),
        out_shape=jax.ShapeDtypeStruct((count, pairs * wide), bf),
        scratch_shapes=[pltpu.VMEM((2, count, wide), bf), pltpu.VMEM((2, count, wide), bf)],
        compiler_params=pltpu.CompilerParams(vmem_limit_bytes=40 * 1024 * 1024),
        cost_estimate=pl.CostEstimate(
            flops=24 * pairs * count * count * wide, bytes_accessed=6 * count * cols, transcendentals=2 * pairs * count * count
        ),
        name="attend_forward",
    )(head_cols, head_cols, cos_table, sin_table, start[:, None])


def attend_backward(head_cols, grad_heads, cos_table, sin_table, start):
    count, cols = head_cols.shape
    wide = 2 * HEAD
    pairs = cols // wide - 1
    fixed = lambda j: (0, 0)
    at_pair = lambda j: (0, jnp.minimum(j, pairs - 1))
    return pl.pallas_call(
        backward_kernel,
        grid=(pairs + 1,),
        in_specs=[
            pl.BlockSpec((count, wide), at_pair),
            pl.BlockSpec((count, wide), lambda j: (0, pairs)),
            pl.BlockSpec((count, wide), at_pair),
            pl.BlockSpec((count, wide), fixed),
            pl.BlockSpec((count, wide), fixed),
            pl.BlockSpec((1, count), fixed),
        ],
        out_specs=pl.BlockSpec((count, wide), lambda j: (0, j)),
        out_shape=jax.ShapeDtypeStruct((count, cols), bf),
        scratch_shapes=[
            pltpu.VMEM((2, count, wide), bf),
            pltpu.VMEM((2, count, wide), bf),
            pltpu.VMEM((count, wide), f32),
            pltpu.VMEM((count, wide), f32),
        ],
        compiler_params=pltpu.CompilerParams(vmem_limit_bytes=40 * 1024 * 1024),
        cost_estimate=pl.CostEstimate(
            flops=60 * pairs * count * count * wide, bytes_accessed=8 * count * cols, transcendentals=2 * pairs * count * count
        ),
        name="attend_backward",
    )(head_cols, head_cols, grad_heads, cos_table, sin_table, start[None, :])


def swap(value, axis):
    return lax.ppermute(value, axis, [(0, 1), (1, 0)])


def cross(value):
    return lax.ppermute(value, ("y", "x"), [(i, 3 - i) for i in range(4)])


def pick(value, axis, dim, other=False):
    index = lax.axis_index(axis)
    if other:
        index = 1 - index
    return lax.dynamic_index_in_dim(value, index, dim, keepdims=False)


def pair(mine, theirs, axis, dim):
    zero = lax.axis_index(axis) == 0
    first = jnp.where(zero, mine, theirs)
    second = jnp.where(zero, theirs, mine)
    return jnp.stack([first, second], axis=dim)


def gather_pair(value, axis, dim):
    return pair(value, swap(value, axis), axis, dim)


def reduce_pair(value, axis, dim):
    theirs = swap(pick(value, axis, dim, other=True), axis)
    return pick(value, axis, dim).astype(f32) + theirs.astype(f32)


def rotations(value):
    depth = lax.axis_size("z")
    pieces = [value]
    for r in range(1, depth):
        pieces.append(lax.ppermute(value, "z", [((i + r) % depth, i) for i in range(depth)]))
    return pieces


def gather_near(value):
    chips = jnp.concatenate([value, swap(value, "x"), swap(value, "y"), cross(value)], axis=0)
    return jnp.concatenate([chips, swap(chips, "c")], axis=0)


def reduce_near(value):
    half = value.shape[0] // 2
    rows = half // 4
    chips = (value[:half].astype(f32) + swap(value[half:], "c").astype(f32)).astype(bf)
    own, over_x, over_y, over_both = (chips[i * rows : (i + 1) * rows] for i in range(4))
    return (
        own.astype(f32)
        + swap(over_x, "x").astype(f32)
        + swap(over_y, "y").astype(f32)
        + cross(over_both).astype(f32)
    )


def to_units(value, depth, unit_rows):
    rows = value.shape[0]
    parts = value.reshape(rows, 2, depth, 8, unit_rows).transpose(3, 0, 1, 2, 4)
    parts = parts.reshape(8, rows, 2, depth * unit_rows)
    gate, up = parts[:, :, 0], parts[:, :, 1]
    return jnp.concatenate(
        [gate[..., :-TAIL], up[..., :-TAIL], gate[..., -TAIL:], up[..., -TAIL:]], axis=-1
    )


def from_units(value, depth, unit_rows):
    _, rows, width = value.shape
    main = width // 2 - TAIL
    gate = jnp.concatenate([value[..., :main], value[..., 2 * main : 2 * main + TAIL]], axis=-1)
    up = jnp.concatenate([value[..., main : 2 * main], value[..., 2 * main + TAIL :]], axis=-1)
    parts = jnp.stack([gate, up], axis=2).reshape(8, rows, 2, depth, unit_rows)
    return parts.transpose(1, 2, 3, 0, 4).reshape(rows, 2 * FF)


def activations(gate, up, grad_act):
    sig = 1.0 / (1.0 + jnp.exp(-gate))
    swished = gate * sig
    grad_gate = grad_act * up * sig * (1.0 + gate * (1.0 - sig))
    return swished * up, grad_gate, grad_act * swished


def units_kernel(tok_ref, out_ref, w_ref, down_ref, act_ref, grad_ref):
    main = act_ref.shape[1] - TAIL
    hidden = jnp.dot(tok_ref[...], w_ref[...], preferred_element_type=f32)
    grad_act = lax.dot_general(
        out_ref[...], down_ref[...], (((1,), (1,)), ((), ())), preferred_element_type=f32
    )
    act, grad_gate, grad_up = activations(
        hidden[:, :main], hidden[:, main : 2 * main], grad_act[:, :main]
    )
    act_ref[:, :main] = act.astype(bf)
    grad_ref[:, :main] = grad_gate.astype(bf)
    grad_ref[:, main : 2 * main] = grad_up.astype(bf)
    tail = hidden[:, 2 * main :]
    turned = pltpu.roll(tail, TAIL, 1)
    first = lax.broadcasted_iota(jnp.int32, tail.shape, 1) < TAIL
    act, grad_gate, grad_up = activations(
        jnp.where(first, tail, turned), jnp.where(first, turned, tail), grad_act[:, main:]
    )
    act_ref[:, main:] = act[:, :TAIL].astype(bf)
    grad_ref[:, 2 * main :] = jnp.where(first, grad_gate, grad_up).astype(bf)


def run_units(tokens, grads, w_both, w_down):
    count, width = tokens.shape
    units = w_down.shape[0]
    block = min(256, count)
    down = jnp.concatenate([w_down, w_down[-TAIL:]], axis=0)
    whole = lambda i: (0, 0)
    once = pl.Buffered(1)
    return pl.pallas_call(
        units_kernel,
        grid=(count // block,),
        in_specs=[
            pl.BlockSpec((block, width), lambda i: (i, 0)),
            pl.BlockSpec((block, width), lambda i: (i, 0)),
            pl.BlockSpec((width, 2 * units), whole, pipeline_mode=once),
            pl.BlockSpec((units + TAIL, width), whole, pipeline_mode=once),
        ],
        out_specs=[
            pl.BlockSpec((block, units), lambda i: (i, 0)),
            pl.BlockSpec((block, 2 * units), lambda i: (i, 0)),
        ],
        out_shape=[
            jax.ShapeDtypeStruct((count, units), bf),
            jax.ShapeDtypeStruct((count, 2 * units), bf),
        ],
        compiler_params=pltpu.CompilerParams(vmem_limit_bytes=48 * 1024 * 1024),
        cost_estimate=pl.CostEstimate(
            flops=6 * count * width * units,
            bytes_accessed=2 * (2 * count * width + 3 * units * width + 3 * count * units),
            transcendentals=count * units,
        ),
        name="units",
    )(tokens, grads, w_both, down)


def body(layer_in, doc_lengths, norm_attn, w_qkv, w_out, norm_mlp, w_gateup, w_down, grad_out):
    depth = lax.axis_size("z")
    z_at = lax.axis_index("z")
    rows, width = layer_in.shape
    group_rows = rows * 4
    per_group = HEADS // KVH
    q_width = per_group * HEAD
    cols = q_width + 2 * HEAD
    w_rows = w_qkv.shape[0]
    ff_rows = w_down.shape[0]
    units = ff_rows * depth
    gain_one = norm_attn.astype(f32)[:, None]
    gain_two = norm_mlp.astype(f32)[:, None]

    group_in = gather_pair(gather_pair(layer_in, "x", 0), "c", 1).reshape(group_rows, width)
    qkv = (w_qkv.astype(f32) * gain_one).astype(bf).reshape(w_rows, 4, cols).transpose(1, 0, 2)
    qkv = lax.all_to_all(qkv, ("x", "c"), 0, 0, tiled=True).reshape(4 * w_rows, cols)
    full_qkv = jnp.zeros((depth, 2, 4 * w_rows, cols), bf)
    for r, piece in enumerate(rotations(qkv)):
        full_qkv = lax.dynamic_update_index_in_dim(
            full_qkv, gather_pair(piece, "y", 0), (z_at + r) % depth, 0
        )
    qkv = full_qkv.reshape(-1, cols)

    full_down = lax.all_gather(w_down, "z", axis=0, tiled=True)
    gateup = to_units((w_gateup.astype(f32) * gain_two).astype(bf), depth, ff_rows)
    gateup = lax.all_to_all(gateup, QUAD, 0, 0, tiled=True).reshape(8 * w_rows, 2 * units)
    full_gateup = lax.all_gather(gateup, "z", axis=0, tiled=True)

    out_z = jnp.zeros((depth,) + w_out.shape, bf)
    for r, piece in enumerate(rotations(w_out)):
        out_z = lax.dynamic_update_index_in_dim(out_z, piece, (z_at + r) % depth, 0)
    y_at, x_at = lax.axis_index("y"), lax.axis_index("x")
    out_chip = jnp.zeros((depth, 2, 2) + w_out.shape, bf)
    for dy, dx, piece in (
        (0, 0, out_z),
        (0, 1, swap(out_z, "x")),
        (1, 0, swap(out_z, "y")),
        (1, 1, cross(out_z)),
    ):
        place = (0, y_at ^ dy, x_at ^ dx, 0, 0)
        out_chip = lax.dynamic_update_slice(out_chip, piece[:, None, None], place)
    full_out = gather_pair(out_chip, "c", 3).reshape(-1, width)

    position = doc_layout(doc_lengths[0], group_rows)
    start = jnp.arange(group_rows, dtype=jnp.int32) - position
    cos_table, sin_table = angle_tables(position)
    wide_in = group_in.astype(f32)
    normed_one = (
        wide_in * lax.rsqrt(jnp.mean(wide_in * wide_in, axis=-1, keepdims=True) + epsilon)
    ).astype(bf)
    head_cols = jnp.dot(normed_one, qkv, preferred_element_type=f32).astype(bf)
    mixed_heads = attend_forward(head_cols, cos_table, sin_table, start)
    mixed_tok = lax.all_to_all(
        mixed_heads, ("x", "c"), split_axis=0, concat_axis=1, tiled=True
    )
    resid_in = layer_in.astype(f32)
    resid_mid = resid_in + jnp.dot(mixed_tok, full_out, preferred_element_type=f32)

    inv_two = lax.rsqrt(jnp.mean(resid_mid * resid_mid, axis=-1, keepdims=True) + epsilon)
    many_out = gather_near(grad_out)
    normed_two = gather_near((resid_mid * inv_two).astype(bf))
    activated, grad_gate_up = run_units(normed_two, many_out, full_gateup, full_down)
    scaled_two = reduce_near(contract_cols(grad_gate_up, full_gateup).astype(bf))
    grad_gateup = contract_rows(normed_two, grad_gate_up).astype(bf)
    grad_down = contract_rows(activated, many_out).astype(bf)
    sum_gateup = lax.psum_scatter(grad_gateup, "z", scatter_dimension=0, tiled=True)
    grad_w_down = lax.psum_scatter(grad_down, "z", scatter_dimension=0, tiled=True).astype(f32)
    layer_out = resid_mid + reduce_near(
        jnp.dot(activated, full_down, preferred_element_type=f32).astype(bf)
    )

    grad_mid = grad_out.astype(f32) + norm_back(scaled_two, resid_mid, inv_two)
    grad_mid_low = grad_mid.astype(bf)
    grad_mixed = contract_cols(grad_mid_low, full_out).astype(bf)
    grad_heads = lax.all_to_all(grad_mixed, ("x", "c"), split_axis=1, concat_axis=0, tiled=True)
    grad_cols = attend_backward(head_cols, grad_heads, cos_table, sin_table, start)
    part_one = contract_cols(grad_cols, qkv).astype(bf).reshape(2, 2, rows, width)
    scaled_one = reduce_pair(reduce_pair(part_one, "c", 1).astype(bf), "x", 0)
    inv_one = lax.rsqrt(jnp.mean(resid_in * resid_in, axis=-1, keepdims=True) + epsilon)
    grad_in = grad_mid + norm_back(scaled_one, resid_in, inv_one)

    sum_gateup = lax.all_to_all(sum_gateup.reshape(8, w_rows, 2 * units), QUAD, 0, 0, tiled=True)
    sum_gateup = from_units(sum_gateup, depth, ff_rows).astype(f32)
    grad_w_gateup = sum_gateup * gain_two
    grad_norm_mlp = jnp.sum(sum_gateup * w_gateup.astype(f32), axis=1)

    grad_out_w = contract_rows(mixed_tok, grad_mid_low).astype(bf)
    grad_out_w = reduce_pair(grad_out_w.reshape(depth, 4, 2, w_rows, width), "c", 2).astype(bf)
    grad_out_w = lax.all_to_all(grad_out_w.transpose(1, 0, 2, 3), ("y", "x"), 0, 0, tiled=True)
    grad_out_w = jnp.sum(grad_out_w.astype(f32), axis=0).astype(bf)
    grad_w_out = lax.psum_scatter(grad_out_w, "z", scatter_dimension=0, tiled=False).astype(f32)

    grad_qkv = contract_rows(normed_one, grad_cols).astype(bf)
    grad_qkv = reduce_pair(grad_qkv.reshape(depth, 2, 4 * w_rows, cols), "y", 1).astype(bf)
    grad_qkv = lax.all_to_all(grad_qkv, "z", 0, 0, tiled=True)
    sum_qkv = jnp.sum(grad_qkv.astype(f32), axis=0).astype(bf).reshape(4, w_rows, cols)
    sum_qkv = lax.all_to_all(sum_qkv, ("x", "c"), 0, 0, tiled=True)
    sum_qkv = sum_qkv.transpose(1, 0, 2).reshape(w_rows, 4 * cols).astype(f32)
    grad_w_qkv = sum_qkv * gain_one
    grad_norm_attn = jnp.sum(sum_qkv * w_qkv.astype(f32), axis=1)

    return (
        layer_out,
        grad_in,
        grad_norm_attn,
        grad_w_qkv,
        grad_w_out,
        grad_norm_mlp,
        grad_w_gateup,
        grad_w_down,
    )


def solution(mesh):
    n_dp, n_seq = mesh.devices.shape
    fine = Mesh(mesh.devices.reshape(n_dp // 2, 2, n_seq // 2, 2), ("z", "y", "x", "c"))
    all_axes = ("z", "y", "x", "c")
    rows = P(all_axes, None)
    flat = P(all_axes)
    return jax.shard_map(
        body,
        mesh=fine,
        in_specs=(rows, P(("z", "y"), None), flat, rows, rows, flat, rows, rows, rows),
        out_specs=(rows, rows, flat, rows, rows, flat, rows, rows),
        check_vma=False,
    )
```

time: 2570 us -> 819 us (0.32)
  waiting for transfers between devices: 2030 us -> 322 us
  matrix products: 260 us -> 80.9 us
  blocking collectives: 113 us -> 0 us
  starting transfers between devices: 14.4 us -> 97.4 us
  Pallas kernels: 0 us -> 70.9 us
  other arithmetic: 49.9 us -> 111 us
  local copies, waits for them, and re-layouts: 71.6 us -> 107 us
    reduce_scatter x4 -> x3, waiting for transfers between devices: 1570 us -> 0.02 us  [the longest x1 0.02 us: body(): lax.psum_scatter(grad_gateup, 'z', scatter_dimension=0, tiled=True)]
    all_gather x4 -> x2, waiting for transfers between devices: 405 us -> 0.01 us  [the longest x1 0.01 us: body(): full_down = lax.all_gather(w_down, 'z', axis=0, tiled=True)]
    ppermute x0 -> x36, waiting for transfers between devices: none -> 295 us  [the longest x25 203 us: swap(): return lax.ppermute(value, axis, [(0, 1), (1, 0)])]
    dot_general x18 -> x3, matrix products: 131 us -> 18.9 us  [the longest x1 7.34 us: body(): jnp.dot(activated, full_down, preferred_element_type=f32).astype(bf)]
    unnamed x2 -> x0, blocking collectives: 82.8 us -> none
    pallas_call x0 -> x3, Pallas kernels: none -> 70.9 us  [the longest x1 28.6 us: attend_backward(): pl.pallas_call(backward_kernel, grid=(pairs + 1,), in_specs=[pl.BlockSpec...]
    all_to_all x3 -> x8, starting transfers between devices: 13.8 us -> 57.6 us  [the longest x1 19.7 us: body(): grad_qkv = lax.all_to_all(grad_qkv, 'z', 0, 0, tiled=True)]
    ppermute x0 -> x36, starting transfers between devices: none -> 39.3 us  [the longest x25 26.3 us: swap(): return lax.ppermute(value, axis, [(0, 1), (1, 0)])]
  transfers between devices with their start and end apart: 11 -> 49, of which waited for: 10 -> 15; matrix products, arithmetic and copies ran while one was open for 13% -> 33% of each run, Pallas kernels for 0% -> 5%
where the time goes in v2:
time: 819 us; the launch traced here: 805 us
  waiting for transfers between devices  322 us (39%)
  other arithmetic  111 us (14%)
  local copies, waits for them, and re-layouts  107 us (13%)
  starting transfers between devices  97.4 us (12%)
  matrix products  80.9 us (10%)
  Pallas kernels  70.9 us (9%)
  between operations  15.2 us (2%)
    ppermute x25, waiting for transfers between devices, swap(): return lax.ppermute(value, axis, [(0, 1), (1, 0)])  203 us
    ppermute x5, waiting for transfers between devices, cross(): return lax.ppermute(value, ('y', 'x'), [(i, 3 - i) for i in range(4)])  65 us
    dot_general x4, matrix products, contract_rows(): lax.dot_general(left, right, (((0,), (0,)), ((), ())), preferred_element_...  37.1 us
    pallas_call x1, Pallas kernels, attend_backward(): pl.pallas_call(backward_kernel, grid=(pairs + 1,), in_specs=[pl.BlockSpec...  28.6 us
    pallas_call x1, Pallas kernels, run_units(): pl.pallas_call(units_kernel, grid=(count // block,), in_specs=[pl.BlockSp...  27 us
    ppermute x6, waiting for transfers between devices, rotations(): lax.ppermute(value, 'z', [((i + r) % depth, i) for i in range(depth)])  26.5 us
    ppermute x25, starting transfers between devices, swap(): return lax.ppermute(value, axis, [(0, 1), (1, 0)])  26.3 us
    dot_general x3, matrix products, contract_cols(): lax.dot_general(left, right, (((1,), (1,)), ((), ())), preferred_element_...  24.9 us
  transfers between devices with their start and end apart: 49, of which 15 were waited for; matrix products, arithmetic and copies ran while one was open for 33% of the time, Pallas kernels for 5%

profile of v2, /device:TPU:11, one launch (start us, length us, event | category | flops | bytes accessed | tf_op | source)
XLA Modules:
  0.0 804.8 jit_solution(3318125619675407308)
XLA Ops:
  8.8 4.1 collective-permute-start.10
  15.5 5.7 all-to-all-start
  24.0 2.8 fusion.4
  26.8 5.8 reshape.220
  32.6 3.9 copy.93
  36.5 4.8 reshape.221
  50.8 3.3 concatenate.39
  54.1 4.9 all-to-all-start.2
  65.5 2.5 broadcast_in_dim.104
  69.1 26.5 %collective-permute-done.3 = bf16[256,640]{1,0:T(8,128)(2,1)S(1)} collective-permute-done((bf16[256,640]{1,0:T(8,128)(2,1)}, bf16[256,640]{1,0:T(8,128)(2,1)S(1)}, u32[]{:S(2)}, u32[]{:S(2)}) %collective-permute-start.3) | collective-permute-done | bytes 327712 | tf_op jit(solution)/shard_map/ppermute | solution.py:258
  105.1 17.0 %collective-permute-done.6 = bf16[256,640]{1,0:T(8,128)(2,1)S(1)} collective-permute-done((bf16[256,640]{1,0:T(8,128)(2,1)S(1)}, bf16[256,640]{1,0:T(8,128)(2,1)S(1)}, u32[]{:S(2)}, u32[]{:S(2)}) %collective-permute-start.6) | collective-permute-done | bytes 327712 | tf_op jit(solution)/shard_map/ppermute | solution.py:224
  126.7 20.6 %collective-permute-done.12 = bf16[4,64,2048]{2,1,0:T(8,128)(2,1)S(1)} collective-permute-done((bf16[4,64,2048]{2,1,0:T(8,128)(2,1)S(1)}, bf16[4,64,2048]{2,1,0:T(8,128)(2,1)S(1)}, u32[]{:S(2)}, u32[]{:S(2)}) %collective-permute-start.12) | collective-permute-done | bytes 1048608 | tf_op jit(solution)/shard_map/ppermute | solution.py:224
  147.3 10.4 %collective-permute-start.1 = (bf16[2,256,2048]{2,1,0:T(8,128)(2,1)}, bf16[2,256,2048]{2,1,0:T(8,128)(2,1)}, u32[]{:S(2)}, u32[]{:S(2)}) collective-permute-start(bf16[2,256,2048]{2,1,0:T(8,128)(2,1)} %pad_maximum_fusion.4), channel_id=1, source_target_pairs={{0,1},{1,0},{2,3},{3,2},{4,5},{5,4},{6,7},{7,6},{8,9},{9,8},{10,11... | collective-permute-start | bytes 6291464 | tf_op jit(solution)/shard_map/ppermute | solution.py:224
  164.8 26.1 %collective-permute-done.8 = bf16[256,640]{1,0:T(8,128)(2,1)S(1)} collective-permute-done((bf16[256,640]{1,0:T(8,128)(2,1)S(1)}, bf16[256,640]{1,0:T(8,128)(2,1)S(1)}, u32[]{:S(2)}, u32[]{:S(2)}) %collective-permute-start.8) | collective-permute-done | bytes 327712 | tf_op jit(solution)/shard_map/ppermute | solution.py:224
  196.3 5.2 convolution_convert_fusion.8.query_ref.both_ref
  201.5 15.2 %attend_forward.1 = bf16[1024,512]{1,0:T(8,128)(2,1)S(1)} custom-call(bf16[1024,640]{1,0:T(8,128)(2,1)S(1)} %convolution_convert_fusion.8.query_ref.both_ref, bf16[1024,640]{1,0:T(8,128)(2,1)S(1)} %convolution_convert_fusion.8.query_ref.both_ref, f32[1024,128]{1,0:T(8,128)S(1)} %get-tuple-element.61.cos_ref, f32[1024,128]{1,0:T(8,128)S(1)} %get-tuple-element.62.sin_ref, ...), custom_call_target="tpu_custom_call" | custom-call | flops 12884901888 | bytes 3932160 | tf_op jit(solution)/shard_map/attend_forward/pallas_call | solution.py:169
  218.1 5.6 all-to-all-start.1
  223.9 5.2 select_bitcast_fusion.1
  229.1 6.3 pad_maximum_fusion
  237.3 6.4 multiply_reduce_fusion.2
  247.7 3.8 pad_maximum_fusion.2
  252.8 17.4 %collective-permute-done.18 = bf16[256,2048]{1,0:T(8,128)(2,1)S(1)} collective-permute-done((bf16[256,2048]{1,0:T(8,128)(2,1)S(1)}, bf16[256,2048]{1,0:T(8,128)(2,1)S(1)}, u32[]{:S(2)}, u32[]{:S(2)}) %collective-permute-start.18) | collective-permute-done | bytes 1048608 | tf_op jit(solution)/shard_map/ppermute | solution.py:228
  270.2 23.4 %collective-permute-done.17 = bf16[256,2048]{1,0:T(8,128)(2,1)S(1)} collective-permute-done((bf16[256,2048]{1,0:T(8,128)(2,1)S(1)}, bf16[256,2048]{1,0:T(8,128)(2,1)S(1)}, u32[]{:S(2)}, u32[]{:S(2)}) %collective-permute-start.17) | collective-permute-done | bytes 1048608 | tf_op jit(solution)/shard_map/ppermute | solution.py:224
  306.8 3.9 pad_maximum_fusion.3.down_ref
  310.7 4.8 constant_dynamic-update-slice_fusion.5.out_ref
  318.8 4.7 constant_dynamic-update-slice_fusion.tok_ref
  323.5 27.0 %units.1 = (bf16[2048,704]{1,0:T(8,128)(2,1)S(1)}, bf16[2048,1408]{1,0:T(8,128)(2,1)}) custom-call(bf16[2048,2048]{1,0:T(8,128)(2,1)} %constant_dynamic-update-slice_fusion.tok_ref, bf16[2048,2048]{1,0:T(8,128)(2,1)} %constant_dynamic-update-slice_fusion.5.out_ref, bf16[2048,1408]{1,0:T(8,128)(2,1)} %all-gather.3.cloned.1.call-done.w_ref, ...), custom_call_target="tpu_custom_call" | custom-call | flops 17716740096 | bytes 34078720 | tf_op jit(solution)/shard_map/units/pallas_call | solution.py:335
  350.5 16.9 %convolution_convert_fusion.1 = bf16[2048,2048]{1,0:T(8,128)(2,1)S(1)} fusion(bf16[2048,1408]{1,0:T(8,128)(2,1)} %get-tuple-element.11, bf16[2048,1408]{1,0:T(8,128)(2,1)} %all-gather.3.cloned.1.call-done.w_ref), kind=kOutput, calls=%fused_computation.10 | convolution fusion | flops 11815354368 | bytes 19922944 | tf_op jit(solution)/shard_map/dot_general | solution.py:52
  367.4 2.6 slice.106
  372.7 7.3 convolution_convert_fusion.2
  382.3 3.2 copy-done.18
  386.0 3.8 maximum_convert_fusion
  389.8 9.7 %convolution_convert_fusion.5 = bf16[704,2048]{1,0:T(8,128)(2,1)} fusion(bf16[2048,704]{1,0:T(8,128)(2,1)S(1)} %get-tuple-element.10, bf16[2048,2048]{1,0:T(8,128)(2,1)} %constant_dynamic-update-slice_fusion.5.out_ref), kind=kOutput, calls=%fused_computation.31 | convolution fusion | flops 5907021824 | bytes 14155776 | tf_op jit(solution)/shard_map/dot_general | solution.py:48
  399.6 6.1 fusion.1
  405.7 5.5 add_convert_fusion
  413.6 4.1 add_convert_fusion.1
  424.4 13.4 %collective-permute-done.29 = bf16[256,2048]{1,0:T(8,128)(2,1)} collective-permute-done((bf16[256,2048]{1,0:T(8,128)(2,1)S(1)}, bf16[256,2048]{1,0:T(8,128)(2,1)}, u32[]{:S(2)}, u32[]{:S(2)}) %collective-permute-start.29) | collective-permute-done | bytes 1048608 | tf_op jit(solution)/shard_map/ppermute | solution.py:224
  438.3 19.5 %convolution_convert_fusion.3 = bf16[2048,1408]{1,0:T(8,128)(2,1)} fusion(bf16[2048,2048]{1,0:T(8,128)(2,1)} %constant_dynamic-update-slice_fusion.tok_ref, bf16[2048,1408]{1,0:T(8,128)(2,1)} %get-tuple-element.11), kind=kOutput, calls=%fused_computation.12 | convolution fusion | flops 11814043648 | bytes 19922944 | tf_op jit(solution)/shard_map/dot_general | solution.py:48
  457.8 47.6 %collective-permute-done.31 = bf16[256,2048]{1,0:T(8,128)(2,1)} collective-permute-done((bf16[256,2048]{1,0:T(8,128)(2,1)}, bf16[256,2048]{1,0:T(8,128)(2,1)}, u32[]{:S(2)}, u32[]{:S(2)}) %collective-permute-start.31) | collective-permute-done | bytes 1048608 | tf_op jit(solution)/shard_map/ppermute | solution.py:228
  505.4 8.9 %collective-permute-done.30 = bf16[256,2048]{1,0:T(8,128)(2,1)} collective-permute-done((bf16[256,2048]{1,0:T(8,128)(2,1)}, bf16[256,2048]{1,0:T(8,128)(2,1)}, u32[]{:S(2)}, u32[]{:S(2)}) %collective-permute-start.30) | collective-permute-done | bytes 1048608 | tf_op jit(solution)/shard_map/ppermute | solution.py:224
  514.3 3.1 multiply_reduce_fusion.1
  517.5 7.6 subtract_add_fusion
  528.6 5.8 all-to-all-start.3
  534.5 3.9 convolution_convert_fusion
  538.4 4.3 constant_dynamic-slice_fusion.1
  542.7 4.8 copy.113
  549.2 28.6 %attend_backward.1 = bf16[1024,640]{1,0:T(8,128)(2,1)S(1)} custom-call(bf16[1024,640]{1,0:T(8,128)(2,1)S(1)} %copy-done.1, bf16[1024,640]{1,0:T(8,128)(2,1)S(1)} %copy-done.1, bf16[1024,512]{1,0:T(8,128)(2,1)S(1)} %bitcast.174, f32[1024,128]{1,0:T(8,128)S(1)} %get-tuple-element.61.cos_ref, f32[1024,128]{1,0:T(8,128)S(1)} %get-tuple-element.62.sin_ref, ...), custom_call_target="tpu_custom_call" | custom-call | flops 32212254720 | bytes 5242880 | tf_op jit(solution)/shard_map/attend_backward/pallas_call | solution.py:196
  577.9 4.0 convolution_convert_fusion.6
  583.2 29.1 %collective-permute-done.34 = bf16[4,256,640]{2,1,0:T(8,128)(2,1)S(1)} collective-permute-done((bf16[4,256,640]{2,1,0:T(8,128)(2,1)S(1)}, bf16[4,256,640]{2,1,0:T(8,128)(2,1)S(1)}, u32[]{:S(2)}, u32[]{:S(2)}) %collective-permute-start.34) | collective-permute-done | bytes 1310752 | tf_op jit(solution)/shard_map/ppermute | solution.py:224
  613.7 19.7 %all-to-all-start.4 = ((bf16[4,256,640]{2,1,0:T(8,128)(2,1)}), bf16[4,256,640]{2,1,0:T(8,128)(2,1)}, u32[]{:S(2)}, u32[]{:S(2)}) async-start(bf16[4,256,640]{2,1,0:T(8,128)(2,1)} %fusion.6), calls=%async_computation.4 | async-start | bytes 2621440 | tf_op jit(solution)/shard_map/all_to_all | solution.py:457
  633.3 5.5 convolution_convert_fusion.4
  642.3 18.5 %all-to-all-done.4 = bf16[4,256,640]{2,1,0:T(8,128)(2,1)} async-done(((bf16[4,256,640]{2,1,0:T(8,128)(2,1)}), bf16[4,256,640]{2,1,0:T(8,128)(2,1)}, u32[]{:S(2)}, u32[]{:S(2)}) %all-to-all-start.4) | async-done | bytes 1310752 | tf_op jit(solution)/shard_map/all_to_all | solution.py:457
  663.1 4.8 all-to-all-start.5
  667.9 7.8 fusion.2
  675.7 4.9 all-to-all-start.6
  680.5 3.0 fusion.3
  684.8 2.6 convert_element_type.281
  687.4 62.0 %collective-permute-done.33 = bf16[256,2048]{1,0:T(8,128)(2,1)} collective-permute-done((bf16[256,2048]{1,0:T(8,128)(2,1)}, bf16[256,2048]{1,0:T(8,128)(2,1)}, u32[]{:S(2)}, u32[]{:S(2)}) %collective-permute-start.33) | collective-permute-done | bytes 1048608 | tf_op jit(solution)/shard_map/ppermute | solution.py:224
  751.3 6.2 all-to-all-start.7
  757.7 4.4 reduce_sum.133
  762.2 3.6 fusion.10
  767.4 8.2 %all-to-all-done.7 = bf16[8,64,1408]{2,1,0:T(8,128)(2,1)} async-done(((bf16[8,64,1408]{2,1,0:T(8,128)(2,1)}), bf16[8,64,1408]{2,1,0:T(8,128)(2,1)}, u32[]{:S(2)}, u32[]{:S(2)}) %all-to-all-start.7) | async-done | bytes 1441824 | tf_op jit(solution)/shard_map/all_to_all | solution.py:444
  786.1 5.6 reshape.235
  791.6 4.4 broadcast_multiply_fusion
  (254 shorter events, 121.1 us)
Async XLA Ops:
  7.2 14.1 %copy-start.10 = (bf16[256,2048]{1,0:T(8,128)(2,1)S(1)}, bf16[256,2048]{1,0:T(8,128)(2,1)}, u32[]{:S(2)}) copy-start(bf16[256,2048]{1,0:T(8,128)(2,1)} %param.9) | copy-start | bytes 3145732
  7.2 16.5 %copy-start.38 = (s32[1,8]{1,0:T(1,128)S(1)}, s32[1,8]{1,0:T(1,128)}, u32[]{:S(2)}) copy-start(s32[1,8]{1,0:T(1,128)} %param.10) | copy-start | bytes 100
  7.2 16.7 %copy-start.39 = (bf16[64]{0:T(256)(128)(2,1)S(1)}, bf16[64]{0:T(256)(128)(2,1)}, u32[]{:S(2)}) copy-start(bf16[64]{0:T(256)(128)(2,1)} %param.14) | copy-start | bytes 388
  7.2 298.6 %all-gather.5.cloned.1.call-start = ((), (), s32[]{:S(2)}) async-start(), calls=%async_computation.12 | async-start | bytes 3604480 | tf_op jit(solution)/shard_map/all_gather | solution.py:386
  7.2 51.8 %collective-permute-start.9 = (bf16[64,2048]{1,0:T(8,128)(2,1)}, bf16[64,2048]{1,0:T(8,128)(2,1)}, u32[]{:S(2)}, u32[]{:S(2)}) collective-permute-start(bf16[64,2048]{1,0:T(8,128)(2,1)} %param.13), channel_id=1, source_target_pairs={{8,0},{16,8},{24,16},{0,24},{9,1},{17,9},{25,17},{1,25},{10,2},{18... | collective-permute-start | bytes 786440 | tf_op jit(solution)/shard_map/ppermute | solution.py:258
  7.5 55.1 %collective-permute-start.11 = (bf16[64,2048]{1,0:T(8,128)(2,1)}, bf16[64,2048]{1,0:T(8,128)(2,1)}, u32[]{:S(2)}, u32[]{:S(2)}) collective-permute-start(bf16[64,2048]{1,0:T(8,128)(2,1)} %param.13), channel_id=1, source_target_pairs={{24,0},{0,8},{8,16},{16,24},{25,1},{1,9},{9,17},{17,25},{26,2},{2,... | collective-permute-start | bytes 786440 | tf_op jit(solution)/shard_map/ppermute | solution.py:258
  8.8 52.0 %collective-permute-start.10 = (bf16[64,2048]{1,0:T(8,128)(2,1)}, bf16[64,2048]{1,0:T(8,128)(2,1)}, u32[]{:S(2)}, u32[]{:S(2)}) collective-permute-start(bf16[64,2048]{1,0:T(8,128)(2,1)} %param.13), channel_id=1, source_target_pairs={{16,0},{24,8},{0,16},{8,24},{17,1},{25,9},{1,17},{9,25},{18,2},{26... | collective-permute-start | bytes 786440 | tf_op jit(solution)/shard_map/ppermute | solution.py:258
  13.6 19.0 %copy-start.34 = (f32[64]{0:T(128)}, f32[64]{0:T(128)S(1)}, u32[]{:S(2)}) copy-start(f32[64]{0:T(128)S(1)} %convert_element_type.222) | copy-start | bytes 772
  15.5 38.6 %all-to-all-start = ((bf16[4,64,640]{2,1,0:T(8,128)(2,1)}), bf16[4,64,640]{2,1,0:T(8,128)(2,1)}, u32[]{:S(2)}, u32[]{:S(2)}) async-start(bf16[4,64,640]{2,1,0:T(8,128)(2,1)} %copy.85), calls=%async_computation | async-start | bytes 655360 | tf_op jit(solution)/shard_map/all_to_all | solution.py:378
  21.3 101.3 %collective-permute-start = (bf16[256,2048]{1,0:T(8,128)(2,1)S(1)}, bf16[256,2048]{1,0:T(8,128)(2,1)}, u32[]{:S(2)}, u32[]{:S(2)}) collective-permute-start(bf16[256,2048]{1,0:T(8,128)(2,1)S(1)} %copy-done.10), channel_id=1, source_target_pairs={{0,2},{2,0},{1,3},{3,1},{4,6},{6,4},{5,7},{7,5},{8,10},{10,8},{9,1... | collective-permute-start | bytes 3145736 | tf_op jit(solution)/shard_map/ppermute | solution.py:224
  21.3 226.0 %collective-permute-start.22 = (bf16[256,2048]{1,0:T(8,128)(2,1)}, bf16[256,2048]{1,0:T(8,128)(2,1)}, u32[]{:S(2)}, u32[]{:S(2)}) collective-permute-start(bf16[256,2048]{1,0:T(8,128)(2,1)} %param.17), channel_id=1, source_target_pairs={{0,6},{2,4},{4,2},{6,0},{1,7},{3,5},{5,3},{7,1},{8,14},{10,12},{12... | collective-permute-start | bytes 3145736 | tf_op jit(solution)/shard_map/ppermute | solution.py:228
  23.9 8.7 %copy-start.36 = (f32[64]{0:T(128)}, f32[64]{0:T(128)S(1)}, u32[]{:S(2)}) copy-start(f32[64]{0:T(128)S(1)} %convert_element_type.229) | copy-start | bytes 772
  54.1 138.0 %all-to-all-start.2 = ((bf16[8,64,1408]{2,1,0:T(8,128)(2,1)}), bf16[8,64,1408]{2,1,0:T(8,128)(2,1)}, u32[]{:S(2)}, u32[]{:S(2)}) async-start(bf16[8,64,1408]{2,1,0:T(8,128)(2,1)} %concatenate.39), calls=%async_computation.2 | async-start | bytes 2883584 | tf_op jit(solution)/shard_map/all_to_all | solution.py:388
  59.0 264.5 %all-gather.3.cloned.1.call-start = ((), (), s32[]{:S(2)}) async-start(), calls=%async_computation.11 | async-start | bytes 7208960 | tf_op jit(solution)/shard_map/all_gather | solution.py:389
  59.0 36.5 %collective-permute-start.3 = (bf16[256,640]{1,0:T(8,128)(2,1)}, bf16[256,640]{1,0:T(8,128)(2,1)S(1)}, u32[]{:S(2)}, u32[]{:S(2)}) collective-permute-start(bf16[256,640]{1,0:T(8,128)(2,1)} %bitcast.7), channel_id=1, source_target_pairs={{8,0},{16,8},{24,16},{0,24},{9,1},{17,9},{25,17},{1,25},{10,2},{18... | collective-permute-start | bytes 983048 | tf_op jit(solution)/shard_map/ppermute | solution.py:258
  60.8 35.3 %collective-permute-start.5 = (bf16[256,640]{1,0:T(8,128)(2,1)}, bf16[256,640]{1,0:T(8,128)(2,1)S(1)}, u32[]{:S(2)}, u32[]{:S(2)}) collective-permute-start(bf16[256,640]{1,0:T(8,128)(2,1)} %bitcast.7), channel_id=1, source_target_pairs={{16,0},{24,8},{0,16},{8,24},{17,1},{25,9},{1,17},{9,25},{18,2},{26... | collective-permute-start | bytes 983048 | tf_op jit(solution)/shard_map/ppermute | solution.py:258
  62.6 34.8 %collective-permute-start.2 = (bf16[256,640]{1,0:T(8,128)(2,1)}, bf16[256,640]{1,0:T(8,128)(2,1)S(1)}, u32[]{:S(2)}, u32[]{:S(2)}) collective-permute-start(bf16[256,640]{1,0:T(8,128)(2,1)} %bitcast.7), channel_id=1, source_target_pairs={{0,4},{4,0},{1,5},{5,1},{2,6},{6,2},{3,7},{7,3},{8,12},{12,8},{9,1... | collective-permute-start | bytes 983048 | tf_op jit(solution)/shard_map/ppermute | solution.py:224
  95.6 63.2 %collective-permute-start.7 = (bf16[256,640]{1,0:T(8,128)(2,1)}, bf16[256,640]{1,0:T(8,128)(2,1)S(1)}, u32[]{:S(2)}, u32[]{:S(2)}) collective-permute-start(bf16[256,640]{1,0:T(8,128)(2,1)} %bitcast.7), channel_id=1, source_target_pairs={{24,0},{0,8},{8,16},{16,24},{25,1},{1,9},{9,17},{17,25},{26,2},{2,... | collective-permute-start | bytes 983048 | tf_op jit(solution)/shard_map/ppermute | solution.py:258
  96.0 7.8 collective-permute-start.4
  97.3 24.8 %collective-permute-start.6 = (bf16[256,640]{1,0:T(8,128)(2,1)S(1)}, bf16[256,640]{1,0:T(8,128)(2,1)S(1)}, u32[]{:S(2)}, u32[]{:S(2)}) collective-permute-start(bf16[256,640]{1,0:T(8,128)(2,1)S(1)} %collective-permute-done.5), channel_id=1, source_target_pairs={{0,4},{4,0},{1,5},{5,1},{2,6},{6,2},{3,7},{7,3},{8,12},{12,8},{9,1... | collective-permute-start | bytes 983048 | tf_op jit(solution)/shard_map/ppermute | solution.py:224
  103.8 57.5 %collective-permute-start.14 = (bf16[4,64,2048]{2,1,0:T(8,128)(2,1)S(1)}, bf16[4,64,2048]{2,1,0:T(8,128)(2,1)S(1)}, u32[]{:S(2)}, u32[]{:S(2)}) collective-permute-start(bf16[4,64,2048]{2,1,0:T(8,128)(2,1)S(1)} %copy-done.24), channel_id=1, source_target_pairs={{0,6},{2,4},{4,2},{6,0},{1,7},{3,5},{5,3},{7,1},{8,14},{10,12},{12... | collective-permute-start | bytes 3145736 | tf_op jit(solution)/shard_map/ppermute | solution.py:228
  122.1 25.2 %collective-permute-start.12 = (bf16[4,64,2048]{2,1,0:T(8,128)(2,1)S(1)}, bf16[4,64,2048]{2,1,0:T(8,128)(2,1)S(1)}, u32[]{:S(2)}, u32[]{:S(2)}) collective-permute-start(bf16[4,64,2048]{2,1,0:T(8,128)(2,1)S(1)} %copy-done.24), channel_id=1, source_target_pairs={{0,2},{2,0},{1,3},{3,1},{4,6},{6,4},{5,7},{7,5},{8,10},{10,8},{9,1... | collective-permute-start | bytes 3145736 | tf_op jit(solution)/shard_map/ppermute | solution.py:224
  122.6 36.5 %collective-permute-start.13 = (bf16[4,64,2048]{2,1,0:T(8,128)(2,1)S(1)}, bf16[4,64,2048]{2,1,0:T(8,128)(2,1)S(1)}, u32[]{:S(2)}, u32[]{:S(2)}) collective-permute-start(bf16[4,64,2048]{2,1,0:T(8,128)(2,1)S(1)} %copy-done.24), channel_id=1, source_target_pairs={{0,4},{4,0},{1,5},{5,1},{2,6},{6,2},{3,7},{7,3},{8,12},{12,8},{9,1... | collective-permute-start | bytes 3145736 | tf_op jit(solution)/shard_map/ppermute | solution.py:224
  125.1 33.7 %copy-start.15 = (bf16[1,256,2048]{2,1,0:T(8,128)(2,1)}, bf16[1,256,2048]{2,1,0:T(8,128)(2,1)S(1)}, u32[]{:S(2)}) copy-start(bf16[1,256,2048]{2,1,0:T(8,128)(2,1)S(1)} %get-tuple-element.32) | copy-start | bytes 3145732
  125.1 33.7 %copy-start.17 = (bf16[1,256,2048]{2,1,0:T(8,128)(2,1)}, bf16[1,256,2048]{2,1,0:T(8,128)(2,1)S(1)}, u32[]{:S(2)}) copy-start(bf16[1,256,2048]{2,1,0:T(8,128)(2,1)S(1)} %get-tuple-element.33) | copy-start | bytes 3145732
  147.3 44.9 %collective-permute-start.1 = (bf16[2,256,2048]{2,1,0:T(8,128)(2,1)}, bf16[2,256,2048]{2,1,0:T(8,128)(2,1)}, u32[]{:S(2)}, u32[]{:S(2)}) collective-permute-start(bf16[2,256,2048]{2,1,0:T(8,128)(2,1)} %pad_maximum_fusion.4), channel_id=1, source_target_pairs={{0,1},{1,0},{2,3},{3,2},{4,5},{5,4},{6,7},{7,6},{8,9},{9,8},{10,11... | collective-permute-start | bytes 6291464 | tf_op jit(solution)/shard_map/ppermute | solution.py:224
  158.8 88.9 %collective-permute-start.21 = (bf16[256,2048]{1,0:T(8,128)(2,1)}, bf16[256,2048]{1,0:T(8,128)(2,1)}, u32[]{:S(2)}, u32[]{:S(2)}) collective-permute-start(bf16[256,2048]{1,0:T(8,128)(2,1)} %param.17), channel_id=1, source_target_pairs={{0,4},{4,0},{1,5},{5,1},{2,6},{6,2},{3,7},{7,3},{8,12},{12,8},{9,1... | collective-permute-start | bytes 3145736 | tf_op jit(solution)/shard_map/ppermute | solution.py:224
  159.1 31.8 %collective-permute-start.8 = (bf16[256,640]{1,0:T(8,128)(2,1)S(1)}, bf16[256,640]{1,0:T(8,128)(2,1)S(1)}, u32[]{:S(2)}, u32[]{:S(2)}) collective-permute-start(bf16[256,640]{1,0:T(8,128)(2,1)S(1)} %collective-permute-done.7), channel_id=1, source_target_pairs={{0,4},{4,0},{1,5},{5,1},{2,6},{6,2},{3,7},{7,3},{8,12},{12,8},{9,1... | collective-permute-start | bytes 983048 | tf_op jit(solution)/shard_map/ppermute | solution.py:224
  162.4 61.5 %collective-permute-start.15 = (bf16[4,2,2,64,2048]{4,3,2,1,0:T(8,128)(2,1)}, bf16[4,2,2,64,2048]{4,3,2,1,0:T(8,128)(2,1)}, u32[]{:S(2)}, u32[]{:S(2)}) collective-permute-start(bf16[4,2,2,64,2048]{4,3,2,1,0:T(8,128)(2,1)} %bitcast_dynamic-update-slice_fusion.3), channel_id=1, source_target_pairs={{0,1},{1,0},{2,3},{3,2},{4,5},{5,4},{6,7},{7,6},{8,9},{9,8},{10,11... | collective-permute-start | bytes 12582920 | tf_op jit(solution)/shard_map/ppermute | solution.py:224
  163.0 29.2 %copy-start.16 = (bf16[1,256,2048]{2,1,0:T(8,128)(2,1)S(1)}, bf16[1,256,2048]{2,1,0:T(8,128)(2,1)}, u32[]{:S(2)}) copy-start(bf16[1,256,2048]{2,1,0:T(8,128)(2,1)} %copy-done.15) | copy-start | bytes 3145732
  190.9 56.8 %collective-permute-start.20 = (bf16[256,2048]{1,0:T(8,128)(2,1)}, bf16[256,2048]{1,0:T(8,128)(2,1)}, u32[]{:S(2)}, u32[]{:S(2)}) collective-permute-start(bf16[256,2048]{1,0:T(8,128)(2,1)} %param.17), channel_id=1, source_target_pairs={{0,2},{2,0},{1,3},{3,1},{4,6},{6,4},{5,7},{7,5},{8,10},{10,8},{9,1... | collective-permute-start | bytes 3145736 | tf_op jit(solution)/shard_map/ppermute | solution.py:224
  201.5 15.3 %copy-start = (bf16[1024,640]{1,0:T(8,128)(2,1)}, bf16[1024,640]{1,0:T(8,128)(2,1)S(1)}, u32[]{:S(2)}) copy-start(bf16[1024,640]{1,0:T(8,128)(2,1)S(1)} %convolution_convert_fusion.8.query_ref.both_ref) | copy-start | bytes 3932164
  218.1 18.3 %all-to-all-start.1 = ((bf16[4,256,512]{1,2,0:T(8,128)(2,1)}), bf16[4,256,512]{1,2,0:T(8,128)(2,1)S(1)}, u32[]{:S(2)}, u32[]{:S(2)}) async-start(bf16[4,256,512]{1,2,0:T(8,128)(2,1)} %copy.88), calls=%async_computation.1 | async-start | bytes 2097152 | tf_op jit(solution)/shard_map/all_to_all | solution.py:415
  223.7 461.1 %reduce-scatter.8.cloned.1.call-start = ((), (), s32[]{:S(2)}) async-start(), calls=%async_computation.15 | async-start | bytes 3604480 | tf_op jit(solution)/shard_map/reduce_scatter | solution.py:429
  245.0 25.2 %collective-permute-start.18 = (bf16[256,2048]{1,0:T(8,128)(2,1)S(1)}, bf16[256,2048]{1,0:T(8,128)(2,1)S(1)}, u32[]{:S(2)}, u32[]{:S(2)}) collective-permute-start(bf16[256,2048]{1,0:T(8,128)(2,1)S(1)} %get-tuple-element.15), channel_id=1, source_target_pairs={{0,6},{2,4},{4,2},{6,0},{1,7},{3,5},{5,3},{7,1},{8,14},{10,12},{12... | collective-permute-start | bytes 3145736 | tf_op jit(solution)/shard_map/ppermute | solution.py:228
  246.1 47.5 %collective-permute-start.17 = (bf16[256,2048]{1,0:T(8,128)(2,1)S(1)}, bf16[256,2048]{1,0:T(8,128)(2,1)S(1)}, u32[]{:S(2)}, u32[]{:S(2)}) collective-permute-start(bf16[256,2048]{1,0:T(8,128)(2,1)S(1)} %get-tuple-element.15), channel_id=1, source_target_pairs={{0,4},{4,0},{1,5},{5,1},{2,6},{6,2},{3,7},{7,3},{8,12},{12,8},{9,1... | collective-permute-start | bytes 3145736 | tf_op jit(solution)/shard_map/ppermute | solution.py:224
  247.3 46.3 %collective-permute-start.16 = (bf16[256,2048]{1,0:T(8,128)(2,1)S(1)}, bf16[256,2048]{1,0:T(8,128)(2,1)S(1)}, u32[]{:S(2)}, u32[]{:S(2)}) collective-permute-start(bf16[256,2048]{1,0:T(8,128)(2,1)S(1)} %get-tuple-element.15), channel_id=1, source_target_pairs={{0,2},{2,0},{1,3},{3,1},{4,6},{6,4},{5,7},{7,5},{8,10},{10,8},{9,1... | collective-permute-start | bytes 3145736 | tf_op jit(solution)/shard_map/ppermute | solution.py:224
  251.5 59.2 %collective-permute-start.23 = (bf16[1024,2048]{1,0:T(8,128)(2,1)}, bf16[1024,2048]{1,0:T(8,128)(2,1)}, u32[]{:S(2)}, u32[]{:S(2)}) collective-permute-start(bf16[1024,2048]{1,0:T(8,128)(2,1)} %pad_maximum_fusion.2), channel_id=1, source_target_pairs={{0,1},{1,0},{2,3},{3,2},{4,5},{5,4},{6,7},{7,6},{8,9},{9,8},{10,11... | collective-permute-start | bytes 12582920 | tf_op jit(solution)/shard_map/ppermute | solution.py:224
  270.2 25.9 %copy-start.25 = (bf16[256,2048]{1,0:T(8,128)(2,1)}, bf16[256,2048]{1,0:T(8,128)(2,1)S(1)}, u32[]{:S(2)}) copy-start(bf16[256,2048]{1,0:T(8,128)(2,1)S(1)} %collective-permute-done.18) | copy-start | bytes 3145732
  296.2 22.5 %collective-permute-start.19 = (bf16[1024,2048]{1,0:T(8,128)(2,1)}, bf16[1024,2048]{1,0:T(8,128)(2,1)}, u32[]{:S(2)}, u32[]{:S(2)}) collective-permute-start(bf16[1024,2048]{1,0:T(8,128)(2,1)} %pad_maximum_fusion.1), channel_id=1, source_target_pairs={{0,1},{1,0},{2,3},{3,2},{4,5},{5,4},{6,7},{7,6},{8,9},{9,8},{10,11... | collective-permute-start | bytes 12582920 | tf_op jit(solution)/shard_map/ppermute | solution.py:224
  372.5 33.2 %collective-permute-start.28 = (bf16[1024,2048]{1,0:T(8,128)(2,1)}, bf16[1024,2048]{1,0:T(8,128)(2,1)}, u32[]{:S(2)}, u32[]{:S(2)}) collective-permute-start(bf16[1024,2048]{1,0:T(8,128)(2,1)} %slice.106), channel_id=1, source_target_pairs={{0,1},{1,0},{2,3},{3,2},{4,5},{5,4},{6,7},{7,6},{8,9},{9,8},{10,11... | collective-permute-start | bytes 12582920 | tf_op jit(solution)/shard_map/ppermute | solution.py:224
  385.6 28.0 %collective-permute-start.24 = (bf16[1024,2048]{1,0:T(8,128)(2,1)}, bf16[1024,2048]{1,0:T(8,128)(2,1)}, u32[]{:S(2)}, u32[]{:S(2)}) collective-permute-start(bf16[1024,2048]{1,0:T(8,128)(2,1)} %slice.100), channel_id=1, source_target_pairs={{0,1},{1,0},{2,3},{3,2},{4,5},{5,4},{6,7},{7,6},{8,9},{9,8},{10,11... | collective-permute-start | bytes 12582920 | tf_op jit(solution)/shard_map/ppermute | solution.py:224
  399.5 351.7 %reduce-scatter.6.cloned.1.call-start = ((), (), s32[]{:S(2)}) async-start(), calls=%async_computation.14 | async-start | bytes 7208960 | tf_op jit(solution)/shard_map/reduce_scatter | solution.py:428
  399.6 14.0 %slice-start.2 = ((s8[8388608]{0:T(1024)(128)(4,1)}), s8[4194304]{0:T(1024)(128)(4,1)S(1)}, s32[]{:S(2)}) async-start(s8[8388608]{0:T(1024)(128)(4,1)} %bitcast.183), calls=%async_computation.18 | async-start | bytes 8388608
  413.1 24.7 %collective-permute-start.29 = (bf16[256,2048]{1,0:T(8,128)(2,1)S(1)}, bf16[256,2048]{1,0:T(8,128)(2,1)}, u32[]{:S(2)}, u32[]{:S(2)}) collective-permute-start(bf16[256,2048]{1,0:T(8,128)(2,1)S(1)} %get-tuple-element.20), channel_id=1, source_target_pairs={{0,2},{2,0},{1,3},{3,1},{4,6},{6,4},{5,7},{7,5},{8,10},{10,8},{9,1... | collective-permute-start | bytes 3145736 | tf_op jit(solution)/shard_map/ppermute | solution.py:224
  420.7 96.7 %collective-permute-start.25 = (bf16[256,2048]{1,0:T(8,128)(2,1)}, bf16[256,2048]{1,0:T(8,128)(2,1)}, u32[]{:S(2)}, u32[]{:S(2)}) collective-permute-start(bf16[256,2048]{1,0:T(8,128)(2,1)} %get-tuple-element.23), channel_id=1, source_target_pairs={{0,2},{2,0},{1,3},{3,1},{4,6},{6,4},{5,7},{7,5},{8,10},{10,8},{9,1... | collective-permute-start | bytes 3145736 | tf_op jit(solution)/shard_map/ppermute | solution.py:224
  421.7 95.7 %collective-permute-start.27 = (bf16[256,2048]{1,0:T(8,128)(2,1)}, bf16[256,2048]{1,0:T(8,128)(2,1)}, u32[]{:S(2)}, u32[]{:S(2)}) collective-permute-start(bf16[256,2048]{1,0:T(8,128)(2,1)} %get-tuple-element.24), channel_id=1, source_target_pairs={{0,6},{2,4},{4,2},{6,0},{1,7},{3,5},{5,3},{7,1},{8,14},{10,12},{12... | collective-permute-start | bytes 3145736 | tf_op jit(solution)/shard_map/ppermute | solution.py:228
  422.8 94.6 %collective-permute-start.26 = (bf16[256,2048]{1,0:T(8,128)(2,1)}, bf16[256,2048]{1,0:T(8,128)(2,1)}, u32[]{:S(2)}, u32[]{:S(2)}) collective-permute-start(bf16[256,2048]{1,0:T(8,128)(2,1)} %get-tuple-element.25), channel_id=1, source_target_pairs={{0,4},{4,0},{1,5},{5,1},{2,6},{6,2},{3,7},{7,3},{8,12},{12,8},{9,1... | collective-permute-start | bytes 3145736 | tf_op jit(solution)/shard_map/ppermute | solution.py:224
  423.4 82.1 %collective-permute-start.31 = (bf16[256,2048]{1,0:T(8,128)(2,1)}, bf16[256,2048]{1,0:T(8,128)(2,1)}, u32[]{:S(2)}, u32[]{:S(2)}) collective-permute-start(bf16[256,2048]{1,0:T(8,128)(2,1)} %get-tuple-element.21), channel_id=1, source_target_pairs={{0,6},{2,4},{4,2},{6,0},{1,7},{3,5},{5,3},{7,1},{8,14},{10,12},{12... | collective-permute-start | bytes 3145736 | tf_op jit(solution)/shard_map/ppermute | solution.py:228
  437.8 76.5 %collective-permute-start.30 = (bf16[256,2048]{1,0:T(8,128)(2,1)}, bf16[256,2048]{1,0:T(8,128)(2,1)}, u32[]{:S(2)}, u32[]{:S(2)}) collective-permute-start(bf16[256,2048]{1,0:T(8,128)(2,1)} %get-tuple-element.22), channel_id=1, source_target_pairs={{0,4},{4,0},{1,5},{5,1},{2,6},{6,2},{3,7},{7,3},{8,12},{12,8},{9,1... | collective-permute-start | bytes 3145736 | tf_op jit(solution)/shard_map/ppermute | solution.py:224
  514.3 10.7 %slice-start = ((s8[8388608]{0:T(1024)(128)(4,1)}), s8[4194304]{0:T(1024)(128)(4,1)S(1)}, s32[]{:S(2)}) async-start(s8[8388608]{0:T(1024)(128)(4,1)} %bitcast.178), calls=%async_computation.16 | async-start | bytes 8388608
  528.6 19.3 %all-to-all-start.3 = ((bf16[256,4,512]{2,0,1:T(8,128)(2,1)}), bf16[256,4,512]{2,0,1:T(8,128)(2,1)S(1)}, u32[]{:S(2)}, u32[]{:S(2)}) async-start(bf16[256,4,512]{2,0,1:T(8,128)(2,1)} %bitcast.188), calls=%async_computation.3 | async-start | bytes 2097152 | tf_op jit(solution)/shard_map/all_to_all | solution.py:437
  547.5 120.4 %collective-permute-start.35 = (bf16[4,4,64,2048]{3,2,0,1:T(8,128)(2,1)}, bf16[4,4,64,2048]{3,2,0,1:T(8,128)(2,1)}, u32[]{:S(2)}, u32[]{:S(2)}) collective-permute-start(bf16[4,4,64,2048]{3,2,0,1:T(8,128)(2,1)} %bitcast.172), channel_id=1, source_target_pairs={{0,1},{1,0},{2,3},{3,2},{4,5},{5,4},{6,7},{7,6},{8,9},{9,8},{10,11... | collective-permute-start | bytes 12582920 | tf_op jit(solution)/shard_map/ppermute | solution.py:224
  549.2 28.7 %copy-start.22 = (bf16[1024,2048]{1,0:T(8,128)(2,1)S(1)}, bf16[1024,2048]{1,0:T(8,128)(2,1)}, u32[]{:S(2)}) copy-start(bf16[1024,2048]{1,0:T(8,128)(2,1)} %fusion.1) | copy-start | bytes 12582916
  582.0 30.3 %collective-permute-start.34 = (bf16[4,256,640]{2,1,0:T(8,128)(2,1)S(1)}, bf16[4,256,640]{2,1,0:T(8,128)(2,1)S(1)}, u32[]{:S(2)}, u32[]{:S(2)}) collective-permute-start(bf16[4,256,640]{2,1,0:T(8,128)(2,1)S(1)} %dynamic-slice_bitcast_fusion.1), channel_id=1, source_target_pairs={{0,4},{4,0},{1,5},{5,1},{2,6},{6,2},{3,7},{7,3},{8,12},{12,8},{9,1... | collective-permute-start | bytes 3932168 | tf_op jit(solution)/shard_map/ppermute | solution.py:224
  613.7 47.1 %all-to-all-start.4 = ((bf16[4,256,640]{2,1,0:T(8,128)(2,1)}), bf16[4,256,640]{2,1,0:T(8,128)(2,1)}, u32[]{:S(2)}, u32[]{:S(2)}) async-start(bf16[4,256,640]{2,1,0:T(8,128)(2,1)} %fusion.6), calls=%async_computation.4 | async-start | bytes 2621440 | tf_op jit(solution)/shard_map/all_to_all | solution.py:457
  641.0 39.6 %collective-permute-start.32 = (bf16[2,256,2048]{2,1,0:T(8,128)(2,1)S(1)}, bf16[2,256,2048]{2,1,0:T(8,128)(2,1)}, u32[]{:S(2)}, u32[]{:S(2)}) collective-permute-start(bf16[2,256,2048]{2,1,0:T(8,128)(2,1)S(1)} %dynamic-slice_bitcast_fusion), channel_id=1, source_target_pairs={{0,1},{1,0},{2,3},{3,2},{4,5},{5,4},{6,7},{7,6},{8,9},{9,8},{10,11... | collective-permute-start | bytes 6291464 | tf_op jit(solution)/shard_map/ppermute | solution.py:224
  663.1 12.6 %all-to-all-start.5 = ((bf16[4,64,640]{2,1,0:T(8,128)(2,1)}), bf16[4,64,640]{2,1,0:T(8,128)(2,1)S(1)}, u32[]{:S(2)}, u32[]{:S(2)}) async-start(bf16[4,64,640]{2,1,0:T(8,128)(2,1)} %bitcast.59), calls=%async_computation.5 | async-start | bytes 655360 | tf_op jit(solution)/shard_map/all_to_all | solution.py:459
  675.7 75.6 %all-to-all-start.6 = ((bf16[4,4,64,2048]{3,2,1,0:T(8,128)(2,1)}), bf16[4,4,64,2048]{3,2,1,0:T(8,128)(2,1)}, u32[]{:S(2)}, u32[]{:S(2)}) async-start(bf16[4,4,64,2048]{3,2,1,0:T(8,128)(2,1)} %fusion.2), calls=%async_computation.6 | async-start | bytes 8388608 | tf_op jit(solution)/shard_map/all_to_all | solution.py:451
  683.6 67.7 %copy-start.14 = (bf16[2,256,2048]{2,1,0:T(8,128)(2,1)}, bf16[2,256,2048]{2,1,0:T(8,128)(2,1)S(1)}, u32[]{:S(2)}) copy-start(bf16[2,256,2048]{2,1,0:T(8,128)(2,1)S(1)} %fusion.3) | copy-start | bytes 6291460
  683.6 65.8 %copy-start.11 = (bf16[256,2048]{1,0:T(8,128)(2,1)S(1)}, bf16[256,2048]{1,0:T(8,128)(2,1)}, u32[]{:S(2)}) copy-start(bf16[256,2048]{1,0:T(8,128)(2,1)} %param.9) | copy-start | bytes 3145732
  684.7 64.6 %collective-permute-start.33 = (bf16[256,2048]{1,0:T(8,128)(2,1)}, bf16[256,2048]{1,0:T(8,128)(2,1)}, u32[]{:S(2)}, u32[]{:S(2)}) collective-permute-start(bf16[256,2048]{1,0:T(8,128)(2,1)} %dynamic-slice_bitcast_fusion.2), channel_id=1, source_target_pairs={{0,2},{2,0},{1,3},{3,1},{4,6},{6,4},{5,7},{7,5},{8,10},{10,8},{9,1... | collective-permute-start | bytes 3145736 | tf_op jit(solution)/shard_map/ppermute | solution.py:224
  751.3 24.3 %all-to-all-start.7 = ((bf16[8,64,1408]{2,1,0:T(8,128)(2,1)}), bf16[8,64,1408]{2,1,0:T(8,128)(2,1)}, u32[]{:S(2)}, u32[]{:S(2)}) async-start(bf16[8,64,1408]{2,1,0:T(8,128)(2,1)} %bitcast.193), calls=%async_computation.9 | async-start | bytes 2883584 | tf_op jit(solution)/shard_map/all_to_all | solution.py:444
  757.4 38.6 %reduce-scatter.4.cloned.1.call-start = ((), (), s32[]{:S(2)}) async-start(), calls=%async_computation.13 | async-start | bytes 1310720 | tf_op jit(solution)/shard_map/reduce_scatter | solution.py:453
  (29 other events, 123.0 us)
Sparse Core Ops, SparseCore 0:
  13.0 89.0 all-gather.4
  192.3 116.5 all-gather.2
  399.6 67.4 reduce-scatter.7
  469.3 104.2 reduce-scatter.5
  762.2 26.7 reduce-scatter.3

commit v3 on v2

--- a/solution.py
+++ b/solution.py
@@ -220,6 +220,12 @@
     )(head_cols, head_cols, grad_heads, cos_table, sin_table, start[None, :])
 
 
+def after(value, *others):
+    for other in others:
+        value = lax.optimization_barrier((value, other))[0]
+    return value
+
+
 def swap(value, axis):
     return lax.ppermute(value, axis, [(0, 1), (1, 0)])
 
@@ -259,22 +265,32 @@
     return pieces
 
 
-def gather_near(value):
-    chips = jnp.concatenate([value, swap(value, "x"), swap(value, "y"), cross(value)], axis=0)
-    return jnp.concatenate([chips, swap(chips, "c")], axis=0)
-
-
-def reduce_near(value):
-    half = value.shape[0] // 2
-    rows = half // 4
-    chips = (value[:half].astype(f32) + swap(value[half:], "c").astype(f32)).astype(bf)
-    own, over_x, over_y, over_both = (chips[i * rows : (i + 1) * rows] for i in range(4))
-    return (
-        own.astype(f32)
-        + swap(over_x, "x").astype(f32)
-        + swap(over_y, "y").astype(f32)
-        + cross(over_both).astype(f32)
-    )
+def forward(over_x, over_y, dim):
+    half = over_x.shape[dim] // 2
+    by_y = swap(lax.slice_in_dim(over_x, 0, half, axis=dim), "y")
+    by_x = swap(lax.slice_in_dim(over_y, half, over_y.shape[dim], axis=dim), "x")
+    return jnp.concatenate([by_y, by_x], axis=dim)
+
+
+def send_near(value, dim):
+    over_x, over_y = swap(value, "x"), swap(value, "y")
+    return [forward(over_x, over_y, dim), over_x, over_y, value]
+
+
+def near_tokens(pieces):
+    both = [(piece, swap(piece, "c")) for piece in pieces]
+    order = [both[i][j] for pair_of in ((0, 3), (1, 2)) for j in (0, 1) for i in pair_of]
+    return jnp.concatenate(order, axis=0)
+
+
+def over_core(left, right):
+    half = left.shape[0] // 2
+    theirs = swap(right(left[half:]).astype(bf), "c")
+    return (right(left[:half]) + theirs.astype(f32)).astype(bf)
+
+
+def total(parts):
+    return sum(part.astype(f32) for part in parts)
 
 
 def to_units(value, depth, unit_rows):
@@ -306,9 +322,7 @@
 def units_kernel(tok_ref, out_ref, w_ref, down_ref, act_ref, grad_ref):
     main = act_ref.shape[1] - TAIL
     hidden = jnp.dot(tok_ref[...], w_ref[...], preferred_element_type=f32)
-    grad_act = lax.dot_general(
-        out_ref[...], down_ref[...], (((1,), (1,)), ((), ())), preferred_element_type=f32
-    )
+    grad_act = contract_cols(out_ref[...], down_ref[...])
     act, grad_gate, grad_up = activations(
         hidden[:, :main], hidden[:, main : 2 * main], grad_act[:, :main]
     )
@@ -331,20 +345,18 @@
     block = min(256, count)
     down = jnp.concatenate([w_down, w_down[-TAIL:]], axis=0)
     whole = lambda i: (0, 0)
+    mine = lambda i: (i, 0)
     once = pl.Buffered(1)
     return pl.pallas_call(
         units_kernel,
         grid=(count // block,),
         in_specs=[
-            pl.BlockSpec((block, width), lambda i: (i, 0)),
-            pl.BlockSpec((block, width), lambda i: (i, 0)),
+            pl.BlockSpec((block, width), mine),
+            pl.BlockSpec((block, width), mine),
             pl.BlockSpec((width, 2 * units), whole, pipeline_mode=once),
             pl.BlockSpec((units + TAIL, width), whole, pipeline_mode=once),
         ],
-        out_specs=[
-            pl.BlockSpec((block, units), lambda i: (i, 0)),
-            pl.BlockSpec((block, 2 * units), lambda i: (i, 0)),
-        ],
+        out_specs=[pl.BlockSpec((block, units), mine), pl.BlockSpec((block, 2 * units), mine)],
         out_shape=[
             jax.ShapeDtypeStruct((count, units), bf),
             jax.ShapeDtypeStruct((count, 2 * units), bf),
@@ -373,35 +385,28 @@
     gain_one = norm_attn.astype(f32)[:, None]
     gain_two = norm_mlp.astype(f32)[:, None]
 
-    group_in = gather_pair(gather_pair(layer_in, "x", 0), "c", 1).reshape(group_rows, width)
     qkv = (w_qkv.astype(f32) * gain_one).astype(bf).reshape(w_rows, 4, cols).transpose(1, 0, 2)
     qkv = lax.all_to_all(qkv, ("x", "c"), 0, 0, tiled=True).reshape(4 * w_rows, cols)
+    over_x = swap(layer_in, "x")
+    group_in = gather_pair(pair(layer_in, over_x, "x", 0), "c", 1).reshape(group_rows, width)
     full_qkv = jnp.zeros((depth, 2, 4 * w_rows, cols), bf)
-    for r, piece in enumerate(rotations(qkv)):
-        full_qkv = lax.dynamic_update_index_in_dim(
-            full_qkv, gather_pair(piece, "y", 0), (z_at + r) % depth, 0
-        )
+    qkv_own = qkv
+    qkv_pieces = rotations(qkv)
+    over_y = [swap(piece, "y") for piece in qkv_pieces]
+    over_y_last = over_y[depth - 1]
+    out_near = [swap(after(grad_out, qkv), "x"), swap(after(grad_out, over_y_last), "y")]
+    for r in range(depth):
+        piece = pair(qkv_pieces[r], over_y[r], "y", 0)
+        full_qkv = lax.dynamic_update_index_in_dim(full_qkv, piece, (z_at + r) % depth, 0)
     qkv = full_qkv.reshape(-1, cols)
 
-    full_down = lax.all_gather(w_down, "z", axis=0, tiled=True)
-    gateup = to_units((w_gateup.astype(f32) * gain_two).astype(bf), depth, ff_rows)
-    gateup = lax.all_to_all(gateup, QUAD, 0, 0, tiled=True).reshape(8 * w_rows, 2 * units)
-    full_gateup = lax.all_gather(gateup, "z", axis=0, tiled=True)
-
-    out_z = jnp.zeros((depth,) + w_out.shape, bf)
-    for r, piece in enumerate(rotations(w_out)):
-        out_z = lax.dynamic_update_index_in_dim(out_z, piece, (z_at + r) % depth, 0)
-    y_at, x_at = lax.axis_index("y"), lax.axis_index("x")
-    out_chip = jnp.zeros((depth, 2, 2) + w_out.shape, bf)
-    for dy, dx, piece in (
-        (0, 0, out_z),
-        (0, 1, swap(out_z, "x")),
-        (1, 0, swap(out_z, "y")),
-        (1, 1, cross(out_z)),
-    ):
-        place = (0, y_at ^ dy, x_at ^ dx, 0, 0)
-        out_chip = lax.dynamic_update_slice(out_chip, piece[:, None, None], place)
-    full_out = gather_pair(out_chip, "c", 3).reshape(-1, width)
+    out_z = lax.all_gather(w_out, "z", axis=0, tiled=False)
+    out_pieces = send_near(after(out_z, *over_y), 1)
+
+    full_down = lax.all_gather(after(w_down, qkv_own), "z", axis=0, tiled=True)
+    gateup = to_units((after(w_gateup, qkv_pieces[1]).astype(f32) * gain_two).astype(bf), depth, ff_rows)
+    gateup = lax.all_to_all(after(gateup, out_near[0]), QUAD, 0, 0, tiled=True)
+    full_gateup = lax.all_gather(gateup.reshape(8 * w_rows, 2 * units), "z", axis=0, tiled=True)
 
     position = doc_layout(doc_lengths[0], group_rows)
     start = jnp.arange(group_rows, dtype=jnp.int32) - position
@@ -411,55 +416,103 @@
         wide_in * lax.rsqrt(jnp.mean(wide_in * wide_in, axis=-1, keepdims=True) + epsilon)
     ).astype(bf)
     head_cols = jnp.dot(normed_one, qkv, preferred_element_type=f32).astype(bf)
-    mixed_heads = attend_forward(head_cols, cos_table, sin_table, start)
-    mixed_tok = lax.all_to_all(
-        mixed_heads, ("x", "c"), split_axis=0, concat_axis=1, tiled=True
-    )
+    mixed_heads = attend_forward(after(head_cols, gateup), cos_table, sin_table, start)
+    mixed_tok = lax.all_to_all(mixed_heads, ("x", "c"), split_axis=0, concat_axis=1, tiled=True)
+    y_at, x_at, c_at = lax.axis_index("y"), lax.axis_index("x"), lax.axis_index("c")
+    full_out = jnp.zeros((depth, 2, 2, 2) + w_out.shape, bf)
+    out_pieces = [after(piece, mixed_tok) for piece in out_pieces[:3]] + out_pieces[3:]
+    for i, piece in enumerate(out_pieces + [swap(piece, "c") for piece in out_pieces]):
+        dy, dx, dc = (1, 0, 1, 0)[i % 4], (1, 1, 0, 0)[i % 4], i // 4
+        place = (0, y_at ^ dy, x_at ^ dx, c_at ^ dc, 0, 0)
+        full_out = lax.dynamic_update_slice(full_out, piece[:, None, None, None], place)
+    full_out = full_out.reshape(-1, width)
     resid_in = layer_in.astype(f32)
-    resid_mid = resid_in + jnp.dot(mixed_tok, full_out, preferred_element_type=f32)
+    resid_mid = resid_in + jnp.dot(after(mixed_tok, out_near[1]), full_out, preferred_element_type=f32)
 
     inv_two = lax.rsqrt(jnp.mean(resid_mid * resid_mid, axis=-1, keepdims=True) + epsilon)
-    many_out = gather_near(grad_out)
-    normed_two = gather_near((resid_mid * inv_two).astype(bf))
+    two_near = send_near((resid_mid * inv_two).astype(bf), 0)
+    out_near = out_near + [grad_out]
+    out_near = [forward(after(out_near[0], two_near[1]), after(out_near[1], two_near[2]), 0)] + out_near
+    many_out = near_tokens(out_near)
+    normed_two = near_tokens(two_near)
+    half = normed_two.shape[0] // 2
     activated, grad_gate_up = run_units(normed_two, many_out, full_gateup, full_down)
-    scaled_two = reduce_near(contract_cols(grad_gate_up, full_gateup).astype(bf))
+    by_units = lambda left: contract_cols(left, full_gateup)
+    by_down = lambda left: jnp.dot(left, full_down, preferred_element_type=f32)
     grad_gateup = contract_rows(normed_two, grad_gate_up).astype(bf)
+    sum_gateup = lax.psum_scatter(grad_gateup, "z", scatter_dimension=0, tiled=True)
+    grad_gate_up = after(grad_gate_up, grad_gateup)
+    first = over_core(grad_gate_up[:half], by_units)
+    second = over_core(grad_gate_up[half:], by_units)
+    over_both, over_x, over_y = cross(first[:rows]), swap(second[:rows], "x"), swap(second[rows:], "y")
+    activated = after(activated, first, second)
     grad_down = contract_rows(activated, many_out).astype(bf)
-    sum_gateup = lax.psum_scatter(grad_gateup, "z", scatter_dimension=0, tiled=True)
-    grad_w_down = lax.psum_scatter(grad_down, "z", scatter_dimension=0, tiled=True).astype(f32)
-    layer_out = resid_mid + reduce_near(
-        jnp.dot(activated, full_down, preferred_element_type=f32).astype(bf)
-    )
+    grad_w_down = lax.psum_scatter(grad_down, "z", scatter_dimension=0, tiled=True)
+    over_both, over_x, over_y = (after(part, grad_down) for part in (over_both, over_x, over_y))
+    scaled_two = total([first[rows:], over_both, over_x, over_y])
 
     grad_mid = grad_out.astype(f32) + norm_back(scaled_two, resid_mid, inv_two)
     grad_mid_low = grad_mid.astype(bf)
     grad_mixed = contract_cols(grad_mid_low, full_out).astype(bf)
+    activated = after(activated, grad_mixed)
+    out_second = over_core(activated[half:], by_down)
+    out_first = over_core(activated[:half], by_down)
+    out_sent = [swap(out_second[:rows], "x"), swap(out_second[rows:], "y"), cross(out_first[:rows])]
+    mixed_by_core = mixed_tok.reshape(rows, depth, 4, 2, w_rows).transpose(0, 3, 2, 1, 4)
+    mixed_by_core = mixed_by_core.reshape(rows, 2, -1)
+    low_grads = after(grad_mid_low, grad_mixed)
+    theirs = contract_rows(pick(mixed_by_core, "c", 1, other=True), low_grads).astype(bf)
+    theirs = swap(theirs, "c")
+    grad_out_w = contract_rows(pick(mixed_by_core, "c", 1), low_grads)
+    grad_out_w = (grad_out_w + theirs.astype(f32)).astype(bf).reshape(4, depth, w_rows, width)
+    out_w_near = []
+    for dy, dx, move in ((0, 1, lambda v: swap(v, "x")), (1, 0, lambda v: swap(v, "y")), (1, 1, cross)):
+        chip = (y_at ^ dy) * 2 + (x_at ^ dx)
+        out_w_near.append(move(lax.dynamic_index_in_dim(grad_out_w, chip, 0, keepdims=False)))
     grad_heads = lax.all_to_all(grad_mixed, ("x", "c"), split_axis=1, concat_axis=0, tiled=True)
+    out_sent = [after(part, grad_heads) for part in out_sent]
+    grad_heads = after(grad_heads, grad_out_w, *out_sent)
     grad_cols = attend_backward(head_cols, grad_heads, cos_table, sin_table, start)
-    part_one = contract_cols(grad_cols, qkv).astype(bf).reshape(2, 2, rows, width)
-    scaled_one = reduce_pair(reduce_pair(part_one, "c", 1).astype(bf), "x", 0)
+    grad_cols = after(grad_cols, *out_w_near)
+    grad_qkv = contract_rows(normed_one, grad_cols).astype(bf)
+    cols_by_core = after(grad_cols, grad_qkv).reshape(2, 2, rows, cols)
+    grad_qkv = grad_qkv.reshape(depth, 2, 4 * w_rows, cols)
+    over_y = swap(pick(grad_qkv, "y", 1, other=True), "y")
+    sum_gateup = after(sum_gateup, grad_cols).reshape(8, w_rows, 2 * units)
+    sum_gateup = lax.all_to_all(sum_gateup, QUAD, 0, 0, tiled=True)
+    over_y = after(over_y, sum_gateup)
+    grad_qkv = (pick(grad_qkv, "y", 1).astype(f32) + over_y.astype(f32)).astype(bf)
+    grad_qkv = lax.all_to_all(
+        grad_qkv.reshape(depth * 4, w_rows, cols), ("z", "x", "c"), 0, 0, tiled=True
+    )
+
+    theirs = contract_cols(pick(cols_by_core, "c", 1, other=True).reshape(-1, cols), qkv).astype(bf)
+    theirs = swap(theirs, "c")
+    part_one = contract_cols(pick(cols_by_core, "c", 1).reshape(-1, cols), qkv)
+    part_one = (part_one + theirs.astype(f32)).astype(bf).reshape(2, rows, width)
+    over_x = swap(pick(part_one, "x", 0, other=True), "x")
+    scaled_one = pick(part_one, "x", 0).astype(f32) + after(over_x, over_y).astype(f32)
     inv_one = lax.rsqrt(jnp.mean(resid_in * resid_in, axis=-1, keepdims=True) + epsilon)
     grad_in = grad_mid + norm_back(scaled_one, resid_in, inv_one)
 
-    sum_gateup = lax.all_to_all(sum_gateup.reshape(8, w_rows, 2 * units), QUAD, 0, 0, tiled=True)
+    own = lax.dynamic_index_in_dim(grad_out_w, y_at * 2 + x_at, 0, keepdims=False)
+    grad_out_w = total([own] + out_w_near).astype(bf)
+    out_w_parts = []
+    for r in range(1, depth):
+        part = lax.dynamic_index_in_dim(grad_out_w, (z_at + r) % depth, 0, keepdims=False)
+        out_w_parts.append(lax.ppermute(part, "z", [(i, (i + r) % depth) for i in range(depth)]))
+    layer_out = resid_mid + total([out_first[rows:]] + out_sent)
+
+    sum_qkv = jnp.sum(grad_qkv.reshape(depth, 4, w_rows, cols).astype(f32), axis=0)
+    sum_qkv = sum_qkv.transpose(1, 0, 2).reshape(w_rows, 4 * cols)
+    grad_w_qkv = sum_qkv * gain_one
+    grad_norm_attn = jnp.sum(sum_qkv * w_qkv.astype(f32), axis=1)
+    own = lax.dynamic_index_in_dim(grad_out_w, z_at, 0, keepdims=False)
+    grad_w_out = total([own] + [after(part, grad_qkv) for part in out_w_parts])
     sum_gateup = from_units(sum_gateup, depth, ff_rows).astype(f32)
     grad_w_gateup = sum_gateup * gain_two
     grad_norm_mlp = jnp.sum(sum_gateup * w_gateup.astype(f32), axis=1)
-
-    grad_out_w = contract_rows(mixed_tok, grad_mid_low).astype(bf)
-    grad_out_w = reduce_pair(grad_out_w.reshape(depth, 4, 2, w_rows, width), "c", 2).astype(bf)
-    grad_out_w = lax.all_to_all(grad_out_w.transpose(1, 0, 2, 3), ("y", "x"), 0, 0, tiled=True)
-    grad_out_w = jnp.sum(grad_out_w.astype(f32), axis=0).astype(bf)
-    grad_w_out = lax.psum_scatter(grad_out_w, "z", scatter_dimension=0, tiled=False).astype(f32)
-
-    grad_qkv = contract_rows(normed_one, grad_cols).astype(bf)
-    grad_qkv = reduce_pair(grad_qkv.reshape(depth, 2, 4 * w_rows, cols), "y", 1).astype(bf)
-    grad_qkv = lax.all_to_all(grad_qkv, "z", 0, 0, tiled=True)
-    sum_qkv = jnp.sum(grad_qkv.astype(f32), axis=0).astype(bf).reshape(4, w_rows, cols)
-    sum_qkv = lax.all_to_all(sum_qkv, ("x", "c"), 0, 0, tiled=True)
-    sum_qkv = sum_qkv.transpose(1, 0, 2).reshape(w_rows, 4 * cols).astype(f32)
-    grad_w_qkv = sum_qkv * gain_one
-    grad_norm_attn = jnp.sum(sum_qkv * w_qkv.astype(f32), axis=1)
+    grad_w_down = grad_w_down.astype(f32)
 
     return (
         layer_out,

time: 819 us -> 670 us (0.82)
  waiting for transfers between devices: 322 us -> 234 us
  other arithmetic: 111 us -> 67.6 us
  local copies, waits for them, and re-layouts: 107 us -> 91.3 us
  matrix products: 80.9 us -> 93.3 us
  starting transfers between devices: 97.4 us -> 88.7 us
    ppermute x25 -> x44, waiting for transfers between devices: 203 us -> 113 us  [swap(): return lax.ppermute(value, axis, [(0, 1), (1, 0)])]
    all_to_all x5 -> x3, starting transfers between devices: 40.4 us -> 17.6 us  [the longest x1 7.11 us: body(): lax.all_to_all(grad_qkv.reshape(depth * 4, w_rows, cols), ('z', 'x', 'c')...]
    ppermute x25 -> x44, starting transfers between devices: 26.3 us -> 44.8 us  [swap(): return lax.ppermute(value, axis, [(0, 1), (1, 0)])]
    all_to_all x1, waiting for transfers between devices: 0.01 us -> 14.9 us  [body(): lax.all_to_all(qkv, ('x', 'c'), 0, 0, tiled=True).reshape(4 * w_rows, cols)]
    dynamic_slice x2 -> x1, local copies, waits for them, and re-layouts: 9.1 us -> 0.12 us  [pick(): return lax.dynamic_index_in_dim(value, index, dim, keepdims=False)]
    another operation x9 -> x7, other arithmetic: 17.9 us -> 9.16 us  [pair(): return jnp.stack([first, second], axis=dim)]
    convert_element_type x7 -> x6, other arithmetic: 21.1 us -> 12.6 us  [the longest x1 4.75 us: body(): grad_mid_low = grad_mid.astype(bf)]
    concatenate x2, local copies, waits for them, and re-layouts: 9.57 us -> 1.12 us  [near_tokens(): return jnp.concatenate(order, axis=0)]
  transfers between devices with their start and end apart: 49 -> 64, of which waited for: 15 -> 18; matrix products, arithmetic and copies ran while one was open for 33% -> 30% of each run, Pallas kernels for 5% -> 7%
where the time goes in v3:
time: 670 us; the launch traced here: 662 us
  waiting for transfers between devices  234 us (35%)
  matrix products  93.3 us (14%)
  local copies, waits for them, and re-layouts  91.3 us (14%)
  starting transfers between devices  88.7 us (13%)
  Pallas kernels  71.7 us (11%)
  other arithmetic  67.6 us (10%)
  between operations  15.2 us (2%)
    ppermute x44, waiting for transfers between devices, swap(): return lax.ppermute(value, axis, [(0, 1), (1, 0)])  113 us
    ppermute x3, waiting for transfers between devices, cross(): return lax.ppermute(value, ('y', 'x'), [(i, 3 - i) for i in range(4)])  57 us
    ppermute x44, starting transfers between devices, swap(): return lax.ppermute(value, axis, [(0, 1), (1, 0)])  44.8 us
    dot_general x5, matrix products, contract_rows(): lax.dot_general(left, right, (((0,), (0,)), ((), ())), preferred_element_...  38.5 us
    dot_general x7, matrix products, contract_cols(): lax.dot_general(left, right, (((1,), (1,)), ((), ())), preferred_element_...  31.6 us
    unnamed x150, local copies, waits for them, and re-layouts  30.9 us
    pallas_call x1, Pallas kernels, attend_backward(): pl.pallas_call(backward_kernel, grid=(pairs + 1,), in_specs=[pl.BlockSpec...  28.9 us
    pallas_call x1, Pallas kernels, run_units(): pl.pallas_call(units_kernel, grid=(count // block,), in_specs=[pl.BlockSp...  27.6 us
  transfers between devices with their start and end apart: 64, of which 18 were waited for; matrix products, arithmetic and copies ran while one was open for 30% of the time, Pallas kernels for 7%

profile of v3, /device:TPU:11, one launch (start us, length us, event | category | flops | bytes accessed | tf_op | source)
XLA Modules:
  0.0 661.8 jit_solution(14576847185480889010)
XLA Ops:
  11.0 5.2 all-to-all-start
  17.6 3.0 fusion.45
  20.6 14.9 %all-to-all-done = bf16[4,64,640]{2,1,0:T(8,128)(2,1)S(1)} async-done(((bf16[4,64,640]{2,1,0:T(8,128)(2,1)}), bf16[4,64,640]{2,1,0:T(8,128)(2,1)S(1)}, u32[]{:S(2)}, u32[]{:S(2)}) %all-to-all-start) | async-done | bytes 327712 | tf_op jit(solution)/shard_map/all_to_all | solution.py:389
  35.6 2.8 pad_maximum_fusion.7
  48.5 3.2 collective-permute-start.1
  52.0 5.0 reshape.238
  57.1 3.9 copy.114
  61.0 3.9 reshape.239
  72.9 24.3 %collective-permute-done.7 = bf16[256,640]{1,0:T(8,128)(2,1)} collective-permute-done((bf16[256,640]{1,0:T(8,128)(2,1)S(1)}, bf16[256,640]{1,0:T(8,128)(2,1)}, u32[]{:S(2)}, u32[]{:S(2)}) %collective-permute-start.7) | collective-permute-done | bytes 327712 | tf_op jit(solution)/shard_map/ppermute | solution.py:264
  109.1 5.9 all-to-all-start.1
  120.7 6.2 convolution_convert_fusion.10.query_ref.both_ref
  126.9 6.2 all-to-all-done.1
  134.4 15.2 %attend_forward.1 = bf16[1024,512]{1,0:T(8,128)(2,1)S(1)} custom-call(bf16[1024,640]{1,0:T(8,128)(2,1)S(1)} %copy-done.3, bf16[1024,640]{1,0:T(8,128)(2,1)S(1)} %copy-done.3, f32[1024,128]{1,0:T(8,128)S(1)} %get-tuple-element.143.cos_ref, f32[1024,128]{1,0:T(8,128)S(1)} %get-tuple-element.144.sin_ref, s32[1024,1]{1,0:T(8,128)S(1)} %subtract_subtract_fusion.start_ref), custom_call_target="tpu_custom_call" | custom-call | flops 12884901888 | bytes 3932160 | tf_op jit(solution)/shard_map/attend_forward/pallas_call | solution.py:169
  151.0 5.6 all-to-all-start.2
  161.6 18.8 %collective-permute-done.14 = bf16[4,32,2048]{2,1,0:T(8,128)(2,1)} collective-permute-done((bf16[4,32,2048]{2,1,0:T(8,128)(2,1)S(1)}, bf16[4,32,2048]{2,1,0:T(8,128)(2,1)}, u32[]{:S(2)}, u32[]{:S(2)}) %collective-permute-start.14) | collective-permute-done | bytes 524320 | tf_op jit(solution)/shard_map/ppermute | solution.py:230
  188.2 6.5 collective-permute-done.10
  196.9 2.5 multiply_reduce_fusion.3
  201.6 22.3 %collective-permute-done.19 = bf16[256,2048]{1,0:T(8,128)(2,1)S(1)} collective-permute-done((bf16[256,2048]{1,0:T(8,128)(2,1)S(1)}, bf16[256,2048]{1,0:T(8,128)(2,1)S(1)}, u32[]{:S(2)}, u32[]{:S(2)}) %collective-permute-start.19) | collective-permute-done | bytes 1048608 | tf_op jit(solution)/shard_map/ppermute | solution.py:230
  227.5 2.9 collective-permute-start.30
  234.4 3.9 pad_maximum_fusion.down_ref
  238.3 3.6 collective-permute-start.31
  247.7 2.8 collective-permute-start.23
  270.7 2.4 copy-done.55
  274.1 27.6 %units.1 = (bf16[2048,704]{1,0:T(8,128)(2,1)S(1)}, bf16[2048,1408]{1,0:T(8,128)(2,1)}) custom-call(bf16[2048,2048]{1,0:T(8,128)(2,1)} %copy-done.55, bf16[2048,2048]{1,0:T(8,128)(2,1)} %constant_dynamic-update-slice_fusion.9.out_ref, bf16[2048,1408]{1,0:T(8,128)(2,1)} %all-gather.5.cloned.1.call-done.w_ref, bf16[768,2048]{1,0:T(8,128)(2,1)} %pad_maximum_fusion.down_ref), custom_call_target="tpu_custom_call" | custom-call | flops 17716740096 | bytes 34078720 | tf_op jit(solution)/shard_map/units/pallas_call | solution.py:350
  303.3 16.6 %convolution_convert_fusion = bf16[2048,1408]{1,0:T(8,128)(2,1)} fusion(bf16[2048,2048]{1,0:T(8,128)(2,1)S(1)} %copy-done.56, bf16[2048,1408]{1,0:T(8,128)(2,1)} %get-tuple-element.69), kind=kOutput, calls=%fused_computation.5 | convolution fusion | flops 11814043648 | bytes 19922944 | tf_op jit(solution)/shard_map/dot_general | solution.py:48
  319.9 6.7 %convolution_convert_fusion.8 = bf16[512,2048]{1,0:T(8,128)(2,1)S(1)} fusion(bf16[2048,1408]{1,0:T(8,128)(2,1)} %all-gather.5.cloned.1.call-done.w_ref, bf16[2048,1408]{1,0:T(8,128)(2,1)} %get-tuple-element.69), kind=kOutput, calls=%fused_computation.25 | convolution fusion | flops 2953838592 | bytes 9306112 | tf_op jit(solution)/shard_map/dot_general | solution.py:52
  326.7 3.7 convolution_convert_fusion.7
  330.9 4.7 add_convert_fusion.5
  335.6 4.8 add_convert_fusion.4
  340.4 9.7 %convolution_convert_fusion.2 = bf16[704,2048]{1,0:T(8,128)(2,1)} fusion(bf16[2048,704]{1,0:T(8,128)(2,1)S(1)} %copy-done.1, bf16[2048,2048]{1,0:T(8,128)(2,1)} %constant_dynamic-update-slice_fusion.9.out_ref), kind=kOutput, calls=%fused_computation.18 | convolution fusion | flops 5907021824 | bytes 14155776 | tf_op jit(solution)/shard_map/dot_general | solution.py:48
  350.1 3.3 fusion.52
  357.1 2.5 copy.126
  359.7 18.8 %collective-permute-done.37 = bf16[256,2048]{1,0:T(8,128)(2,1)} collective-permute-done((bf16[256,2048]{1,0:T(8,128)(2,1)}, bf16[256,2048]{1,0:T(8,128)(2,1)}, u32[]{:S(2)}, u32[]{:S(2)}) %collective-permute-start.37) | collective-permute-done | bytes 1048608 | tf_op jit(solution)/shard_map/ppermute | solution.py:230
  379.4 22.4 %collective-permute-done.35 = bf16[256,2048]{1,0:T(8,128)(2,1)} collective-permute-done((bf16[256,2048]{1,0:T(8,128)(2,1)}, bf16[256,2048]{1,0:T(8,128)(2,1)}, u32[]{:S(2)}, u32[]{:S(2)}) %collective-permute-start.35) | collective-permute-done | bytes 1048608 | tf_op jit(solution)/shard_map/ppermute | solution.py:234
  401.8 3.1 multiply_reduce_fusion.2
  404.9 4.8 fusion.50
  412.8 3.1 convolution_convert_fusion.5
  417.1 3.1 convolution_convert_fusion.4
  420.3 3.3 convolution_convert_fusion.1
  425.1 4.3 all-to-all-start.3
  429.4 4.6 add_convert_fusion.3
  436.2 3.7 add_convert_fusion.2
  443.7 2.5 fusion
  446.1 19.4 %collective-permute-done.42 = bf16[256,2048]{1,0:T(8,128)(2,1)} collective-permute-done((bf16[256,2048]{1,0:T(8,128)(2,1)}, bf16[256,2048]{1,0:T(8,128)(2,1)}, u32[]{:S(2)}, u32[]{:S(2)}) %collective-permute-start.42) | collective-permute-done | bytes 1048608 | tf_op jit(solution)/shard_map/ppermute | solution.py:234
  465.5 22.6 %collective-permute-done.41 = bf16[256,2048]{1,0:T(8,128)(2,1)} collective-permute-done((bf16[256,2048]{1,0:T(8,128)(2,1)}, bf16[256,2048]{1,0:T(8,128)(2,1)}, u32[]{:S(2)}, u32[]{:S(2)}) %collective-permute-start.41) | collective-permute-done | bytes 1048608 | tf_op jit(solution)/shard_map/ppermute | solution.py:230
  488.1 3.6 add_convert_fusion
  496.4 28.9 %attend_backward.1 = bf16[1024,640]{1,0:T(8,128)(2,1)S(1)} custom-call(bf16[1024,640]{1,0:T(8,128)(2,1)S(1)} %copy-done.4, bf16[1024,640]{1,0:T(8,128)(2,1)S(1)} %copy-done.4, bf16[1024,512]{1,0:T(8,128)(2,1)S(1)} %bitcast.203, f32[1024,128]{1,0:T(8,128)S(1)} %get-tuple-element.143.cos_ref, f32[1024,128]{1,0:T(8,128)S(1)} %get-tuple-element.144.sin_ref, ...), custom_call_target="tpu_custom_call" | custom-call | flops 32212254720 | bytes 5242880 | tf_op jit(solution)/shard_map/attend_backward/pallas_call | solution.py:196
  525.4 15.2 %collective-permute-done.46 = bf16[4,64,2048]{2,1,0:T(8,128)(2,1)S(1)} collective-permute-done((bf16[4,64,2048]{2,1,0:T(8,128)(2,1)S(1)}, bf16[4,64,2048]{2,1,0:T(8,128)(2,1)S(1)}, u32[]{:S(2)}, u32[]{:S(2)}) %collective-permute-start.46) | collective-permute-done | bytes 1048608 | tf_op jit(solution)/shard_map/ppermute | solution.py:234
  540.6 5.3 convolution_convert_fusion.3
  546.1 5.1 convolution_convert_fusion.6
  551.2 2.6 collective-permute-start.47
  553.8 4.2 add_add_fusion
  560.4 2.5 dynamic-slice_bitcast_fusion
  563.2 4.6 all-to-all-start.4
  567.7 4.3 add_convert_fusion.1
  577.7 3.6 collective-permute-start.51
  581.3 20.0 %collective-permute-done.49 = bf16[4,256,640]{2,1,0:T(8,128)(2,1)} collective-permute-done((bf16[4,256,640]{2,1,0:T(8,128)(2,1)}, bf16[4,256,640]{2,1,0:T(8,128)(2,1)}, u32[]{:S(2)}, u32[]{:S(2)}) %collective-permute-start.49) | collective-permute-done | bytes 1310752 | tf_op jit(solution)/shard_map/ppermute | solution.py:230
  601.3 7.6 %all-to-all-done.4 = bf16[8,64,1408]{2,1,0:T(8,128)(2,1)S(1)} async-done(((bf16[8,64,1408]{2,1,0:T(8,128)(2,1)}), bf16[8,64,1408]{2,1,0:T(8,128)(2,1)S(1)}, u32[]{:S(2)}, u32[]{:S(2)}) %all-to-all-start.4) | async-done | bytes 1441824 | tf_op jit(solution)/shard_map/all_to_all | solution.py:482
  609.0 3.1 fusion.1
  612.0 7.1 %all-to-all-start.5 = ((bf16[16,64,640]{2,1,0:T(8,128)(2,1)}), bf16[16,64,640]{2,1,0:T(8,128)(2,1)}, u32[]{:S(2)}, u32[]{:S(2)}) async-start(bf16[16,64,640]{2,1,0:T(8,128)(2,1)} %bitcast.214), calls=%async_computation.6 | async-start | bytes 2621440 | tf_op jit(solution)/shard_map/all_to_all | solution.py:485
  625.3 2.5 convert_bitcast_fusion
  627.8 5.6 reshape.259
  638.6 2.6 broadcast_multiply_fusion
  641.2 8.5 %all-to-all-done.5 = bf16[16,64,640]{2,1,0:T(8,128)(2,1)} async-done(((bf16[16,64,640]{2,1,0:T(8,128)(2,1)}), bf16[16,64,640]{2,1,0:T(8,128)(2,1)}, u32[]{:S(2)}, u32[]{:S(2)}) %all-to-all-start.5) | async-done | bytes 1310752 | tf_op jit(solution)/shard_map/all_to_all | solution.py:485
  (348 shorter events, 143.5 us)
Async XLA Ops:
  7.2 107.9 %all-gather.9.cloned.1.call-start = ((), (), s32[]{:S(2)}) async-start(), calls=%async_computation.12 | async-start | bytes 1310720 | tf_op jit(solution)/shard_map/all_gather | solution.py:403
  7.2 37.5 %collective-permute-start = (bf16[256,2048]{1,0:T(8,128)(2,1)}, bf16[256,2048]{1,0:T(8,128)(2,1)}, u32[]{:S(2)}, u32[]{:S(2)}) collective-permute-start(bf16[256,2048]{1,0:T(8,128)(2,1)} %param.9), channel_id=1, source_target_pairs={{0,2},{2,0},{1,3},{3,1},{4,6},{6,4},{5,7},{7,5},{8,10},{10,8},{9,1... | collective-permute-start | bytes 3145736 | tf_op jit(solution)/shard_map/ppermute | solution.py:230
  11.0 24.4 %all-to-all-start = ((bf16[4,64,640]{2,1,0:T(8,128)(2,1)}), bf16[4,64,640]{2,1,0:T(8,128)(2,1)S(1)}, u32[]{:S(2)}, u32[]{:S(2)}) async-start(bf16[4,64,640]{2,1,0:T(8,128)(2,1)} %copy.113), calls=%async_computation | async-start | bytes 655360 | tf_op jit(solution)/shard_map/all_to_all | solution.py:389
  16.2 214.2 %all-gather.7.cloned.1.call-start = ((), (), s32[]{:S(2)}) async-start(), calls=%async_computation.9 | async-start | bytes 3604480 | tf_op jit(solution)/shard_map/all_gather | solution.py:406
  35.4 8.9 %collective-permute-start.3 = (bf16[256,640]{1,0:T(8,128)(2,1)S(1)}, bf16[256,640]{1,0:T(8,128)(2,1)}, u32[]{:S(2)}, u32[]{:S(2)}) collective-permute-start(bf16[256,640]{1,0:T(8,128)(2,1)S(1)} %bitcast.227), channel_id=1, source_target_pairs={{8,0},{16,8},{24,16},{0,24},{9,1},{17,9},{25,17},{1,25},{10,2},{18... | collective-permute-start | bytes 983048 | tf_op jit(solution)/shard_map/ppermute | solution.py:264
  38.5 28.9 %collective-permute-start.2 = (bf16[256,640]{1,0:T(8,128)(2,1)S(1)}, bf16[256,640]{1,0:T(8,128)(2,1)}, u32[]{:S(2)}, u32[]{:S(2)}) collective-permute-start(bf16[256,640]{1,0:T(8,128)(2,1)S(1)} %bitcast.228), channel_id=1, source_target_pairs={{0,4},{4,0},{1,5},{5,1},{2,6},{6,2},{3,7},{7,3},{8,12},{12,8},{9,1... | collective-permute-start | bytes 983048 | tf_op jit(solution)/shard_map/ppermute | solution.py:230
  39.8 31.7 %collective-permute-start.5 = (bf16[256,640]{1,0:T(8,128)(2,1)S(1)}, bf16[256,640]{1,0:T(8,128)(2,1)}, u32[]{:S(2)}, u32[]{:S(2)}) collective-permute-start(bf16[256,640]{1,0:T(8,128)(2,1)S(1)} %bitcast.229), channel_id=1, source_target_pairs={{16,0},{24,8},{0,16},{8,24},{17,1},{25,9},{1,17},{9,25},{18,2},{26... | collective-permute-start | bytes 983048 | tf_op jit(solution)/shard_map/ppermute | solution.py:264
  42.1 55.0 %collective-permute-start.7 = (bf16[256,640]{1,0:T(8,128)(2,1)S(1)}, bf16[256,640]{1,0:T(8,128)(2,1)}, u32[]{:S(2)}, u32[]{:S(2)}) collective-permute-start(bf16[256,640]{1,0:T(8,128)(2,1)S(1)} %bitcast.230), channel_id=1, source_target_pairs={{24,0},{0,8},{8,16},{16,24},{25,1},{1,9},{9,17},{17,25},{26,2},{2,... | collective-permute-start | bytes 983048 | tf_op jit(solution)/shard_map/ppermute | solution.py:264
  44.4 64.8 %collective-permute-start.9 = (bf16[256,2048]{1,0:T(8,128)(2,1)}, bf16[256,2048]{1,0:T(8,128)(2,1)}, u32[]{:S(2)}, u32[]{:S(2)}) collective-permute-start(bf16[256,2048]{1,0:T(8,128)(2,1)} %param.17), channel_id=1, source_target_pairs={{0,2},{2,0},{1,3},{3,1},{4,6},{6,4},{5,7},{7,5},{8,10},{10,8},{9,1... | collective-permute-start | bytes 3145736 | tf_op jit(solution)/shard_map/ppermute | solution.py:230
  48.5 68.1 %collective-permute-start.1 = (bf16[2,256,2048]{2,1,0:T(8,128)(2,1)}, bf16[2,256,2048]{2,1,0:T(8,128)(2,1)}, u32[]{:S(2)}, u32[]{:S(2)}) collective-permute-start(bf16[2,256,2048]{2,1,0:T(8,128)(2,1)} %pad_maximum_fusion.1), channel_id=1, source_target_pairs={{0,1},{1,0},{2,3},{3,2},{4,5},{5,4},{6,7},{7,6},{8,9},{9,8},{10,11... | collective-permute-start | bytes 6291464 | tf_op jit(solution)/shard_map/ppermute | solution.py:230
  67.4 34.8 %collective-permute-start.4 = (bf16[256,640]{1,0:T(8,128)(2,1)}, bf16[256,640]{1,0:T(8,128)(2,1)S(1)}, u32[]{:S(2)}, u32[]{:S(2)}) collective-permute-start(bf16[256,640]{1,0:T(8,128)(2,1)} %collective-permute-done.3), channel_id=1, source_target_pairs={{0,4},{4,0},{1,5},{5,1},{2,6},{6,2},{3,7},{7,3},{8,12},{12,8},{9,1... | collective-permute-start | bytes 983048 | tf_op jit(solution)/shard_map/ppermute | solution.py:230
  71.5 32.6 %collective-permute-start.6 = (bf16[256,640]{1,0:T(8,128)(2,1)}, bf16[256,640]{1,0:T(8,128)(2,1)S(1)}, u32[]{:S(2)}, u32[]{:S(2)}) collective-permute-start(bf16[256,640]{1,0:T(8,128)(2,1)} %collective-permute-done.5), channel_id=1, source_target_pairs={{0,4},{4,0},{1,5},{5,1},{2,6},{6,2},{3,7},{7,3},{8,12},{12,8},{9,1... | collective-permute-start | bytes 983048 | tf_op jit(solution)/shard_map/ppermute | solution.py:230
  97.2 9.1 %collective-permute-start.8 = (bf16[256,640]{1,0:T(8,128)(2,1)}, bf16[256,640]{1,0:T(8,128)(2,1)S(1)}, u32[]{:S(2)}, u32[]{:S(2)}) collective-permute-start(bf16[256,640]{1,0:T(8,128)(2,1)} %collective-permute-done.7), channel_id=1, source_target_pairs={{0,4},{4,0},{1,5},{5,1},{2,6},{6,2},{3,7},{7,3},{8,12},{12,8},{9,1... | collective-permute-start | bytes 983048 | tf_op jit(solution)/shard_map/ppermute | solution.py:230
  109.1 24.0 %all-to-all-start.1 = ((bf16[8,64,1408]{2,1,0:T(8,128)(2,1)}), bf16[8,64,1408]{2,1,0:T(8,128)(2,1)}, u32[]{:S(2)}, u32[]{:S(2)}) async-start(bf16[8,64,1408]{2,1,0:T(8,128)(2,1)} %concatenate.36), calls=%async_computation.1 | async-start | bytes 2883584 | tf_op jit(solution)/shard_map/all_to_all | solution.py:408
  115.1 41.5 %collective-permute-start.13 = (bf16[4,64,2048]{2,1,0:T(8,128)(2,1)}, bf16[4,64,2048]{2,1,0:T(8,128)(2,1)}, u32[]{:S(2)}, u32[]{:S(2)}) collective-permute-start(bf16[4,64,2048]{2,1,0:T(8,128)(2,1)} %bitcast.31), channel_id=1, source_target_pairs={{0,4},{4,0},{1,5},{5,1},{2,6},{6,2},{3,7},{7,3},{8,12},{12,8},{9,1... | collective-permute-start | bytes 3145736 | tf_op jit(solution)/shard_map/ppermute | solution.py:230
  116.3 41.5 %collective-permute-start.11 = (bf16[4,64,2048]{2,1,0:T(8,128)(2,1)}, bf16[4,64,2048]{2,1,0:T(8,128)(2,1)}, u32[]{:S(2)}, u32[]{:S(2)}) collective-permute-start(bf16[4,64,2048]{2,1,0:T(8,128)(2,1)} %bitcast.31), channel_id=1, source_target_pairs={{0,2},{2,0},{1,3},{3,1},{4,6},{6,4},{5,7},{7,5},{8,10},{10,8},{9,1... | collective-permute-start | bytes 3145736 | tf_op jit(solution)/shard_map/ppermute | solution.py:230
  151.0 30.8 %all-to-all-start.2 = ((bf16[4,256,512]{1,2,0:T(8,128)(2,1)}), bf16[4,256,512]{1,2,0:T(8,128)(2,1)S(1)}, u32[]{:S(2)}, u32[]{:S(2)}) async-start(bf16[4,256,512]{1,2,0:T(8,128)(2,1)} %copy.117), calls=%async_computation.2 | async-start | bytes 2097152 | tf_op jit(solution)/shard_map/all_to_all | solution.py:420
  156.6 117.6 %all-gather.5.cloned.1.call-start = ((), (), s32[]{:S(2)}) async-start(), calls=%async_computation.8 | async-start | bytes 7208960 | tf_op jit(solution)/shard_map/all_gather | solution.py:409
  157.6 22.8 %collective-permute-start.14 = (bf16[4,32,2048]{2,1,0:T(8,128)(2,1)S(1)}, bf16[4,32,2048]{2,1,0:T(8,128)(2,1)}, u32[]{:S(2)}, u32[]{:S(2)}) collective-permute-start(bf16[4,32,2048]{2,1,0:T(8,128)(2,1)S(1)} %slice.151), channel_id=1, source_target_pairs={{0,2},{2,0},{1,3},{3,1},{4,6},{6,4},{5,7},{7,5},{8,10},{10,8},{9,1... | collective-permute-start | bytes 1572872 | tf_op jit(solution)/shard_map/ppermute | solution.py:230
  158.9 21.6 %collective-permute-start.12 = (bf16[4,32,2048]{2,1,0:T(8,128)(2,1)S(1)}, bf16[4,32,2048]{2,1,0:T(8,128)(2,1)}, u32[]{:S(2)}, u32[]{:S(2)}) collective-permute-start(bf16[4,32,2048]{2,1,0:T(8,128)(2,1)S(1)} %slice.150), channel_id=1, source_target_pairs={{0,4},{4,0},{1,5},{5,1},{2,6},{6,2},{3,7},{7,3},{8,12},{12,8},{9,1... | collective-permute-start | bytes 1572872 | tf_op jit(solution)/shard_map/ppermute | solution.py:230
  159.2 35.5 %collective-permute-start.10 = (bf16[256,2048]{1,0:T(8,128)(2,1)}, bf16[256,2048]{1,0:T(8,128)(2,1)}, u32[]{:S(2)}, u32[]{:S(2)}) collective-permute-start(bf16[256,2048]{1,0:T(8,128)(2,1)} %param.17), channel_id=1, source_target_pairs={{0,4},{4,0},{1,5},{5,1},{2,6},{6,2},{3,7},{7,3},{8,12},{12,8},{9,1... | collective-permute-start | bytes 3145736 | tf_op jit(solution)/shard_map/ppermute | solution.py:230
  160.4 34.7 %collective-permute-start.18 = (bf16[4,64,2048]{2,1,0:T(8,128)(2,1)}, bf16[4,64,2048]{2,1,0:T(8,128)(2,1)}, u32[]{:S(2)}, u32[]{:S(2)}) collective-permute-start(bf16[4,64,2048]{2,1,0:T(8,128)(2,1)} %bitcast.31), channel_id=1, source_target_pairs={{0,1},{1,0},{2,3},{3,2},{4,5},{5,4},{6,7},{7,6},{8,9},{9,8},{10,11... | collective-permute-start | bytes 3145736 | tf_op jit(solution)/shard_map/ppermute | solution.py:230
  161.4 396.7 %reduce-scatter.5.cloned.1.call-start = ((), (), s32[]{:S(2)}) async-start(), calls=%async_computation.11 | async-start | bytes 3604480 | tf_op jit(solution)/shard_map/reduce_scatter | solution.py:450
  181.8 12.9 %collective-permute-start.15 = (bf16[4,64,2048]{2,1,0:T(8,128)(2,1)S(1)}, bf16[4,64,2048]{2,1,0:T(8,128)(2,1)S(1)}, u32[]{:S(2)}, u32[]{:S(2)}) collective-permute-start(bf16[4,64,2048]{2,1,0:T(8,128)(2,1)S(1)} %pad_maximum_fusion.2), channel_id=1, source_target_pairs={{0,1},{1,0},{2,3},{3,2},{4,5},{5,4},{6,7},{7,6},{8,9},{9,8},{10,11... | collective-permute-start | bytes 3145736 | tf_op jit(solution)/shard_map/ppermute | solution.py:230
  182.4 12.4 %collective-permute-start.16 = (bf16[4,64,2048]{2,1,0:T(8,128)(2,1)}, bf16[4,64,2048]{2,1,0:T(8,128)(2,1)S(1)}, u32[]{:S(2)}, u32[]{:S(2)}) collective-permute-start(bf16[4,64,2048]{2,1,0:T(8,128)(2,1)} %collective-permute-done.11), channel_id=1, source_target_pairs={{0,1},{1,0},{2,3},{3,2},{4,5},{5,4},{6,7},{7,6},{8,9},{9,8},{10,11... | collective-permute-start | bytes 3145736 | tf_op jit(solution)/shard_map/ppermute | solution.py:230
  182.5 12.5 %collective-permute-start.17 = (bf16[4,64,2048]{2,1,0:T(8,128)(2,1)}, bf16[4,64,2048]{2,1,0:T(8,128)(2,1)S(1)}, u32[]{:S(2)}, u32[]{:S(2)}) collective-permute-start(bf16[4,64,2048]{2,1,0:T(8,128)(2,1)} %collective-permute-done.13), channel_id=1, source_target_pairs={{0,1},{1,0},{2,3},{3,2},{4,5},{5,4},{6,7},{7,6},{8,9},{9,8},{10,11... | collective-permute-start | bytes 3145736 | tf_op jit(solution)/shard_map/ppermute | solution.py:230
  200.2 23.6 %collective-permute-start.19 = (bf16[256,2048]{1,0:T(8,128)(2,1)S(1)}, bf16[256,2048]{1,0:T(8,128)(2,1)S(1)}, u32[]{:S(2)}, u32[]{:S(2)}) collective-permute-start(bf16[256,2048]{1,0:T(8,128)(2,1)S(1)} %multiply_convert_fusion.2), channel_id=1, source_target_pairs={{0,2},{2,0},{1,3},{3,1},{4,6},{6,4},{5,7},{7,5},{8,10},{10,8},{9,1... | collective-permute-start | bytes 3145736 | tf_op jit(solution)/shard_map/ppermute | solution.py:230
  201.3 23.7 %collective-permute-start.21 = (bf16[256,2048]{1,0:T(8,128)(2,1)S(1)}, bf16[256,2048]{1,0:T(8,128)(2,1)S(1)}, u32[]{:S(2)}, u32[]{:S(2)}) collective-permute-start(bf16[256,2048]{1,0:T(8,128)(2,1)S(1)} %multiply_convert_fusion.2), channel_id=1, source_target_pairs={{0,4},{4,0},{1,5},{5,1},{2,6},{6,2},{3,7},{7,3},{8,12},{12,8},{9,1... | collective-permute-start | bytes 3145736 | tf_op jit(solution)/shard_map/ppermute | solution.py:230
  224.7 13.6 %collective-permute-start.20 = (bf16[128,2048]{1,0:T(8,128)(2,1)}, bf16[128,2048]{1,0:T(8,128)(2,1)}, u32[]{:S(2)}, u32[]{:S(2)}) collective-permute-start(bf16[128,2048]{1,0:T(8,128)(2,1)} %slice.152), channel_id=1, source_target_pairs={{0,4},{4,0},{1,5},{5,1},{2,6},{6,2},{3,7},{7,3},{8,12},{12,8},{9,1... | collective-permute-start | bytes 1572872 | tf_op jit(solution)/shard_map/ppermute | solution.py:230
  226.8 15.1 %collective-permute-start.22 = (bf16[128,2048]{1,0:T(8,128)(2,1)}, bf16[128,2048]{1,0:T(8,128)(2,1)}, u32[]{:S(2)}, u32[]{:S(2)}) collective-permute-start(bf16[128,2048]{1,0:T(8,128)(2,1)} %slice.153), channel_id=1, source_target_pairs={{0,2},{2,0},{1,3},{3,1},{4,6},{6,4},{5,7},{7,5},{8,10},{10,8},{9,1... | collective-permute-start | bytes 1572872 | tf_op jit(solution)/shard_map/ppermute | solution.py:230
  227.5 34.7 %collective-permute-start.30 = (bf16[256,2048]{1,0:T(8,128)(2,1)}, bf16[256,2048]{1,0:T(8,128)(2,1)}, u32[]{:S(2)}, u32[]{:S(2)}) collective-permute-start(bf16[256,2048]{1,0:T(8,128)(2,1)} %param.17), channel_id=1, source_target_pairs={{0,1},{1,0},{2,3},{3,2},{4,5},{5,4},{6,7},{7,6},{8,9},{9,8},{10,11... | collective-permute-start | bytes 3145736 | tf_op jit(solution)/shard_map/ppermute | solution.py:230
  231.5 16.1 %collective-permute-start.27 = (bf16[128,2048]{1,0:T(8,128)(2,1)S(1)}, bf16[128,2048]{1,0:T(8,128)(2,1)S(1)}, u32[]{:S(2)}, u32[]{:S(2)}) collective-permute-start(bf16[128,2048]{1,0:T(8,128)(2,1)S(1)} %slice.121), channel_id=1, source_target_pairs={{0,4},{4,0},{1,5},{5,1},{2,6},{6,2},{3,7},{7,3},{8,12},{12,8},{9,1... | collective-permute-start | bytes 1572872 | tf_op jit(solution)/shard_map/ppermute | solution.py:230
  233.9 16.6 %collective-permute-start.28 = (bf16[128,2048]{1,0:T(8,128)(2,1)S(1)}, bf16[128,2048]{1,0:T(8,128)(2,1)S(1)}, u32[]{:S(2)}, u32[]{:S(2)}) collective-permute-start(bf16[128,2048]{1,0:T(8,128)(2,1)S(1)} %slice.122), channel_id=1, source_target_pairs={{0,2},{2,0},{1,3},{3,1},{4,6},{6,4},{5,7},{7,5},{8,10},{10,8},{9,1... | collective-permute-start | bytes 1572872 | tf_op jit(solution)/shard_map/ppermute | solution.py:230
  238.3 31.2 %collective-permute-start.31 = (bf16[256,2048]{1,0:T(8,128)(2,1)}, bf16[256,2048]{1,0:T(8,128)(2,1)S(1)}, u32[]{:S(2)}, u32[]{:S(2)}) collective-permute-start(bf16[256,2048]{1,0:T(8,128)(2,1)} %collective-permute-done.9), channel_id=1, source_target_pairs={{0,1},{1,0},{2,3},{3,2},{4,5},{5,4},{6,7},{7,6},{8,9},{9,8},{10,11... | collective-permute-start | bytes 3145736 | tf_op jit(solution)/shard_map/ppermute | solution.py:230
  241.9 17.4 %collective-permute-start.24 = (bf16[256,2048]{1,0:T(8,128)(2,1)S(1)}, bf16[256,2048]{1,0:T(8,128)(2,1)S(1)}, u32[]{:S(2)}, u32[]{:S(2)}) collective-permute-start(bf16[256,2048]{1,0:T(8,128)(2,1)S(1)} %copy-done.46), channel_id=1, source_target_pairs={{0,1},{1,0},{2,3},{3,2},{4,5},{5,4},{6,7},{7,6},{8,9},{9,8},{10,11... | collective-permute-start | bytes 3145736 | tf_op jit(solution)/shard_map/ppermute | solution.py:230
  247.7 11.5 %collective-permute-start.23 = (bf16[256,2048]{1,0:T(8,128)(2,1)S(1)}, bf16[256,2048]{1,0:T(8,128)(2,1)S(1)}, u32[]{:S(2)}, u32[]{:S(2)}) collective-permute-start(bf16[256,2048]{1,0:T(8,128)(2,1)S(1)} %pad_maximum_fusion.3), channel_id=1, source_target_pairs={{0,1},{1,0},{2,3},{3,2},{4,5},{5,4},{6,7},{7,6},{8,9},{9,8},{10,11... | collective-permute-start | bytes 3145736 | tf_op jit(solution)/shard_map/ppermute | solution.py:230
  250.6 10.0 %collective-permute-start.29 = (bf16[256,2048]{1,0:T(8,128)(2,1)S(1)}, bf16[256,2048]{1,0:T(8,128)(2,1)S(1)}, u32[]{:S(2)}, u32[]{:S(2)}) collective-permute-start(bf16[256,2048]{1,0:T(8,128)(2,1)S(1)} %pad_maximum_fusion.4), channel_id=1, source_target_pairs={{0,1},{1,0},{2,3},{3,2},{4,5},{5,4},{6,7},{7,6},{8,9},{9,8},{10,11... | collective-permute-start | bytes 3145736 | tf_op jit(solution)/shard_map/ppermute | solution.py:230
  259.2 11.5 %collective-permute-start.32 = (bf16[256,2048]{1,0:T(8,128)(2,1)}, bf16[256,2048]{1,0:T(8,128)(2,1)S(1)}, u32[]{:S(2)}, u32[]{:S(2)}) collective-permute-start(bf16[256,2048]{1,0:T(8,128)(2,1)} %collective-permute-done.10), channel_id=1, source_target_pairs={{0,1},{1,0},{2,3},{3,2},{4,5},{5,4},{6,7},{7,6},{8,9},{9,8},{10,11... | collective-permute-start | bytes 3145736 | tf_op jit(solution)/shard_map/ppermute | solution.py:230
  259.3 9.9 %collective-permute-start.25 = (bf16[256,2048]{1,0:T(8,128)(2,1)S(1)}, bf16[256,2048]{1,0:T(8,128)(2,1)S(1)}, u32[]{:S(2)}, u32[]{:S(2)}) collective-permute-start(bf16[256,2048]{1,0:T(8,128)(2,1)S(1)} %copy-done.41), channel_id=1, source_target_pairs={{0,1},{1,0},{2,3},{3,2},{4,5},{5,4},{6,7},{7,6},{8,9},{9,8},{10,11... | collective-permute-start | bytes 3145736 | tf_op jit(solution)/shard_map/ppermute | solution.py:230
  260.6 8.7 %collective-permute-start.26 = (bf16[256,2048]{1,0:T(8,128)(2,1)S(1)}, bf16[256,2048]{1,0:T(8,128)(2,1)S(1)}, u32[]{:S(2)}, u32[]{:S(2)}) collective-permute-start(bf16[256,2048]{1,0:T(8,128)(2,1)S(1)} %copy-done.39), channel_id=1, source_target_pairs={{0,1},{1,0},{2,3},{3,2},{4,5},{5,4},{6,7},{7,6},{8,9},{9,8},{10,11... | collective-permute-start | bytes 3145736 | tf_op jit(solution)/shard_map/ppermute | solution.py:230
  326.6 4.3 collective-permute-start.33
  330.4 5.2 collective-permute-start.34
  350.1 213.1 %reduce-scatter.3.cloned.1.call-start = ((), (), s32[]{:S(2)}) async-start(), calls=%async_computation.10 | async-start | bytes 7208960 | tf_op jit(solution)/shard_map/reduce_scatter | solution.py:443
  353.5 25.0 %collective-permute-start.37 = (bf16[256,2048]{1,0:T(8,128)(2,1)}, bf16[256,2048]{1,0:T(8,128)(2,1)}, u32[]{:S(2)}, u32[]{:S(2)}) collective-permute-start(bf16[256,2048]{1,0:T(8,128)(2,1)} %get-tuple-element.108), channel_id=1, source_target_pairs={{0,4},{4,0},{1,5},{5,1},{2,6},{6,2},{3,7},{7,3},{8,12},{12,8},{9,1... | collective-permute-start | bytes 3145736 | tf_op jit(solution)/shard_map/ppermute | solution.py:230
  354.7 24.7 %collective-permute-start.36 = (bf16[256,2048]{1,0:T(8,128)(2,1)}, bf16[256,2048]{1,0:T(8,128)(2,1)}, u32[]{:S(2)}, u32[]{:S(2)}) collective-permute-start(bf16[256,2048]{1,0:T(8,128)(2,1)} %get-tuple-element.107), channel_id=1, source_target_pairs={{0,2},{2,0},{1,3},{3,1},{4,6},{6,4},{5,7},{7,5},{8,10},{10,8},{9,1... | collective-permute-start | bytes 3145736 | tf_op jit(solution)/shard_map/ppermute | solution.py:230
  356.4 45.4 %collective-permute-start.35 = (bf16[256,2048]{1,0:T(8,128)(2,1)}, bf16[256,2048]{1,0:T(8,128)(2,1)}, u32[]{:S(2)}, u32[]{:S(2)}) collective-permute-start(bf16[256,2048]{1,0:T(8,128)(2,1)} %slice.156), channel_id=1, source_target_pairs={{0,6},{2,4},{4,2},{6,0},{1,7},{3,5},{5,3},{7,1},{8,14},{10,12},{12... | collective-permute-start | bytes 3145736 | tf_op jit(solution)/shard_map/ppermute | solution.py:234
  416.0 13.5 %collective-permute-start.38 = (bf16[512,2048]{1,0:T(8,128)(2,1)}, bf16[512,2048]{1,0:T(8,128)(2,1)}, u32[]{:S(2)}, u32[]{:S(2)}) collective-permute-start(bf16[512,2048]{1,0:T(8,128)(2,1)} %convolution_convert_fusion.5), channel_id=1, source_target_pairs={{0,1},{1,0},{2,3},{3,2},{4,5},{5,4},{6,7},{7,6},{8,9},{9,8},{10,11... | collective-permute-start | bytes 6291464 | tf_op jit(solution)/shard_map/ppermute | solution.py:230
  420.2 16.0 %collective-permute-start.39 = (bf16[512,2048]{1,0:T(8,128)(2,1)}, bf16[512,2048]{1,0:T(8,128)(2,1)}, u32[]{:S(2)}, u32[]{:S(2)}) collective-permute-start(bf16[512,2048]{1,0:T(8,128)(2,1)} %convolution_convert_fusion.4), channel_id=1, source_target_pairs={{0,1},{1,0},{2,3},{3,2},{4,5},{5,4},{6,7},{7,6},{8,9},{9,8},{10,11... | collective-permute-start | bytes 6291464 | tf_op jit(solution)/shard_map/ppermute | solution.py:230
  423.6 64.5 %collective-permute-start.43 = (bf16[1024,2048]{1,0:T(8,128)(2,1)}, bf16[1024,2048]{1,0:T(8,128)(2,1)}, u32[]{:S(2)}, u32[]{:S(2)}) collective-permute-start(bf16[1024,2048]{1,0:T(8,128)(2,1)} %convolution_convert_fusion.1), channel_id=1, source_target_pairs={{0,1},{1,0},{2,3},{3,2},{4,5},{5,4},{6,7},{7,6},{8,9},{9,8},{10,11... | collective-permute-start | bytes 12582920 | tf_op jit(solution)/shard_map/ppermute | solution.py:230
  425.1 21.0 %all-to-all-start.3 = ((bf16[256,4,512]{2,0,1:T(8,128)(2,1)}), bf16[256,4,512]{2,0,1:T(8,128)(2,1)S(1)}, u32[]{:S(2)}, u32[]{:S(2)}) async-start(bf16[256,4,512]{2,0,1:T(8,128)(2,1)} %bitcast.201), calls=%async_computation.3 | async-start | bytes 2097152 | tf_op jit(solution)/shard_map/all_to_all | solution.py:472
  435.2 30.3 %collective-permute-start.42 = (bf16[256,2048]{1,0:T(8,128)(2,1)}, bf16[256,2048]{1,0:T(8,128)(2,1)}, u32[]{:S(2)}, u32[]{:S(2)}) collective-permute-start(bf16[256,2048]{1,0:T(8,128)(2,1)} %slice.162), channel_id=1, source_target_pairs={{0,6},{2,4},{4,2},{6,0},{1,7},{3,5},{5,3},{7,1},{8,14},{10,12},{12... | collective-permute-start | bytes 3145736 | tf_op jit(solution)/shard_map/ppermute | solution.py:234
  441.4 46.6 %collective-permute-start.41 = (bf16[256,2048]{1,0:T(8,128)(2,1)}, bf16[256,2048]{1,0:T(8,128)(2,1)}, u32[]{:S(2)}, u32[]{:S(2)}) collective-permute-start(bf16[256,2048]{1,0:T(8,128)(2,1)} %get-tuple-element.106), channel_id=1, source_target_pairs={{0,4},{4,0},{1,5},{5,1},{2,6},{6,2},{3,7},{7,3},{8,12},{12,8},{9,1... | collective-permute-start | bytes 3145736 | tf_op jit(solution)/shard_map/ppermute | solution.py:230
  442.2 45.9 %collective-permute-start.40 = (bf16[256,2048]{1,0:T(8,128)(2,1)}, bf16[256,2048]{1,0:T(8,128)(2,1)}, u32[]{:S(2)}, u32[]{:S(2)}) collective-permute-start(bf16[256,2048]{1,0:T(8,128)(2,1)} %get-tuple-element.105), channel_id=1, source_target_pairs={{0,2},{2,0},{1,3},{3,1},{4,6},{6,4},{5,7},{7,5},{8,10},{10,8},{9,1... | collective-permute-start | bytes 3145736 | tf_op jit(solution)/shard_map/ppermute | solution.py:230
  493.8 31.6 %collective-permute-start.44 = (bf16[4,64,2048]{2,1,0:T(8,128)(2,1)S(1)}, bf16[4,64,2048]{2,1,0:T(8,128)(2,1)S(1)}, u32[]{:S(2)}, u32[]{:S(2)}) collective-permute-start(bf16[4,64,2048]{2,1,0:T(8,128)(2,1)S(1)} %get-tuple-element.100), channel_id=1, source_target_pairs={{0,2},{2,0},{1,3},{3,1},{4,6},{6,4},{5,7},{7,5},{8,10},{10,8},{9,1... | collective-permute-start | bytes 3145736 | tf_op jit(solution)/shard_map/ppermute | solution.py:230
  495.1 30.2 %collective-permute-start.45 = (bf16[4,64,2048]{2,1,0:T(8,128)(2,1)S(1)}, bf16[4,64,2048]{2,1,0:T(8,128)(2,1)S(1)}, u32[]{:S(2)}, u32[]{:S(2)}) collective-permute-start(bf16[4,64,2048]{2,1,0:T(8,128)(2,1)S(1)} %get-tuple-element.99), channel_id=1, source_target_pairs={{0,4},{4,0},{1,5},{5,1},{2,6},{6,2},{3,7},{7,3},{8,12},{12,8},{9,1... | collective-permute-start | bytes 3145736 | tf_op jit(solution)/shard_map/ppermute | solution.py:230
  495.4 45.2 %collective-permute-start.46 = (bf16[4,64,2048]{2,1,0:T(8,128)(2,1)S(1)}, bf16[4,64,2048]{2,1,0:T(8,128)(2,1)S(1)}, u32[]{:S(2)}, u32[]{:S(2)}) collective-permute-start(bf16[4,64,2048]{2,1,0:T(8,128)(2,1)S(1)} %get-tuple-element.98), channel_id=1, source_target_pairs={{0,6},{2,4},{4,2},{6,0},{1,7},{3,5},{5,3},{7,1},{8,14},{10,12},{12... | collective-permute-start | bytes 3145736 | tf_op jit(solution)/shard_map/ppermute | solution.py:234
  551.2 16.6 %collective-permute-start.47 = (bf16[512,2048]{1,0:T(8,128)(2,1)}, bf16[512,2048]{1,0:T(8,128)(2,1)}, u32[]{:S(2)}, u32[]{:S(2)}) collective-permute-start(bf16[512,2048]{1,0:T(8,128)(2,1)} %convolution_convert_fusion.6), channel_id=1, source_target_pairs={{0,1},{1,0},{2,3},{3,2},{4,5},{5,4},{6,7},{7,6},{8,9},{9,8},{10,11... | collective-permute-start | bytes 6291464 | tf_op jit(solution)/shard_map/ppermute | solution.py:230
  562.9 38.4 %collective-permute-start.49 = (bf16[4,256,640]{2,1,0:T(8,128)(2,1)}, bf16[4,256,640]{2,1,0:T(8,128)(2,1)}, u32[]{:S(2)}, u32[]{:S(2)}) collective-permute-start(bf16[4,256,640]{2,1,0:T(8,128)(2,1)} %dynamic-slice_bitcast_fusion), channel_id=1, source_target_pairs={{0,4},{4,0},{1,5},{5,1},{2,6},{6,2},{3,7},{7,3},{8,12},{12,8},{9,1... | collective-permute-start | bytes 3932168 | tf_op jit(solution)/shard_map/ppermute | solution.py:230
  563.2 45.8 %all-to-all-start.4 = ((bf16[8,64,1408]{2,1,0:T(8,128)(2,1)}), bf16[8,64,1408]{2,1,0:T(8,128)(2,1)S(1)}, u32[]{:S(2)}, u32[]{:S(2)}) async-start(bf16[8,64,1408]{2,1,0:T(8,128)(2,1)} %bitcast.225), calls=%async_computation.5 | async-start | bytes 2883584 | tf_op jit(solution)/shard_map/all_to_all | solution.py:482
  573.1 46.2 %collective-permute-start.48 = (bf16[256,2048]{1,0:T(8,128)(2,1)}, bf16[256,2048]{1,0:T(8,128)(2,1)S(1)}, u32[]{:S(2)}, u32[]{:S(2)}) collective-permute-start(bf16[256,2048]{1,0:T(8,128)(2,1)} %dynamic-slice_bitcast_fusion.1), channel_id=1, source_target_pairs={{0,2},{2,0},{1,3},{3,1},{4,6},{6,4},{5,7},{7,5},{8,10},{10,8},{9,1... | collective-permute-start | bytes 3145736 | tf_op jit(solution)/shard_map/ppermute | solution.py:230
  577.7 73.6 %collective-permute-start.52 = (bf16[64,2048]{1,0:T(8,128)(2,1)}, bf16[64,2048]{1,0:T(8,128)(2,1)}, u32[]{:S(2)}, u32[]{:S(2)}) collective-permute-start(bf16[64,2048]{1,0:T(8,128)(2,1)} %get-tuple-element.120), channel_id=1, source_target_pairs={{0,24},{8,0},{16,8},{24,16},{1,25},{9,1},{17,9},{25,17},{2,26},{10... | collective-permute-start | bytes 786440 | tf_op jit(solution)/shard_map/ppermute | solution.py:503
  577.7 73.6 %collective-permute-start.51 = (bf16[64,2048]{1,0:T(8,128)(2,1)}, bf16[64,2048]{1,0:T(8,128)(2,1)}, u32[]{:S(2)}, u32[]{:S(2)}) collective-permute-start(bf16[64,2048]{1,0:T(8,128)(2,1)} %get-tuple-element.121), channel_id=1, source_target_pairs={{0,16},{8,24},{16,0},{24,8},{1,17},{9,25},{17,1},{25,9},{2,18},{10... | collective-permute-start | bytes 786440 | tf_op jit(solution)/shard_map/ppermute | solution.py:503
  581.3 71.6 %collective-permute-start.50 = (bf16[64,2048]{1,0:T(8,128)(2,1)}, bf16[64,2048]{1,0:T(8,128)(2,1)}, u32[]{:S(2)}, u32[]{:S(2)}) collective-permute-start(bf16[64,2048]{1,0:T(8,128)(2,1)} %get-tuple-element.119), channel_id=1, source_target_pairs={{0,8},{8,16},{16,24},{24,0},{1,9},{9,17},{17,25},{25,1},{2,10},{10... | collective-permute-start | bytes 786440 | tf_op jit(solution)/shard_map/ppermute | solution.py:503
  612.0 37.6 %all-to-all-start.5 = ((bf16[16,64,640]{2,1,0:T(8,128)(2,1)}), bf16[16,64,640]{2,1,0:T(8,128)(2,1)}, u32[]{:S(2)}, u32[]{:S(2)}) async-start(bf16[16,64,640]{2,1,0:T(8,128)(2,1)} %bitcast.214), calls=%async_computation.6 | async-start | bytes 2621440 | tf_op jit(solution)/shard_map/all_to_all | solution.py:485
  (68 other events, 758.3 us)
Sparse Core Ops, SparseCore 0:
  9.6 28.8 all-gather.8
  44.5 69.1 all-gather.6
  161.5 104.3 all-gather.4
  350.2 56.3 reduce-scatter.4
  408.7 102.7 reduce-scatter.2

commit v4 on v3

--- a/solution.py
+++ b/solution.py
@@ -387,7 +387,7 @@
 
     qkv = (w_qkv.astype(f32) * gain_one).astype(bf).reshape(w_rows, 4, cols).transpose(1, 0, 2)
     qkv = lax.all_to_all(qkv, ("x", "c"), 0, 0, tiled=True).reshape(4 * w_rows, cols)
-    over_x = swap(layer_in, "x")
+    over_x = swap(after(layer_in, qkv), "x")
     group_in = gather_pair(pair(layer_in, over_x, "x", 0), "c", 1).reshape(group_rows, width)
     full_qkv = jnp.zeros((depth, 2, 4 * w_rows, cols), bf)
     qkv_own = qkv
@@ -398,14 +398,14 @@
     for r in range(depth):
         piece = pair(qkv_pieces[r], over_y[r], "y", 0)
         full_qkv = lax.dynamic_update_index_in_dim(full_qkv, piece, (z_at + r) % depth, 0)
-    qkv = full_qkv.reshape(-1, cols)
+    qkv = after(full_qkv, out_near[0]).reshape(-1, cols)
 
     out_z = lax.all_gather(w_out, "z", axis=0, tiled=False)
     out_pieces = send_near(after(out_z, *over_y), 1)
 
     full_down = lax.all_gather(after(w_down, qkv_own), "z", axis=0, tiled=True)
     gateup = to_units((after(w_gateup, qkv_pieces[1]).astype(f32) * gain_two).astype(bf), depth, ff_rows)
-    gateup = lax.all_to_all(after(gateup, out_near[0]), QUAD, 0, 0, tiled=True)
+    gateup = lax.all_to_all(after(gateup, *over_y[1:]), QUAD, 0, 0, tiled=True)
     full_gateup = lax.all_gather(gateup.reshape(8 * w_rows, 2 * units), "z", axis=0, tiled=True)
 
     position = doc_layout(doc_lengths[0], group_rows)
@@ -416,8 +416,8 @@
         wide_in * lax.rsqrt(jnp.mean(wide_in * wide_in, axis=-1, keepdims=True) + epsilon)
     ).astype(bf)
     head_cols = jnp.dot(normed_one, qkv, preferred_element_type=f32).astype(bf)
-    mixed_heads = attend_forward(after(head_cols, gateup), cos_table, sin_table, start)
-    mixed_tok = lax.all_to_all(mixed_heads, ("x", "c"), split_axis=0, concat_axis=1, tiled=True)
+    mixed_heads = attend_forward(head_cols, cos_table, sin_table, start)
+    mixed_tok = lax.all_to_all(after(mixed_heads, gateup), ("x", "c"), split_axis=0, concat_axis=1, tiled=True)
     y_at, x_at, c_at = lax.axis_index("y"), lax.axis_index("x"), lax.axis_index("c")
     full_out = jnp.zeros((depth, 2, 2, 2) + w_out.shape, bf)
     out_pieces = [after(piece, mixed_tok) for piece in out_pieces[:3]] + out_pieces[3:]
@@ -446,18 +446,18 @@
     second = over_core(grad_gate_up[half:], by_units)
     over_both, over_x, over_y = cross(first[:rows]), swap(second[:rows], "x"), swap(second[rows:], "y")
     activated = after(activated, first, second)
-    grad_down = contract_rows(activated, many_out).astype(bf)
-    grad_w_down = lax.psum_scatter(grad_down, "z", scatter_dimension=0, tiled=True)
-    over_both, over_x, over_y = (after(part, grad_down) for part in (over_both, over_x, over_y))
+    out_second = over_core(activated[half:], by_down)
+    out_first = over_core(activated[:half], by_down)
+    over_both, over_x, over_y = (after(part, out_first, out_second) for part in (over_both, over_x, over_y))
     scaled_two = total([first[rows:], over_both, over_x, over_y])
 
     grad_mid = grad_out.astype(f32) + norm_back(scaled_two, resid_mid, inv_two)
     grad_mid_low = grad_mid.astype(bf)
     grad_mixed = contract_cols(grad_mid_low, full_out).astype(bf)
-    activated = after(activated, grad_mixed)
-    out_second = over_core(activated[half:], by_down)
-    out_first = over_core(activated[:half], by_down)
+    out_first, out_second = after(out_first, over_x), after(out_second, over_x)
     out_sent = [swap(out_second[:rows], "x"), swap(out_second[rows:], "y"), cross(out_first[:rows])]
+    grad_down = contract_rows(after(activated, grad_mixed), many_out).astype(bf)
+    grad_w_down = lax.psum_scatter(grad_down, "z", scatter_dimension=0, tiled=True)
     mixed_by_core = mixed_tok.reshape(rows, depth, 4, 2, w_rows).transpose(0, 3, 2, 1, 4)
     mixed_by_core = mixed_by_core.reshape(rows, 2, -1)
     low_grads = after(grad_mid_low, grad_mixed)
@@ -501,7 +501,7 @@
     for r in range(1, depth):
         part = lax.dynamic_index_in_dim(grad_out_w, (z_at + r) % depth, 0, keepdims=False)
         out_w_parts.append(lax.ppermute(part, "z", [(i, (i + r) % depth) for i in range(depth)]))
-    layer_out = resid_mid + total([out_first[rows:]] + out_sent)
+    layer_out = resid_mid + total([out_first[rows:]] + [after(part, over_y) for part in out_sent])
 
     sum_qkv = jnp.sum(grad_qkv.reshape(depth, 4, w_rows, cols).astype(f32), axis=0)
     sum_qkv = sum_qkv.transpose(1, 0, 2).reshape(w_rows, 4 * cols)

time: 670 us -> 648 us (0.967)
  waiting for transfers between devices: 234 us -> 207 us
  matrix products: 93.3 us -> 105 us
    ppermute x3, waiting for transfers between devices: 57 us -> 14.8 us  [cross(): return lax.ppermute(value, ('y', 'x'), [(i, 3 - i) for i in range(4)])]
    ppermute x44, waiting for transfers between devices: 113 us -> 143 us  [swap(): return lax.ppermute(value, axis, [(0, 1), (1, 0)])]
    all_to_all x1, waiting for transfers between devices: 0.01 us -> 17 us  [body(): lax.all_to_all(grad_mixed, ('x', 'c'), split_axis=1, concat_axis=0, tiled...]
    ppermute x3, waiting for transfers between devices: 26.2 us -> 14.5 us  [rotations(): lax.ppermute(value, 'z', [((i + r) % depth, i) for i in range(depth)])]
    dot_general x7, matrix products: 31.6 us -> 42.7 us  [contract_cols(): lax.dot_general(left, right, (((1,), (1,)), ((), ())), preferred_element_...]
    all_to_all x1, waiting for transfers between devices: 14.9 us -> 4.65 us  [body(): lax.all_to_all(qkv, ('x', 'c'), 0, 0, tiled=True).reshape(4 * w_rows, cols)]
    unnamed x150 -> x146, local copies, waits for them, and re-layouts: 30.9 us -> 25.5 us
  transfers between devices with their start and end apart: 64 -> 64, of which waited for: 18 -> 19; matrix products, arithmetic and copies ran while one was open for 30% -> 35% of each run, Pallas kernels for 7% -> 7%
where the time goes in v4:
time: 648 us; the launch traced here: 639 us
  waiting for transfers between devices  207 us (32%)
  matrix products  105 us (16%)
  local copies, waits for them, and re-layouts  87.6 us (14%)
  starting transfers between devices  85.2 us (13%)
  Pallas kernels  71.2 us (11%)
  other arithmetic  67.5 us (10%)
  between operations  15.4 us (2%)
    ppermute x44, waiting for transfers between devices, swap(): return lax.ppermute(value, axis, [(0, 1), (1, 0)])  143 us
    dot_general x7, matrix products, contract_cols(): lax.dot_general(left, right, (((1,), (1,)), ((), ())), preferred_element_...  42.7 us
    ppermute x44, starting transfers between devices, swap(): return lax.ppermute(value, axis, [(0, 1), (1, 0)])  41.3 us
    dot_general x5, matrix products, contract_rows(): lax.dot_general(left, right, (((0,), (0,)), ((), ())), preferred_element_...  38.2 us
    pallas_call x1, Pallas kernels, attend_backward(): pl.pallas_call(backward_kernel, grid=(pairs + 1,), in_specs=[pl.BlockSpec...  28.7 us
    pallas_call x1, Pallas kernels, run_units(): pl.pallas_call(units_kernel, grid=(count // block,), in_specs=[pl.BlockSp...  27.3 us
    unnamed x146, local copies, waits for them, and re-layouts  25.5 us
    all_to_all x1, waiting for transfers between devices, body(): lax.all_to_all(grad_mixed, ('x', 'c'), split_axis=1, concat_axis=0, tiled...  17 us
  transfers between devices with their start and end apart: 64, of which 19 were waited for; matrix products, arithmetic and copies ran while one was open for 35% of the time, Pallas kernels for 7%

profile of v4, /device:TPU:11, one launch (start us, length us, event | category | flops | bytes accessed | tf_op | source)
XLA Modules:
  0.0 638.5 jit_solution(11281997839976928633)
XLA Ops:
  11.0 4.9 all-to-all-start
  16.2 4.6 all-to-all-done
  31.3 14.5 %collective-permute-done.3 = bf16[256,640]{1,0:T(8,128)(2,1)S(1)} collective-permute-done((bf16[256,640]{1,0:T(8,128)(2,1)}, bf16[256,640]{1,0:T(8,128)(2,1)S(1)}, u32[]{:S(2)}, u32[]{:S(2)}) %collective-permute-start.3) | collective-permute-done | bytes 327712 | tf_op jit(solution)/shard_map/ppermute | solution.py:264
  50.1 2.8 collective-permute-start.1
  54.3 5.8 reshape.238
  60.0 3.9 copy.116
  64.0 4.8 reshape.239
  79.0 3.2 collective-permute-done.4
  82.3 6.9 %collective-permute-done.6 = bf16[256,640]{1,0:T(8,128)(2,1)S(1)} collective-permute-done((bf16[256,640]{1,0:T(8,128)(2,1)}, bf16[256,640]{1,0:T(8,128)(2,1)S(1)}, u32[]{:S(2)}, u32[]{:S(2)}) %collective-permute-start.6) | collective-permute-done | bytes 327712 | tf_op jit(solution)/shard_map/ppermute | solution.py:230
  89.2 7.0 %collective-permute-done.8 = bf16[256,640]{1,0:T(8,128)(2,1)S(1)} collective-permute-done((bf16[256,640]{1,0:T(8,128)(2,1)}, bf16[256,640]{1,0:T(8,128)(2,1)S(1)}, u32[]{:S(2)}, u32[]{:S(2)}) %collective-permute-start.8) | collective-permute-done | bytes 327712 | tf_op jit(solution)/shard_map/ppermute | solution.py:230
  96.2 6.6 %all-to-all-start.1 = ((bf16[8,64,1408]{2,1,0:T(8,128)(2,1)}), bf16[8,64,1408]{2,1,0:T(8,128)(2,1)}, u32[]{:S(2)}, u32[]{:S(2)}) async-start(bf16[8,64,1408]{2,1,0:T(8,128)(2,1)} %concatenate.38), calls=%async_computation.1 | async-start | bytes 2883584 | tf_op jit(solution)/shard_map/all_to_all | solution.py:408
  113.4 5.2 convolution_convert_fusion.10.query_ref.both_ref
  118.5 15.2 %attend_forward.1 = bf16[1024,512]{1,0:T(8,128)(2,1)S(1)} custom-call(bf16[1024,640]{1,0:T(8,128)(2,1)S(1)} %convolution_convert_fusion.10.query_ref.both_ref, bf16[1024,640]{1,0:T(8,128)(2,1)S(1)} %convolution_convert_fusion.10.query_ref.both_ref, f32[1024,128]{1,0:T(8,128)S(1)} %get-tuple-element.167.cos_ref, f32[1024,128]{1,0:T(8,128)S(1)} %get-tuple-element.168.sin_ref, ...), custom_call_target="tpu_custom_call" | custom-call | flops 12884901888 | bytes 3932160 | tf_op jit(solution)/shard_map/attend_forward/pallas_call | solution.py:169
  136.2 5.7 all-to-all-start.2
  150.7 15.1 %collective-permute-done.14 = bf16[4,32,2048]{2,1,0:T(8,128)(2,1)} collective-permute-done((bf16[4,32,2048]{2,1,0:T(8,128)(2,1)}, bf16[4,32,2048]{2,1,0:T(8,128)(2,1)}, u32[]{:S(2)}, u32[]{:S(2)}) %collective-permute-start.14) | collective-permute-done | bytes 524320 | tf_op jit(solution)/shard_map/ppermute | solution.py:230
  173.3 9.1 %collective-permute-done.10 = bf16[256,2048]{1,0:T(8,128)(2,1)} collective-permute-done((bf16[256,2048]{1,0:T(8,128)(2,1)S(1)}, bf16[256,2048]{1,0:T(8,128)(2,1)}, u32[]{:S(2)}, u32[]{:S(2)}) %collective-permute-start.10) | collective-permute-done | bytes 1048608 | tf_op jit(solution)/shard_map/ppermute | solution.py:230
  184.3 2.5 multiply_reduce_fusion.3
  189.7 21.6 %collective-permute-done.19 = bf16[256,2048]{1,0:T(8,128)(2,1)S(1)} collective-permute-done((bf16[256,2048]{1,0:T(8,128)(2,1)S(1)}, bf16[256,2048]{1,0:T(8,128)(2,1)S(1)}, u32[]{:S(2)}, u32[]{:S(2)}) %collective-permute-start.19) | collective-permute-done | bytes 1048608 | tf_op jit(solution)/shard_map/ppermute | solution.py:230
  214.7 3.0 collective-permute-start.30
  221.5 4.0 pad_maximum_fusion.down_ref
  225.5 4.4 collective-permute-start.31
  234.8 3.2 collective-permute-start.23
  255.9 2.4 copy-done.54
  259.4 27.3 %units.1 = (bf16[2048,704]{1,0:T(8,128)(2,1)S(1)}, bf16[2048,1408]{1,0:T(8,128)(2,1)}) custom-call(bf16[2048,2048]{1,0:T(8,128)(2,1)} %copy-done.54, bf16[2048,2048]{1,0:T(8,128)(2,1)} %constant_dynamic-update-slice_fusion.9.out_ref, bf16[2048,1408]{1,0:T(8,128)(2,1)} %all-gather.5.cloned.1.call-done.w_ref, bf16[768,2048]{1,0:T(8,128)(2,1)} %pad_maximum_fusion.down_ref), custom_call_target="tpu_custom_call" | custom-call | flops 17716740096 | bytes 34078720 | tf_op jit(solution)/shard_map/units/pallas_call | solution.py:350
  288.3 16.6 %convolution_convert_fusion = bf16[2048,1408]{1,0:T(8,128)(2,1)} fusion(bf16[2048,2048]{1,0:T(8,128)(2,1)S(1)} %copy-done.55, bf16[2048,1408]{1,0:T(8,128)(2,1)} %get-tuple-element.85), kind=kOutput, calls=%fused_computation.5 | convolution fusion | flops 11814043648 | bytes 19922944 | tf_op jit(solution)/shard_map/dot_general | solution.py:48
  304.9 8.0 %convolution_convert_fusion.8 = bf16[512,2048]{1,0:T(8,128)(2,1)} fusion(bf16[2048,1408]{1,0:T(8,128)(2,1)} %all-gather.5.cloned.1.call-done.w_ref, bf16[2048,1408]{1,0:T(8,128)(2,1)} %get-tuple-element.85), kind=kOutput, calls=%fused_computation.25 | convolution fusion | flops 2953838592 | bytes 9306112 | tf_op jit(solution)/shard_map/dot_general | solution.py:52
  313.1 6.4 convolution_convert_fusion.7
  319.8 8.5 %add_convert_fusion.5 = bf16[512,2048]{1,0:T(8,128)(2,1)} fusion(bf16[512,2048]{1,0:T(8,128)(2,1)} %collective-permute-done.33, bf16[2048,1408]{1,0:T(8,128)(2,1)} %all-gather.5.cloned.1.call-done.w_ref, bf16[2048,1408]{1,0:T(8,128)(2,1)} %get-tuple-element.85), kind=kOutput, calls=%fused_computation.12 | convolution fusion | flops 2955935744 | bytes 11403264 | tf_op jit(solution)/shard_map/dot_general | solution.py:52
  328.3 7.3 %add_convert_fusion.4 = bf16[512,2048]{1,0:T(8,128)(2,1)S(1)} fusion(bf16[512,2048]{1,0:T(8,128)(2,1)} %collective-permute-done.34, bf16[2048,1408]{1,0:T(8,128)(2,1)} %all-gather.5.cloned.1.call-done.w_ref, bf16[2048,1408]{1,0:T(8,128)(2,1)} %get-tuple-element.85), kind=kOutput, calls=%fused_computation.11 | convolution fusion | flops 2955935744 | bytes 11403264 | tf_op jit(solution)/shard_map/dot_general | solution.py:52
  335.6 3.1 convolution_convert_fusion.5
  338.9 3.1 convolution_convert_fusion.4
  348.5 5.6 add_convert_fusion.3
  354.1 14.7 %collective-permute-done.36 = bf16[256,2048]{1,0:T(8,128)(2,1)} collective-permute-done((bf16[256,2048]{1,0:T(8,128)(2,1)}, bf16[256,2048]{1,0:T(8,128)(2,1)}, u32[]{:S(2)}, u32[]{:S(2)}) %collective-permute-start.36) | collective-permute-done | bytes 1048608 | tf_op jit(solution)/shard_map/ppermute | solution.py:230
  368.8 4.7 add_convert_fusion.2
  373.6 20.3 %collective-permute-done.40 = bf16[256,2048]{1,0:T(8,128)(2,1)S(1)} collective-permute-done((bf16[256,2048]{1,0:T(8,128)(2,1)S(1)}, bf16[256,2048]{1,0:T(8,128)(2,1)S(1)}, u32[]{:S(2)}, u32[]{:S(2)}) %collective-permute-start.40) | collective-permute-done | bytes 1048608 | tf_op jit(solution)/shard_map/ppermute | solution.py:230
  396.0 3.7 fusion.50
  399.8 3.5 convolution_convert_fusion.9
  403.3 3.3 convolution_convert_fusion.1
  410.0 2.5 fusion
  415.8 5.1 all-to-all-start.3
  421.0 3.3 fusion.51
  424.4 9.8 %convolution_convert_fusion.2 = bf16[704,2048]{1,0:T(8,128)(2,1)} fusion(bf16[2048,704]{1,0:T(8,128)(2,1)S(1)} %copy-done.3, bf16[2048,2048]{1,0:T(8,128)(2,1)} %constant_dynamic-update-slice_fusion.9.out_ref), kind=kOutput, calls=%fused_computation.18 | convolution fusion | flops 5907021824 | bytes 14155776 | tf_op jit(solution)/shard_map/dot_general | solution.py:48
  434.2 17.0 %all-to-all-done.3 = bf16[256,4,512]{2,0,1:T(8,128)(2,1)S(1)} async-done(((bf16[256,4,512]{2,0,1:T(8,128)(2,1)}), bf16[256,4,512]{2,0,1:T(8,128)(2,1)S(1)}, u32[]{:S(2)}, u32[]{:S(2)}) %all-to-all-start.3) | async-done | bytes 1048608 | tf_op jit(solution)/shard_map/all_to_all | solution.py:472
  451.1 22.5 %collective-permute-done.38 = bf16[256,2048]{1,0:T(8,128)(2,1)} collective-permute-done((bf16[256,2048]{1,0:T(8,128)(2,1)}, bf16[256,2048]{1,0:T(8,128)(2,1)}, u32[]{:S(2)}, u32[]{:S(2)}) %collective-permute-start.38) | collective-permute-done | bytes 1048608 | tf_op jit(solution)/shard_map/ppermute | solution.py:230
  473.6 3.6 add_convert_fusion
  481.9 28.7 %attend_backward.1 = bf16[1024,640]{1,0:T(8,128)(2,1)S(1)} custom-call(bf16[1024,640]{1,0:T(8,128)(2,1)S(1)} %copy-done.5, bf16[1024,640]{1,0:T(8,128)(2,1)S(1)} %copy-done.5, bf16[1024,512]{1,0:T(8,128)(2,1)S(1)} %bitcast.203, f32[1024,128]{1,0:T(8,128)S(1)} %get-tuple-element.167.cos_ref, f32[1024,128]{1,0:T(8,128)S(1)} %get-tuple-element.168.sin_ref, ...), custom_call_target="tpu_custom_call" | custom-call | flops 32212254720 | bytes 5242880 | tf_op jit(solution)/shard_map/attend_backward/pallas_call | solution.py:196
  510.6 14.8 %collective-permute-done.46 = bf16[4,64,2048]{2,1,0:T(8,128)(2,1)S(1)} collective-permute-done((bf16[4,64,2048]{2,1,0:T(8,128)(2,1)S(1)}, bf16[4,64,2048]{2,1,0:T(8,128)(2,1)S(1)}, u32[]{:S(2)}, u32[]{:S(2)}) %collective-permute-start.46) | collective-permute-done | bytes 1048608 | tf_op jit(solution)/shard_map/ppermute | solution.py:234
  525.5 5.0 convolution_convert_fusion.3
  531.4 4.9 convolution_convert_fusion.6
  538.2 2.5 dynamic-slice_bitcast_fusion
  541.8 4.0 all-to-all-start.4
  545.9 2.6 fusion.9
  552.5 2.4 convert_element_type.312
  554.9 4.2 add_convert_fusion.1
  560.8 18.4 %collective-permute-done.47 = bf16[4,256,640]{2,1,0:T(8,128)(2,1)} collective-permute-done((bf16[4,256,640]{2,1,0:T(8,128)(2,1)}, bf16[4,256,640]{2,1,0:T(8,128)(2,1)}, u32[]{:S(2)}, u32[]{:S(2)}) %collective-permute-start.47) | collective-permute-done | bytes 1310752 | tf_op jit(solution)/shard_map/ppermute | solution.py:230
  579.1 7.6 %all-to-all-done.4 = bf16[8,64,1408]{2,1,0:T(8,128)(2,1)S(1)} async-done(((bf16[8,64,1408]{2,1,0:T(8,128)(2,1)}), bf16[8,64,1408]{2,1,0:T(8,128)(2,1)S(1)}, u32[]{:S(2)}, u32[]{:S(2)}) %all-to-all-start.4) | async-done | bytes 1441824 | tf_op jit(solution)/shard_map/all_to_all | solution.py:482
  586.7 3.1 fusion.1
  589.8 5.8 all-to-all-start.5
  601.4 2.5 convert_bitcast_fusion
  603.9 5.6 reshape.259
  611.6 3.4 fusion.5
  615.0 4.1 add_add_fusion
  619.1 2.6 broadcast_multiply_fusion
  621.7 4.5 all-to-all-done.5
  (344 shorter events, 140.3 us)
Async XLA Ops:
  7.2 100.6 %all-gather.9.cloned.1.call-start = ((), (), s32[]{:S(2)}) async-start(), calls=%async_computation.12 | async-start | bytes 1310720 | tf_op jit(solution)/shard_map/all_gather | solution.py:403
  11.0 9.8 %all-to-all-start = ((bf16[4,64,640]{2,1,0:T(8,128)(2,1)}), bf16[4,64,640]{2,1,0:T(8,128)(2,1)}, u32[]{:S(2)}, u32[]{:S(2)}) async-start(bf16[4,64,640]{2,1,0:T(8,128)(2,1)} %copy.112), calls=%async_computation | async-start | bytes 655360 | tf_op jit(solution)/shard_map/all_to_all | solution.py:389
  16.0 201.8 %all-gather.7.cloned.1.call-start = ((), (), s32[]{:S(2)}) async-start(), calls=%async_computation.9 | async-start | bytes 3604480 | tf_op jit(solution)/shard_map/all_gather | solution.py:406
  20.9 25.3 %collective-permute-start = (bf16[256,2048]{1,0:T(8,128)(2,1)S(1)}, bf16[256,2048]{1,0:T(8,128)(2,1)}, u32[]{:S(2)}, u32[]{:S(2)}) collective-permute-start(bf16[256,2048]{1,0:T(8,128)(2,1)S(1)} %copy-done.14), channel_id=1, source_target_pairs={{0,2},{2,0},{1,3},{3,1},{4,6},{6,4},{5,7},{7,5},{8,10},{10,8},{9,1... | collective-permute-start | bytes 3145736 | tf_op jit(solution)/shard_map/ppermute | solution.py:230
  24.3 21.5 %collective-permute-start.3 = (bf16[256,640]{1,0:T(8,128)(2,1)}, bf16[256,640]{1,0:T(8,128)(2,1)S(1)}, u32[]{:S(2)}, u32[]{:S(2)}) collective-permute-start(bf16[256,640]{1,0:T(8,128)(2,1)} %bitcast.1), channel_id=1, source_target_pairs={{8,0},{16,8},{24,16},{0,24},{9,1},{17,9},{25,17},{1,25},{10,2},{18... | collective-permute-start | bytes 983048 | tf_op jit(solution)/shard_map/ppermute | solution.py:264
  25.3 47.3 %collective-permute-start.2 = (bf16[256,640]{1,0:T(8,128)(2,1)}, bf16[256,640]{1,0:T(8,128)(2,1)}, u32[]{:S(2)}, u32[]{:S(2)}) collective-permute-start(bf16[256,640]{1,0:T(8,128)(2,1)} %bitcast.1), channel_id=1, source_target_pairs={{0,4},{4,0},{1,5},{5,1},{2,6},{6,2},{3,7},{7,3},{8,12},{12,8},{9,1... | collective-permute-start | bytes 983048 | tf_op jit(solution)/shard_map/ppermute | solution.py:230
  26.8 47.0 %collective-permute-start.5 = (bf16[256,640]{1,0:T(8,128)(2,1)}, bf16[256,640]{1,0:T(8,128)(2,1)}, u32[]{:S(2)}, u32[]{:S(2)}) collective-permute-start(bf16[256,640]{1,0:T(8,128)(2,1)} %bitcast.1), channel_id=1, source_target_pairs={{16,0},{24,8},{0,16},{8,24},{17,1},{25,9},{1,17},{9,25},{18,2},{26... | collective-permute-start | bytes 983048 | tf_op jit(solution)/shard_map/ppermute | solution.py:264
  29.1 45.0 %collective-permute-start.7 = (bf16[256,640]{1,0:T(8,128)(2,1)}, bf16[256,640]{1,0:T(8,128)(2,1)}, u32[]{:S(2)}, u32[]{:S(2)}) collective-permute-start(bf16[256,640]{1,0:T(8,128)(2,1)} %bitcast.1), channel_id=1, source_target_pairs={{24,0},{0,8},{8,16},{16,24},{25,1},{1,9},{9,17},{17,25},{26,2},{2,... | collective-permute-start | bytes 983048 | tf_op jit(solution)/shard_map/ppermute | solution.py:264
  45.8 62.0 %collective-permute-start.9 = (bf16[256,2048]{1,0:T(8,128)(2,1)}, bf16[256,2048]{1,0:T(8,128)(2,1)}, u32[]{:S(2)}, u32[]{:S(2)}) collective-permute-start(bf16[256,2048]{1,0:T(8,128)(2,1)} %param.17), channel_id=1, source_target_pairs={{0,2},{2,0},{1,3},{3,1},{4,6},{6,4},{5,7},{7,5},{8,10},{10,8},{9,1... | collective-permute-start | bytes 3145736 | tf_op jit(solution)/shard_map/ppermute | solution.py:230
  50.1 59.2 %collective-permute-start.1 = (bf16[2,256,2048]{2,1,0:T(8,128)(2,1)}, bf16[2,256,2048]{2,1,0:T(8,128)(2,1)}, u32[]{:S(2)}, u32[]{:S(2)}) collective-permute-start(bf16[2,256,2048]{2,1,0:T(8,128)(2,1)} %pad_maximum_fusion.1), channel_id=1, source_target_pairs={{0,1},{1,0},{2,3},{3,2},{4,5},{5,4},{6,7},{7,6},{8,9},{9,8},{10,11... | collective-permute-start | bytes 6291464 | tf_op jit(solution)/shard_map/ppermute | solution.py:230
  72.6 9.6 %collective-permute-start.4 = (bf16[256,640]{1,0:T(8,128)(2,1)}, bf16[256,640]{1,0:T(8,128)(2,1)S(1)}, u32[]{:S(2)}, u32[]{:S(2)}) collective-permute-start(bf16[256,640]{1,0:T(8,128)(2,1)} %copy-done.52), channel_id=1, source_target_pairs={{0,4},{4,0},{1,5},{5,1},{2,6},{6,2},{3,7},{7,3},{8,12},{12,8},{9,1... | collective-permute-start | bytes 983048 | tf_op jit(solution)/shard_map/ppermute | solution.py:230
  73.7 15.5 %collective-permute-start.6 = (bf16[256,640]{1,0:T(8,128)(2,1)}, bf16[256,640]{1,0:T(8,128)(2,1)S(1)}, u32[]{:S(2)}, u32[]{:S(2)}) collective-permute-start(bf16[256,640]{1,0:T(8,128)(2,1)} %collective-permute-done.5), channel_id=1, source_target_pairs={{0,4},{4,0},{1,5},{5,1},{2,6},{6,2},{3,7},{7,3},{8,12},{12,8},{9,1... | collective-permute-start | bytes 983048 | tf_op jit(solution)/shard_map/ppermute | solution.py:230
  74.1 22.1 %collective-permute-start.8 = (bf16[256,640]{1,0:T(8,128)(2,1)}, bf16[256,640]{1,0:T(8,128)(2,1)S(1)}, u32[]{:S(2)}, u32[]{:S(2)}) collective-permute-start(bf16[256,640]{1,0:T(8,128)(2,1)} %collective-permute-done.7), channel_id=1, source_target_pairs={{0,4},{4,0},{1,5},{5,1},{2,6},{6,2},{3,7},{7,3},{8,12},{12,8},{9,1... | collective-permute-start | bytes 983048 | tf_op jit(solution)/shard_map/ppermute | solution.py:230
  96.2 38.6 %all-to-all-start.1 = ((bf16[8,64,1408]{2,1,0:T(8,128)(2,1)}), bf16[8,64,1408]{2,1,0:T(8,128)(2,1)}, u32[]{:S(2)}, u32[]{:S(2)}) async-start(bf16[8,64,1408]{2,1,0:T(8,128)(2,1)} %concatenate.38), calls=%async_computation.1 | async-start | bytes 2883584 | tf_op jit(solution)/shard_map/all_to_all | solution.py:408
  107.8 35.6 %collective-permute-start.13 = (bf16[4,64,2048]{2,1,0:T(8,128)(2,1)}, bf16[4,64,2048]{2,1,0:T(8,128)(2,1)}, u32[]{:S(2)}, u32[]{:S(2)}) collective-permute-start(bf16[4,64,2048]{2,1,0:T(8,128)(2,1)} %bitcast.227), channel_id=1, source_target_pairs={{0,4},{4,0},{1,5},{5,1},{2,6},{6,2},{3,7},{7,3},{8,12},{12,8},{9,1... | collective-permute-start | bytes 3145736 | tf_op jit(solution)/shard_map/ppermute | solution.py:230
  109.0 36.3 %collective-permute-start.11 = (bf16[4,64,2048]{2,1,0:T(8,128)(2,1)}, bf16[4,64,2048]{2,1,0:T(8,128)(2,1)}, u32[]{:S(2)}, u32[]{:S(2)}) collective-permute-start(bf16[4,64,2048]{2,1,0:T(8,128)(2,1)} %bitcast.228), channel_id=1, source_target_pairs={{0,2},{2,0},{1,3},{3,1},{4,6},{6,4},{5,7},{7,5},{8,10},{10,8},{9,1... | collective-permute-start | bytes 3145736 | tf_op jit(solution)/shard_map/ppermute | solution.py:230
  136.2 31.9 %all-to-all-start.2 = ((bf16[4,256,512]{1,2,0:T(8,128)(2,1)}), bf16[4,256,512]{1,2,0:T(8,128)(2,1)S(1)}, u32[]{:S(2)}, u32[]{:S(2)}) async-start(bf16[4,256,512]{1,2,0:T(8,128)(2,1)} %copy.117), calls=%async_computation.2 | async-start | bytes 2097152 | tf_op jit(solution)/shard_map/all_to_all | solution.py:420
  141.8 117.5 %all-gather.5.cloned.1.call-start = ((), (), s32[]{:S(2)}) async-start(), calls=%async_computation.8 | async-start | bytes 7208960 | tf_op jit(solution)/shard_map/all_gather | solution.py:409
  145.3 20.4 %collective-permute-start.14 = (bf16[4,32,2048]{2,1,0:T(8,128)(2,1)}, bf16[4,32,2048]{2,1,0:T(8,128)(2,1)}, u32[]{:S(2)}, u32[]{:S(2)}) collective-permute-start(bf16[4,32,2048]{2,1,0:T(8,128)(2,1)} %slice.151), channel_id=1, source_target_pairs={{0,2},{2,0},{1,3},{3,1},{4,6},{6,4},{5,7},{7,5},{8,10},{10,8},{9,1... | collective-permute-start | bytes 1572872 | tf_op jit(solution)/shard_map/ppermute | solution.py:230
  147.2 18.6 %collective-permute-start.12 = (bf16[4,32,2048]{2,1,0:T(8,128)(2,1)}, bf16[4,32,2048]{2,1,0:T(8,128)(2,1)}, u32[]{:S(2)}, u32[]{:S(2)}) collective-permute-start(bf16[4,32,2048]{2,1,0:T(8,128)(2,1)} %slice.150), channel_id=1, source_target_pairs={{0,4},{4,0},{1,5},{5,1},{2,6},{6,2},{3,7},{7,3},{8,12},{12,8},{9,1... | collective-permute-start | bytes 1572872 | tf_op jit(solution)/shard_map/ppermute | solution.py:230
  147.3 35.1 %collective-permute-start.10 = (bf16[256,2048]{1,0:T(8,128)(2,1)S(1)}, bf16[256,2048]{1,0:T(8,128)(2,1)}, u32[]{:S(2)}, u32[]{:S(2)}) collective-permute-start(bf16[256,2048]{1,0:T(8,128)(2,1)S(1)} %copy-done.30), channel_id=1, source_target_pairs={{0,4},{4,0},{1,5},{5,1},{2,6},{6,2},{3,7},{7,3},{8,12},{12,8},{9,1... | collective-permute-start | bytes 3145736 | tf_op jit(solution)/shard_map/ppermute | solution.py:230
  148.6 34.2 %collective-permute-start.18 = (bf16[4,64,2048]{2,1,0:T(8,128)(2,1)}, bf16[4,64,2048]{2,1,0:T(8,128)(2,1)}, u32[]{:S(2)}, u32[]{:S(2)}) collective-permute-start(bf16[4,64,2048]{2,1,0:T(8,128)(2,1)} %bitcast.229), channel_id=1, source_target_pairs={{0,1},{1,0},{2,3},{3,2},{4,5},{5,4},{6,7},{7,6},{8,9},{9,8},{10,11... | collective-permute-start | bytes 3145736 | tf_op jit(solution)/shard_map/ppermute | solution.py:230
  150.2 391.6 %reduce-scatter.3.cloned.1.call-start = ((), (), s32[]{:S(2)}) async-start(), calls=%async_computation.10 | async-start | bytes 7208960 | tf_op jit(solution)/shard_map/reduce_scatter | solution.py:443
  168.0 14.4 %collective-permute-start.15 = (bf16[4,64,2048]{2,1,0:T(8,128)(2,1)}, bf16[4,64,2048]{2,1,0:T(8,128)(2,1)S(1)}, u32[]{:S(2)}, u32[]{:S(2)}) collective-permute-start(bf16[4,64,2048]{2,1,0:T(8,128)(2,1)} %pad_maximum_fusion.2), channel_id=1, source_target_pairs={{0,1},{1,0},{2,3},{3,2},{4,5},{5,4},{6,7},{7,6},{8,9},{9,8},{10,11... | collective-permute-start | bytes 3145736 | tf_op jit(solution)/shard_map/ppermute | solution.py:230
  168.6 13.9 %collective-permute-start.16 = (bf16[4,64,2048]{2,1,0:T(8,128)(2,1)}, bf16[4,64,2048]{2,1,0:T(8,128)(2,1)S(1)}, u32[]{:S(2)}, u32[]{:S(2)}) collective-permute-start(bf16[4,64,2048]{2,1,0:T(8,128)(2,1)} %collective-permute-done.11), channel_id=1, source_target_pairs={{0,1},{1,0},{2,3},{3,2},{4,5},{5,4},{6,7},{7,6},{8,9},{9,8},{10,11... | collective-permute-start | bytes 3145736 | tf_op jit(solution)/shard_map/ppermute | solution.py:230
  168.7 14.0 %collective-permute-start.17 = (bf16[4,64,2048]{2,1,0:T(8,128)(2,1)}, bf16[4,64,2048]{2,1,0:T(8,128)(2,1)S(1)}, u32[]{:S(2)}, u32[]{:S(2)}) collective-permute-start(bf16[4,64,2048]{2,1,0:T(8,128)(2,1)} %collective-permute-done.13), channel_id=1, source_target_pairs={{0,1},{1,0},{2,3},{3,2},{4,5},{5,4},{6,7},{7,6},{8,9},{9,8},{10,11... | collective-permute-start | bytes 3145736 | tf_op jit(solution)/shard_map/ppermute | solution.py:230
  187.8 23.5 %collective-permute-start.19 = (bf16[256,2048]{1,0:T(8,128)(2,1)S(1)}, bf16[256,2048]{1,0:T(8,128)(2,1)S(1)}, u32[]{:S(2)}, u32[]{:S(2)}) collective-permute-start(bf16[256,2048]{1,0:T(8,128)(2,1)S(1)} %multiply_convert_fusion.2), channel_id=1, source_target_pairs={{0,2},{2,0},{1,3},{3,1},{4,6},{6,4},{5,7},{7,5},{8,10},{10,8},{9,1... | collective-permute-start | bytes 3145736 | tf_op jit(solution)/shard_map/ppermute | solution.py:230
  189.7 22.9 %collective-permute-start.21 = (bf16[256,2048]{1,0:T(8,128)(2,1)S(1)}, bf16[256,2048]{1,0:T(8,128)(2,1)S(1)}, u32[]{:S(2)}, u32[]{:S(2)}) collective-permute-start(bf16[256,2048]{1,0:T(8,128)(2,1)S(1)} %multiply_convert_fusion.2), channel_id=1, source_target_pairs={{0,4},{4,0},{1,5},{5,1},{2,6},{6,2},{3,7},{7,3},{8,12},{12,8},{9,1... | collective-permute-start | bytes 3145736 | tf_op jit(solution)/shard_map/ppermute | solution.py:230
  212.2 13.2 %collective-permute-start.20 = (bf16[128,2048]{1,0:T(8,128)(2,1)}, bf16[128,2048]{1,0:T(8,128)(2,1)}, u32[]{:S(2)}, u32[]{:S(2)}) collective-permute-start(bf16[128,2048]{1,0:T(8,128)(2,1)} %slice.152), channel_id=1, source_target_pairs={{0,4},{4,0},{1,5},{5,1},{2,6},{6,2},{3,7},{7,3},{8,12},{12,8},{9,1... | collective-permute-start | bytes 1572872 | tf_op jit(solution)/shard_map/ppermute | solution.py:230
  213.5 16.4 %collective-permute-start.22 = (bf16[128,2048]{1,0:T(8,128)(2,1)}, bf16[128,2048]{1,0:T(8,128)(2,1)}, u32[]{:S(2)}, u32[]{:S(2)}) collective-permute-start(bf16[128,2048]{1,0:T(8,128)(2,1)} %slice.153), channel_id=1, source_target_pairs={{0,2},{2,0},{1,3},{3,1},{4,6},{6,4},{5,7},{7,5},{8,10},{10,8},{9,1... | collective-permute-start | bytes 1572872 | tf_op jit(solution)/shard_map/ppermute | solution.py:230
  214.7 32.8 %collective-permute-start.30 = (bf16[256,2048]{1,0:T(8,128)(2,1)S(1)}, bf16[256,2048]{1,0:T(8,128)(2,1)}, u32[]{:S(2)}, u32[]{:S(2)}) collective-permute-start(bf16[256,2048]{1,0:T(8,128)(2,1)S(1)} %copy-done.30), channel_id=1, source_target_pairs={{0,1},{1,0},{2,3},{3,2},{4,5},{5,4},{6,7},{7,6},{8,9},{9,8},{10,11... | collective-permute-start | bytes 3145736 | tf_op jit(solution)/shard_map/ppermute | solution.py:230
  218.9 15.9 %collective-permute-start.27 = (bf16[128,2048]{1,0:T(8,128)(2,1)S(1)}, bf16[128,2048]{1,0:T(8,128)(2,1)S(1)}, u32[]{:S(2)}, u32[]{:S(2)}) collective-permute-start(bf16[128,2048]{1,0:T(8,128)(2,1)S(1)} %slice.121), channel_id=1, source_target_pairs={{0,4},{4,0},{1,5},{5,1},{2,6},{6,2},{3,7},{7,3},{8,12},{12,8},{9,1... | collective-permute-start | bytes 1572872 | tf_op jit(solution)/shard_map/ppermute | solution.py:230
  221.4 16.6 %collective-permute-start.28 = (bf16[128,2048]{1,0:T(8,128)(2,1)S(1)}, bf16[128,2048]{1,0:T(8,128)(2,1)S(1)}, u32[]{:S(2)}, u32[]{:S(2)}) collective-permute-start(bf16[128,2048]{1,0:T(8,128)(2,1)S(1)} %slice.122), channel_id=1, source_target_pairs={{0,2},{2,0},{1,3},{3,1},{4,6},{6,4},{5,7},{7,5},{8,10},{10,8},{9,1... | collective-permute-start | bytes 1572872 | tf_op jit(solution)/shard_map/ppermute | solution.py:230
  225.5 29.2 %collective-permute-start.31 = (bf16[256,2048]{1,0:T(8,128)(2,1)}, bf16[256,2048]{1,0:T(8,128)(2,1)S(1)}, u32[]{:S(2)}, u32[]{:S(2)}) collective-permute-start(bf16[256,2048]{1,0:T(8,128)(2,1)} %collective-permute-done.9), channel_id=1, source_target_pairs={{0,1},{1,0},{2,3},{3,2},{4,5},{5,4},{6,7},{7,6},{8,9},{9,8},{10,11... | collective-permute-start | bytes 3145736 | tf_op jit(solution)/shard_map/ppermute | solution.py:230
  229.9 14.9 %collective-permute-start.24 = (bf16[256,2048]{1,0:T(8,128)(2,1)S(1)}, bf16[256,2048]{1,0:T(8,128)(2,1)S(1)}, u32[]{:S(2)}, u32[]{:S(2)}) collective-permute-start(bf16[256,2048]{1,0:T(8,128)(2,1)S(1)} %copy-done.46), channel_id=1, source_target_pairs={{0,1},{1,0},{2,3},{3,2},{4,5},{5,4},{6,7},{7,6},{8,9},{9,8},{10,11... | collective-permute-start | bytes 3145736 | tf_op jit(solution)/shard_map/ppermute | solution.py:230
  234.8 9.7 %collective-permute-start.23 = (bf16[256,2048]{1,0:T(8,128)(2,1)S(1)}, bf16[256,2048]{1,0:T(8,128)(2,1)S(1)}, u32[]{:S(2)}, u32[]{:S(2)}) collective-permute-start(bf16[256,2048]{1,0:T(8,128)(2,1)S(1)} %pad_maximum_fusion.3), channel_id=1, source_target_pairs={{0,1},{1,0},{2,3},{3,2},{4,5},{5,4},{6,7},{7,6},{8,9},{9,8},{10,11... | collective-permute-start | bytes 3145736 | tf_op jit(solution)/shard_map/ppermute | solution.py:230
  238.1 8.0 %collective-permute-start.29 = (bf16[256,2048]{1,0:T(8,128)(2,1)S(1)}, bf16[256,2048]{1,0:T(8,128)(2,1)S(1)}, u32[]{:S(2)}, u32[]{:S(2)}) collective-permute-start(bf16[256,2048]{1,0:T(8,128)(2,1)S(1)} %pad_maximum_fusion.4), channel_id=1, source_target_pairs={{0,1},{1,0},{2,3},{3,2},{4,5},{5,4},{6,7},{7,6},{8,9},{9,8},{10,11... | collective-permute-start | bytes 3145736 | tf_op jit(solution)/shard_map/ppermute | solution.py:230
  244.5 11.4 %collective-permute-start.32 = (bf16[256,2048]{1,0:T(8,128)(2,1)}, bf16[256,2048]{1,0:T(8,128)(2,1)S(1)}, u32[]{:S(2)}, u32[]{:S(2)}) collective-permute-start(bf16[256,2048]{1,0:T(8,128)(2,1)} %collective-permute-done.10), channel_id=1, source_target_pairs={{0,1},{1,0},{2,3},{3,2},{4,5},{5,4},{6,7},{7,6},{8,9},{9,8},{10,11... | collective-permute-start | bytes 3145736 | tf_op jit(solution)/shard_map/ppermute | solution.py:230
  245.0 9.5 %collective-permute-start.25 = (bf16[256,2048]{1,0:T(8,128)(2,1)S(1)}, bf16[256,2048]{1,0:T(8,128)(2,1)S(1)}, u32[]{:S(2)}, u32[]{:S(2)}) collective-permute-start(bf16[256,2048]{1,0:T(8,128)(2,1)S(1)} %copy-done.40), channel_id=1, source_target_pairs={{0,1},{1,0},{2,3},{3,2},{4,5},{5,4},{6,7},{7,6},{8,9},{9,8},{10,11... | collective-permute-start | bytes 3145736 | tf_op jit(solution)/shard_map/ppermute | solution.py:230
  246.1 8.5 %collective-permute-start.26 = (bf16[256,2048]{1,0:T(8,128)(2,1)S(1)}, bf16[256,2048]{1,0:T(8,128)(2,1)S(1)}, u32[]{:S(2)}, u32[]{:S(2)}) collective-permute-start(bf16[256,2048]{1,0:T(8,128)(2,1)S(1)} %copy-done.38), channel_id=1, source_target_pairs={{0,1},{1,0},{2,3},{3,2},{4,5},{5,4},{6,7},{7,6},{8,9},{9,8},{10,11... | collective-permute-start | bytes 3145736 | tf_op jit(solution)/shard_map/ppermute | solution.py:230
  312.8 7.0 %collective-permute-start.33 = (bf16[512,2048]{1,0:T(8,128)(2,1)}, bf16[512,2048]{1,0:T(8,128)(2,1)}, u32[]{:S(2)}, u32[]{:S(2)}) collective-permute-start(bf16[512,2048]{1,0:T(8,128)(2,1)} %convolution_convert_fusion.8), channel_id=1, source_target_pairs={{0,1},{1,0},{2,3},{3,2},{4,5},{5,4},{6,7},{7,6},{8,9},{9,8},{10,11... | collective-permute-start | bytes 6291464 | tf_op jit(solution)/shard_map/ppermute | solution.py:230
  319.4 8.9 %collective-permute-start.34 = (bf16[512,2048]{1,0:T(8,128)(2,1)}, bf16[512,2048]{1,0:T(8,128)(2,1)}, u32[]{:S(2)}, u32[]{:S(2)}) collective-permute-start(bf16[512,2048]{1,0:T(8,128)(2,1)} %convolution_convert_fusion.7), channel_id=1, source_target_pairs={{0,1},{1,0},{2,3},{3,2},{4,5},{5,4},{6,7},{7,6},{8,9},{9,8},{10,11... | collective-permute-start | bytes 6291464 | tf_op jit(solution)/shard_map/ppermute | solution.py:230
  338.7 9.8 %collective-permute-start.35 = (bf16[512,2048]{1,0:T(8,128)(2,1)}, bf16[512,2048]{1,0:T(8,128)(2,1)}, u32[]{:S(2)}, u32[]{:S(2)}) collective-permute-start(bf16[512,2048]{1,0:T(8,128)(2,1)} %convolution_convert_fusion.5), channel_id=1, source_target_pairs={{0,1},{1,0},{2,3},{3,2},{4,5},{5,4},{6,7},{7,6},{8,9},{9,8},{10,11... | collective-permute-start | bytes 6291464 | tf_op jit(solution)/shard_map/ppermute | solution.py:230
  342.1 26.8 %collective-permute-start.37 = (bf16[512,2048]{1,0:T(8,128)(2,1)}, bf16[512,2048]{1,0:T(8,128)(2,1)}, u32[]{:S(2)}, u32[]{:S(2)}) collective-permute-start(bf16[512,2048]{1,0:T(8,128)(2,1)} %convolution_convert_fusion.4), channel_id=1, source_target_pairs={{0,1},{1,0},{2,3},{3,2},{4,5},{5,4},{6,7},{7,6},{8,9},{9,8},{10,11... | collective-permute-start | bytes 6291464 | tf_op jit(solution)/shard_map/ppermute | solution.py:230
  343.9 24.9 %collective-permute-start.36 = (bf16[256,2048]{1,0:T(8,128)(2,1)}, bf16[256,2048]{1,0:T(8,128)(2,1)}, u32[]{:S(2)}, u32[]{:S(2)}) collective-permute-start(bf16[256,2048]{1,0:T(8,128)(2,1)} %get-tuple-element.132), channel_id=1, source_target_pairs={{0,2},{2,0},{1,3},{3,1},{4,6},{6,4},{5,7},{7,5},{8,10},{10,8},{9,1... | collective-permute-start | bytes 3145736 | tf_op jit(solution)/shard_map/ppermute | solution.py:230
  347.1 46.8 %collective-permute-start.40 = (bf16[256,2048]{1,0:T(8,128)(2,1)S(1)}, bf16[256,2048]{1,0:T(8,128)(2,1)S(1)}, u32[]{:S(2)}, u32[]{:S(2)}) collective-permute-start(bf16[256,2048]{1,0:T(8,128)(2,1)S(1)} %copy-done.50), channel_id=1, source_target_pairs={{0,4},{4,0},{1,5},{5,1},{2,6},{6,2},{3,7},{7,3},{8,12},{12,8},{9,1... | collective-permute-start | bytes 3145736 | tf_op jit(solution)/shard_map/ppermute | solution.py:230
  348.5 45.4 %collective-permute-start.39 = (bf16[256,2048]{1,0:T(8,128)(2,1)S(1)}, bf16[256,2048]{1,0:T(8,128)(2,1)S(1)}, u32[]{:S(2)}, u32[]{:S(2)}) collective-permute-start(bf16[256,2048]{1,0:T(8,128)(2,1)S(1)} %slice.157), channel_id=1, source_target_pairs={{0,6},{2,4},{4,2},{6,0},{1,7},{3,5},{5,3},{7,1},{8,14},{10,12},{12... | collective-permute-start | bytes 3145736 | tf_op jit(solution)/shard_map/ppermute | solution.py:234
  406.6 67.0 %collective-permute-start.41 = (bf16[1024,2048]{1,0:T(8,128)(2,1)}, bf16[1024,2048]{1,0:T(8,128)(2,1)}, u32[]{:S(2)}, u32[]{:S(2)}) collective-permute-start(bf16[1024,2048]{1,0:T(8,128)(2,1)} %convolution_convert_fusion.1), channel_id=1, source_target_pairs={{0,1},{1,0},{2,3},{3,2},{4,5},{5,4},{6,7},{7,6},{8,9},{9,8},{10,11... | collective-permute-start | bytes 12582920 | tf_op jit(solution)/shard_map/ppermute | solution.py:230
  413.6 37.5 %collective-permute-start.43 = (bf16[256,2048]{1,0:T(8,128)(2,1)}, bf16[256,2048]{1,0:T(8,128)(2,1)}, u32[]{:S(2)}, u32[]{:S(2)}) collective-permute-start(bf16[256,2048]{1,0:T(8,128)(2,1)} %slice.139), channel_id=1, source_target_pairs={{0,6},{2,4},{4,2},{6,0},{1,7},{3,5},{5,3},{7,1},{8,14},{10,12},{12... | collective-permute-start | bytes 3145736 | tf_op jit(solution)/shard_map/ppermute | solution.py:234
  415.8 35.3 %all-to-all-start.3 = ((bf16[256,4,512]{2,0,1:T(8,128)(2,1)}), bf16[256,4,512]{2,0,1:T(8,128)(2,1)S(1)}, u32[]{:S(2)}, u32[]{:S(2)}) async-start(bf16[256,4,512]{2,0,1:T(8,128)(2,1)} %bitcast.201), calls=%async_computation.3 | async-start | bytes 2097152 | tf_op jit(solution)/shard_map/all_to_all | solution.py:472
  421.0 131.5 %reduce-scatter.5.cloned.1.call-start = ((), (), s32[]{:S(2)}) async-start(), calls=%async_computation.11 | async-start | bytes 3604480 | tf_op jit(solution)/shard_map/reduce_scatter | solution.py:460
  424.3 49.3 %collective-permute-start.38 = (bf16[256,2048]{1,0:T(8,128)(2,1)}, bf16[256,2048]{1,0:T(8,128)(2,1)}, u32[]{:S(2)}, u32[]{:S(2)}) collective-permute-start(bf16[256,2048]{1,0:T(8,128)(2,1)} %get-tuple-element.130), channel_id=1, source_target_pairs={{0,2},{2,0},{1,3},{3,1},{4,6},{6,4},{5,7},{7,5},{8,10},{10,8},{9,1... | collective-permute-start | bytes 3145736 | tf_op jit(solution)/shard_map/ppermute | solution.py:230
  424.4 49.2 %collective-permute-start.42 = (bf16[256,2048]{1,0:T(8,128)(2,1)}, bf16[256,2048]{1,0:T(8,128)(2,1)}, u32[]{:S(2)}, u32[]{:S(2)}) collective-permute-start(bf16[256,2048]{1,0:T(8,128)(2,1)} %get-tuple-element.129), channel_id=1, source_target_pairs={{0,4},{4,0},{1,5},{5,1},{2,6},{6,2},{3,7},{7,3},{8,12},{12,8},{9,1... | collective-permute-start | bytes 3145736 | tf_op jit(solution)/shard_map/ppermute | solution.py:230
  479.3 31.3 %collective-permute-start.44 = (bf16[4,64,2048]{2,1,0:T(8,128)(2,1)S(1)}, bf16[4,64,2048]{2,1,0:T(8,128)(2,1)S(1)}, u32[]{:S(2)}, u32[]{:S(2)}) collective-permute-start(bf16[4,64,2048]{2,1,0:T(8,128)(2,1)S(1)} %get-tuple-element.124), channel_id=1, source_target_pairs={{0,2},{2,0},{1,3},{3,1},{4,6},{6,4},{5,7},{7,5},{8,10},{10,8},{9,1... | collective-permute-start | bytes 3145736 | tf_op jit(solution)/shard_map/ppermute | solution.py:230
  479.3 31.3 %collective-permute-start.45 = (bf16[4,64,2048]{2,1,0:T(8,128)(2,1)S(1)}, bf16[4,64,2048]{2,1,0:T(8,128)(2,1)S(1)}, u32[]{:S(2)}, u32[]{:S(2)}) collective-permute-start(bf16[4,64,2048]{2,1,0:T(8,128)(2,1)S(1)} %get-tuple-element.123), channel_id=1, source_target_pairs={{0,4},{4,0},{1,5},{5,1},{2,6},{6,2},{3,7},{7,3},{8,12},{12,8},{9,1... | collective-permute-start | bytes 3145736 | tf_op jit(solution)/shard_map/ppermute | solution.py:230
  479.6 45.9 %collective-permute-start.46 = (bf16[4,64,2048]{2,1,0:T(8,128)(2,1)S(1)}, bf16[4,64,2048]{2,1,0:T(8,128)(2,1)S(1)}, u32[]{:S(2)}, u32[]{:S(2)}) collective-permute-start(bf16[4,64,2048]{2,1,0:T(8,128)(2,1)S(1)} %get-tuple-element.122), channel_id=1, source_target_pairs={{0,6},{2,4},{4,2},{6,0},{1,7},{3,5},{5,3},{7,1},{8,14},{10,12},{12... | collective-permute-start | bytes 3145736 | tf_op jit(solution)/shard_map/ppermute | solution.py:234
  536.3 18.6 %collective-permute-start.48 = (bf16[512,2048]{1,0:T(8,128)(2,1)}, bf16[512,2048]{1,0:T(8,128)(2,1)}, u32[]{:S(2)}, u32[]{:S(2)}) collective-permute-start(bf16[512,2048]{1,0:T(8,128)(2,1)} %convolution_convert_fusion.6), channel_id=1, source_target_pairs={{0,1},{1,0},{2,3},{3,2},{4,5},{5,4},{6,7},{7,6},{8,9},{9,8},{10,11... | collective-permute-start | bytes 6291464 | tf_op jit(solution)/shard_map/ppermute | solution.py:230
  540.7 38.4 %collective-permute-start.47 = (bf16[4,256,640]{2,1,0:T(8,128)(2,1)}, bf16[4,256,640]{2,1,0:T(8,128)(2,1)}, u32[]{:S(2)}, u32[]{:S(2)}) collective-permute-start(bf16[4,256,640]{2,1,0:T(8,128)(2,1)} %dynamic-slice_bitcast_fusion), channel_id=1, source_target_pairs={{0,4},{4,0},{1,5},{5,1},{2,6},{6,2},{3,7},{7,3},{8,12},{12,8},{9,1... | collective-permute-start | bytes 3932168 | tf_op jit(solution)/shard_map/ppermute | solution.py:230
  541.8 44.9 %all-to-all-start.4 = ((bf16[8,64,1408]{2,1,0:T(8,128)(2,1)}), bf16[8,64,1408]{2,1,0:T(8,128)(2,1)S(1)}, u32[]{:S(2)}, u32[]{:S(2)}) async-start(bf16[8,64,1408]{2,1,0:T(8,128)(2,1)} %bitcast.225), calls=%async_computation.5 | async-start | bytes 2883584 | tf_op jit(solution)/shard_map/all_to_all | solution.py:482
  549.3 78.5 %collective-permute-start.52 = (bf16[64,2048]{1,0:T(8,128)(2,1)}, bf16[64,2048]{1,0:T(8,128)(2,1)}, u32[]{:S(2)}, u32[]{:S(2)}) collective-permute-start(bf16[64,2048]{1,0:T(8,128)(2,1)} %get-tuple-element.144), channel_id=1, source_target_pairs={{0,24},{8,0},{16,8},{24,16},{1,25},{9,1},{17,9},{25,17},{2,26},{10... | collective-permute-start | bytes 786440 | tf_op jit(solution)/shard_map/ppermute | solution.py:503
  549.3 78.5 %collective-permute-start.51 = (bf16[64,2048]{1,0:T(8,128)(2,1)}, bf16[64,2048]{1,0:T(8,128)(2,1)}, u32[]{:S(2)}, u32[]{:S(2)}) collective-permute-start(bf16[64,2048]{1,0:T(8,128)(2,1)} %get-tuple-element.145), channel_id=1, source_target_pairs={{0,16},{8,24},{16,0},{24,8},{1,17},{9,25},{17,1},{25,9},{2,18},{10... | collective-permute-start | bytes 786440 | tf_op jit(solution)/shard_map/ppermute | solution.py:503
  550.4 79.1 %collective-permute-start.50 = (bf16[64,2048]{1,0:T(8,128)(2,1)}, bf16[64,2048]{1,0:T(8,128)(2,1)}, u32[]{:S(2)}, u32[]{:S(2)}) collective-permute-start(bf16[64,2048]{1,0:T(8,128)(2,1)} %get-tuple-element.143), channel_id=1, source_target_pairs={{0,8},{8,16},{16,24},{24,0},{1,9},{9,17},{17,25},{25,1},{2,10},{10... | collective-permute-start | bytes 786440 | tf_op jit(solution)/shard_map/ppermute | solution.py:503
  560.3 43.7 %collective-permute-start.49 = (bf16[256,2048]{1,0:T(8,128)(2,1)}, bf16[256,2048]{1,0:T(8,128)(2,1)}, u32[]{:S(2)}, u32[]{:S(2)}) collective-permute-start(bf16[256,2048]{1,0:T(8,128)(2,1)} %dynamic-slice_bitcast_fusion.1), channel_id=1, source_target_pairs={{0,2},{2,0},{1,3},{3,1},{4,6},{6,4},{5,7},{7,5},{8,10},{10,8},{9,1... | collective-permute-start | bytes 3145736 | tf_op jit(solution)/shard_map/ppermute | solution.py:230
  589.8 36.3 %all-to-all-start.5 = ((bf16[16,64,640]{2,1,0:T(8,128)(2,1)}), bf16[16,64,640]{2,1,0:T(8,128)(2,1)}, u32[]{:S(2)}, u32[]{:S(2)}) async-start(bf16[16,64,640]{2,1,0:T(8,128)(2,1)} %bitcast.214), calls=%async_computation.6 | async-start | bytes 2621440 | tf_op jit(solution)/shard_map/all_to_all | solution.py:485
  (66 other events, 643.9 us)
Sparse Core Ops, SparseCore 0:
  9.6 44.0 all-gather.8
  55.2 59.2 all-gather.6
  150.3 102.1 all-gather.4
  319.9 101.6 reduce-scatter.2
  434.3 55.7 reduce-scatter.4

commit v5 on v4

--- a/solution.py
+++ b/solution.py
@@ -289,6 +289,27 @@
     return (right(left[:half]) + theirs.astype(f32)).astype(bf)
 
 
+def sum_first(own, over_x, over_y, over_both):
+    half = own.shape[0] // 2
+    by_x = swap(jnp.concatenate([over_x[:half], over_both[:half]], axis=0), "x")
+    by_y = swap(jnp.concatenate([over_y[half:], over_both[half:]], axis=0), "y")
+    return by_x, by_y
+
+
+def sum_second(own, over_x, over_y, by_x, by_y):
+    half = own.shape[0] // 2
+    last_y = swap((over_y[:half].astype(f32) + by_x[half:].astype(f32)).astype(bf), "y")
+    last_x = swap((over_x[half:].astype(f32) + by_y[half:].astype(f32)).astype(bf), "x")
+    return last_x, last_y
+
+
+def sum_last(own, by_x, by_y, last_x, last_y):
+    half = own.shape[0] // 2
+    return jnp.concatenate(
+        [total([own[:half], by_x[:half], last_y]), total([own[half:], by_y[:half], last_x])], axis=0
+    )
+
+
 def total(parts):
     return sum(part.astype(f32) for part in parts)
 
@@ -455,9 +476,12 @@
     grad_mid_low = grad_mid.astype(bf)
     grad_mixed = contract_cols(grad_mid_low, full_out).astype(bf)
     out_first, out_second = after(out_first, over_x), after(out_second, over_x)
-    out_sent = [swap(out_second[:rows], "x"), swap(out_second[rows:], "y"), cross(out_first[:rows])]
+    out_parts = [out_first[rows:], out_second[:rows], out_second[rows:], out_first[:rows]]
+    out_hop = sum_first(*out_parts)
     grad_down = contract_rows(after(activated, grad_mixed), many_out).astype(bf)
-    grad_w_down = lax.psum_scatter(grad_down, "z", scatter_dimension=0, tiled=True)
+    grad_w_down = lax.psum_scatter(
+        after(grad_down, sum_gateup), "z", scatter_dimension=0, tiled=True
+    )
     mixed_by_core = mixed_tok.reshape(rows, depth, 4, 2, w_rows).transpose(0, 3, 2, 1, 4)
     mixed_by_core = mixed_by_core.reshape(rows, 2, -1)
     low_grads = after(grad_mid_low, grad_mixed)
@@ -465,22 +489,26 @@
     theirs = swap(theirs, "c")
     grad_out_w = contract_rows(pick(mixed_by_core, "c", 1), low_grads)
     grad_out_w = (grad_out_w + theirs.astype(f32)).astype(bf).reshape(4, depth, w_rows, width)
-    out_w_near = []
-    for dy, dx, move in ((0, 1, lambda v: swap(v, "x")), (1, 0, lambda v: swap(v, "y")), (1, 1, cross)):
-        chip = (y_at ^ dy) * 2 + (x_at ^ dx)
-        out_w_near.append(move(lax.dynamic_index_in_dim(grad_out_w, chip, 0, keepdims=False)))
+    chips = [
+        lax.dynamic_index_in_dim(grad_out_w, (y_at ^ dy) * 2 + (x_at ^ dx), 0, keepdims=False)
+        for dy, dx in ((0, 0), (0, 1), (1, 0), (1, 1))
+    ]
+    chips_hop = sum_first(*chips)
     grad_heads = lax.all_to_all(grad_mixed, ("x", "c"), split_axis=1, concat_axis=0, tiled=True)
-    out_sent = [after(part, grad_heads) for part in out_sent]
-    grad_heads = after(grad_heads, grad_out_w, *out_sent)
+    out_hop = [after(part, grad_heads) for part in out_hop]
+    out_last = sum_second(*out_parts[:3], *out_hop)
+    grad_heads = after(grad_heads, grad_out_w, sum_gateup, *out_hop)
     grad_cols = attend_backward(head_cols, grad_heads, cos_table, sin_table, start)
-    grad_cols = after(grad_cols, *out_w_near)
+    chips_hop = [after(part, grad_cols) for part in chips_hop]
+    grad_cols = after(grad_cols, *out_last, *chips_hop)
+    chips_last = sum_second(*chips[:3], *chips_hop)
     grad_qkv = contract_rows(normed_one, grad_cols).astype(bf)
     cols_by_core = after(grad_cols, grad_qkv).reshape(2, 2, rows, cols)
     grad_qkv = grad_qkv.reshape(depth, 2, 4 * w_rows, cols)
     over_y = swap(pick(grad_qkv, "y", 1, other=True), "y")
     sum_gateup = after(sum_gateup, grad_cols).reshape(8, w_rows, 2 * units)
     sum_gateup = lax.all_to_all(sum_gateup, QUAD, 0, 0, tiled=True)
-    over_y = after(over_y, sum_gateup)
+    over_y = after(over_y, sum_gateup, grad_w_down)
     grad_qkv = (pick(grad_qkv, "y", 1).astype(f32) + over_y.astype(f32)).astype(bf)
     grad_qkv = lax.all_to_all(
         grad_qkv.reshape(depth * 4, w_rows, cols), ("z", "x", "c"), 0, 0, tiled=True
@@ -495,13 +523,13 @@
     inv_one = lax.rsqrt(jnp.mean(resid_in * resid_in, axis=-1, keepdims=True) + epsilon)
     grad_in = grad_mid + norm_back(scaled_one, resid_in, inv_one)
 
-    own = lax.dynamic_index_in_dim(grad_out_w, y_at * 2 + x_at, 0, keepdims=False)
-    grad_out_w = total([own] + out_w_near).astype(bf)
+    grad_out_w = sum_last(chips[0], *chips_hop, *chips_last).astype(bf)
     out_w_parts = []
     for r in range(1, depth):
         part = lax.dynamic_index_in_dim(grad_out_w, (z_at + r) % depth, 0, keepdims=False)
         out_w_parts.append(lax.ppermute(part, "z", [(i, (i + r) % depth) for i in range(depth)]))
-    layer_out = resid_mid + total([out_first[rows:]] + [after(part, over_y) for part in out_sent])
+    out_last = [after(part, over_y) for part in out_last]
+    layer_out = resid_mid + sum_last(out_parts[0], *out_hop, *out_last)
 
     sum_qkv = jnp.sum(grad_qkv.reshape(depth, 4, w_rows, cols).astype(f32), axis=0)
     sum_qkv = sum_qkv.transpose(1, 0, 2).reshape(w_rows, 4 * cols)

time: 648 us -> 625 us (0.965)
  waiting for transfers between devices: 207 us -> 173 us
  other arithmetic: 67.5 us -> 79.1 us
    ppermute x44 -> x48, waiting for transfers between devices: 143 us -> 107 us  [swap(): return lax.ppermute(value, axis, [(0, 1), (1, 0)])]
    ppermute x3 -> x1, waiting for transfers between devices: 14.8 us -> 0.01 us  [cross(): return lax.ppermute(value, ('y', 'x'), [(i, 3 - i) for i in range(4)])]
    all_to_all x1, waiting for transfers between devices: 4.48 us -> 15.3 us  [body(): lax.all_to_all(grad_qkv.reshape(depth * 4, w_rows, cols), ('z', 'x', 'c')...]
    ppermute x44 -> x48, starting transfers between devices: 41.3 us -> 48.7 us  [swap(): return lax.ppermute(value, axis, [(0, 1), (1, 0)])]
    unnamed x146 -> x136, local copies, waits for them, and re-layouts: 25.5 us -> 30.7 us
  transfers between devices with their start and end apart: 64 -> 66, of which waited for: 19 -> 18; matrix products, arithmetic and copies ran while one was open for 35% -> 37% of each run, Pallas kernels for 7% -> 7%
where the time goes in v5:
time: 625 us; the launch traced here: 616 us
  waiting for transfers between devices  173 us (28%)
  matrix products  104 us (17%)
  starting transfers between devices  87.3 us (14%)
  local copies, waits for them, and re-layouts  85.4 us (14%)
  other arithmetic  79.1 us (13%)
  Pallas kernels  72 us (12%)
  between operations  15.4 us (2%)
    ppermute x48, waiting for transfers between devices, swap(): return lax.ppermute(value, axis, [(0, 1), (1, 0)])  107 us
    ppermute x48, starting transfers between devices, swap(): return lax.ppermute(value, axis, [(0, 1), (1, 0)])  48.7 us
    dot_general x7, matrix products, contract_cols(): lax.dot_general(left, right, (((1,), (1,)), ((), ())), preferred_element_...  41.5 us
    dot_general x5, matrix products, contract_rows(): lax.dot_general(left, right, (((0,), (0,)), ((), ())), preferred_element_...  38.9 us
    unnamed x136, local copies, waits for them, and re-layouts  30.7 us
    pallas_call x1, Pallas kernels, attend_backward(): pl.pallas_call(backward_kernel, grid=(pairs + 1,), in_specs=[pl.BlockSpec...  29.1 us
    pallas_call x1, Pallas kernels, run_units(): pl.pallas_call(units_kernel, grid=(count // block,), in_specs=[pl.BlockSp...  27.6 us
    ppermute x3, waiting for transfers between devices, rotations(): lax.ppermute(value, 'z', [((i + r) % depth, i) for i in range(depth)])  17.1 us
  transfers between devices with their start and end apart: 66, of which 18 were waited for; matrix products, arithmetic and copies ran while one was open for 37% of the time, Pallas kernels for 7%

profile of v5, /device:TPU:11, one launch (start us, length us, event | category | flops | bytes accessed | tf_op | source)
XLA Modules:
  0.0 615.7 jit_solution(3283472934445810710)
XLA Ops:
  10.5 4.3 all-to-all-start
  15.1 4.5 all-to-all-done
  30.1 17.1 %collective-permute-done.3 = bf16[256,640]{1,0:T(8,128)(2,1)} collective-permute-done((bf16[256,640]{1,0:T(8,128)(2,1)S(1)}, bf16[256,640]{1,0:T(8,128)(2,1)}, u32[]{:S(2)}, u32[]{:S(2)}) %collective-permute-start.3) | collective-permute-done | bytes 327712 | tf_op jit(solution)/shard_map/ppermute | solution.py:264
  51.5 2.9 collective-permute-start.1
  54.8 5.0 reshape.252
  59.8 3.9 copy.116
  63.7 4.0 reshape.253
  76.4 3.4 collective-permute-done.4
  79.9 7.0 %collective-permute-done.6 = bf16[256,640]{1,0:T(8,128)(2,1)S(1)} collective-permute-done((bf16[256,640]{1,0:T(8,128)(2,1)}, bf16[256,640]{1,0:T(8,128)(2,1)S(1)}, u32[]{:S(2)}, u32[]{:S(2)}) %collective-permute-start.6) | collective-permute-done | bytes 327712 | tf_op jit(solution)/shard_map/ppermute | solution.py:230
  86.9 6.9 %collective-permute-done.8 = bf16[256,640]{1,0:T(8,128)(2,1)S(1)} collective-permute-done((bf16[256,640]{1,0:T(8,128)(2,1)}, bf16[256,640]{1,0:T(8,128)(2,1)S(1)}, u32[]{:S(2)}, u32[]{:S(2)}) %collective-permute-start.8) | collective-permute-done | bytes 327712 | tf_op jit(solution)/shard_map/ppermute | solution.py:230
  93.8 6.6 %all-to-all-start.1 = ((bf16[8,64,1408]{2,1,0:T(8,128)(2,1)}), bf16[8,64,1408]{2,1,0:T(8,128)(2,1)}, u32[]{:S(2)}, u32[]{:S(2)}) async-start(bf16[8,64,1408]{2,1,0:T(8,128)(2,1)} %concatenate.57), calls=%async_computation.1 | async-start | bytes 2883584 | tf_op jit(solution)/shard_map/all_to_all | solution.py:429
  111.9 5.2 convolution_convert_fusion.10.query_ref.both_ref
  117.1 15.2 %attend_forward.1 = bf16[1024,512]{1,0:T(8,128)(2,1)S(1)} custom-call(bf16[1024,640]{1,0:T(8,128)(2,1)S(1)} %convolution_convert_fusion.10.query_ref.both_ref, bf16[1024,640]{1,0:T(8,128)(2,1)S(1)} %convolution_convert_fusion.10.query_ref.both_ref, f32[1024,128]{1,0:T(8,128)S(1)} %get-tuple-element.184.cos_ref, f32[1024,128]{1,0:T(8,128)S(1)} %get-tuple-element.185.sin_ref, ...), custom_call_target="tpu_custom_call" | custom-call | flops 12884901888 | bytes 3932160 | tf_op jit(solution)/shard_map/attend_forward/pallas_call | solution.py:169
  134.7 5.5 all-to-all-start.2
  146.6 17.6 %collective-permute-done.14 = bf16[4,32,2048]{2,1,0:T(8,128)(2,1)} collective-permute-done((bf16[4,32,2048]{2,1,0:T(8,128)(2,1)S(1)}, bf16[4,32,2048]{2,1,0:T(8,128)(2,1)}, u32[]{:S(2)}, u32[]{:S(2)}) %collective-permute-start.14) | collective-permute-done | bytes 524320 | tf_op jit(solution)/shard_map/ppermute | solution.py:230
  171.9 6.4 %collective-permute-done.10 = bf16[256,2048]{1,0:T(8,128)(2,1)} collective-permute-done((bf16[256,2048]{1,0:T(8,128)(2,1)}, bf16[256,2048]{1,0:T(8,128)(2,1)}, u32[]{:S(2)}, u32[]{:S(2)}) %collective-permute-start.10) | collective-permute-done | bytes 1048608 | tf_op jit(solution)/shard_map/ppermute | solution.py:230
  180.5 2.5 multiply_reduce_fusion.3
  185.7 21.6 %collective-permute-done.19 = bf16[256,2048]{1,0:T(8,128)(2,1)S(1)} collective-permute-done((bf16[256,2048]{1,0:T(8,128)(2,1)S(1)}, bf16[256,2048]{1,0:T(8,128)(2,1)S(1)}, u32[]{:S(2)}, u32[]{:S(2)}) %collective-permute-start.19) | collective-permute-done | bytes 1048608 | tf_op jit(solution)/shard_map/ppermute | solution.py:230
  211.6 3.0 collective-permute-start.30
  218.3 4.0 pad_maximum_fusion.down_ref
  222.3 3.5 collective-permute-start.31
  225.8 2.4 collective-permute-start.24
  230.7 3.3 collective-permute-start.23
  240.2 2.4 constant_dynamic-update-slice_fusion.15
  254.2 2.4 copy-done.49
  257.6 27.6 %units.1 = (bf16[2048,704]{1,0:T(8,128)(2,1)S(1)}, bf16[2048,1408]{1,0:T(8,128)(2,1)}) custom-call(bf16[2048,2048]{1,0:T(8,128)(2,1)} %copy-done.49, bf16[2048,2048]{1,0:T(8,128)(2,1)} %constant_dynamic-update-slice_fusion.9.out_ref, bf16[2048,1408]{1,0:T(8,128)(2,1)} %all-gather.5.cloned.1.call-done.w_ref, bf16[768,2048]{1,0:T(8,128)(2,1)} %pad_maximum_fusion.down_ref), custom_call_target="tpu_custom_call" | custom-call | flops 17716740096 | bytes 34078720 | tf_op jit(solution)/shard_map/units/pallas_call | solution.py:371
  286.9 16.6 %convolution_convert_fusion = bf16[2048,1408]{1,0:T(8,128)(2,1)} fusion(bf16[2048,2048]{1,0:T(8,128)(2,1)S(1)} %copy-done.50, bf16[2048,1408]{1,0:T(8,128)(2,1)} %get-tuple-element.88), kind=kOutput, calls=%fused_computation.5 | convolution fusion | flops 11814043648 | bytes 19922944 | tf_op jit(solution)/shard_map/dot_general | solution.py:48
  303.5 8.0 %convolution_convert_fusion.8 = bf16[512,2048]{1,0:T(8,128)(2,1)} fusion(bf16[2048,1408]{1,0:T(8,128)(2,1)} %all-gather.5.cloned.1.call-done.w_ref, bf16[2048,1408]{1,0:T(8,128)(2,1)} %get-tuple-element.88), kind=kOutput, calls=%fused_computation.25 | convolution fusion | flops 2953838592 | bytes 9306112 | tf_op jit(solution)/shard_map/dot_general | solution.py:52
  311.5 6.1 convolution_convert_fusion.7
  318.3 8.5 %add_convert_fusion.5 = bf16[512,2048]{1,0:T(8,128)(2,1)} fusion(bf16[512,2048]{1,0:T(8,128)(2,1)} %collective-permute-done.33, bf16[2048,1408]{1,0:T(8,128)(2,1)} %all-gather.5.cloned.1.call-done.w_ref, bf16[2048,1408]{1,0:T(8,128)(2,1)} %get-tuple-element.88), kind=kOutput, calls=%fused_computation.12 | convolution fusion | flops 2955935744 | bytes 11403264 | tf_op jit(solution)/shard_map/dot_general | solution.py:52
  326.8 7.3 %add_convert_fusion.4 = bf16[512,2048]{1,0:T(8,128)(2,1)S(1)} fusion(bf16[512,2048]{1,0:T(8,128)(2,1)} %collective-permute-done.34, bf16[2048,1408]{1,0:T(8,128)(2,1)} %all-gather.5.cloned.1.call-done.w_ref, bf16[2048,1408]{1,0:T(8,128)(2,1)} %get-tuple-element.88), kind=kOutput, calls=%fused_computation.11 | convolution fusion | flops 2955935744 | bytes 11403264 | tf_op jit(solution)/shard_map/dot_general | solution.py:52
  334.1 3.1 convolution_convert_fusion.5
  337.2 3.1 convolution_convert_fusion.4
  343.8 2.9 maximum_convert_fusion
  349.8 4.8 add_convert_fusion.3
  354.6 12.9 %collective-permute-done.36 = bf16[256,2048]{1,0:T(8,128)(2,1)} collective-permute-done((bf16[256,2048]{1,0:T(8,128)(2,1)}, bf16[256,2048]{1,0:T(8,128)(2,1)}, u32[]{:S(2)}, u32[]{:S(2)}) %collective-permute-start.36) | collective-permute-done | bytes 1048608 | tf_op jit(solution)/shard_map/ppermute | solution.py:230
  367.5 4.7 add_convert_fusion.2
  372.3 23.2 %collective-permute-done.40 = bf16[256,2048]{1,0:T(8,128)(2,1)S(1)} collective-permute-done((bf16[256,2048]{1,0:T(8,128)(2,1)S(1)}, bf16[256,2048]{1,0:T(8,128)(2,1)S(1)}, u32[]{:S(2)}, u32[]{:S(2)}) %collective-permute-start.40) | collective-permute-done | bytes 1048608 | tf_op jit(solution)/shard_map/ppermute | solution.py:230
  397.6 4.2 fusion.61
  401.8 2.4 convolution_convert_fusion.9
  404.2 3.3 convolution_convert_fusion.1
  408.6 2.5 fusion
  415.2 4.9 all-to-all-start.3
  422.6 10.7 %convolution_convert_fusion.2 = bf16[704,2048]{1,0:T(8,128)(2,1)} fusion(bf16[2048,704]{1,0:T(8,128)(2,1)} %copy-done, bf16[2048,2048]{1,0:T(8,128)(2,1)} %constant_dynamic-update-slice_fusion.9.out_ref), kind=kOutput, calls=%fused_computation.18 | convolution fusion | flops 5907021824 | bytes 14155776 | tf_op jit(solution)/shard_map/dot_general | solution.py:48
  433.3 16.9 %all-to-all-done.3 = bf16[256,4,512]{2,0,1:T(8,128)(2,1)S(1)} async-done(((bf16[256,4,512]{2,0,1:T(8,128)(2,1)}), bf16[256,4,512]{2,0,1:T(8,128)(2,1)S(1)}, u32[]{:S(2)}, u32[]{:S(2)}) %all-to-all-start.3) | async-done | bytes 1048608 | tf_op jit(solution)/shard_map/all_to_all | solution.py:497
  450.2 3.0 add_convert_fusion.7
  454.6 3.5 add_convert_fusion
  463.8 29.1 %attend_backward.1 = bf16[1024,640]{1,0:T(8,128)(2,1)S(1)} custom-call(bf16[1024,640]{1,0:T(8,128)(2,1)S(1)} %copy-done.4, bf16[1024,640]{1,0:T(8,128)(2,1)S(1)} %copy-done.4, bf16[1024,512]{1,0:T(8,128)(2,1)S(1)} %bitcast.224, f32[1024,128]{1,0:T(8,128)S(1)} %get-tuple-element.184.cos_ref, f32[1024,128]{1,0:T(8,128)S(1)} %get-tuple-element.185.sin_ref, ...), custom_call_target="tpu_custom_call" | custom-call | flops 32212254720 | bytes 5242880 | tf_op jit(solution)/shard_map/attend_backward/pallas_call | solution.py:196
  492.9 4.8 convolution_convert_fusion.3
  498.7 4.9 convolution_convert_fusion.6
  508.9 5.6 all-to-all-start.4
  514.5 2.5 dynamic-slice_bitcast_fusion
  518.2 2.8 collective-permute-done.51
  525.6 10.8 %all-to-all-done.4 = bf16[8,64,1408]{2,1,0:T(8,128)(2,1)S(1)} async-done(((bf16[8,64,1408]{2,1,0:T(8,128)(2,1)}), bf16[8,64,1408]{2,1,0:T(8,128)(2,1)S(1)}, u32[]{:S(2)}, u32[]{:S(2)}) %all-to-all-start.4) | async-done | bytes 1441824 | tf_op jit(solution)/shard_map/all_to_all | solution.py:510
  538.2 4.4 add_convert_fusion.1
  549.3 3.0 stack.81
  553.4 2.5 convert_bitcast_fusion
  555.9 5.5 reshape.276
  561.3 3.2 collective-permute-done.47
  564.6 3.1 fusion.1
  567.7 5.4 all-to-all-start.5
  573.1 4.6 broadcast_multiply_fusion
  582.0 3.4 fusion.5
  588.2 15.3 %all-to-all-done.5 = bf16[16,64,640]{2,1,0:T(8,128)(2,1)} async-done(((bf16[16,64,640]{2,1,0:T(8,128)(2,1)}), bf16[16,64,640]{2,1,0:T(8,128)(2,1)}, u32[]{:S(2)}, u32[]{:S(2)}) %all-to-all-start.5) | async-done | bytes 1310752 | tf_op jit(solution)/shard_map/all_to_all | solution.py:513
  (345 shorter events, 148.8 us)
Async XLA Ops:
  7.2 99.2 %all-gather.9.cloned.1.call-start = ((), (), s32[]{:S(2)}) async-start(), calls=%async_computation.12 | async-start | bytes 1310720 | tf_op jit(solution)/shard_map/all_gather | solution.py:424
  10.5 9.1 %all-to-all-start = ((bf16[4,64,640]{2,1,0:T(8,128)(2,1)}), bf16[4,64,640]{2,1,0:T(8,128)(2,1)S(1)}, u32[]{:S(2)}, u32[]{:S(2)}) async-start(bf16[4,64,640]{2,1,0:T(8,128)(2,1)} %copy.112), calls=%async_computation | async-start | bytes 655360 | tf_op jit(solution)/shard_map/all_to_all | solution.py:410
  14.8 199.7 %all-gather.7.cloned.1.call-start = ((), (), s32[]{:S(2)}) async-start(), calls=%async_computation.9 | async-start | bytes 3604480 | tf_op jit(solution)/shard_map/all_gather | solution.py:427
  19.6 28.0 %collective-permute-start = (bf16[256,2048]{1,0:T(8,128)(2,1)S(1)}, bf16[256,2048]{1,0:T(8,128)(2,1)}, u32[]{:S(2)}, u32[]{:S(2)}) collective-permute-start(bf16[256,2048]{1,0:T(8,128)(2,1)S(1)} %copy-done.11), channel_id=1, source_target_pairs={{0,2},{2,0},{1,3},{3,1},{4,6},{6,4},{5,7},{7,5},{8,10},{10,8},{9,1... | collective-permute-start | bytes 3145736 | tf_op jit(solution)/shard_map/ppermute | solution.py:230
  23.1 24.1 %collective-permute-start.3 = (bf16[256,640]{1,0:T(8,128)(2,1)S(1)}, bf16[256,640]{1,0:T(8,128)(2,1)}, u32[]{:S(2)}, u32[]{:S(2)}) collective-permute-start(bf16[256,640]{1,0:T(8,128)(2,1)S(1)} %bitcast.249), channel_id=1, source_target_pairs={{8,0},{16,8},{24,16},{0,24},{9,1},{17,9},{25,17},{1,25},{10,2},{18... | collective-permute-start | bytes 983048 | tf_op jit(solution)/shard_map/ppermute | solution.py:264
  24.1 46.1 %collective-permute-start.2 = (bf16[256,640]{1,0:T(8,128)(2,1)S(1)}, bf16[256,640]{1,0:T(8,128)(2,1)}, u32[]{:S(2)}, u32[]{:S(2)}) collective-permute-start(bf16[256,640]{1,0:T(8,128)(2,1)S(1)} %bitcast.250), channel_id=1, source_target_pairs={{0,4},{4,0},{1,5},{5,1},{2,6},{6,2},{3,7},{7,3},{8,12},{12,8},{9,1... | collective-permute-start | bytes 983048 | tf_op jit(solution)/shard_map/ppermute | solution.py:230
  25.5 45.8 %collective-permute-start.5 = (bf16[256,640]{1,0:T(8,128)(2,1)S(1)}, bf16[256,640]{1,0:T(8,128)(2,1)}, u32[]{:S(2)}, u32[]{:S(2)}) collective-permute-start(bf16[256,640]{1,0:T(8,128)(2,1)S(1)} %bitcast.251), channel_id=1, source_target_pairs={{16,0},{24,8},{0,16},{8,24},{17,1},{25,9},{1,17},{9,25},{18,2},{26... | collective-permute-start | bytes 983048 | tf_op jit(solution)/shard_map/ppermute | solution.py:264
  27.9 43.8 %collective-permute-start.7 = (bf16[256,640]{1,0:T(8,128)(2,1)S(1)}, bf16[256,640]{1,0:T(8,128)(2,1)}, u32[]{:S(2)}, u32[]{:S(2)}) collective-permute-start(bf16[256,640]{1,0:T(8,128)(2,1)S(1)} %bitcast.252), channel_id=1, source_target_pairs={{24,0},{0,8},{8,16},{16,24},{25,1},{1,9},{9,17},{17,25},{26,2},{2,... | collective-permute-start | bytes 983048 | tf_op jit(solution)/shard_map/ppermute | solution.py:264
  47.2 59.3 %collective-permute-start.9 = (bf16[256,2048]{1,0:T(8,128)(2,1)}, bf16[256,2048]{1,0:T(8,128)(2,1)}, u32[]{:S(2)}, u32[]{:S(2)}) collective-permute-start(bf16[256,2048]{1,0:T(8,128)(2,1)} %param.17), channel_id=1, source_target_pairs={{0,2},{2,0},{1,3},{3,1},{4,6},{6,4},{5,7},{7,5},{8,10},{10,8},{9,1... | collective-permute-start | bytes 3145736 | tf_op jit(solution)/shard_map/ppermute | solution.py:230
  51.5 56.4 %collective-permute-start.1 = (bf16[2,256,2048]{2,1,0:T(8,128)(2,1)}, bf16[2,256,2048]{2,1,0:T(8,128)(2,1)}, u32[]{:S(2)}, u32[]{:S(2)}) collective-permute-start(bf16[2,256,2048]{2,1,0:T(8,128)(2,1)} %pad_maximum_fusion.1), channel_id=1, source_target_pairs={{0,1},{1,0},{2,3},{3,2},{4,5},{5,4},{6,7},{7,6},{8,9},{9,8},{10,11... | collective-permute-start | bytes 6291464 | tf_op jit(solution)/shard_map/ppermute | solution.py:230
  70.2 9.7 %collective-permute-start.4 = (bf16[256,640]{1,0:T(8,128)(2,1)}, bf16[256,640]{1,0:T(8,128)(2,1)S(1)}, u32[]{:S(2)}, u32[]{:S(2)}) collective-permute-start(bf16[256,640]{1,0:T(8,128)(2,1)} %collective-permute-done.3), channel_id=1, source_target_pairs={{0,4},{4,0},{1,5},{5,1},{2,6},{6,2},{3,7},{7,3},{8,12},{12,8},{9,1... | collective-permute-start | bytes 983048 | tf_op jit(solution)/shard_map/ppermute | solution.py:230
  71.3 15.6 %collective-permute-start.6 = (bf16[256,640]{1,0:T(8,128)(2,1)}, bf16[256,640]{1,0:T(8,128)(2,1)S(1)}, u32[]{:S(2)}, u32[]{:S(2)}) collective-permute-start(bf16[256,640]{1,0:T(8,128)(2,1)} %collective-permute-done.5), channel_id=1, source_target_pairs={{0,4},{4,0},{1,5},{5,1},{2,6},{6,2},{3,7},{7,3},{8,12},{12,8},{9,1... | collective-permute-start | bytes 983048 | tf_op jit(solution)/shard_map/ppermute | solution.py:230
  71.7 22.1 %collective-permute-start.8 = (bf16[256,640]{1,0:T(8,128)(2,1)}, bf16[256,640]{1,0:T(8,128)(2,1)S(1)}, u32[]{:S(2)}, u32[]{:S(2)}) collective-permute-start(bf16[256,640]{1,0:T(8,128)(2,1)} %collective-permute-done.7), channel_id=1, source_target_pairs={{0,4},{4,0},{1,5},{5,1},{2,6},{6,2},{3,7},{7,3},{8,12},{12,8},{9,1... | collective-permute-start | bytes 983048 | tf_op jit(solution)/shard_map/ppermute | solution.py:230
  93.8 39.6 %all-to-all-start.1 = ((bf16[8,64,1408]{2,1,0:T(8,128)(2,1)}), bf16[8,64,1408]{2,1,0:T(8,128)(2,1)}, u32[]{:S(2)}, u32[]{:S(2)}) async-start(bf16[8,64,1408]{2,1,0:T(8,128)(2,1)} %concatenate.57), calls=%async_computation.1 | async-start | bytes 2883584 | tf_op jit(solution)/shard_map/all_to_all | solution.py:429
  106.4 34.5 %collective-permute-start.13 = (bf16[4,64,2048]{2,1,0:T(8,128)(2,1)}, bf16[4,64,2048]{2,1,0:T(8,128)(2,1)}, u32[]{:S(2)}, u32[]{:S(2)}) collective-permute-start(bf16[4,64,2048]{2,1,0:T(8,128)(2,1)} %bitcast.31), channel_id=1, source_target_pairs={{0,4},{4,0},{1,5},{5,1},{2,6},{6,2},{3,7},{7,3},{8,12},{12,8},{9,1... | collective-permute-start | bytes 3145736 | tf_op jit(solution)/shard_map/ppermute | solution.py:230
  107.7 34.5 %collective-permute-start.11 = (bf16[4,64,2048]{2,1,0:T(8,128)(2,1)}, bf16[4,64,2048]{2,1,0:T(8,128)(2,1)}, u32[]{:S(2)}, u32[]{:S(2)}) collective-permute-start(bf16[4,64,2048]{2,1,0:T(8,128)(2,1)} %bitcast.31), channel_id=1, source_target_pairs={{0,2},{2,0},{1,3},{3,1},{4,6},{6,4},{5,7},{7,5},{8,10},{10,8},{9,1... | collective-permute-start | bytes 3145736 | tf_op jit(solution)/shard_map/ppermute | solution.py:230
  134.7 30.7 %all-to-all-start.2 = ((bf16[4,256,512]{1,2,0:T(8,128)(2,1)}), bf16[4,256,512]{1,2,0:T(8,128)(2,1)S(1)}, u32[]{:S(2)}, u32[]{:S(2)}) async-start(bf16[4,256,512]{1,2,0:T(8,128)(2,1)} %copy.117), calls=%async_computation.2 | async-start | bytes 2097152 | tf_op jit(solution)/shard_map/all_to_all | solution.py:441
  140.3 117.4 %all-gather.5.cloned.1.call-start = ((), (), s32[]{:S(2)}) async-start(), calls=%async_computation.8 | async-start | bytes 7208960 | tf_op jit(solution)/shard_map/all_gather | solution.py:430
  142.0 22.1 %collective-permute-start.14 = (bf16[4,32,2048]{2,1,0:T(8,128)(2,1)S(1)}, bf16[4,32,2048]{2,1,0:T(8,128)(2,1)}, u32[]{:S(2)}, u32[]{:S(2)}) collective-permute-start(bf16[4,32,2048]{2,1,0:T(8,128)(2,1)S(1)} %slice.263), channel_id=1, source_target_pairs={{0,2},{2,0},{1,3},{3,1},{4,6},{6,4},{5,7},{7,5},{8,10},{10,8},{9,1... | collective-permute-start | bytes 1572872 | tf_op jit(solution)/shard_map/ppermute | solution.py:230
  143.2 20.9 %collective-permute-start.12 = (bf16[4,32,2048]{2,1,0:T(8,128)(2,1)S(1)}, bf16[4,32,2048]{2,1,0:T(8,128)(2,1)}, u32[]{:S(2)}, u32[]{:S(2)}) collective-permute-start(bf16[4,32,2048]{2,1,0:T(8,128)(2,1)S(1)} %slice.262), channel_id=1, source_target_pairs={{0,4},{4,0},{1,5},{5,1},{2,6},{6,2},{3,7},{7,3},{8,12},{12,8},{9,1... | collective-permute-start | bytes 1572872 | tf_op jit(solution)/shard_map/ppermute | solution.py:230
  143.4 35.0 %collective-permute-start.10 = (bf16[256,2048]{1,0:T(8,128)(2,1)}, bf16[256,2048]{1,0:T(8,128)(2,1)}, u32[]{:S(2)}, u32[]{:S(2)}) collective-permute-start(bf16[256,2048]{1,0:T(8,128)(2,1)} %param.17), channel_id=1, source_target_pairs={{0,4},{4,0},{1,5},{5,1},{2,6},{6,2},{3,7},{7,3},{8,12},{12,8},{9,1... | collective-permute-start | bytes 3145736 | tf_op jit(solution)/shard_map/ppermute | solution.py:230
  144.8 34.0 %collective-permute-start.18 = (bf16[4,64,2048]{2,1,0:T(8,128)(2,1)}, bf16[4,64,2048]{2,1,0:T(8,128)(2,1)}, u32[]{:S(2)}, u32[]{:S(2)}) collective-permute-start(bf16[4,64,2048]{2,1,0:T(8,128)(2,1)} %bitcast.31), channel_id=1, source_target_pairs={{0,1},{1,0},{2,3},{3,2},{4,5},{5,4},{6,7},{7,6},{8,9},{9,8},{10,11... | collective-permute-start | bytes 3145736 | tf_op jit(solution)/shard_map/ppermute | solution.py:230
  146.3 317.4 %reduce-scatter.3.cloned.1.call-start = ((), (), s32[]{:S(2)}) async-start(), calls=%async_computation.10 | async-start | bytes 7208960 | tf_op jit(solution)/shard_map/reduce_scatter | solution.py:464
  165.5 12.8 %collective-permute-start.15 = (bf16[4,64,2048]{2,1,0:T(8,128)(2,1)S(1)}, bf16[4,64,2048]{2,1,0:T(8,128)(2,1)S(1)}, u32[]{:S(2)}, u32[]{:S(2)}) collective-permute-start(bf16[4,64,2048]{2,1,0:T(8,128)(2,1)S(1)} %pad_maximum_fusion.2), channel_id=1, source_target_pairs={{0,1},{1,0},{2,3},{3,2},{4,5},{5,4},{6,7},{7,6},{8,9},{9,8},{10,11... | collective-permute-start | bytes 3145736 | tf_op jit(solution)/shard_map/ppermute | solution.py:230
  166.1 12.3 %collective-permute-start.16 = (bf16[4,64,2048]{2,1,0:T(8,128)(2,1)}, bf16[4,64,2048]{2,1,0:T(8,128)(2,1)S(1)}, u32[]{:S(2)}, u32[]{:S(2)}) collective-permute-start(bf16[4,64,2048]{2,1,0:T(8,128)(2,1)} %collective-permute-done.11), channel_id=1, source_target_pairs={{0,1},{1,0},{2,3},{3,2},{4,5},{5,4},{6,7},{7,6},{8,9},{9,8},{10,11... | collective-permute-start | bytes 3145736 | tf_op jit(solution)/shard_map/ppermute | solution.py:230
  166.2 12.4 %collective-permute-start.17 = (bf16[4,64,2048]{2,1,0:T(8,128)(2,1)}, bf16[4,64,2048]{2,1,0:T(8,128)(2,1)S(1)}, u32[]{:S(2)}, u32[]{:S(2)}) collective-permute-start(bf16[4,64,2048]{2,1,0:T(8,128)(2,1)} %collective-permute-done.13), channel_id=1, source_target_pairs={{0,1},{1,0},{2,3},{3,2},{4,5},{5,4},{6,7},{7,6},{8,9},{9,8},{10,11... | collective-permute-start | bytes 3145736 | tf_op jit(solution)/shard_map/ppermute | solution.py:230
  183.8 23.4 %collective-permute-start.19 = (bf16[256,2048]{1,0:T(8,128)(2,1)S(1)}, bf16[256,2048]{1,0:T(8,128)(2,1)S(1)}, u32[]{:S(2)}, u32[]{:S(2)}) collective-permute-start(bf16[256,2048]{1,0:T(8,128)(2,1)S(1)} %multiply_convert_fusion.2), channel_id=1, source_target_pairs={{0,2},{2,0},{1,3},{3,1},{4,6},{6,4},{5,7},{7,5},{8,10},{10,8},{9,1... | collective-permute-start | bytes 3145736 | tf_op jit(solution)/shard_map/ppermute | solution.py:230
  185.6 22.9 %collective-permute-start.21 = (bf16[256,2048]{1,0:T(8,128)(2,1)S(1)}, bf16[256,2048]{1,0:T(8,128)(2,1)S(1)}, u32[]{:S(2)}, u32[]{:S(2)}) collective-permute-start(bf16[256,2048]{1,0:T(8,128)(2,1)S(1)} %multiply_convert_fusion.2), channel_id=1, source_target_pairs={{0,4},{4,0},{1,5},{5,1},{2,6},{6,2},{3,7},{7,3},{8,12},{12,8},{9,1... | collective-permute-start | bytes 3145736 | tf_op jit(solution)/shard_map/ppermute | solution.py:230
  208.2 14.1 %collective-permute-start.20 = (bf16[128,2048]{1,0:T(8,128)(2,1)}, bf16[128,2048]{1,0:T(8,128)(2,1)}, u32[]{:S(2)}, u32[]{:S(2)}) collective-permute-start(bf16[128,2048]{1,0:T(8,128)(2,1)} %slice.264), channel_id=1, source_target_pairs={{0,4},{4,0},{1,5},{5,1},{2,6},{6,2},{3,7},{7,3},{8,12},{12,8},{9,1... | collective-permute-start | bytes 1572872 | tf_op jit(solution)/shard_map/ppermute | solution.py:230
  210.3 15.5 %collective-permute-start.22 = (bf16[128,2048]{1,0:T(8,128)(2,1)}, bf16[128,2048]{1,0:T(8,128)(2,1)}, u32[]{:S(2)}, u32[]{:S(2)}) collective-permute-start(bf16[128,2048]{1,0:T(8,128)(2,1)} %slice.265), channel_id=1, source_target_pairs={{0,2},{2,0},{1,3},{3,1},{4,6},{6,4},{5,7},{7,5},{8,10},{10,8},{9,1... | collective-permute-start | bytes 1572872 | tf_op jit(solution)/shard_map/ppermute | solution.py:230
  211.6 34.2 %collective-permute-start.30 = (bf16[256,2048]{1,0:T(8,128)(2,1)}, bf16[256,2048]{1,0:T(8,128)(2,1)}, u32[]{:S(2)}, u32[]{:S(2)}) collective-permute-start(bf16[256,2048]{1,0:T(8,128)(2,1)} %param.17), channel_id=1, source_target_pairs={{0,1},{1,0},{2,3},{3,2},{4,5},{5,4},{6,7},{7,6},{8,9},{9,8},{10,11... | collective-permute-start | bytes 3145736 | tf_op jit(solution)/shard_map/ppermute | solution.py:230
  215.7 15.0 %collective-permute-start.27 = (bf16[128,2048]{1,0:T(8,128)(2,1)S(1)}, bf16[128,2048]{1,0:T(8,128)(2,1)S(1)}, u32[]{:S(2)}, u32[]{:S(2)}) collective-permute-start(bf16[128,2048]{1,0:T(8,128)(2,1)S(1)} %slice.209), channel_id=1, source_target_pairs={{0,4},{4,0},{1,5},{5,1},{2,6},{6,2},{3,7},{7,3},{8,12},{12,8},{9,1... | collective-permute-start | bytes 1572872 | tf_op jit(solution)/shard_map/ppermute | solution.py:230
  218.2 15.7 %collective-permute-start.28 = (bf16[128,2048]{1,0:T(8,128)(2,1)S(1)}, bf16[128,2048]{1,0:T(8,128)(2,1)S(1)}, u32[]{:S(2)}, u32[]{:S(2)}) collective-permute-start(bf16[128,2048]{1,0:T(8,128)(2,1)S(1)} %slice.210), channel_id=1, source_target_pairs={{0,2},{2,0},{1,3},{3,1},{4,6},{6,4},{5,7},{7,5},{8,10},{10,8},{9,1... | collective-permute-start | bytes 1572872 | tf_op jit(solution)/shard_map/ppermute | solution.py:230
  222.3 30.7 %collective-permute-start.31 = (bf16[256,2048]{1,0:T(8,128)(2,1)}, bf16[256,2048]{1,0:T(8,128)(2,1)S(1)}, u32[]{:S(2)}, u32[]{:S(2)}) collective-permute-start(bf16[256,2048]{1,0:T(8,128)(2,1)} %collective-permute-done.9), channel_id=1, source_target_pairs={{0,1},{1,0},{2,3},{3,2},{4,5},{5,4},{6,7},{7,6},{8,9},{9,8},{10,11... | collective-permute-start | bytes 3145736 | tf_op jit(solution)/shard_map/ppermute | solution.py:230
  225.8 17.0 %collective-permute-start.24 = (bf16[256,2048]{1,0:T(8,128)(2,1)S(1)}, bf16[256,2048]{1,0:T(8,128)(2,1)S(1)}, u32[]{:S(2)}, u32[]{:S(2)}) collective-permute-start(bf16[256,2048]{1,0:T(8,128)(2,1)S(1)} %copy-done.42), channel_id=1, source_target_pairs={{0,1},{1,0},{2,3},{3,2},{4,5},{5,4},{6,7},{7,6},{8,9},{9,8},{10,11... | collective-permute-start | bytes 3145736 | tf_op jit(solution)/shard_map/ppermute | solution.py:230
  230.7 12.0 %collective-permute-start.23 = (bf16[256,2048]{1,0:T(8,128)(2,1)S(1)}, bf16[256,2048]{1,0:T(8,128)(2,1)S(1)}, u32[]{:S(2)}, u32[]{:S(2)}) collective-permute-start(bf16[256,2048]{1,0:T(8,128)(2,1)S(1)} %pad_maximum_fusion.3), channel_id=1, source_target_pairs={{0,1},{1,0},{2,3},{3,2},{4,5},{5,4},{6,7},{7,6},{8,9},{9,8},{10,11... | collective-permute-start | bytes 3145736 | tf_op jit(solution)/shard_map/ppermute | solution.py:230
  234.0 10.1 %collective-permute-start.29 = (bf16[256,2048]{1,0:T(8,128)(2,1)S(1)}, bf16[256,2048]{1,0:T(8,128)(2,1)S(1)}, u32[]{:S(2)}, u32[]{:S(2)}) collective-permute-start(bf16[256,2048]{1,0:T(8,128)(2,1)S(1)} %pad_maximum_fusion.4), channel_id=1, source_target_pairs={{0,1},{1,0},{2,3},{3,2},{4,5},{5,4},{6,7},{7,6},{8,9},{9,8},{10,11... | collective-permute-start | bytes 3145736 | tf_op jit(solution)/shard_map/ppermute | solution.py:230
  242.7 11.5 %collective-permute-start.32 = (bf16[256,2048]{1,0:T(8,128)(2,1)}, bf16[256,2048]{1,0:T(8,128)(2,1)S(1)}, u32[]{:S(2)}, u32[]{:S(2)}) collective-permute-start(bf16[256,2048]{1,0:T(8,128)(2,1)} %collective-permute-done.10), channel_id=1, source_target_pairs={{0,1},{1,0},{2,3},{3,2},{4,5},{5,4},{6,7},{7,6},{8,9},{9,8},{10,11... | collective-permute-start | bytes 3145736 | tf_op jit(solution)/shard_map/ppermute | solution.py:230
  242.8 9.9 %collective-permute-start.25 = (bf16[256,2048]{1,0:T(8,128)(2,1)S(1)}, bf16[256,2048]{1,0:T(8,128)(2,1)S(1)}, u32[]{:S(2)}, u32[]{:S(2)}) collective-permute-start(bf16[256,2048]{1,0:T(8,128)(2,1)S(1)} %copy-done.36), channel_id=1, source_target_pairs={{0,1},{1,0},{2,3},{3,2},{4,5},{5,4},{6,7},{7,6},{8,9},{9,8},{10,11... | collective-permute-start | bytes 3145736 | tf_op jit(solution)/shard_map/ppermute | solution.py:230
  317.7 9.1 %collective-permute-start.34 = (bf16[512,2048]{1,0:T(8,128)(2,1)}, bf16[512,2048]{1,0:T(8,128)(2,1)}, u32[]{:S(2)}, u32[]{:S(2)}) collective-permute-start(bf16[512,2048]{1,0:T(8,128)(2,1)} %convolution_convert_fusion.7), channel_id=1, source_target_pairs={{0,1},{1,0},{2,3},{3,2},{4,5},{5,4},{6,7},{7,6},{8,9},{9,8},{10,11... | collective-permute-start | bytes 6291464 | tf_op jit(solution)/shard_map/ppermute | solution.py:230
  337.2 12.6 %collective-permute-start.35 = (bf16[512,2048]{1,0:T(8,128)(2,1)}, bf16[512,2048]{1,0:T(8,128)(2,1)}, u32[]{:S(2)}, u32[]{:S(2)}) collective-permute-start(bf16[512,2048]{1,0:T(8,128)(2,1)} %convolution_convert_fusion.5), channel_id=1, source_target_pairs={{0,1},{1,0},{2,3},{3,2},{4,5},{5,4},{6,7},{7,6},{8,9},{9,8},{10,11... | collective-permute-start | bytes 6291464 | tf_op jit(solution)/shard_map/ppermute | solution.py:230
  340.3 27.2 %collective-permute-start.37 = (bf16[512,2048]{1,0:T(8,128)(2,1)}, bf16[512,2048]{1,0:T(8,128)(2,1)}, u32[]{:S(2)}, u32[]{:S(2)}) collective-permute-start(bf16[512,2048]{1,0:T(8,128)(2,1)} %convolution_convert_fusion.4), channel_id=1, source_target_pairs={{0,1},{1,0},{2,3},{3,2},{4,5},{5,4},{6,7},{7,6},{8,9},{9,8},{10,11... | collective-permute-start | bytes 6291464 | tf_op jit(solution)/shard_map/ppermute | solution.py:230
  342.4 25.1 %collective-permute-start.36 = (bf16[256,2048]{1,0:T(8,128)(2,1)}, bf16[256,2048]{1,0:T(8,128)(2,1)}, u32[]{:S(2)}, u32[]{:S(2)}) collective-permute-start(bf16[256,2048]{1,0:T(8,128)(2,1)} %get-tuple-element.149), channel_id=1, source_target_pairs={{0,2},{2,0},{1,3},{3,1},{4,6},{6,4},{5,7},{7,5},{8,10},{10,8},{9,1... | collective-permute-start | bytes 3145736 | tf_op jit(solution)/shard_map/ppermute | solution.py:230
  348.4 47.0 %collective-permute-start.40 = (bf16[256,2048]{1,0:T(8,128)(2,1)S(1)}, bf16[256,2048]{1,0:T(8,128)(2,1)S(1)}, u32[]{:S(2)}, u32[]{:S(2)}) collective-permute-start(bf16[256,2048]{1,0:T(8,128)(2,1)S(1)} %copy-done.43), channel_id=1, source_target_pairs={{0,4},{4,0},{1,5},{5,1},{2,6},{6,2},{3,7},{7,3},{8,12},{12,8},{9,1... | collective-permute-start | bytes 3145736 | tf_op jit(solution)/shard_map/ppermute | solution.py:230
  349.8 45.6 %collective-permute-start.39 = (bf16[256,2048]{1,0:T(8,128)(2,1)S(1)}, bf16[256,2048]{1,0:T(8,128)(2,1)S(1)}, u32[]{:S(2)}, u32[]{:S(2)}) collective-permute-start(bf16[256,2048]{1,0:T(8,128)(2,1)S(1)} %slice.269), channel_id=1, source_target_pairs={{0,6},{2,4},{4,2},{6,0},{1,7},{3,5},{5,3},{7,1},{8,14},{10,12},{12... | collective-permute-start | bytes 3145736 | tf_op jit(solution)/shard_map/ppermute | solution.py:234
  407.6 47.0 %collective-permute-start.42 = (bf16[1024,2048]{1,0:T(8,128)(2,1)}, bf16[1024,2048]{1,0:T(8,128)(2,1)}, u32[]{:S(2)}, u32[]{:S(2)}) collective-permute-start(bf16[1024,2048]{1,0:T(8,128)(2,1)} %convolution_convert_fusion.1), channel_id=1, source_target_pairs={{0,1},{1,0},{2,3},{3,2},{4,5},{5,4},{6,7},{7,6},{8,9},{9,8},{10,11... | collective-permute-start | bytes 12582920 | tf_op jit(solution)/shard_map/ppermute | solution.py:230
  413.9 36.3 %collective-permute-start.38 = (bf16[256,2048]{1,0:T(8,128)(2,1)}, bf16[256,2048]{1,0:T(8,128)(2,1)}, u32[]{:S(2)}, u32[]{:S(2)}) collective-permute-start(bf16[256,2048]{1,0:T(8,128)(2,1)} %pad_maximum_fusion.5), channel_id=1, source_target_pairs={{0,2},{2,0},{1,3},{3,1},{4,6},{6,4},{5,7},{7,5},{8,10},{10,8},{9,1... | collective-permute-start | bytes 3145736 | tf_op jit(solution)/shard_map/ppermute | solution.py:230
  415.2 35.0 %all-to-all-start.3 = ((bf16[256,4,512]{2,0,1:T(8,128)(2,1)}), bf16[256,4,512]{2,0,1:T(8,128)(2,1)S(1)}, u32[]{:S(2)}, u32[]{:S(2)}) async-start(bf16[256,4,512]{2,0,1:T(8,128)(2,1)} %bitcast.222), calls=%async_computation.3 | async-start | bytes 2097152 | tf_op jit(solution)/shard_map/all_to_all | solution.py:497
  420.1 144.5 %reduce-scatter.5.cloned.1.call-start = ((), (), s32[]{:S(2)}) async-start(), calls=%async_computation.11 | async-start | bytes 3604480 | tf_op jit(solution)/shard_map/reduce_scatter | solution.py:482
  421.2 29.0 %collective-permute-start.43 = (bf16[256,2048]{1,0:T(8,128)(2,1)}, bf16[256,2048]{1,0:T(8,128)(2,1)}, u32[]{:S(2)}, u32[]{:S(2)}) collective-permute-start(bf16[256,2048]{1,0:T(8,128)(2,1)} %pad_maximum_fusion.6), channel_id=1, source_target_pairs={{0,4},{4,0},{1,5},{5,1},{2,6},{6,2},{3,7},{7,3},{8,12},{12,8},{9,1... | collective-permute-start | bytes 3145736 | tf_op jit(solution)/shard_map/ppermute | solution.py:230
  453.2 39.7 %collective-permute-start.41 = (bf16[128,2048]{1,0:T(8,128)(2,1)}, bf16[128,2048]{1,0:T(8,128)(2,1)}, u32[]{:S(2)}, u32[]{:S(2)}) collective-permute-start(bf16[128,2048]{1,0:T(8,128)(2,1)} %get-tuple-element.142), channel_id=1, source_target_pairs={{0,4},{4,0},{1,5},{5,1},{2,6},{6,2},{3,7},{7,3},{8,12},{12,8},{9,1... | collective-permute-start | bytes 1572872 | tf_op jit(solution)/shard_map/ppermute | solution.py:230
  454.5 38.4 %collective-permute-start.44 = (bf16[128,2048]{1,0:T(8,128)(2,1)}, bf16[128,2048]{1,0:T(8,128)(2,1)}, u32[]{:S(2)}, u32[]{:S(2)}) collective-permute-start(bf16[128,2048]{1,0:T(8,128)(2,1)} %get-tuple-element.143), channel_id=1, source_target_pairs={{0,2},{2,0},{1,3},{3,1},{4,6},{6,4},{5,7},{7,5},{8,10},{10,8},{9,1... | collective-permute-start | bytes 1572872 | tf_op jit(solution)/shard_map/ppermute | solution.py:230
  461.2 31.7 %collective-permute-start.45 = (bf16[4,64,2048]{2,1,0:T(8,128)(2,1)}, bf16[4,64,2048]{2,1,0:T(8,128)(2,1)}, u32[]{:S(2)}, u32[]{:S(2)}) collective-permute-start(bf16[4,64,2048]{2,1,0:T(8,128)(2,1)} %pad_maximum_fusion.7), channel_id=1, source_target_pairs={{0,2},{2,0},{1,3},{3,1},{4,6},{6,4},{5,7},{7,5},{8,10},{10,8},{9,1... | collective-permute-start | bytes 3145736 | tf_op jit(solution)/shard_map/ppermute | solution.py:230
  463.6 29.3 %collective-permute-start.46 = (bf16[4,64,2048]{2,1,0:T(8,128)(2,1)}, bf16[4,64,2048]{2,1,0:T(8,128)(2,1)}, u32[]{:S(2)}, u32[]{:S(2)}) collective-permute-start(bf16[4,64,2048]{2,1,0:T(8,128)(2,1)} %pad_maximum_fusion.8), channel_id=1, source_target_pairs={{0,4},{4,0},{1,5},{5,1},{2,6},{6,2},{3,7},{7,3},{8,12},{12,8},{9,1... | collective-permute-start | bytes 3145736 | tf_op jit(solution)/shard_map/ppermute | solution.py:230
  503.6 34.6 %collective-permute-start.48 = (bf16[512,2048]{1,0:T(8,128)(2,1)}, bf16[512,2048]{1,0:T(8,128)(2,1)}, u32[]{:S(2)}, u32[]{:S(2)}) collective-permute-start(bf16[512,2048]{1,0:T(8,128)(2,1)} %convolution_convert_fusion.6), channel_id=1, source_target_pairs={{0,1},{1,0},{2,3},{3,2},{4,5},{5,4},{6,7},{7,6},{8,9},{9,8},{10,11... | collective-permute-start | bytes 6291464 | tf_op jit(solution)/shard_map/ppermute | solution.py:230
  507.4 13.6 %collective-permute-start.51 = (bf16[2,64,2048]{2,1,0:T(8,128)(2,1)S(1)}, bf16[2,64,2048]{2,1,0:T(8,128)(2,1)S(1)}, u32[]{:S(2)}, u32[]{:S(2)}) collective-permute-start(bf16[2,64,2048]{2,1,0:T(8,128)(2,1)S(1)} %get-tuple-element.130), channel_id=1, source_target_pairs={{0,2},{2,0},{1,3},{3,1},{4,6},{6,4},{5,7},{7,5},{8,10},{10,8},{9,1... | collective-permute-start | bytes 1572872 | tf_op jit(solution)/shard_map/ppermute | solution.py:230
  507.7 13.3 %collective-permute-start.50 = (bf16[2,64,2048]{2,1,0:T(8,128)(2,1)S(1)}, bf16[2,64,2048]{2,1,0:T(8,128)(2,1)S(1)}, u32[]{:S(2)}, u32[]{:S(2)}) collective-permute-start(bf16[2,64,2048]{2,1,0:T(8,128)(2,1)S(1)} %get-tuple-element.131), channel_id=1, source_target_pairs={{0,4},{4,0},{1,5},{5,1},{2,6},{6,2},{3,7},{7,3},{8,12},{12,8},{9,1... | collective-permute-start | bytes 1572872 | tf_op jit(solution)/shard_map/ppermute | solution.py:230
  508.9 27.6 %all-to-all-start.4 = ((bf16[8,64,1408]{2,1,0:T(8,128)(2,1)}), bf16[8,64,1408]{2,1,0:T(8,128)(2,1)S(1)}, u32[]{:S(2)}, u32[]{:S(2)}) async-start(bf16[8,64,1408]{2,1,0:T(8,128)(2,1)} %bitcast.247), calls=%async_computation.5 | async-start | bytes 2883584 | tf_op jit(solution)/shard_map/all_to_all | solution.py:510
  517.0 47.6 %collective-permute-start.47 = (bf16[4,256,640]{2,1,0:T(8,128)(2,1)}, bf16[4,256,640]{2,1,0:T(8,128)(2,1)}, u32[]{:S(2)}, u32[]{:S(2)}) collective-permute-start(bf16[4,256,640]{2,1,0:T(8,128)(2,1)} %dynamic-slice_bitcast_fusion), channel_id=1, source_target_pairs={{0,4},{4,0},{1,5},{5,1},{2,6},{6,2},{3,7},{7,3},{8,12},{12,8},{9,1... | collective-permute-start | bytes 3932168 | tf_op jit(solution)/shard_map/ppermute | solution.py:230
  524.2 81.0 %collective-permute-start.54 = (bf16[64,2048]{1,0:T(8,128)(2,1)}, bf16[64,2048]{1,0:T(8,128)(2,1)}, u32[]{:S(2)}, u32[]{:S(2)}) collective-permute-start(bf16[64,2048]{1,0:T(8,128)(2,1)} %get-tuple-element.162), channel_id=1, source_target_pairs={{0,24},{8,0},{16,8},{24,16},{1,25},{9,1},{17,9},{25,17},{2,26},{10... | collective-permute-start | bytes 786440 | tf_op jit(solution)/shard_map/ppermute | solution.py:530
  524.2 81.1 %collective-permute-start.53 = (bf16[64,2048]{1,0:T(8,128)(2,1)}, bf16[64,2048]{1,0:T(8,128)(2,1)}, u32[]{:S(2)}, u32[]{:S(2)}) collective-permute-start(bf16[64,2048]{1,0:T(8,128)(2,1)} %get-tuple-element.161), channel_id=1, source_target_pairs={{0,16},{8,24},{16,0},{24,8},{1,17},{9,25},{17,1},{25,9},{2,18},{10... | collective-permute-start | bytes 786440 | tf_op jit(solution)/shard_map/ppermute | solution.py:530
  524.2 82.7 %collective-permute-start.52 = (bf16[64,2048]{1,0:T(8,128)(2,1)}, bf16[64,2048]{1,0:T(8,128)(2,1)}, u32[]{:S(2)}, u32[]{:S(2)}) collective-permute-start(bf16[64,2048]{1,0:T(8,128)(2,1)} %get-tuple-element.160), channel_id=1, source_target_pairs={{0,8},{8,16},{16,24},{24,0},{1,9},{9,17},{17,25},{25,1},{2,10},{10... | collective-permute-start | bytes 786440 | tf_op jit(solution)/shard_map/ppermute | solution.py:530
  545.0 32.7 %collective-permute-start.49 = (bf16[256,2048]{1,0:T(8,128)(2,1)}, bf16[256,2048]{1,0:T(8,128)(2,1)}, u32[]{:S(2)}, u32[]{:S(2)}) collective-permute-start(bf16[256,2048]{1,0:T(8,128)(2,1)} %dynamic-slice_bitcast_fusion.1), channel_id=1, source_target_pairs={{0,2},{2,0},{1,3},{3,1},{4,6},{6,4},{5,7},{7,5},{8,10},{10,8},{9,1... | collective-permute-start | bytes 3145736 | tf_op jit(solution)/shard_map/ppermute | solution.py:230
  567.7 35.9 %all-to-all-start.5 = ((bf16[16,64,640]{2,1,0:T(8,128)(2,1)}), bf16[16,64,640]{2,1,0:T(8,128)(2,1)}, u32[]{:S(2)}, u32[]{:S(2)}) async-start(bf16[16,64,640]{2,1,0:T(8,128)(2,1)} %bitcast.236), calls=%async_computation.7 | async-start | bytes 2621440 | tf_op jit(solution)/shard_map/all_to_all | solution.py:513
  (63 other events, 708.3 us)
Sparse Core Ops, SparseCore 0:
  9.6 44.7 all-gather.8
  55.9 59.2 all-gather.6
  146.4 101.6 all-gather.4
  318.4 101.1 reduce-scatter.2
  463.9 55.9 reduce-scatter.4

commit v6 on v5

--- a/solution.py
+++ b/solution.py
@@ -503,7 +503,6 @@
     grad_cols = after(grad_cols, *out_last, *chips_hop)
     chips_last = sum_second(*chips[:3], *chips_hop)
     grad_qkv = contract_rows(normed_one, grad_cols).astype(bf)
-    cols_by_core = after(grad_cols, grad_qkv).reshape(2, 2, rows, cols)
     grad_qkv = grad_qkv.reshape(depth, 2, 4 * w_rows, cols)
     over_y = swap(pick(grad_qkv, "y", 1, other=True), "y")
     sum_gateup = after(sum_gateup, grad_cols).reshape(8, w_rows, 2 * units)
@@ -514,6 +513,7 @@
         grad_qkv.reshape(depth * 4, w_rows, cols), ("z", "x", "c"), 0, 0, tiled=True
     )
 
+    cols_by_core = after(grad_cols, sum_gateup).reshape(2, 2, rows, cols)
     theirs = contract_cols(pick(cols_by_core, "c", 1, other=True).reshape(-1, cols), qkv).astype(bf)
     theirs = swap(theirs, "c")
     part_one = contract_cols(pick(cols_by_core, "c", 1).reshape(-1, cols), qkv)

time: 625 us -> 626 us (level)
  waiting for transfers between devices: 173 us -> 163 us
  other arithmetic: 79.1 us -> 86.4 us
    ppermute x48, waiting for transfers between devices: 107 us -> 101 us  [swap(): return lax.ppermute(value, axis, [(0, 1), (1, 0)])]
    unnamed x136 -> x140, local copies, waits for them, and re-layouts: 30.7 us -> 29.7 us
  transfers between devices with their start and end apart: 66 -> 66, of which waited for: 18 -> 17; matrix products, arithmetic and copies ran while one was open for 37% -> 38% of each run, Pallas kernels for 7% -> 7%
where the time goes in v6:
time: 626 us; the launch traced here: 617 us
  waiting for transfers between devices  163 us (26%)
  matrix products  103 us (16%)
  starting transfers between devices  89.3 us (14%)
  local copies, waits for them, and re-layouts  87.8 us (14%)
  other arithmetic  86.4 us (14%)
  Pallas kernels  71.8 us (11%)
  between operations  15.3 us (2%)
    ppermute x48, waiting for transfers between devices, swap(): return lax.ppermute(value, axis, [(0, 1), (1, 0)])  101 us
    ppermute x48, starting transfers between devices, swap(): return lax.ppermute(value, axis, [(0, 1), (1, 0)])  47 us
    dot_general x7, matrix products, contract_cols(): lax.dot_general(left, right, (((1,), (1,)), ((), ())), preferred_element_...  40.9 us
    dot_general x5, matrix products, contract_rows(): lax.dot_general(left, right, (((0,), (0,)), ((), ())), preferred_element_...  37.8 us
    unnamed x140, local copies, waits for them, and re-layouts  29.7 us
    pallas_call x1, Pallas kernels, attend_backward(): pl.pallas_call(backward_kernel, grid=(pairs + 1,), in_specs=[pl.BlockSpec...  29.1 us
    pallas_call x1, Pallas kernels, run_units(): pl.pallas_call(units_kernel, grid=(count // block,), in_specs=[pl.BlockSp...  27.5 us
    ppermute x3, waiting for transfers between devices, rotations(): lax.ppermute(value, 'z', [((i + r) % depth, i) for i in range(depth)])  17.1 us
  transfers between devices with their start and end apart: 66, of which 17 were waited for; matrix products, arithmetic and copies ran while one was open for 38% of the time, Pallas kernels for 7%

profile of v6, /device:TPU:11, one launch (start us, length us, event | category | flops | bytes accessed | tf_op | source)
XLA Modules:
  0.0 617.1 jit_solution(17788021837327325294)
XLA Ops:
  10.5 4.3 all-to-all-start
  15.1 4.5 all-to-all-done
  30.1 17.1 %collective-permute-done.3 = bf16[256,640]{1,0:T(8,128)(2,1)} collective-permute-done((bf16[256,640]{1,0:T(8,128)(2,1)S(1)}, bf16[256,640]{1,0:T(8,128)(2,1)}, u32[]{:S(2)}, u32[]{:S(2)}) %collective-permute-start.3) | collective-permute-done | bytes 327712 | tf_op jit(solution)/shard_map/ppermute | solution.py:264
  51.5 2.9 collective-permute-start.1
  54.8 5.0 reshape.252
  59.8 3.9 copy.116
  63.7 4.0 reshape.253
  76.4 3.4 collective-permute-done.4
  79.9 7.0 %collective-permute-done.6 = bf16[256,640]{1,0:T(8,128)(2,1)S(1)} collective-permute-done((bf16[256,640]{1,0:T(8,128)(2,1)}, bf16[256,640]{1,0:T(8,128)(2,1)S(1)}, u32[]{:S(2)}, u32[]{:S(2)}) %collective-permute-start.6) | collective-permute-done | bytes 327712 | tf_op jit(solution)/shard_map/ppermute | solution.py:230
  86.9 6.9 %collective-permute-done.8 = bf16[256,640]{1,0:T(8,128)(2,1)S(1)} collective-permute-done((bf16[256,640]{1,0:T(8,128)(2,1)}, bf16[256,640]{1,0:T(8,128)(2,1)S(1)}, u32[]{:S(2)}, u32[]{:S(2)}) %collective-permute-start.8) | collective-permute-done | bytes 327712 | tf_op jit(solution)/shard_map/ppermute | solution.py:230
  93.8 6.5 %all-to-all-start.1 = ((bf16[8,64,1408]{2,1,0:T(8,128)(2,1)}), bf16[8,64,1408]{2,1,0:T(8,128)(2,1)}, u32[]{:S(2)}, u32[]{:S(2)}) async-start(bf16[8,64,1408]{2,1,0:T(8,128)(2,1)} %concatenate.57), calls=%async_computation.1 | async-start | bytes 2883584 | tf_op jit(solution)/shard_map/all_to_all | solution.py:429
  112.1 5.2 convolution_convert_fusion.10.query_ref.both_ref
  117.2 15.2 %attend_forward.1 = bf16[1024,512]{1,0:T(8,128)(2,1)S(1)} custom-call(bf16[1024,640]{1,0:T(8,128)(2,1)S(1)} %convolution_convert_fusion.10.query_ref.both_ref, bf16[1024,640]{1,0:T(8,128)(2,1)S(1)} %convolution_convert_fusion.10.query_ref.both_ref, f32[1024,128]{1,0:T(8,128)S(1)} %get-tuple-element.184.cos_ref, f32[1024,128]{1,0:T(8,128)S(1)} %get-tuple-element.185.sin_ref, ...), custom_call_target="tpu_custom_call" | custom-call | flops 12884901888 | bytes 3932160 | tf_op jit(solution)/shard_map/attend_forward/pallas_call | solution.py:169
  134.9 5.5 all-to-all-start.2
  146.5 17.7 %collective-permute-done.14 = bf16[4,32,2048]{2,1,0:T(8,128)(2,1)} collective-permute-done((bf16[4,32,2048]{2,1,0:T(8,128)(2,1)S(1)}, bf16[4,32,2048]{2,1,0:T(8,128)(2,1)}, u32[]{:S(2)}, u32[]{:S(2)}) %collective-permute-start.14) | collective-permute-done | bytes 524320 | tf_op jit(solution)/shard_map/ppermute | solution.py:230
  172.0 6.2 %collective-permute-done.10 = bf16[256,2048]{1,0:T(8,128)(2,1)} collective-permute-done((bf16[256,2048]{1,0:T(8,128)(2,1)}, bf16[256,2048]{1,0:T(8,128)(2,1)}, u32[]{:S(2)}, u32[]{:S(2)}) %collective-permute-start.10) | collective-permute-done | bytes 1048608 | tf_op jit(solution)/shard_map/ppermute | solution.py:230
  180.4 2.5 multiply_reduce_fusion.3
  185.6 21.6 %collective-permute-done.19 = bf16[256,2048]{1,0:T(8,128)(2,1)S(1)} collective-permute-done((bf16[256,2048]{1,0:T(8,128)(2,1)S(1)}, bf16[256,2048]{1,0:T(8,128)(2,1)S(1)}, u32[]{:S(2)}, u32[]{:S(2)}) %collective-permute-start.19) | collective-permute-done | bytes 1048608 | tf_op jit(solution)/shard_map/ppermute | solution.py:230
  211.5 3.0 collective-permute-start.30
  218.3 4.0 pad_maximum_fusion.down_ref
  222.2 3.5 collective-permute-start.31
  225.8 2.4 collective-permute-start.24
  230.6 3.3 collective-permute-start.23
  240.2 2.4 constant_dynamic-update-slice_fusion.15
  245.7 2.3 constant_dynamic-update-slice_fusion.13
  250.4 2.3 constant_dynamic-update-slice_fusion.11
  254.2 2.4 copy-done.51
  257.6 27.5 %units.1 = (bf16[2048,704]{1,0:T(8,128)(2,1)S(1)}, bf16[2048,1408]{1,0:T(8,128)(2,1)}) custom-call(bf16[2048,2048]{1,0:T(8,128)(2,1)} %copy-done.51, bf16[2048,2048]{1,0:T(8,128)(2,1)} %constant_dynamic-update-slice_fusion.9.out_ref, bf16[2048,1408]{1,0:T(8,128)(2,1)} %all-gather.5.cloned.1.call-done.w_ref, bf16[768,2048]{1,0:T(8,128)(2,1)} %pad_maximum_fusion.down_ref), custom_call_target="tpu_custom_call" | custom-call | flops 17716740096 | bytes 34078720 | tf_op jit(solution)/shard_map/units/pallas_call | solution.py:371
  286.8 16.6 %convolution_convert_fusion = bf16[2048,1408]{1,0:T(8,128)(2,1)} fusion(bf16[2048,2048]{1,0:T(8,128)(2,1)S(1)} %copy-done.52, bf16[2048,1408]{1,0:T(8,128)(2,1)} %get-tuple-element.88), kind=kOutput, calls=%fused_computation.5 | convolution fusion | flops 11814043648 | bytes 19922944 | tf_op jit(solution)/shard_map/dot_general | solution.py:48
  303.5 8.0 %convolution_convert_fusion.8 = bf16[512,2048]{1,0:T(8,128)(2,1)} fusion(bf16[2048,1408]{1,0:T(8,128)(2,1)} %all-gather.5.cloned.1.call-done.w_ref, bf16[2048,1408]{1,0:T(8,128)(2,1)} %get-tuple-element.88), kind=kOutput, calls=%fused_computation.25 | convolution fusion | flops 2953838592 | bytes 9306112 | tf_op jit(solution)/shard_map/dot_general | solution.py:52
  311.4 6.1 convolution_convert_fusion.7
  318.2 8.5 %add_convert_fusion.5 = bf16[512,2048]{1,0:T(8,128)(2,1)} fusion(bf16[512,2048]{1,0:T(8,128)(2,1)} %collective-permute-done.33, bf16[2048,1408]{1,0:T(8,128)(2,1)} %all-gather.5.cloned.1.call-done.w_ref, bf16[2048,1408]{1,0:T(8,128)(2,1)} %get-tuple-element.88), kind=kOutput, calls=%fused_computation.12 | convolution fusion | flops 2955935744 | bytes 11403264 | tf_op jit(solution)/shard_map/dot_general | solution.py:52
  326.6 7.3 %add_convert_fusion.4 = bf16[512,2048]{1,0:T(8,128)(2,1)S(1)} fusion(bf16[512,2048]{1,0:T(8,128)(2,1)} %collective-permute-done.34, bf16[2048,1408]{1,0:T(8,128)(2,1)} %all-gather.5.cloned.1.call-done.w_ref, bf16[2048,1408]{1,0:T(8,128)(2,1)} %get-tuple-element.88), kind=kOutput, calls=%fused_computation.11 | convolution fusion | flops 2955935744 | bytes 11403264 | tf_op jit(solution)/shard_map/dot_general | solution.py:52
  334.0 3.1 convolution_convert_fusion.5
  337.1 3.1 convolution_convert_fusion.4
  348.3 5.7 add_convert_fusion.3
  354.0 13.4 %collective-permute-done.36 = bf16[256,2048]{1,0:T(8,128)(2,1)} collective-permute-done((bf16[256,2048]{1,0:T(8,128)(2,1)}, bf16[256,2048]{1,0:T(8,128)(2,1)}, u32[]{:S(2)}, u32[]{:S(2)}) %collective-permute-start.36) | collective-permute-done | bytes 1048608 | tf_op jit(solution)/shard_map/ppermute | solution.py:230
  367.4 4.7 add_convert_fusion.2
  372.1 21.8 %collective-permute-done.40 = bf16[256,2048]{1,0:T(8,128)(2,1)S(1)} collective-permute-done((bf16[256,2048]{1,0:T(8,128)(2,1)S(1)}, bf16[256,2048]{1,0:T(8,128)(2,1)S(1)}, u32[]{:S(2)}, u32[]{:S(2)}) %collective-permute-start.40) | collective-permute-done | bytes 1048608 | tf_op jit(solution)/shard_map/ppermute | solution.py:230
  396.1 4.1 fusion.61
  400.1 3.6 convolution_convert_fusion.9
  403.7 3.2 convolution_convert_fusion.1
  408.0 5.6 maximum_convert_fusion
  417.9 4.8 all-to-all-start.3
  425.1 10.7 %convolution_convert_fusion.2 = bf16[704,2048]{1,0:T(8,128)(2,1)} fusion(bf16[2048,704]{1,0:T(8,128)(2,1)} %copy-done, bf16[2048,2048]{1,0:T(8,128)(2,1)} %constant_dynamic-update-slice_fusion.9.out_ref), kind=kOutput, calls=%fused_computation.18 | convolution fusion | flops 5907021824 | bytes 14155776 | tf_op jit(solution)/shard_map/dot_general | solution.py:48
  435.9 16.8 %all-to-all-done.3 = bf16[256,4,512]{2,0,1:T(8,128)(2,1)S(1)} async-done(((bf16[256,4,512]{2,0,1:T(8,128)(2,1)}), bf16[256,4,512]{2,0,1:T(8,128)(2,1)S(1)}, u32[]{:S(2)}, u32[]{:S(2)}) %all-to-all-start.3) | async-done | bytes 1048608 | tf_op jit(solution)/shard_map/all_to_all | solution.py:497
  452.7 3.0 add_convert_fusion.7
  457.0 3.5 add_convert_fusion
  466.7 29.1 %attend_backward.1 = bf16[1024,640]{1,0:T(8,128)(2,1)S(1)} custom-call(bf16[1024,640]{1,0:T(8,128)(2,1)S(1)} %copy-done.4, bf16[1024,640]{1,0:T(8,128)(2,1)S(1)} %copy-done.4, bf16[1024,512]{1,0:T(8,128)(2,1)S(1)} %bitcast.224, f32[1024,128]{1,0:T(8,128)S(1)} %get-tuple-element.184.cos_ref, f32[1024,128]{1,0:T(8,128)S(1)} %get-tuple-element.185.sin_ref, ...), custom_call_target="tpu_custom_call" | custom-call | flops 32212254720 | bytes 5242880 | tf_op jit(solution)/shard_map/attend_backward/pallas_call | solution.py:196
  495.8 6.4 %all-to-all-start.4 = ((bf16[8,64,1408]{2,1,0:T(8,128)(2,1)}), bf16[8,64,1408]{2,1,0:T(8,128)(2,1)}, u32[]{:S(2)}, u32[]{:S(2)}) async-start(bf16[8,64,1408]{2,1,0:T(8,128)(2,1)} %bitcast.247), calls=%async_computation.5 | async-start | bytes 2883584 | tf_op jit(solution)/shard_map/all_to_all | solution.py:509
  502.3 6.0 fusion
  508.2 2.9 fusion.17
  512.6 7.8 %all-to-all-done.4 = bf16[8,64,1408]{2,1,0:T(8,128)(2,1)} async-done(((bf16[8,64,1408]{2,1,0:T(8,128)(2,1)}), bf16[8,64,1408]{2,1,0:T(8,128)(2,1)}, u32[]{:S(2)}, u32[]{:S(2)}) %all-to-all-start.4) | async-done | bytes 1441824 | tf_op jit(solution)/shard_map/all_to_all | solution.py:509
  520.5 3.8 convolution_convert_fusion.6
  524.9 3.8 convolution_convert_fusion.3
  540.2 3.6 add_convert_fusion.1
  550.6 3.2 stack.81
  554.9 2.5 convert_bitcast_fusion
  557.4 5.5 reshape.276
  562.9 3.2 fusion.1
  566.1 8.2 %all-to-all-start.5 = ((bf16[16,64,640]{2,1,0:T(8,128)(2,1)}), bf16[16,64,640]{2,1,0:T(8,128)(2,1)}, u32[]{:S(2)}, u32[]{:S(2)}) async-start(bf16[16,64,640]{2,1,0:T(8,128)(2,1)} %bitcast.236), calls=%async_computation.7 | async-start | bytes 2621440 | tf_op jit(solution)/shard_map/all_to_all | solution.py:512
  574.3 4.6 broadcast_multiply_fusion
  583.2 3.4 fusion.5
  589.5 15.5 %all-to-all-done.5 = bf16[16,64,640]{2,1,0:T(8,128)(2,1)} async-done(((bf16[16,64,640]{2,1,0:T(8,128)(2,1)}), bf16[16,64,640]{2,1,0:T(8,128)(2,1)}, u32[]{:S(2)}, u32[]{:S(2)}) %all-to-all-start.5) | async-done | bytes 1310752 | tf_op jit(solution)/shard_map/all_to_all | solution.py:512
  (349 shorter events, 146.2 us)
Async XLA Ops:
  7.2 99.2 %all-gather.9.cloned.1.call-start = ((), (), s32[]{:S(2)}) async-start(), calls=%async_computation.12 | async-start | bytes 1310720 | tf_op jit(solution)/shard_map/all_gather | solution.py:424
  10.5 9.1 %all-to-all-start = ((bf16[4,64,640]{2,1,0:T(8,128)(2,1)}), bf16[4,64,640]{2,1,0:T(8,128)(2,1)S(1)}, u32[]{:S(2)}, u32[]{:S(2)}) async-start(bf16[4,64,640]{2,1,0:T(8,128)(2,1)} %copy.112), calls=%async_computation | async-start | bytes 655360 | tf_op jit(solution)/shard_map/all_to_all | solution.py:410
  14.8 199.7 %all-gather.7.cloned.1.call-start = ((), (), s32[]{:S(2)}) async-start(), calls=%async_computation.9 | async-start | bytes 3604480 | tf_op jit(solution)/shard_map/all_gather | solution.py:427
  19.6 28.0 %collective-permute-start = (bf16[256,2048]{1,0:T(8,128)(2,1)S(1)}, bf16[256,2048]{1,0:T(8,128)(2,1)}, u32[]{:S(2)}, u32[]{:S(2)}) collective-permute-start(bf16[256,2048]{1,0:T(8,128)(2,1)S(1)} %copy-done.12), channel_id=1, source_target_pairs={{0,2},{2,0},{1,3},{3,1},{4,6},{6,4},{5,7},{7,5},{8,10},{10,8},{9,1... | collective-permute-start | bytes 3145736 | tf_op jit(solution)/shard_map/ppermute | solution.py:230
  23.1 24.1 %collective-permute-start.3 = (bf16[256,640]{1,0:T(8,128)(2,1)S(1)}, bf16[256,640]{1,0:T(8,128)(2,1)}, u32[]{:S(2)}, u32[]{:S(2)}) collective-permute-start(bf16[256,640]{1,0:T(8,128)(2,1)S(1)} %bitcast.249), channel_id=1, source_target_pairs={{8,0},{16,8},{24,16},{0,24},{9,1},{17,9},{25,17},{1,25},{10,2},{18... | collective-permute-start | bytes 983048 | tf_op jit(solution)/shard_map/ppermute | solution.py:264
  24.1 46.1 %collective-permute-start.2 = (bf16[256,640]{1,0:T(8,128)(2,1)S(1)}, bf16[256,640]{1,0:T(8,128)(2,1)}, u32[]{:S(2)}, u32[]{:S(2)}) collective-permute-start(bf16[256,640]{1,0:T(8,128)(2,1)S(1)} %bitcast.250), channel_id=1, source_target_pairs={{0,4},{4,0},{1,5},{5,1},{2,6},{6,2},{3,7},{7,3},{8,12},{12,8},{9,1... | collective-permute-start | bytes 983048 | tf_op jit(solution)/shard_map/ppermute | solution.py:230
  25.5 45.8 %collective-permute-start.5 = (bf16[256,640]{1,0:T(8,128)(2,1)S(1)}, bf16[256,640]{1,0:T(8,128)(2,1)}, u32[]{:S(2)}, u32[]{:S(2)}) collective-permute-start(bf16[256,640]{1,0:T(8,128)(2,1)S(1)} %bitcast.251), channel_id=1, source_target_pairs={{16,0},{24,8},{0,16},{8,24},{17,1},{25,9},{1,17},{9,25},{18,2},{26... | collective-permute-start | bytes 983048 | tf_op jit(solution)/shard_map/ppermute | solution.py:264
  27.9 43.8 %collective-permute-start.7 = (bf16[256,640]{1,0:T(8,128)(2,1)S(1)}, bf16[256,640]{1,0:T(8,128)(2,1)}, u32[]{:S(2)}, u32[]{:S(2)}) collective-permute-start(bf16[256,640]{1,0:T(8,128)(2,1)S(1)} %bitcast.252), channel_id=1, source_target_pairs={{24,0},{0,8},{8,16},{16,24},{25,1},{1,9},{9,17},{17,25},{26,2},{2,... | collective-permute-start | bytes 983048 | tf_op jit(solution)/shard_map/ppermute | solution.py:264
  47.2 59.2 %collective-permute-start.9 = (bf16[256,2048]{1,0:T(8,128)(2,1)}, bf16[256,2048]{1,0:T(8,128)(2,1)}, u32[]{:S(2)}, u32[]{:S(2)}) collective-permute-start(bf16[256,2048]{1,0:T(8,128)(2,1)} %param.17), channel_id=1, source_target_pairs={{0,2},{2,0},{1,3},{3,1},{4,6},{6,4},{5,7},{7,5},{8,10},{10,8},{9,1... | collective-permute-start | bytes 3145736 | tf_op jit(solution)/shard_map/ppermute | solution.py:230
  51.5 56.4 %collective-permute-start.1 = (bf16[2,256,2048]{2,1,0:T(8,128)(2,1)}, bf16[2,256,2048]{2,1,0:T(8,128)(2,1)}, u32[]{:S(2)}, u32[]{:S(2)}) collective-permute-start(bf16[2,256,2048]{2,1,0:T(8,128)(2,1)} %pad_maximum_fusion.1), channel_id=1, source_target_pairs={{0,1},{1,0},{2,3},{3,2},{4,5},{5,4},{6,7},{7,6},{8,9},{9,8},{10,11... | collective-permute-start | bytes 6291464 | tf_op jit(solution)/shard_map/ppermute | solution.py:230
  70.2 9.7 %collective-permute-start.4 = (bf16[256,640]{1,0:T(8,128)(2,1)}, bf16[256,640]{1,0:T(8,128)(2,1)S(1)}, u32[]{:S(2)}, u32[]{:S(2)}) collective-permute-start(bf16[256,640]{1,0:T(8,128)(2,1)} %collective-permute-done.3), channel_id=1, source_target_pairs={{0,4},{4,0},{1,5},{5,1},{2,6},{6,2},{3,7},{7,3},{8,12},{12,8},{9,1... | collective-permute-start | bytes 983048 | tf_op jit(solution)/shard_map/ppermute | solution.py:230
  71.3 15.6 %collective-permute-start.6 = (bf16[256,640]{1,0:T(8,128)(2,1)}, bf16[256,640]{1,0:T(8,128)(2,1)S(1)}, u32[]{:S(2)}, u32[]{:S(2)}) collective-permute-start(bf16[256,640]{1,0:T(8,128)(2,1)} %collective-permute-done.5), channel_id=1, source_target_pairs={{0,4},{4,0},{1,5},{5,1},{2,6},{6,2},{3,7},{7,3},{8,12},{12,8},{9,1... | collective-permute-start | bytes 983048 | tf_op jit(solution)/shard_map/ppermute | solution.py:230
  71.7 22.1 %collective-permute-start.8 = (bf16[256,640]{1,0:T(8,128)(2,1)}, bf16[256,640]{1,0:T(8,128)(2,1)S(1)}, u32[]{:S(2)}, u32[]{:S(2)}) collective-permute-start(bf16[256,640]{1,0:T(8,128)(2,1)} %collective-permute-done.7), channel_id=1, source_target_pairs={{0,4},{4,0},{1,5},{5,1},{2,6},{6,2},{3,7},{7,3},{8,12},{12,8},{9,1... | collective-permute-start | bytes 983048 | tf_op jit(solution)/shard_map/ppermute | solution.py:230
  93.8 39.7 %all-to-all-start.1 = ((bf16[8,64,1408]{2,1,0:T(8,128)(2,1)}), bf16[8,64,1408]{2,1,0:T(8,128)(2,1)}, u32[]{:S(2)}, u32[]{:S(2)}) async-start(bf16[8,64,1408]{2,1,0:T(8,128)(2,1)} %concatenate.57), calls=%async_computation.1 | async-start | bytes 2883584 | tf_op jit(solution)/shard_map/all_to_all | solution.py:429
  106.4 34.5 %collective-permute-start.13 = (bf16[4,64,2048]{2,1,0:T(8,128)(2,1)}, bf16[4,64,2048]{2,1,0:T(8,128)(2,1)}, u32[]{:S(2)}, u32[]{:S(2)}) collective-permute-start(bf16[4,64,2048]{2,1,0:T(8,128)(2,1)} %bitcast.31), channel_id=1, source_target_pairs={{0,4},{4,0},{1,5},{5,1},{2,6},{6,2},{3,7},{7,3},{8,12},{12,8},{9,1... | collective-permute-start | bytes 3145736 | tf_op jit(solution)/shard_map/ppermute | solution.py:230
  107.6 34.5 %collective-permute-start.11 = (bf16[4,64,2048]{2,1,0:T(8,128)(2,1)}, bf16[4,64,2048]{2,1,0:T(8,128)(2,1)}, u32[]{:S(2)}, u32[]{:S(2)}) collective-permute-start(bf16[4,64,2048]{2,1,0:T(8,128)(2,1)} %bitcast.31), channel_id=1, source_target_pairs={{0,2},{2,0},{1,3},{3,1},{4,6},{6,4},{5,7},{7,5},{8,10},{10,8},{9,1... | collective-permute-start | bytes 3145736 | tf_op jit(solution)/shard_map/ppermute | solution.py:230
  134.9 30.7 %all-to-all-start.2 = ((bf16[4,256,512]{1,2,0:T(8,128)(2,1)}), bf16[4,256,512]{1,2,0:T(8,128)(2,1)S(1)}, u32[]{:S(2)}, u32[]{:S(2)}) async-start(bf16[4,256,512]{1,2,0:T(8,128)(2,1)} %copy.117), calls=%async_computation.2 | async-start | bytes 2097152 | tf_op jit(solution)/shard_map/all_to_all | solution.py:441
  140.4 117.2 %all-gather.5.cloned.1.call-start = ((), (), s32[]{:S(2)}) async-start(), calls=%async_computation.8 | async-start | bytes 7208960 | tf_op jit(solution)/shard_map/all_gather | solution.py:430
  142.0 22.3 %collective-permute-start.14 = (bf16[4,32,2048]{2,1,0:T(8,128)(2,1)S(1)}, bf16[4,32,2048]{2,1,0:T(8,128)(2,1)}, u32[]{:S(2)}, u32[]{:S(2)}) collective-permute-start(bf16[4,32,2048]{2,1,0:T(8,128)(2,1)S(1)} %slice.263), channel_id=1, source_target_pairs={{0,2},{2,0},{1,3},{3,1},{4,6},{6,4},{5,7},{7,5},{8,10},{10,8},{9,1... | collective-permute-start | bytes 1572872 | tf_op jit(solution)/shard_map/ppermute | solution.py:230
  143.2 21.1 %collective-permute-start.12 = (bf16[4,32,2048]{2,1,0:T(8,128)(2,1)S(1)}, bf16[4,32,2048]{2,1,0:T(8,128)(2,1)}, u32[]{:S(2)}, u32[]{:S(2)}) collective-permute-start(bf16[4,32,2048]{2,1,0:T(8,128)(2,1)S(1)} %slice.262), channel_id=1, source_target_pairs={{0,4},{4,0},{1,5},{5,1},{2,6},{6,2},{3,7},{7,3},{8,12},{12,8},{9,1... | collective-permute-start | bytes 1572872 | tf_op jit(solution)/shard_map/ppermute | solution.py:230
  143.3 35.0 %collective-permute-start.10 = (bf16[256,2048]{1,0:T(8,128)(2,1)}, bf16[256,2048]{1,0:T(8,128)(2,1)}, u32[]{:S(2)}, u32[]{:S(2)}) collective-permute-start(bf16[256,2048]{1,0:T(8,128)(2,1)} %param.17), channel_id=1, source_target_pairs={{0,4},{4,0},{1,5},{5,1},{2,6},{6,2},{3,7},{7,3},{8,12},{12,8},{9,1... | collective-permute-start | bytes 3145736 | tf_op jit(solution)/shard_map/ppermute | solution.py:230
  144.7 34.0 %collective-permute-start.18 = (bf16[4,64,2048]{2,1,0:T(8,128)(2,1)}, bf16[4,64,2048]{2,1,0:T(8,128)(2,1)}, u32[]{:S(2)}, u32[]{:S(2)}) collective-permute-start(bf16[4,64,2048]{2,1,0:T(8,128)(2,1)} %bitcast.31), channel_id=1, source_target_pairs={{0,1},{1,0},{2,3},{3,2},{4,5},{5,4},{6,7},{7,6},{8,9},{9,8},{10,11... | collective-permute-start | bytes 3145736 | tf_op jit(solution)/shard_map/ppermute | solution.py:230
  146.3 319.1 %reduce-scatter.3.cloned.1.call-start = ((), (), s32[]{:S(2)}) async-start(), calls=%async_computation.10 | async-start | bytes 7208960 | tf_op jit(solution)/shard_map/reduce_scatter | solution.py:464
  165.6 12.7 %collective-permute-start.15 = (bf16[4,64,2048]{2,1,0:T(8,128)(2,1)S(1)}, bf16[4,64,2048]{2,1,0:T(8,128)(2,1)S(1)}, u32[]{:S(2)}, u32[]{:S(2)}) collective-permute-start(bf16[4,64,2048]{2,1,0:T(8,128)(2,1)S(1)} %pad_maximum_fusion.2), channel_id=1, source_target_pairs={{0,1},{1,0},{2,3},{3,2},{4,5},{5,4},{6,7},{7,6},{8,9},{9,8},{10,11... | collective-permute-start | bytes 3145736 | tf_op jit(solution)/shard_map/ppermute | solution.py:230
  166.3 12.2 %collective-permute-start.16 = (bf16[4,64,2048]{2,1,0:T(8,128)(2,1)}, bf16[4,64,2048]{2,1,0:T(8,128)(2,1)S(1)}, u32[]{:S(2)}, u32[]{:S(2)}) collective-permute-start(bf16[4,64,2048]{2,1,0:T(8,128)(2,1)} %collective-permute-done.11), channel_id=1, source_target_pairs={{0,1},{1,0},{2,3},{3,2},{4,5},{5,4},{6,7},{7,6},{8,9},{9,8},{10,11... | collective-permute-start | bytes 3145736 | tf_op jit(solution)/shard_map/ppermute | solution.py:230
  166.3 12.2 %collective-permute-start.17 = (bf16[4,64,2048]{2,1,0:T(8,128)(2,1)}, bf16[4,64,2048]{2,1,0:T(8,128)(2,1)S(1)}, u32[]{:S(2)}, u32[]{:S(2)}) collective-permute-start(bf16[4,64,2048]{2,1,0:T(8,128)(2,1)} %collective-permute-done.13), channel_id=1, source_target_pairs={{0,1},{1,0},{2,3},{3,2},{4,5},{5,4},{6,7},{7,6},{8,9},{9,8},{10,11... | collective-permute-start | bytes 3145736 | tf_op jit(solution)/shard_map/ppermute | solution.py:230
  183.8 23.4 %collective-permute-start.19 = (bf16[256,2048]{1,0:T(8,128)(2,1)S(1)}, bf16[256,2048]{1,0:T(8,128)(2,1)S(1)}, u32[]{:S(2)}, u32[]{:S(2)}) collective-permute-start(bf16[256,2048]{1,0:T(8,128)(2,1)S(1)} %multiply_convert_fusion.2), channel_id=1, source_target_pairs={{0,2},{2,0},{1,3},{3,1},{4,6},{6,4},{5,7},{7,5},{8,10},{10,8},{9,1... | collective-permute-start | bytes 3145736 | tf_op jit(solution)/shard_map/ppermute | solution.py:230
  185.6 22.9 %collective-permute-start.21 = (bf16[256,2048]{1,0:T(8,128)(2,1)S(1)}, bf16[256,2048]{1,0:T(8,128)(2,1)S(1)}, u32[]{:S(2)}, u32[]{:S(2)}) collective-permute-start(bf16[256,2048]{1,0:T(8,128)(2,1)S(1)} %multiply_convert_fusion.2), channel_id=1, source_target_pairs={{0,4},{4,0},{1,5},{5,1},{2,6},{6,2},{3,7},{7,3},{8,12},{12,8},{9,1... | collective-permute-start | bytes 3145736 | tf_op jit(solution)/shard_map/ppermute | solution.py:230
  208.1 14.1 %collective-permute-start.20 = (bf16[128,2048]{1,0:T(8,128)(2,1)}, bf16[128,2048]{1,0:T(8,128)(2,1)}, u32[]{:S(2)}, u32[]{:S(2)}) collective-permute-start(bf16[128,2048]{1,0:T(8,128)(2,1)} %slice.264), channel_id=1, source_target_pairs={{0,4},{4,0},{1,5},{5,1},{2,6},{6,2},{3,7},{7,3},{8,12},{12,8},{9,1... | collective-permute-start | bytes 1572872 | tf_op jit(solution)/shard_map/ppermute | solution.py:230
  210.3 15.5 %collective-permute-start.22 = (bf16[128,2048]{1,0:T(8,128)(2,1)}, bf16[128,2048]{1,0:T(8,128)(2,1)}, u32[]{:S(2)}, u32[]{:S(2)}) collective-permute-start(bf16[128,2048]{1,0:T(8,128)(2,1)} %slice.265), channel_id=1, source_target_pairs={{0,2},{2,0},{1,3},{3,1},{4,6},{6,4},{5,7},{7,5},{8,10},{10,8},{9,1... | collective-permute-start | bytes 1572872 | tf_op jit(solution)/shard_map/ppermute | solution.py:230
  211.5 34.2 %collective-permute-start.30 = (bf16[256,2048]{1,0:T(8,128)(2,1)}, bf16[256,2048]{1,0:T(8,128)(2,1)}, u32[]{:S(2)}, u32[]{:S(2)}) collective-permute-start(bf16[256,2048]{1,0:T(8,128)(2,1)} %param.17), channel_id=1, source_target_pairs={{0,1},{1,0},{2,3},{3,2},{4,5},{5,4},{6,7},{7,6},{8,9},{9,8},{10,11... | collective-permute-start | bytes 3145736 | tf_op jit(solution)/shard_map/ppermute | solution.py:230
  215.6 15.0 %collective-permute-start.27 = (bf16[128,2048]{1,0:T(8,128)(2,1)S(1)}, bf16[128,2048]{1,0:T(8,128)(2,1)S(1)}, u32[]{:S(2)}, u32[]{:S(2)}) collective-permute-start(bf16[128,2048]{1,0:T(8,128)(2,1)S(1)} %slice.209), channel_id=1, source_target_pairs={{0,4},{4,0},{1,5},{5,1},{2,6},{6,2},{3,7},{7,3},{8,12},{12,8},{9,1... | collective-permute-start | bytes 1572872 | tf_op jit(solution)/shard_map/ppermute | solution.py:230
  218.2 15.7 %collective-permute-start.28 = (bf16[128,2048]{1,0:T(8,128)(2,1)S(1)}, bf16[128,2048]{1,0:T(8,128)(2,1)S(1)}, u32[]{:S(2)}, u32[]{:S(2)}) collective-permute-start(bf16[128,2048]{1,0:T(8,128)(2,1)S(1)} %slice.210), channel_id=1, source_target_pairs={{0,2},{2,0},{1,3},{3,1},{4,6},{6,4},{5,7},{7,5},{8,10},{10,8},{9,1... | collective-permute-start | bytes 1572872 | tf_op jit(solution)/shard_map/ppermute | solution.py:230
  222.2 30.7 %collective-permute-start.31 = (bf16[256,2048]{1,0:T(8,128)(2,1)}, bf16[256,2048]{1,0:T(8,128)(2,1)S(1)}, u32[]{:S(2)}, u32[]{:S(2)}) collective-permute-start(bf16[256,2048]{1,0:T(8,128)(2,1)} %collective-permute-done.9), channel_id=1, source_target_pairs={{0,1},{1,0},{2,3},{3,2},{4,5},{5,4},{6,7},{7,6},{8,9},{9,8},{10,11... | collective-permute-start | bytes 3145736 | tf_op jit(solution)/shard_map/ppermute | solution.py:230
  225.8 17.0 %collective-permute-start.24 = (bf16[256,2048]{1,0:T(8,128)(2,1)S(1)}, bf16[256,2048]{1,0:T(8,128)(2,1)S(1)}, u32[]{:S(2)}, u32[]{:S(2)}) collective-permute-start(bf16[256,2048]{1,0:T(8,128)(2,1)S(1)} %copy-done.43), channel_id=1, source_target_pairs={{0,1},{1,0},{2,3},{3,2},{4,5},{5,4},{6,7},{7,6},{8,9},{9,8},{10,11... | collective-permute-start | bytes 3145736 | tf_op jit(solution)/shard_map/ppermute | solution.py:230
  230.6 12.0 %collective-permute-start.23 = (bf16[256,2048]{1,0:T(8,128)(2,1)S(1)}, bf16[256,2048]{1,0:T(8,128)(2,1)S(1)}, u32[]{:S(2)}, u32[]{:S(2)}) collective-permute-start(bf16[256,2048]{1,0:T(8,128)(2,1)S(1)} %pad_maximum_fusion.3), channel_id=1, source_target_pairs={{0,1},{1,0},{2,3},{3,2},{4,5},{5,4},{6,7},{7,6},{8,9},{9,8},{10,11... | collective-permute-start | bytes 3145736 | tf_op jit(solution)/shard_map/ppermute | solution.py:230
  234.0 10.1 %collective-permute-start.29 = (bf16[256,2048]{1,0:T(8,128)(2,1)S(1)}, bf16[256,2048]{1,0:T(8,128)(2,1)S(1)}, u32[]{:S(2)}, u32[]{:S(2)}) collective-permute-start(bf16[256,2048]{1,0:T(8,128)(2,1)S(1)} %pad_maximum_fusion.4), channel_id=1, source_target_pairs={{0,1},{1,0},{2,3},{3,2},{4,5},{5,4},{6,7},{7,6},{8,9},{9,8},{10,11... | collective-permute-start | bytes 3145736 | tf_op jit(solution)/shard_map/ppermute | solution.py:230
  242.7 11.5 %collective-permute-start.32 = (bf16[256,2048]{1,0:T(8,128)(2,1)}, bf16[256,2048]{1,0:T(8,128)(2,1)S(1)}, u32[]{:S(2)}, u32[]{:S(2)}) collective-permute-start(bf16[256,2048]{1,0:T(8,128)(2,1)} %collective-permute-done.10), channel_id=1, source_target_pairs={{0,1},{1,0},{2,3},{3,2},{4,5},{5,4},{6,7},{7,6},{8,9},{9,8},{10,11... | collective-permute-start | bytes 3145736 | tf_op jit(solution)/shard_map/ppermute | solution.py:230
  242.8 9.9 %collective-permute-start.25 = (bf16[256,2048]{1,0:T(8,128)(2,1)S(1)}, bf16[256,2048]{1,0:T(8,128)(2,1)S(1)}, u32[]{:S(2)}, u32[]{:S(2)}) collective-permute-start(bf16[256,2048]{1,0:T(8,128)(2,1)S(1)} %copy-done.37), channel_id=1, source_target_pairs={{0,1},{1,0},{2,3},{3,2},{4,5},{5,4},{6,7},{7,6},{8,9},{9,8},{10,11... | collective-permute-start | bytes 3145736 | tf_op jit(solution)/shard_map/ppermute | solution.py:230
  317.6 9.0 %collective-permute-start.34 = (bf16[512,2048]{1,0:T(8,128)(2,1)}, bf16[512,2048]{1,0:T(8,128)(2,1)}, u32[]{:S(2)}, u32[]{:S(2)}) collective-permute-start(bf16[512,2048]{1,0:T(8,128)(2,1)} %convolution_convert_fusion.7), channel_id=1, source_target_pairs={{0,1},{1,0},{2,3},{3,2},{4,5},{5,4},{6,7},{7,6},{8,9},{9,8},{10,11... | collective-permute-start | bytes 6291464 | tf_op jit(solution)/shard_map/ppermute | solution.py:230
  337.1 11.2 %collective-permute-start.35 = (bf16[512,2048]{1,0:T(8,128)(2,1)}, bf16[512,2048]{1,0:T(8,128)(2,1)}, u32[]{:S(2)}, u32[]{:S(2)}) collective-permute-start(bf16[512,2048]{1,0:T(8,128)(2,1)} %convolution_convert_fusion.5), channel_id=1, source_target_pairs={{0,1},{1,0},{2,3},{3,2},{4,5},{5,4},{6,7},{7,6},{8,9},{9,8},{10,11... | collective-permute-start | bytes 6291464 | tf_op jit(solution)/shard_map/ppermute | solution.py:230
  340.2 27.2 %collective-permute-start.37 = (bf16[512,2048]{1,0:T(8,128)(2,1)}, bf16[512,2048]{1,0:T(8,128)(2,1)}, u32[]{:S(2)}, u32[]{:S(2)}) collective-permute-start(bf16[512,2048]{1,0:T(8,128)(2,1)} %convolution_convert_fusion.4), channel_id=1, source_target_pairs={{0,1},{1,0},{2,3},{3,2},{4,5},{5,4},{6,7},{7,6},{8,9},{9,8},{10,11... | collective-permute-start | bytes 6291464 | tf_op jit(solution)/shard_map/ppermute | solution.py:230
  342.3 25.1 %collective-permute-start.36 = (bf16[256,2048]{1,0:T(8,128)(2,1)}, bf16[256,2048]{1,0:T(8,128)(2,1)}, u32[]{:S(2)}, u32[]{:S(2)}) collective-permute-start(bf16[256,2048]{1,0:T(8,128)(2,1)} %get-tuple-element.149), channel_id=1, source_target_pairs={{0,2},{2,0},{1,3},{3,1},{4,6},{6,4},{5,7},{7,5},{8,10},{10,8},{9,1... | collective-permute-start | bytes 3145736 | tf_op jit(solution)/shard_map/ppermute | solution.py:230
  346.8 47.1 %collective-permute-start.40 = (bf16[256,2048]{1,0:T(8,128)(2,1)S(1)}, bf16[256,2048]{1,0:T(8,128)(2,1)S(1)}, u32[]{:S(2)}, u32[]{:S(2)}) collective-permute-start(bf16[256,2048]{1,0:T(8,128)(2,1)S(1)} %copy-done.45), channel_id=1, source_target_pairs={{0,4},{4,0},{1,5},{5,1},{2,6},{6,2},{3,7},{7,3},{8,12},{12,8},{9,1... | collective-permute-start | bytes 3145736 | tf_op jit(solution)/shard_map/ppermute | solution.py:230
  348.3 45.6 %collective-permute-start.39 = (bf16[256,2048]{1,0:T(8,128)(2,1)S(1)}, bf16[256,2048]{1,0:T(8,128)(2,1)S(1)}, u32[]{:S(2)}, u32[]{:S(2)}) collective-permute-start(bf16[256,2048]{1,0:T(8,128)(2,1)S(1)} %slice.269), channel_id=1, source_target_pairs={{0,6},{2,4},{4,2},{6,0},{1,7},{3,5},{5,3},{7,1},{8,14},{10,12},{12... | collective-permute-start | bytes 3145736 | tf_op jit(solution)/shard_map/ppermute | solution.py:234
  407.0 50.1 %collective-permute-start.42 = (bf16[1024,2048]{1,0:T(8,128)(2,1)}, bf16[1024,2048]{1,0:T(8,128)(2,1)}, u32[]{:S(2)}, u32[]{:S(2)}) collective-permute-start(bf16[1024,2048]{1,0:T(8,128)(2,1)} %convolution_convert_fusion.1), channel_id=1, source_target_pairs={{0,1},{1,0},{2,3},{3,2},{4,5},{5,4},{6,7},{7,6},{8,9},{9,8},{10,11... | collective-permute-start | bytes 12582920 | tf_op jit(solution)/shard_map/ppermute | solution.py:230
  416.4 36.2 %collective-permute-start.38 = (bf16[256,2048]{1,0:T(8,128)(2,1)}, bf16[256,2048]{1,0:T(8,128)(2,1)}, u32[]{:S(2)}, u32[]{:S(2)}) collective-permute-start(bf16[256,2048]{1,0:T(8,128)(2,1)} %pad_maximum_fusion.5), channel_id=1, source_target_pairs={{0,2},{2,0},{1,3},{3,1},{4,6},{6,4},{5,7},{7,5},{8,10},{10,8},{9,1... | collective-permute-start | bytes 3145736 | tf_op jit(solution)/shard_map/ppermute | solution.py:230
  417.9 34.8 %all-to-all-start.3 = ((bf16[256,4,512]{2,0,1:T(8,128)(2,1)}), bf16[256,4,512]{2,0,1:T(8,128)(2,1)S(1)}, u32[]{:S(2)}, u32[]{:S(2)}) async-start(bf16[256,4,512]{2,0,1:T(8,128)(2,1)} %bitcast.222), calls=%async_computation.3 | async-start | bytes 2097152 | tf_op jit(solution)/shard_map/all_to_all | solution.py:497
  422.7 140.2 %reduce-scatter.5.cloned.1.call-start = ((), (), s32[]{:S(2)}) async-start(), calls=%async_computation.11 | async-start | bytes 3604480 | tf_op jit(solution)/shard_map/reduce_scatter | solution.py:482
  423.7 28.9 %collective-permute-start.43 = (bf16[256,2048]{1,0:T(8,128)(2,1)}, bf16[256,2048]{1,0:T(8,128)(2,1)}, u32[]{:S(2)}, u32[]{:S(2)}) collective-permute-start(bf16[256,2048]{1,0:T(8,128)(2,1)} %pad_maximum_fusion.6), channel_id=1, source_target_pairs={{0,4},{4,0},{1,5},{5,1},{2,6},{6,2},{3,7},{7,3},{8,12},{12,8},{9,1... | collective-permute-start | bytes 3145736 | tf_op jit(solution)/shard_map/ppermute | solution.py:230
  455.6 40.2 %collective-permute-start.41 = (bf16[128,2048]{1,0:T(8,128)(2,1)}, bf16[128,2048]{1,0:T(8,128)(2,1)}, u32[]{:S(2)}, u32[]{:S(2)}) collective-permute-start(bf16[128,2048]{1,0:T(8,128)(2,1)} %get-tuple-element.142), channel_id=1, source_target_pairs={{0,4},{4,0},{1,5},{5,1},{2,6},{6,2},{3,7},{7,3},{8,12},{12,8},{9,1... | collective-permute-start | bytes 1572872 | tf_op jit(solution)/shard_map/ppermute | solution.py:230
  457.0 38.8 %collective-permute-start.44 = (bf16[128,2048]{1,0:T(8,128)(2,1)}, bf16[128,2048]{1,0:T(8,128)(2,1)}, u32[]{:S(2)}, u32[]{:S(2)}) collective-permute-start(bf16[128,2048]{1,0:T(8,128)(2,1)} %get-tuple-element.143), channel_id=1, source_target_pairs={{0,2},{2,0},{1,3},{3,1},{4,6},{6,4},{5,7},{7,5},{8,10},{10,8},{9,1... | collective-permute-start | bytes 1572872 | tf_op jit(solution)/shard_map/ppermute | solution.py:230
  462.8 33.0 %collective-permute-start.45 = (bf16[4,64,2048]{2,1,0:T(8,128)(2,1)}, bf16[4,64,2048]{2,1,0:T(8,128)(2,1)}, u32[]{:S(2)}, u32[]{:S(2)}) collective-permute-start(bf16[4,64,2048]{2,1,0:T(8,128)(2,1)} %pad_maximum_fusion.7), channel_id=1, source_target_pairs={{0,2},{2,0},{1,3},{3,1},{4,6},{6,4},{5,7},{7,5},{8,10},{10,8},{9,1... | collective-permute-start | bytes 3145736 | tf_op jit(solution)/shard_map/ppermute | solution.py:230
  465.3 30.5 %collective-permute-start.46 = (bf16[4,64,2048]{2,1,0:T(8,128)(2,1)}, bf16[4,64,2048]{2,1,0:T(8,128)(2,1)}, u32[]{:S(2)}, u32[]{:S(2)}) collective-permute-start(bf16[4,64,2048]{2,1,0:T(8,128)(2,1)} %pad_maximum_fusion.8), channel_id=1, source_target_pairs={{0,4},{4,0},{1,5},{5,1},{2,6},{6,2},{3,7},{7,3},{8,12},{12,8},{9,1... | collective-permute-start | bytes 3145736 | tf_op jit(solution)/shard_map/ppermute | solution.py:230
  495.8 24.5 %all-to-all-start.4 = ((bf16[8,64,1408]{2,1,0:T(8,128)(2,1)}), bf16[8,64,1408]{2,1,0:T(8,128)(2,1)}, u32[]{:S(2)}, u32[]{:S(2)}) async-start(bf16[8,64,1408]{2,1,0:T(8,128)(2,1)} %bitcast.247), calls=%async_computation.5 | async-start | bytes 2883584 | tf_op jit(solution)/shard_map/all_to_all | solution.py:509
  511.1 19.6 %collective-permute-start.51 = (bf16[2,64,2048]{2,1,0:T(8,128)(2,1)}, bf16[2,64,2048]{2,1,0:T(8,128)(2,1)S(1)}, u32[]{:S(2)}, u32[]{:S(2)}) collective-permute-start(bf16[2,64,2048]{2,1,0:T(8,128)(2,1)} %get-tuple-element.130), channel_id=1, source_target_pairs={{0,2},{2,0},{1,3},{3,1},{4,6},{6,4},{5,7},{7,5},{8,10},{10,8},{9,1... | collective-permute-start | bytes 1572872 | tf_op jit(solution)/shard_map/ppermute | solution.py:230
  511.2 20.3 %collective-permute-start.50 = (bf16[2,64,2048]{2,1,0:T(8,128)(2,1)}, bf16[2,64,2048]{2,1,0:T(8,128)(2,1)S(1)}, u32[]{:S(2)}, u32[]{:S(2)}) collective-permute-start(bf16[2,64,2048]{2,1,0:T(8,128)(2,1)} %get-tuple-element.131), channel_id=1, source_target_pairs={{0,4},{4,0},{1,5},{5,1},{2,6},{6,2},{3,7},{7,3},{8,12},{12,8},{9,1... | collective-permute-start | bytes 1572872 | tf_op jit(solution)/shard_map/ppermute | solution.py:230
  524.4 15.9 %collective-permute-start.48 = (bf16[512,2048]{1,0:T(8,128)(2,1)S(1)}, bf16[512,2048]{1,0:T(8,128)(2,1)S(1)}, u32[]{:S(2)}, u32[]{:S(2)}) collective-permute-start(bf16[512,2048]{1,0:T(8,128)(2,1)S(1)} %convolution_convert_fusion.6), channel_id=1, source_target_pairs={{0,1},{1,0},{2,3},{3,2},{4,5},{5,4},{6,7},{7,6},{8,9},{9,8},{10,11... | collective-permute-start | bytes 6291464 | tf_op jit(solution)/shard_map/ppermute | solution.py:230
  530.0 32.9 %collective-permute-start.47 = (bf16[4,256,640]{2,1,0:T(8,128)(2,1)}, bf16[4,256,640]{2,1,0:T(8,128)(2,1)}, u32[]{:S(2)}, u32[]{:S(2)}) collective-permute-start(bf16[4,256,640]{2,1,0:T(8,128)(2,1)} %dynamic-slice_bitcast_fusion), channel_id=1, source_target_pairs={{0,4},{4,0},{1,5},{5,1},{2,6},{6,2},{3,7},{7,3},{8,12},{12,8},{9,1... | collective-permute-start | bytes 3932168 | tf_op jit(solution)/shard_map/ppermute | solution.py:230
  534.6 72.0 %collective-permute-start.54 = (bf16[64,2048]{1,0:T(8,128)(2,1)}, bf16[64,2048]{1,0:T(8,128)(2,1)}, u32[]{:S(2)}, u32[]{:S(2)}) collective-permute-start(bf16[64,2048]{1,0:T(8,128)(2,1)} %get-tuple-element.162), channel_id=1, source_target_pairs={{0,24},{8,0},{16,8},{24,16},{1,25},{9,1},{17,9},{25,17},{2,26},{10... | collective-permute-start | bytes 786440 | tf_op jit(solution)/shard_map/ppermute | solution.py:530
  534.6 72.0 %collective-permute-start.53 = (bf16[64,2048]{1,0:T(8,128)(2,1)}, bf16[64,2048]{1,0:T(8,128)(2,1)}, u32[]{:S(2)}, u32[]{:S(2)}) collective-permute-start(bf16[64,2048]{1,0:T(8,128)(2,1)} %get-tuple-element.161), channel_id=1, source_target_pairs={{0,16},{8,24},{16,0},{24,8},{1,17},{9,25},{17,1},{25,9},{2,18},{10... | collective-permute-start | bytes 786440 | tf_op jit(solution)/shard_map/ppermute | solution.py:530
  534.6 73.6 %collective-permute-start.52 = (bf16[64,2048]{1,0:T(8,128)(2,1)}, bf16[64,2048]{1,0:T(8,128)(2,1)}, u32[]{:S(2)}, u32[]{:S(2)}) collective-permute-start(bf16[64,2048]{1,0:T(8,128)(2,1)} %get-tuple-element.160), channel_id=1, source_target_pairs={{0,8},{8,16},{16,24},{24,0},{1,9},{9,17},{17,25},{25,1},{2,10},{10... | collective-permute-start | bytes 786440 | tf_op jit(solution)/shard_map/ppermute | solution.py:530
  546.2 32.7 %collective-permute-start.49 = (bf16[256,2048]{1,0:T(8,128)(2,1)}, bf16[256,2048]{1,0:T(8,128)(2,1)}, u32[]{:S(2)}, u32[]{:S(2)}) collective-permute-start(bf16[256,2048]{1,0:T(8,128)(2,1)} %dynamic-slice_bitcast_fusion.1), channel_id=1, source_target_pairs={{0,2},{2,0},{1,3},{3,1},{4,6},{6,4},{5,7},{7,5},{8,10},{10,8},{9,1... | collective-permute-start | bytes 3145736 | tf_op jit(solution)/shard_map/ppermute | solution.py:230
  566.1 38.9 %all-to-all-start.5 = ((bf16[16,64,640]{2,1,0:T(8,128)(2,1)}), bf16[16,64,640]{2,1,0:T(8,128)(2,1)}, u32[]{:S(2)}, u32[]{:S(2)}) async-start(bf16[16,64,640]{2,1,0:T(8,128)(2,1)} %bitcast.236), calls=%async_computation.7 | async-start | bytes 2621440 | tf_op jit(solution)/shard_map/all_to_all | solution.py:512
  (65 other events, 737.7 us)
Sparse Core Ops, SparseCore 0:
  9.6 44.7 all-gather.8
  55.9 59.2 all-gather.6
  146.4 101.6 all-gather.4
  318.3 101.1 reduce-scatter.2
  465.5 56.0 reduce-scatter.4
